TPU v7x, 32 devices: a whole 2x2x4 slice. The times are simulated.
32 devices in a mesh: ctx: 4 (over y, x), fsdp: 8 (over z, core).
Axes of the slice: x: 2, y: 2, z: 4, core: 2. Of those that a mesh axis runs over, the one named last changes fastest.
Arguments:
- queries: bfloat16 [4096, 2048], P(('ctx', 'fsdp')), may hold values from -8 to 8
- keys: bfloat16 [4096, 1024], P(('ctx', 'fsdp')), may hold values from -8 to 8
- values: bfloat16 [4096, 1024], P(('ctx', 'fsdp')), may hold values from -6 to 6
- grad_out: bfloat16 [4096, 2048], P(('ctx', 'fsdp')), may hold values from -6 to 6
- segment: int32 [4096], P(('ctx', 'fsdp')), may hold values from 0 to 7, never falling along the last dimension, each value on 1 to 2048 neighbouring positions
Outputs:
- grad_queries: bfloat16 [4096, 2048], P(('ctx', 'fsdp'))
- grad_keys: bfloat16 [4096, 1024], P(('ctx', 'fsdp'))
- grad_values: bfloat16 [4096, 1024], P(('ctx', 'fsdp'))
Inputs may be any that keep to these rules, and one draw needn't show every extreme that they name: `segment`: document ids never fall along the sequence; every document holds 1 to 2048 tokens and one holds exactly 2048.
All inputs are finite; a program needn't handle non-finite values.
Results may differ from a plain program's by a relative error of at most 0.0071.
Values may be sent and summed in bfloat16 or wider, within the bound.
No kernel may reach another device: no remote copies, remote signals or barrier semaphores. Data moves between devices by JAX's collectives and lax.ppermute only.
A program may use at most 64 MiB of HBM per device.

v0:
```python
import jax
import jax.numpy as jnp
from jax import lax
from jax.sharding import PartitionSpec as P

HEAD_DIM = 128
WINDOW = 512


softcap = 50.0
inv_scale = 1.0 / 12.0


def from_behind(shard, axis, by):
    devices = lax.axis_size(axis)
    pairs = [(i, i + by) for i in range(devices) if 0 <= i + by < devices]
    return lax.ppermute(shard, axis, pairs)


def tile_grads(query_rows, key_rows, value_rows, grad_rows, visible):
    raw_scores = jnp.einsum(
        "ngrd,mgd->grnm", query_rows, key_rows, preferred_element_type=jnp.float32
    )
    capped = softcap * jnp.tanh(raw_scores * inv_scale / softcap)
    weights = jnp.where(visible[None, None], jnp.exp(capped), jnp.float32(0.0))
    totals = jnp.sum(weights, axis=-1, keepdims=True)
    probs = weights / totals
    probs_low = probs.astype(jnp.bfloat16)
    attended = jnp.einsum(
        "grnm,mgd->ngrd", probs_low, value_rows, preferred_element_type=jnp.float32
    )
    row_terms = jnp.transpose(
        jnp.sum(grad_rows.astype(jnp.float32) * attended, axis=-1), (1, 2, 0)
    )[..., None]
    dprobs = jnp.einsum("ngrd,mgd->grnm", grad_rows, value_rows, preferred_element_type=jnp.float32)
    dscore = probs * (dprobs - row_terms) * (1.0 - (capped / softcap) ** 2) * inv_scale
    dscore_low = dscore.astype(jnp.bfloat16)
    grad_q = jnp.einsum("grnm,mgd->ngrd", dscore_low, key_rows, preferred_element_type=jnp.float32)
    grad_k = jnp.einsum(
        "grnm,ngrd->mgd", dscore_low, query_rows, preferred_element_type=jnp.float32
    )
    grad_v = jnp.einsum("grnm,ngrd->mgd", probs_low, grad_rows, preferred_element_type=jnp.float32)
    return (grad_q, grad_k, grad_v)


def group_grads(query_rows, key_rows, value_rows, grad_rows, visible):
    kv_heads = query_rows.shape[1]
    group_step = 2
    step_count = kv_heads // group_step

    def split_heads(array):
        shaped = array.reshape((array.shape[0], step_count, group_step) + array.shape[2:])
        return jnp.moveaxis(shaped, 1, 0)

    def join_heads(array):
        joined = jnp.moveaxis(array, 0, 1)
        return joined.reshape((joined.shape[0], kv_heads) + joined.shape[3:])

    def per_step(pieces):
        return tile_grads(pieces[0], pieces[1], pieces[2], pieces[3], visible)

    grad_q, grad_k, grad_v = lax.map(
        per_step,
        (
            split_heads(query_rows),
            split_heads(key_rows),
            split_heads(value_rows),
            split_heads(grad_rows),
        ),
    )
    return (join_heads(grad_q), join_heads(grad_k), join_heads(grad_v))


def local(queries, keys, values, grad_out, segment):
    tok_rows = queries.shape[0]
    kv_width = keys.shape[1]
    kv_heads = kv_width // HEAD_DIM
    group_size = queries.shape[1] // kv_width
    reach = (WINDOW + tok_rows - 1) // tok_rows
    block_rows = (reach + 1) * tok_rows
    earlier = []
    for distance in range(1, reach + 1):
        earlier.append(from_behind((keys, values, segment), ("ctx", "fsdp"), distance))
    ordered = earlier[::-1] + [(keys, values, segment)]
    key_block = jnp.concatenate([member[0] for member in ordered], 0)
    value_block = jnp.concatenate([member[1] for member in ordered], 0)
    seg_block = jnp.concatenate([member[2] for member in ordered], 0)
    device_index = lax.axis_index(("ctx", "fsdp"))
    first_row = device_index * tok_rows
    query_pos = first_row + jnp.arange(tok_rows, dtype=jnp.int32)
    key_pos = first_row - reach * tok_rows + jnp.arange(block_rows, dtype=jnp.int32)
    offsets = query_pos[:, None] - key_pos[None, :]
    visible = (
        (segment[:, None] == seg_block[None, :])
        & (offsets >= 0)
        & (offsets < WINDOW)
        & (key_pos[None, :] >= 0)
    )
    query_rows = queries.reshape(tok_rows, kv_heads, group_size, HEAD_DIM)
    grad_rows = grad_out.reshape(tok_rows, kv_heads, group_size, HEAD_DIM)
    key_rows = key_block.reshape(block_rows, kv_heads, HEAD_DIM)
    value_rows = value_block.reshape(block_rows, kv_heads, HEAD_DIM)
    grad_q, grad_k, grad_v = group_grads(query_rows, key_rows, value_rows, grad_rows, visible)
    grad_k = grad_k.reshape(block_rows, kv_width)
    grad_v = grad_v.reshape(block_rows, kv_width)

    def piece_of(array, distance):
        return array[(reach - distance) * tok_rows : (reach - distance + 1) * tok_rows]

    total_k = piece_of(grad_k, 0)
    total_v = piece_of(grad_v, 0)
    for distance in range(1, reach + 1):
        arrived = from_behind(
            (piece_of(grad_k, distance), piece_of(grad_v, distance)), ("ctx", "fsdp"), -distance
        )
        total_k = total_k + arrived[0]
        total_v = total_v + arrived[1]
    grad_queries = grad_q.reshape(tok_rows, queries.shape[1]).astype(jnp.bfloat16)
    return (grad_queries, total_k.astype(jnp.bfloat16), total_v.astype(jnp.bfloat16))


def solution(mesh):
    return jax.shard_map(
        local,
        mesh=mesh,
        in_specs=(
            P(("ctx", "fsdp"), None),
            P(("ctx", "fsdp"), None),
            P(("ctx", "fsdp"), None),
            P(("ctx", "fsdp"), None),
            P(("ctx", "fsdp")),
        ),
        out_specs=(P(("ctx", "fsdp"), None), P(("ctx", "fsdp"), None), P(("ctx", "fsdp"), None)),
        check_vma=False,
    )
```

profile of v0, /device:TPU:26, one launch (start us, length us, event | category | flops | bytes accessed | tf_op | source)
XLA Modules:
  0.0 242.9 jit_solution(18286912084028265497)
XLA Ops:
  0.7 3.2 %collective-permute-start.6 = (s32[128]{0:T(128)}, s32[128]{0:T(128)S(1)}, u32[]{:S(2)}, u32[]{:S(2)}) collective-permute-start(s32[128]{0:T(128)} %param.11), channel_id=1, source_target_pairs={{0,2},{1,3},{2,4},{3,5},{4,6},{5,7},{6,8},{7,9},{8,10},{9,11},{10,... | collective-permute-start | bytes 1544 | tf_op jit(solution)/shard_map/ppermute | solution.py:17
  3.8 2.6 %collective-permute-start.5 = (s32[128]{0:T(128)}, s32[128]{0:T(128)S(1)}, u32[]{:S(2)}, u32[]{:S(2)}) collective-permute-start(s32[128]{0:T(128)} %param.11), channel_id=1, source_target_pairs={{0,3},{1,4},{2,5},{3,6},{4,7},{5,8},{6,9},{7,10},{8,11},{9,12},{10... | collective-permute-start | bytes 1544 | tf_op jit(solution)/shard_map/ppermute | solution.py:17
  6.5 3.6 %collective-permute-start.4 = (s32[128]{0:T(128)}, s32[128]{0:T(128)S(1)}, u32[]{:S(2)}, u32[]{:S(2)}) collective-permute-start(s32[128]{0:T(128)} %param.11), channel_id=1, source_target_pairs={{0,4},{1,5},{2,6},{3,7},{4,8},{5,9},{6,10},{7,11},{8,12},{9,13},{1... | collective-permute-start | bytes 1544 | tf_op jit(solution)/shard_map/ppermute | solution.py:17
  10.1 3.2 %collective-permute-start.7 = (s32[128]{0:T(128)}, s32[128]{0:T(128)S(1)}, u32[]{:S(2)}, u32[]{:S(2)}) collective-permute-start(s32[128]{0:T(128)} %param.11), channel_id=1, source_target_pairs={{0,1},{1,2},{2,3},{3,4},{4,5},{5,6},{6,7},{7,8},{8,9},{9,10},{10,1... | collective-permute-start | bytes 1544 | tf_op jit(solution)/shard_map/ppermute | solution.py:17
  14.4 2.8 %collective-permute-start.11 = (bf16[128,1024]{0,1:T(8,128)(2,1)S(1)}, bf16[128,1024]{0,1:T(8,128)(2,1)}, u32[]{:S(2)}, u32[]{:S(2)}) collective-permute-start(bf16[128,1024]{0,1:T(8,128)(2,1)S(1)} %copy.43), channel_id=1, source_target_pairs={{0,1},{1,2},{2,3},{3,4},{4,5},{5,6},{6,7},{7,8},{8,9},{9,10},{10,1... | collective-permute-start | bytes 786440 | tf_op jit(solution)/shard_map/ppermute | solution.py:17
  19.8 3.5 %collective-permute-start.10 = (bf16[128,1024]{0,1:T(8,128)(2,1)S(1)}, bf16[128,1024]{0,1:T(8,128)(2,1)S(1)}, u32[]{:S(2)}, u32[]{:S(2)}) collective-permute-start(bf16[128,1024]{0,1:T(8,128)(2,1)S(1)} %copy.43), channel_id=1, source_target_pairs={{0,2},{1,3},{2,4},{3,5},{4,6},{5,7},{6,8},{7,9},{8,10},{9,11},{10,... | collective-permute-start | bytes 786440 | tf_op jit(solution)/shard_map/ppermute | solution.py:17
  23.3 2.6 %collective-permute-start.2 = (bf16[128,1024]{0,1:T(8,128)(2,1)S(1)}, bf16[128,1024]{0,1:T(8,128)(2,1)S(1)}, u32[]{:S(2)}, u32[]{:S(2)}) collective-permute-start(bf16[128,1024]{0,1:T(8,128)(2,1)S(1)} %copy.37), channel_id=1, source_target_pairs={{0,2},{1,3},{2,4},{3,5},{4,6},{5,7},{6,8},{7,9},{8,10},{9,11},{10,... | collective-permute-start | bytes 786440 | tf_op jit(solution)/shard_map/ppermute | solution.py:17
  25.9 3.8 %collective-permute-start = (bf16[128,1024]{0,1:T(8,128)(2,1)S(1)}, bf16[128,1024]{0,1:T(8,128)(2,1)S(1)}, u32[]{:S(2)}, u32[]{:S(2)}) collective-permute-start(bf16[128,1024]{0,1:T(8,128)(2,1)S(1)} %copy.37), channel_id=1, source_target_pairs={{0,4},{1,5},{2,6},{3,7},{4,8},{5,9},{6,10},{7,11},{8,12},{9,13},{1... | collective-permute-start | bytes 786440 | tf_op jit(solution)/shard_map/ppermute | solution.py:17
  31.7 17.9 %collective-permute-done = bf16[128,1024]{0,1:T(8,128)(2,1)S(1)} collective-permute-done((bf16[128,1024]{0,1:T(8,128)(2,1)S(1)}, bf16[128,1024]{0,1:T(8,128)(2,1)S(1)}, u32[]{:S(2)}, u32[]{:S(2)}) %collective-permute-start) | collective-permute-done | bytes 262176 | tf_op jit(solution)/shard_map/ppermute | solution.py:17
  52.0 3.6 %collective-permute-done.1 = bf16[128,1024]{0,1:T(8,128)(2,1)S(1)} collective-permute-done((bf16[128,1024]{0,1:T(8,128)(2,1)S(1)}, bf16[128,1024]{0,1:T(8,128)(2,1)S(1)}, u32[]{:S(2)}, u32[]{:S(2)}) %collective-permute-start.1) | collective-permute-done | bytes 262176 | tf_op jit(solution)/shard_map/ppermute | solution.py:17
  55.5 6.3 %collective-permute-start.9 = (bf16[128,1024]{0,1:T(8,128)(2,1)S(1)}, bf16[128,1024]{0,1:T(8,128)(2,1)S(1)}, u32[]{:S(2)}, u32[]{:S(2)}) collective-permute-start(bf16[128,1024]{0,1:T(8,128)(2,1)S(1)} %copy.43), channel_id=1, source_target_pairs={{0,3},{1,4},{2,5},{3,6},{4,7},{5,8},{6,9},{7,10},{8,11},{9,12},{10... | collective-permute-start | bytes 786440 | tf_op jit(solution)/shard_map/ppermute | solution.py:17
  64.1 16.5 %collective-permute-done.8 = bf16[128,1024]{0,1:T(8,128)(2,1)S(1)} collective-permute-done((bf16[128,1024]{0,1:T(8,128)(2,1)S(1)}, bf16[128,1024]{0,1:T(8,128)(2,1)S(1)}, u32[]{:S(2)}, u32[]{:S(2)}) %collective-permute-start.8) | collective-permute-done | bytes 262176 | tf_op jit(solution)/shard_map/ppermute | solution.py:17
  81.9 30.3 %while.17 = (s32[]{:T(128)}, bf16[4,128,2,2,128]{1,4,3,2,0:T(8,128)(2,1)}, f32[4,640,2,128]{1,3,2,0:T(8,128)}, f32[4,640,2,128]{1,3,2,0:T(8,128)}, bf16[4,640,2,...) while((s32[]{:T(128)}, ...), condition=%wide.region_3.4_spmd.clone, body=%wide.region_0.3_spmd.clone.sunk | while | flops 509983744 | bytes 16471885 | solution.py:62
  93.5 2.3 fusion.78
  112.1 2.9 %fusion.38 = (f32[128,4,2,128]{0,3,2,1:T(8,128)}, f32[128,4,2,128]{0,3,2,1:T(8,128)}, f32[128,4,2,128]{0,3,2,1:T(8,128)S(1)}, f32[128,4,2,128]{0,3,2,1:T(8,128)}, f32[128,4,2,128]{0,3,2,1:T(8,128)S(1)}) fusion(f32[640,4,2,128]{0,3,2,1:T(8,128)} %bitcast.183), kind=kLoop, calls=%fused_computation.67 | loop fusion | bytes 5242880 | tf_op jit(solution)/shard_map/slice | solution.py:108
  118.3 3.4 %collective-permute-start.17 = (f32[128,1024]{1,0:T(8,128)}, f32[128,1024]{1,0:T(8,128)}, u32[]{:S(2)}, u32[]{:S(2)}) collective-permute-start(f32[128,1024]{1,0:T(8,128)} %copy.85), channel_id=1, source_target_pairs={{2,0},{3,1},{4,2},{5,3},{6,4},{7,5},{8,6},{9,7},{10,8},{11,9},{12,... | collective-permute-start | bytes 1572872 | tf_op jit(solution)/shard_map/ppermute | solution.py:17
  121.6 6.1 %collective-permute-start.18 = (f32[128,1024]{1,0:T(8,128)}, f32[128,1024]{1,0:T(8,128)}, u32[]{:S(2)}, u32[]{:S(2)}) collective-permute-start(f32[128,1024]{1,0:T(8,128)} %copy.86), channel_id=1, source_target_pairs={{3,0},{4,1},{5,2},{6,3},{7,4},{8,5},{9,6},{10,7},{11,8},{12,9},{13... | collective-permute-start | bytes 1572872 | tf_op jit(solution)/shard_map/ppermute | solution.py:17
  140.9 2.6 %collective-permute-start.13 = (f32[128,1024]{1,0:T(8,128)}, f32[128,1024]{1,0:T(8,128)}, u32[]{:S(2)}, u32[]{:S(2)}) collective-permute-start(f32[128,1024]{1,0:T(8,128)} %copy.80), channel_id=1, source_target_pairs={{2,0},{3,1},{4,2},{5,3},{6,4},{7,5},{8,6},{9,7},{10,8},{11,9},{12,... | collective-permute-start | bytes 1572872 | tf_op jit(solution)/shard_map/ppermute | solution.py:17
  145.4 7.1 %collective-permute-done.18 = f32[128,1024]{1,0:T(8,128)} collective-permute-done((f32[128,1024]{1,0:T(8,128)}, f32[128,1024]{1,0:T(8,128)}, u32[]{:S(2)}, u32[]{:S(2)}) %collective-permute-start.18) | collective-permute-done | bytes 524320 | tf_op jit(solution)/shard_map/ppermute | solution.py:17
  152.6 58.9 %collective-permute-start.15 = (f32[128,1024]{1,0:T(8,128)S(1)}, f32[128,1024]{1,0:T(8,128)}, u32[]{:S(2)}, u32[]{:S(2)}) collective-permute-start(f32[128,1024]{1,0:T(8,128)S(1)} %copy.82), channel_id=1, source_target_pairs={{4,0},{5,1},{6,2},{7,3},{8,4},{9,5},{10,6},{11,7},{12,8},{13,9},{1... | collective-permute-start | bytes 1572872 | tf_op jit(solution)/shard_map/ppermute | solution.py:17
  211.5 6.5 %collective-permute-done.19 = f32[128,1024]{1,0:T(8,128)} collective-permute-done((f32[128,1024]{1,0:T(8,128)}, f32[128,1024]{1,0:T(8,128)}, u32[]{:S(2)}, u32[]{:S(2)}) %collective-permute-start.19) | collective-permute-done | bytes 524320 | tf_op jit(solution)/shard_map/ppermute | solution.py:17
  221.4 2.4 add_convert_fusion
  223.8 16.7 %collective-permute-done.15 = f32[128,1024]{1,0:T(8,128)} collective-permute-done((f32[128,1024]{1,0:T(8,128)S(1)}, f32[128,1024]{1,0:T(8,128)}, u32[]{:S(2)}, u32[]{:S(2)}) %collective-permute-start.15) | collective-permute-done | bytes 524320 | tf_op jit(solution)/shard_map/ppermute | solution.py:17
  240.5 2.4 add_convert_fusion.1
  (132 shorter events, 60.5 us)
Async XLA Ops:
  0.6 18.8 %copy-start.6 = (bf16[128,2048]{1,0:T(8,128)(2,1)S(1)}, bf16[128,2048]{1,0:T(8,128)(2,1)}, u32[]{:S(2)}) copy-start(bf16[128,2048]{1,0:T(8,128)(2,1)} %param.10) | copy-start | bytes 1572868
  0.7 25.3 %collective-permute-start.6 = (s32[128]{0:T(128)}, s32[128]{0:T(128)S(1)}, u32[]{:S(2)}, u32[]{:S(2)}) collective-permute-start(s32[128]{0:T(128)} %param.11), channel_id=1, source_target_pairs={{0,2},{1,3},{2,4},{3,5},{4,6},{5,7},{6,8},{7,9},{8,10},{9,11},{10,... | collective-permute-start | bytes 1544 | tf_op jit(solution)/shard_map/ppermute | solution.py:17
  3.8 19.4 %collective-permute-start.5 = (s32[128]{0:T(128)}, s32[128]{0:T(128)S(1)}, u32[]{:S(2)}, u32[]{:S(2)}) collective-permute-start(s32[128]{0:T(128)} %param.11), channel_id=1, source_target_pairs={{0,3},{1,4},{2,5},{3,6},{4,7},{5,8},{6,9},{7,10},{8,11},{9,12},{10... | collective-permute-start | bytes 1544 | tf_op jit(solution)/shard_map/ppermute | solution.py:17
  6.5 13.3 %collective-permute-start.4 = (s32[128]{0:T(128)}, s32[128]{0:T(128)S(1)}, u32[]{:S(2)}, u32[]{:S(2)}) collective-permute-start(s32[128]{0:T(128)} %param.11), channel_id=1, source_target_pairs={{0,4},{1,5},{2,6},{3,7},{4,8},{5,9},{6,10},{7,11},{8,12},{9,13},{1... | collective-permute-start | bytes 1544 | tf_op jit(solution)/shard_map/ppermute | solution.py:17
  10.1 19.6 %collective-permute-start.7 = (s32[128]{0:T(128)}, s32[128]{0:T(128)S(1)}, u32[]{:S(2)}, u32[]{:S(2)}) collective-permute-start(s32[128]{0:T(128)} %param.11), channel_id=1, source_target_pairs={{0,1},{1,2},{2,3},{3,4},{4,5},{5,6},{6,7},{7,8},{8,9},{9,10},{10,1... | collective-permute-start | bytes 1544 | tf_op jit(solution)/shard_map/ppermute | solution.py:17
  14.4 66.4 %collective-permute-start.11 = (bf16[128,1024]{0,1:T(8,128)(2,1)S(1)}, bf16[128,1024]{0,1:T(8,128)(2,1)}, u32[]{:S(2)}, u32[]{:S(2)}) collective-permute-start(bf16[128,1024]{0,1:T(8,128)(2,1)S(1)} %copy.43), channel_id=1, source_target_pairs={{0,1},{1,2},{2,3},{3,4},{4,5},{5,6},{6,7},{7,8},{8,9},{9,10},{10,1... | collective-permute-start | bytes 786440 | tf_op jit(solution)/shard_map/ppermute | solution.py:17
  19.8 60.9 %collective-permute-start.10 = (bf16[128,1024]{0,1:T(8,128)(2,1)S(1)}, bf16[128,1024]{0,1:T(8,128)(2,1)S(1)}, u32[]{:S(2)}, u32[]{:S(2)}) collective-permute-start(bf16[128,1024]{0,1:T(8,128)(2,1)S(1)} %copy.43), channel_id=1, source_target_pairs={{0,2},{1,3},{2,4},{3,5},{4,6},{5,7},{6,8},{7,9},{8,10},{9,11},{10,... | collective-permute-start | bytes 786440 | tf_op jit(solution)/shard_map/ppermute | solution.py:17
  23.3 38.6 %collective-permute-start.2 = (bf16[128,1024]{0,1:T(8,128)(2,1)S(1)}, bf16[128,1024]{0,1:T(8,128)(2,1)S(1)}, u32[]{:S(2)}, u32[]{:S(2)}) collective-permute-start(bf16[128,1024]{0,1:T(8,128)(2,1)S(1)} %copy.37), channel_id=1, source_target_pairs={{0,2},{1,3},{2,4},{3,5},{4,6},{5,7},{6,8},{7,9},{8,10},{9,11},{10,... | collective-permute-start | bytes 786440 | tf_op jit(solution)/shard_map/ppermute | solution.py:17
  25.9 23.7 %collective-permute-start = (bf16[128,1024]{0,1:T(8,128)(2,1)S(1)}, bf16[128,1024]{0,1:T(8,128)(2,1)S(1)}, u32[]{:S(2)}, u32[]{:S(2)}) collective-permute-start(bf16[128,1024]{0,1:T(8,128)(2,1)S(1)} %copy.37), channel_id=1, source_target_pairs={{0,4},{1,5},{2,6},{3,7},{4,8},{5,9},{6,10},{7,11},{8,12},{9,13},{1... | collective-permute-start | bytes 786440 | tf_op jit(solution)/shard_map/ppermute | solution.py:17
  29.7 25.8 %collective-permute-start.1 = (bf16[128,1024]{0,1:T(8,128)(2,1)S(1)}, bf16[128,1024]{0,1:T(8,128)(2,1)S(1)}, u32[]{:S(2)}, u32[]{:S(2)}) collective-permute-start(bf16[128,1024]{0,1:T(8,128)(2,1)S(1)} %copy.37), channel_id=1, source_target_pairs={{0,3},{1,4},{2,5},{3,6},{4,7},{5,8},{6,9},{7,10},{8,11},{9,12},{10... | collective-permute-start | bytes 786440 | tf_op jit(solution)/shard_map/ppermute | solution.py:17
  49.6 14.3 %collective-permute-start.3 = (bf16[128,1024]{0,1:T(8,128)(2,1)S(1)}, bf16[128,1024]{0,1:T(8,128)(2,1)S(1)}, u32[]{:S(2)}, u32[]{:S(2)}) collective-permute-start(bf16[128,1024]{0,1:T(8,128)(2,1)S(1)} %copy.37), channel_id=1, source_target_pairs={{0,1},{1,2},{2,3},{3,4},{4,5},{5,6},{6,7},{7,8},{8,9},{9,10},{10,1... | collective-permute-start | bytes 786440 | tf_op jit(solution)/shard_map/ppermute | solution.py:17
  55.5 25.1 %collective-permute-start.9 = (bf16[128,1024]{0,1:T(8,128)(2,1)S(1)}, bf16[128,1024]{0,1:T(8,128)(2,1)S(1)}, u32[]{:S(2)}, u32[]{:S(2)}) collective-permute-start(bf16[128,1024]{0,1:T(8,128)(2,1)S(1)} %copy.43), channel_id=1, source_target_pairs={{0,3},{1,4},{2,5},{3,6},{4,7},{5,8},{6,9},{7,10},{8,11},{9,12},{10... | collective-permute-start | bytes 786440 | tf_op jit(solution)/shard_map/ppermute | solution.py:17
  61.9 18.6 %collective-permute-start.8 = (bf16[128,1024]{0,1:T(8,128)(2,1)S(1)}, bf16[128,1024]{0,1:T(8,128)(2,1)S(1)}, u32[]{:S(2)}, u32[]{:S(2)}) collective-permute-start(bf16[128,1024]{0,1:T(8,128)(2,1)S(1)} %copy.43), channel_id=1, source_target_pairs={{0,4},{1,5},{2,6},{3,7},{4,8},{5,9},{6,10},{7,11},{8,12},{9,13},{1... | collective-permute-start | bytes 786440 | tf_op jit(solution)/shard_map/ppermute | solution.py:17
  116.1 19.7 %copy-start = (f32[4,640,2,128]{1,3,2,0:T(8,128)S(1)}, f32[4,640,2,128]{1,3,2,0:T(8,128)}, u32[]{:S(2)}) copy-start(f32[4,640,2,128]{1,3,2,0:T(8,128)} %get-tuple-element.120) | copy-start | bytes 7864324
  118.3 25.2 %collective-permute-start.17 = (f32[128,1024]{1,0:T(8,128)}, f32[128,1024]{1,0:T(8,128)}, u32[]{:S(2)}, u32[]{:S(2)}) collective-permute-start(f32[128,1024]{1,0:T(8,128)} %copy.85), channel_id=1, source_target_pairs={{2,0},{3,1},{4,2},{5,3},{6,4},{7,5},{8,6},{9,7},{10,8},{11,9},{12,... | collective-permute-start | bytes 1572872 | tf_op jit(solution)/shard_map/ppermute | solution.py:17
  121.6 30.9 %collective-permute-start.18 = (f32[128,1024]{1,0:T(8,128)}, f32[128,1024]{1,0:T(8,128)}, u32[]{:S(2)}, u32[]{:S(2)}) collective-permute-start(f32[128,1024]{1,0:T(8,128)} %copy.86), channel_id=1, source_target_pairs={{3,0},{4,1},{5,2},{6,3},{7,4},{8,5},{9,6},{10,7},{11,8},{12,9},{13... | collective-permute-start | bytes 1572872 | tf_op jit(solution)/shard_map/ppermute | solution.py:17
  129.8 88.1 %collective-permute-start.19 = (f32[128,1024]{1,0:T(8,128)}, f32[128,1024]{1,0:T(8,128)}, u32[]{:S(2)}, u32[]{:S(2)}) collective-permute-start(f32[128,1024]{1,0:T(8,128)} %copy.87), channel_id=1, source_target_pairs={{4,0},{5,1},{6,2},{7,3},{8,4},{9,5},{10,6},{11,7},{12,8},{13,9},{1... | collective-permute-start | bytes 1572872 | tf_op jit(solution)/shard_map/ppermute | solution.py:17
  133.8 87.5 %collective-permute-start.16 = (f32[128,1024]{1,0:T(8,128)}, f32[128,1024]{1,0:T(8,128)}, u32[]{:S(2)}, u32[]{:S(2)}) collective-permute-start(f32[128,1024]{1,0:T(8,128)} %copy.84), channel_id=1, source_target_pairs={{1,0},{2,1},{3,2},{4,3},{5,4},{6,5},{7,6},{8,7},{9,8},{10,9},{11,1... | collective-permute-start | bytes 1572872 | tf_op jit(solution)/shard_map/ppermute | solution.py:17
  138.9 81.0 %copy-start.9 = (bf16[4,128,2,2,128]{1,4,3,2,0:T(8,128)(2,1)S(1)}, bf16[4,128,2,2,128]{1,4,3,2,0:T(8,128)(2,1)}, u32[]{:S(2)}) copy-start(bf16[4,128,2,2,128]{1,4,3,2,0:T(8,128)(2,1)} %get-tuple-element.119) | copy-start | bytes 1572868
  140.9 80.2 %copy-start.1 = (f32[128,4,2,128]{0,3,2,1:T(8,128)S(1)}, f32[128,4,2,128]{0,3,2,1:T(8,128)}, u32[]{:S(2)}) copy-start(f32[128,4,2,128]{0,3,2,1:T(8,128)} %get-tuple-element.205) | copy-start | bytes 1572868
  140.9 82.9 %collective-permute-start.13 = (f32[128,1024]{1,0:T(8,128)}, f32[128,1024]{1,0:T(8,128)}, u32[]{:S(2)}, u32[]{:S(2)}) collective-permute-start(f32[128,1024]{1,0:T(8,128)} %copy.80), channel_id=1, source_target_pairs={{2,0},{3,1},{4,2},{5,3},{6,4},{7,5},{8,6},{9,7},{10,8},{11,9},{12,... | collective-permute-start | bytes 1572872 | tf_op jit(solution)/shard_map/ppermute | solution.py:17
  143.5 80.2 %collective-permute-start.14 = (f32[128,1024]{1,0:T(8,128)}, f32[128,1024]{1,0:T(8,128)}, u32[]{:S(2)}, u32[]{:S(2)}) collective-permute-start(f32[128,1024]{1,0:T(8,128)} %copy.81), channel_id=1, source_target_pairs={{3,0},{4,1},{5,2},{6,3},{7,4},{8,5},{9,6},{10,7},{11,8},{12,9},{13... | collective-permute-start | bytes 1572872 | tf_op jit(solution)/shard_map/ppermute | solution.py:17
  152.6 87.9 %collective-permute-start.15 = (f32[128,1024]{1,0:T(8,128)S(1)}, f32[128,1024]{1,0:T(8,128)}, u32[]{:S(2)}, u32[]{:S(2)}) collective-permute-start(f32[128,1024]{1,0:T(8,128)S(1)} %copy.82), channel_id=1, source_target_pairs={{4,0},{5,1},{6,2},{7,3},{8,4},{9,5},{10,6},{11,7},{12,8},{13,9},{1... | collective-permute-start | bytes 1572872 | tf_op jit(solution)/shard_map/ppermute | solution.py:17
  218.0 22.5 %collective-permute-start.12 = (f32[128,1024]{1,0:T(8,128)S(1)}, f32[128,1024]{1,0:T(8,128)}, u32[]{:S(2)}, u32[]{:S(2)}) collective-permute-start(f32[128,1024]{1,0:T(8,128)S(1)} %copy.79), channel_id=1, source_target_pairs={{1,0},{2,1},{3,2},{4,3},{5,4},{6,5},{7,6},{8,7},{9,8},{10,9},{11,1... | collective-permute-start | bytes 1572872 | tf_op jit(solution)/shard_map/ppermute | solution.py:17
  (13 other events, 54.4 us)
where the time goes:
time: 244 us; the launch traced here: 243 us
  starting transfers between devices  116 us (48%)
  waiting for transfers between devices  68.3 us (28%)
  matrix products  25.7 us (11%)
  local copies, waits for them, and re-layouts  23.8 us (10%)
  other arithmetic  7.23 us (3%)
    ppermute x20, starting transfers between devices, from_behind(): return lax.ppermute(shard, axis, pairs)  116 us
    ppermute x20, waiting for transfers between devices, from_behind(): return lax.ppermute(shard, axis, pairs)  68.3 us
    slice x12, local copies, waits for them, and re-layouts, piece_of(): array[(reach - distance) * tok_rows:(reach - distance + 1) * tok_rows]  15.7 us
    dot_general x4, matrix products, tile_grads(): jnp.einsum('grnm,ngrd->mgd', dscore_low, query_rows, preferred_element_ty...  9.06 us
    dot_general x4, matrix products, tile_grads(): jnp.einsum('ngrd,mgd->grnm', query_rows, key_rows, preferred_element_type...  5.96 us
    unnamed x34, local copies, waits for them, and re-layouts  5.01 us
  transfers between devices with their start and end apart: 20, of which 6 were waited for; matrix products, arithmetic and copies ran while one was open for 7% of the time, Pallas kernels for 0%

commit v1 on v0

v1 whole, which is shorter than its diff:
```python
import functools

import jax
import jax.numpy as jnp
from jax import lax
from jax.experimental import pallas as pl
from jax.experimental.pallas import tpu as pltpu
from jax.sharding import PartitionSpec as P

HEAD_DIM = 128
WINDOW = 512
SOFTCAP = 50.0
SCALE = 1.0 / 12.0
LOG2E = 1.4426950408889634
AXES = ("ctx", "fsdp")
NT = (((1,), (1,)), ((), ()))
NN = (((1,), (0,)), ((), ()))
SEG_ROWS = 16


def dot(a, b, dims):
    return lax.dot_general(a, b, dims, preferred_element_type=jnp.float32)


def swap(x):
    n = lax.axis_size(AXES)
    return lax.ppermute(x, AXES, [(i, i ^ 1) for i in range(n)])


def hop(x, chips):
    n = lax.axis_size(AXES)
    by = 2 * chips
    return lax.ppermute(x, AXES, [(i, i + by) for i in range(n) if 0 <= i + by < n])


def fill_starts(core, lo_ref, sega_ref, segb_ref, lo_s, tok):
    lo = lo_ref[...]
    seg0 = lo[2:3, 0:1].astype(jnp.float32)
    far = jnp.where(sega_ref[0:1, : 2 * tok].astype(jnp.float32) == seg0, 1.0, 0.0)
    far = far + jnp.where(segb_ref[0:1, : 2 * tok].astype(jnp.float32) == seg0, 1.0, 0.0)
    count = jnp.sum(far, axis=1, keepdims=True).astype(jnp.int32)
    row = lax.broadcasted_iota(jnp.int32, (1, tok), 1)
    for r in range(2):
        half = lax.bitwise_xor(core, r)
        mine = lo[r : r + 1]
        mine = jnp.where(mine < 0, WINDOW - count, mine) - half * tok
        mine = jnp.maximum(mine, row + 1)
        lo_s[r, 0:1, :] = jnp.concatenate([mine, mine], 1)


def gather_keys(core, pieces, dst, tok):
    for chip, ref in enumerate(pieces):
        for r in range(2):
            at = 2 * tok * chip + tok * lax.bitwise_xor(core, r)
            dst[pl.ds(pl.multiple_of(at, tok), tok), :] = ref[pl.ds(r * tok, tok), :]


def heads_of(ref):
    return jnp.concatenate([ref[:, :HEAD_DIM], ref[:, HEAD_DIM:]], 0)


def weights_of(key_rows, q_rows, lo, jj, last, tok):
    s = dot(key_rows, q_rows, NT)
    t = jnp.tanh(s * (SCALE / SOFTCAP))
    w = jnp.exp2(t * (SOFTCAP * LOG2E))
    pos = lax.broadcasted_iota(jnp.int32, s.shape, 0)
    ok = pos + jj * tok >= lo
    if last:
        col = lax.broadcasted_iota(jnp.int32, s.shape, 1)
        col = jnp.where(col >= tok, col - tok, col)
        ok = ok & (pos <= col)
    return t, jnp.where(ok, w, 0.0)


def fold(x):
    return jnp.sum(x.reshape(x.shape[0] // 8, 8, x.shape[1]), axis=0)


def value_kernel(tok, core_ref, lo_ref, sega, segb, q0, q1, g0, g1, kb, ka, kc,
                 dvb, dva, dvc, inv_ref, lo_s, k_s, w_s, dv_s):
    core = core_ref[0]
    blocks = WINDOW // tok + 1

    @pl.when(pl.program_id(0) == 0)
    def _():
        fill_starts(core, lo_ref, sega, segb, lo_s, tok)

    gather_keys(core, (kb, ka, kc), k_s, tok)
    dv_s[...] = jnp.zeros_like(dv_s)
    for r, (q, g) in enumerate(((q0, g0), (q1, g1))):
        base = lax.bitwise_xor(core, r) * tok
        q_rows, g_rows = heads_of(q), heads_of(g)
        lo = lo_s[r, 0:1, :]
        total = jnp.zeros((8, 2 * tok), jnp.float32)
        for jj in range(blocks):
            rows = pl.ds(pl.multiple_of(base + jj * tok, tok), tok)
            _, w = weights_of(k_s[rows, :], q_rows, lo, jj, jj == blocks - 1, tok)
            w_s[jj] = w
            total = total + fold(w)
        inv = 1.0 / jnp.sum(total, axis=0, keepdims=True)
        inv_ref[0, r : r + 1, :] = inv
        for jj in range(blocks):
            rows = pl.ds(pl.multiple_of(base + jj * tok, tok), tok)
            low = (w_s[jj] * inv).astype(jnp.bfloat16)
            dv_s[rows, :] += dot(low, g_rows, NN)
    put_back(core, dv_s, (dvb, dva, dvc), tok)


def put_back(core, src, outs, tok):
    for chip, ref in enumerate(outs):
        for r in range(2):
            at = 2 * tok * chip + tok * lax.bitwise_xor(core, r)
            piece = src[pl.ds(pl.multiple_of(at, tok), tok), :]
            ref[pl.ds(r * tok, tok), :] = piece.astype(ref.dtype)


def score_kernel(tok, core_ref, lo_ref, sega, segb, q0, q1, g0, g1, kb, ka, kc, vb, va, vc,
                 inv_ref, dkb, dka, dkc, dq0, dq1, lo_s, k_s, v_s, p_s, t_s, dp_s, dk_s):
    core = core_ref[0]
    blocks = WINDOW // tok + 1

    @pl.when(pl.program_id(0) == 0)
    def _():
        fill_starts(core, lo_ref, sega, segb, lo_s, tok)

    gather_keys(core, (kb, ka, kc), k_s, tok)
    gather_keys(core, (vb, va, vc), v_s, tok)
    dk_s[...] = jnp.zeros_like(dk_s)
    for r, (q, g, dq) in enumerate(((q0, g0, dq0), (q1, g1, dq1))):
        base = lax.bitwise_xor(core, r) * tok
        q_rows, g_rows = heads_of(q), heads_of(g)
        lo = lo_s[r, 0:1, :]
        inv = inv_ref[0, r : r + 1, :]
        term = jnp.zeros((8, 2 * tok), jnp.float32)
        for jj in range(blocks):
            rows = pl.ds(pl.multiple_of(base + jj * tok, tok), tok)
            t, w = weights_of(k_s[rows, :], q_rows, lo, jj, jj == blocks - 1, tok)
            p = w * inv
            dp = dot(v_s[rows, :], g_rows, NT)
            term = term + fold(p.astype(jnp.bfloat16).astype(jnp.float32) * dp)
            p_s[jj] = p * (SCALE - t * t * SCALE)
            dp_s[jj] = dp
        term = jnp.sum(term, axis=0, keepdims=True)
        dq_t = jnp.zeros((HEAD_DIM, 2 * tok), jnp.float32)
        for jj in range(blocks):
            rows = pl.ds(pl.multiple_of(base + jj * tok, tok), tok)
            ds = (p_s[jj] * (dp_s[jj] - term)).astype(jnp.bfloat16)
            dk_s[rows, :] += dot(ds, q_rows, NN)
            dq_t = dq_t + dot(k_s[rows, :].T, ds, NN)
        dq_rows = dq_t.T.astype(jnp.bfloat16)
        dq[:, :HEAD_DIM] = dq_rows[:tok]
        dq[:, HEAD_DIM:] = dq_rows[tok:]
    put_back(core, dk_s, (dkb, dka, dkc), tok)


def local(queries, keys, values, grad_out, segment):
    tok = queries.shape[0]
    kv_width = keys.shape[1]
    half = kv_width // 2
    groups = half // HEAD_DIM
    q_half = queries.shape[1] // 2
    bf16, f32 = jnp.bfloat16, jnp.float32
    core = lax.rem(lax.axis_index(AXES), 2)
    core_arr = core.reshape(1).astype(jnp.int32)

    def part(x, which, width):
        return lax.dynamic_slice(x, (0, which * width), (x.shape[0], width))

    seg_row = jnp.pad((segment + 1).astype(bf16)[None, :], ((0, SEG_ROWS - 1), (0, half - tok)))
    k_in = swap(jnp.concatenate([part(keys, 1 - core, half), seg_row], 0))
    v_in = swap(part(values, 1 - core, half))
    qg_in = swap(jnp.concatenate([part(queries, 1 - core, q_half), part(grad_out, 1 - core, q_half)], 0))
    seg_both = jnp.concatenate([(segment + 1).astype(bf16), k_in[tok, :tok]])
    both_row = jnp.pad(seg_both[None, :], ((0, SEG_ROWS - 1), (0, half - 2 * tok)))
    kc = jnp.concatenate([part(keys, core, half), k_in[:tok], both_row], 0)
    vc = jnp.concatenate([part(values, core, half), v_in], 0)
    ka = hop(kc, 1)
    va = hop(vc, 1)
    kb = hop(ka, 1)
    vb = hop(va, 1)

    seg_f = seg_both.astype(f32)
    seg0 = jnp.min(seg_f)
    before = jnp.sum((seg_f[:, None] < seg_f[None, :]).astype(jnp.int32), axis=0)
    starts = jnp.where(seg_f == seg0, -1, WINDOW + before).reshape(2, tok)
    lo = jnp.concatenate([starts, jnp.full((6, tok), seg0.astype(jnp.int32), jnp.int32)], 0)

    def at_own(g, c):
        return (0, c[0] * groups + g)

    def at_g(g, c):
        return (0, g)

    def at_seg(g, c):
        return (2 * tok // SEG_ROWS, 0)

    q_block = (tok, 2 * HEAD_DIM)
    kv_block = (2 * tok, HEAD_DIM)
    common_in = [
        pl.BlockSpec((8, tok), lambda g, c: (0, 0)),
        pl.BlockSpec((SEG_ROWS, half), at_seg),
        pl.BlockSpec((SEG_ROWS, half), at_seg),
        pl.BlockSpec(q_block, at_own),
        pl.BlockSpec(q_block, at_g),
        pl.BlockSpec(q_block, at_own),
        pl.BlockSpec(q_block, lambda g, c: (1, g)),
        pl.BlockSpec(kv_block, at_g),
        pl.BlockSpec(kv_block, at_g),
        pl.BlockSpec(kv_block, at_g),
    ]
    common = (core_arr, lo, ka, kb, queries, qg_in, grad_out, qg_in, kb, ka, kc)
    kv_out = [pl.BlockSpec(kv_block, at_g)] * 3
    inv_spec = pl.BlockSpec((1, 8, 2 * tok), lambda g, c: (g, 0, 0))
    kv_shapes = [
        jax.ShapeDtypeStruct((2 * tok, half), bf16),
        jax.ShapeDtypeStruct((2 * tok, half), f32),
        jax.ShapeDtypeStruct((2 * tok, half), f32),
    ]
    blocks = WINDOW // tok + 1
    window = WINDOW + 2 * tok
    tile = pltpu.VMEM((blocks, tok, 2 * tok), f32)
    lo_s = pltpu.VMEM((2, 8, 2 * tok), jnp.int32)
    k_s = pltpu.VMEM((window, HEAD_DIM), bf16)
    acc_s = pltpu.VMEM((window, HEAD_DIM), f32)
    params = pltpu.CompilerParams(vmem_limit_bytes=32 * 1024 * 1024)
    dvb, dva, dvc, inv = pl.pallas_call(
        functools.partial(value_kernel, tok),
        grid_spec=pltpu.PrefetchScalarGridSpec(
            num_scalar_prefetch=1,
            grid=(groups,),
            in_specs=common_in,
            out_specs=kv_out + [inv_spec],
            scratch_shapes=[lo_s, k_s, tile, acc_s],
        ),
        out_shape=kv_shapes + [jax.ShapeDtypeStruct((groups, 8, 2 * tok), f32)],
        compiler_params=params,
        name="value_grads",
    )(*common)
    cv = hop(dvb, -1)
    dkb, dka, dkc, dq0, dq1 = pl.pallas_call(
        functools.partial(score_kernel, tok),
        grid_spec=pltpu.PrefetchScalarGridSpec(
            num_scalar_prefetch=1,
            grid=(groups,),
            in_specs=common_in + [pl.BlockSpec(kv_block, at_g)] * 3 + [inv_spec],
            out_specs=kv_out + [pl.BlockSpec(q_block, at_g)] * 2,
            scratch_shapes=[lo_s, k_s, k_s, tile, tile, tile, acc_s],
        ),
        out_shape=kv_shapes + [jax.ShapeDtypeStruct((tok, q_half), bf16)] * 2,
        compiler_params=params,
        name="score_grads",
    )(*common, vb, va, vc, inv)
    ck = hop(dkb, -1)
    dv = hop((dva + cv.astype(f32)).astype(bf16), -1)
    dk = hop((dka + ck.astype(f32)).astype(bf16), -1)
    sum_v = dvc + dv.astype(f32)
    sum_k = dkc + dk.astype(f32)

    def settle(total):
        mine = total[:tok]
        other = swap(total[tok:].astype(bf16))
        return mine.astype(bf16), other

    def place(mine, other):
        first = jnp.where(core == 0, mine, other)
        second = jnp.where(core == 0, other, mine)
        return jnp.concatenate([first, second], 1)

    grad_q = place(dq0, swap(dq1))
    grad_k = place(*settle(sum_k))
    grad_v = place(*settle(sum_v))
    return grad_q, grad_k, grad_v


def solution(mesh):
    rows = P(AXES, None)
    return jax.shard_map(
        local,
        mesh=mesh,
        in_specs=(rows, rows, rows, rows, P(AXES)),
        out_specs=(rows, rows, rows),
        check_vma=False,
    )
```

time: 244 us -> 78 us (0.32)
  starting transfers between devices: 116 us -> 29.5 us
  waiting for transfers between devices: 68.3 us -> 19.2 us
  matrix products: 25.7 us -> 0 us
  local copies, waits for them, and re-layouts: 23.8 us -> 6.31 us
  Pallas kernels: 0 us -> 14.6 us
    ppermute x20 -> x14, starting transfers between devices: 116 us -> 29.5 us  [the longest x8 28.6 us: hop(): lax.ppermute(x, AXES, [(i, i + by) for i in range(n) if 0 <= i + by < n])]
    ppermute x20 -> x14, waiting for transfers between devices: 68.3 us -> 19.2 us  [the longest x8 18.2 us: hop(): lax.ppermute(x, AXES, [(i, i + by) for i in range(n) if 0 <= i + by < n])]
    dot_general x24 -> x0, matrix products: 25.7 us -> none  [the longest x4 9.06 us: tile_grads(): jnp.einsum('grnm,ngrd->mgd', dscore_low, query_rows, preferred_element_ty...]
    slice x12 -> x3, local copies, waits for them, and re-layouts: 15.7 us -> 0.03 us  [the longest x2 0.02 us: settle(): other = swap(total[tok:].astype(bf16))]
    pallas_call x0 -> x2, Pallas kernels: none -> 14.6 us  [the longest x1 8.72 us: local(): pl.pallas_call(functools.partial(score_kernel, tok), grid_spec=pltpu.Pref...]
    convert_element_type x6 -> x4, other arithmetic: 5.93 us -> 1.32 us  [the longest x1 1.24 us: local(): dv = hop((dva + cv.astype(f32)).astype(bf16), -1)]
    concatenate x0 -> x7, other arithmetic: none -> 3.17 us  [the longest x3 2.29 us: place(): return jnp.concatenate([first, second], 1)]
    unnamed x34 -> x24, local copies, waits for them, and re-layouts: 5.01 us -> 5.14 us
  transfers between devices with their start and end apart: 20 -> 14, of which waited for: 6 -> 6; matrix products, arithmetic and copies ran while one was open for 7% -> 7% of each run, Pallas kernels for 0% -> 19%
where the time goes in v1:
time: 78 us; the launch traced here: 77.2 us
  starting transfers between devices  29.5 us (38%)
  waiting for transfers between devices  19.2 us (25%)
  Pallas kernels  14.6 us (19%)
  local copies, waits for them, and re-layouts  6.31 us (8%)
  other arithmetic  6.12 us (8%)
  between operations  1.62 us (2%)
    ppermute x8, starting transfers between devices, hop(): lax.ppermute(x, AXES, [(i, i + by) for i in range(n) if 0 <= i + by < n])  28.6 us
    ppermute x8, waiting for transfers between devices, hop(): lax.ppermute(x, AXES, [(i, i + by) for i in range(n) if 0 <= i + by < n])  18.2 us
    pallas_call x1, Pallas kernels, local(): pl.pallas_call(functools.partial(score_kernel, tok), grid_spec=pltpu.Pref...  8.72 us
    pallas_call x1, Pallas kernels, local(): pl.pallas_call(functools.partial(value_kernel, tok), grid_spec=pltpu.Pref...  5.85 us
    unnamed x24, local copies, waits for them, and re-layouts  5.14 us
    concatenate x3, other arithmetic, place(): return jnp.concatenate([first, second], 1)  2.29 us
  transfers between devices with their start and end apart: 14, of which 6 were waited for; matrix products, arithmetic and copies ran while one was open for 7% of the time, Pallas kernels for 19%

profile of v1, /device:TPU:26, one launch (start us, length us, event | category | flops | bytes accessed | tf_op | source)
XLA Modules:
  0.0 77.2 jit_solution(18085041267991020641)
XLA Ops:
  1.3 1.1 %constant_dynamic-slice_fusion.4 = (bf16[128,512]{1,0:T(8,128)(2,1)S(1)}, bf16[128,512]{1,0:T(8,128)(2,1)S(1)}) fusion(bf16[128,1024]{1,0:T(8,128)(2,1)} %param.6, s32[]{:T(128)S(6)} %select_n.56, s32[]{:T(128)S(6)} %select_n.53), kind=kLoop, calls=%fused_computation.27 | loop fusion | bytes 524296 | tf_op jit(solution)/shard_map/dynamic_slice | solution.py:167
  4.5 3.1 %collective-permute-start.1 = (bf16[272,512]{1,0:T(8,128)(2,1)S(1)}, bf16[272,512]{1,0:T(8,128)(2,1)S(1)}, u32[]{:S(2)}, u32[]{:S(2)}) collective-permute-start(bf16[272,512]{1,0:T(8,128)(2,1)S(1)} %fusion.2.kc), channel_id=1, source_target_pairs={{0,2},{1,3},{2,4},{3,5},{4,6},{5,7},{6,8},{7,9},{8,10},{9,11},{10,... | collective-permute-start | bytes 835592 | tf_op jit(solution)/shard_map/ppermute | solution.py:33
  7.6 0.8 %pad_maximum_fusion = bf16[256,1024]{1,0:T(8,128)(2,1)} fusion(bf16[128,1024]{1,0:T(8,128)(2,1)S(1)} %get-tuple-element.35, bf16[128,1024]{1,0:T(8,128)(2,1)S(1)} %get-tuple-element.36), kind=kLoop, calls=%fused_computation.2 | loop fusion | flops 1048576 | bytes 1048576 | tf_op jit(solution)/shard_map/concatenate | solution.py:172
  8.4 3.5 %collective-permute-start.5 = (bf16[256,512]{1,0:T(8,128)(2,1)S(1)}, bf16[256,512]{1,0:T(8,128)(2,1)S(1)}, u32[]{:S(2)}, u32[]{:S(2)}) collective-permute-start(bf16[256,512]{1,0:T(8,128)(2,1)S(1)} %pad_maximum_fusion.2.vc), channel_id=1, source_target_pairs={{0,2},{1,3},{2,4},{3,5},{4,6},{5,7},{6,8},{7,9},{8,10},{9,11},{10,... | collective-permute-start | bytes 786440 | tf_op jit(solution)/shard_map/ppermute | solution.py:33
  11.9 4.0 %collective-permute-done.1.sega.ka = bf16[272,512]{1,0:T(8,128)(2,1)S(1)} collective-permute-done((bf16[272,512]{1,0:T(8,128)(2,1)S(1)}, bf16[272,512]{1,0:T(8,128)(2,1)S(1)}, u32[]{:S(2)}, u32[]{:S(2)}) %collective-permute-start.1) | collective-permute-done | bytes 278560 | tf_op jit(solution)/shard_map/ppermute | solution.py:33
  15.9 6.6 %collective-permute-start.2 = (bf16[272,512]{1,0:T(8,128)(2,1)S(1)}, bf16[272,512]{1,0:T(8,128)(2,1)S(1)}, u32[]{:S(2)}, u32[]{:S(2)}) collective-permute-start(bf16[272,512]{1,0:T(8,128)(2,1)S(1)} %collective-permute-done.1.sega.ka), channel_id=1, source_target_pairs={{0,2},{1,3},{2,4},{3,5},{4,6},{5,7},{6,8},{7,9},{8,10},{9,11},{10,... | collective-permute-start | bytes 835592 | tf_op jit(solution)/shard_map/ppermute | solution.py:33
  22.7 4.7 %collective-permute-start.6 = (bf16[256,512]{1,0:T(8,128)(2,1)S(1)}, bf16[256,512]{1,0:T(8,128)(2,1)}, u32[]{:S(2)}, u32[]{:S(2)}) collective-permute-start(bf16[256,512]{1,0:T(8,128)(2,1)S(1)} %collective-permute-done.5.va), channel_id=1, source_target_pairs={{0,2},{1,3},{2,4},{3,5},{4,6},{5,7},{6,8},{7,9},{8,10},{9,11},{10,... | collective-permute-start | bytes 786440 | tf_op jit(solution)/shard_map/ppermute | solution.py:33
  28.7 5.8 %value_grads.1 = (bf16[256,512]{1,0:T(8,128)(2,1)}, f32[256,512]{1,0:T(8,128)S(1)}, f32[256,512]{1,0:T(8,128)S(1)}, f32[4,8,256]{2,1,0:T(8,128)S(1)}) custom-call(s32[1]{0:T(128)} %bitcast.core_ref, s32[8,128]{1,0:T(8,128)S(1)} %concatenate.37.lo_ref, bf16[272,512]{1,0:T(8,128)(2,1)S(1)} %collective-permute-done.1.sega.ka, ...), custom_call_target="tpu_custom_call" | custom-call | tf_op jit(solution)/shard_map/value_grads/pallas_call | solution.py:226
  34.6 0.8 %copy-done.4 = f32[256,512]{1,0:T(8,128)} copy-done((f32[256,512]{1,0:T(8,128)}, f32[256,512]{1,0:T(8,128)S(1)}, u32[]{:S(2)}) %copy-start.4) | copy-done | bytes 524312
  35.4 1.9 %collective-permute-start.11 = (bf16[256,512]{1,0:T(8,128)(2,1)}, bf16[256,512]{1,0:T(8,128)(2,1)}, u32[]{:S(2)}, u32[]{:S(2)}) collective-permute-start(bf16[256,512]{1,0:T(8,128)(2,1)} %get-tuple-element.20), channel_id=1, source_target_pairs={{2,0},{3,1},{4,2},{5,3},{6,4},{7,5},{8,6},{9,7},{10,8},{11,9},{12,... | collective-permute-start | bytes 786440 | tf_op jit(solution)/shard_map/ppermute | solution.py:33
  37.3 0.9 %copy-done.8 = bf16[256,512]{1,0:T(8,128)(2,1)S(1)} copy-done((bf16[256,512]{1,0:T(8,128)(2,1)S(1)}, bf16[256,512]{1,0:T(8,128)(2,1)}, u32[]{:S(2)}) %copy-start.8) | copy-done | bytes 262168
  38.3 8.7 %score_grads.1 = (bf16[256,512]{1,0:T(8,128)(2,1)}, f32[256,512]{1,0:T(8,128)S(1)}, f32[256,512]{1,0:T(8,128)S(1)}, bf16[128,1024]{1,0:T(8,128)(2,1)S(1)}, bf16[128,1024]{1,0:T(8,128)(2,1)S(1)}) custom-call(s32[1]{0:T(128)} %bitcast.core_ref, s32[8,128]{1,0:T(8,128)S(1)} %concatenate.37.lo_ref, bf16[272,512]{1,0:T(8,128)(2,1)S(1)} %collective-permute-done.1.sega.ka, ...), custom_call_target="tpu_custom_call" | custom-call | tf_op jit(solution)/shard_map/score_grads/pallas_call | solution.py:240
  47.0 0.8 %copy-done.2 = f32[256,512]{1,0:T(8,128)} copy-done((f32[256,512]{1,0:T(8,128)}, f32[256,512]{1,0:T(8,128)S(1)}, u32[]{:S(2)}) %copy-start.2) | copy-done | bytes 524312
  47.8 0.8 %copy-done.5 = f32[256,512]{1,0:T(8,128)} copy-done((f32[256,512]{1,0:T(8,128)}, f32[256,512]{1,0:T(8,128)S(1)}, u32[]{:S(2)}) %copy-start.5) | copy-done | bytes 524312
  49.3 1.9 %collective-permute-start.8 = (bf16[256,512]{1,0:T(8,128)(2,1)}, bf16[256,512]{1,0:T(8,128)(2,1)S(1)}, u32[]{:S(2)}, u32[]{:S(2)}) collective-permute-start(bf16[256,512]{1,0:T(8,128)(2,1)} %get-tuple-element.17), channel_id=1, source_target_pairs={{2,0},{3,1},{4,2},{5,3},{6,4},{7,5},{8,6},{9,7},{10,8},{11,9},{12,... | collective-permute-start | bytes 786440 | tf_op jit(solution)/shard_map/ppermute | solution.py:33
  51.3 1.2 %add_convert_fusion.1 = bf16[256,512]{1,0:T(8,128)(2,1)S(1)} fusion(f32[256,512]{1,0:T(8,128)} %copy-done.4, bf16[256,512]{1,0:T(8,128)(2,1)} %collective-permute-done.11), kind=kLoop, calls=%fused_computation.5 | loop fusion | flops 393216 | bytes 1048576 | tf_op jit(solution)/shard_map/convert_element_type | solution.py:254
  52.6 5.0 %collective-permute-start.12 = (bf16[256,512]{1,0:T(8,128)(2,1)S(1)}, bf16[256,512]{1,0:T(8,128)(2,1)S(1)}, u32[]{:S(2)}, u32[]{:S(2)}) collective-permute-start(bf16[256,512]{1,0:T(8,128)(2,1)S(1)} %add_convert_fusion.1), channel_id=1, source_target_pairs={{2,0},{3,1},{4,2},{5,3},{6,4},{7,5},{8,6},{9,7},{10,8},{11,9},{12,... | collective-permute-start | bytes 786440 | tf_op jit(solution)/shard_map/ppermute | solution.py:33
  57.6 5.4 %collective-permute-done.8 = bf16[256,512]{1,0:T(8,128)(2,1)S(1)} collective-permute-done((bf16[256,512]{1,0:T(8,128)(2,1)}, bf16[256,512]{1,0:T(8,128)(2,1)S(1)}, u32[]{:S(2)}, u32[]{:S(2)}) %collective-permute-start.8) | collective-permute-done | bytes 262176 | tf_op jit(solution)/shard_map/ppermute | solution.py:33
  63.1 1.9 %collective-permute-start.9 = (bf16[256,512]{1,0:T(8,128)(2,1)S(1)}, bf16[256,512]{1,0:T(8,128)(2,1)S(1)}, u32[]{:S(2)}, u32[]{:S(2)}) collective-permute-start(bf16[256,512]{1,0:T(8,128)(2,1)S(1)} %add_convert_fusion.3), channel_id=1, source_target_pairs={{2,0},{3,1},{4,2},{5,3},{6,4},{7,5},{8,6},{9,7},{10,8},{11,9},{12,... | collective-permute-start | bytes 786440 | tf_op jit(solution)/shard_map/ppermute | solution.py:33
  65.1 0.8 %pad_maximum_fusion.1 = bf16[128,2048]{1,0:T(8,128)(2,1)} fusion(bf16[128,1024]{1,0:T(8,128)(2,1)S(1)} %get-tuple-element.24, bf16[128,1024]{1,0:T(8,128)(2,1)S(1)} %get-tuple-element.23), kind=kLoop, calls=%fused_computation.3 | loop fusion | flops 1048576 | bytes 1048576 | tf_op jit(solution)/shard_map/concatenate | solution.py:267
  65.9 1.9 %collective-permute-done.12 = bf16[256,512]{1,0:T(8,128)(2,1)S(1)} collective-permute-done((bf16[256,512]{1,0:T(8,128)(2,1)S(1)}, bf16[256,512]{1,0:T(8,128)(2,1)S(1)}, u32[]{:S(2)}, u32[]{:S(2)}) %collective-permute-start.12) | collective-permute-done | bytes 262176 | tf_op jit(solution)/shard_map/ppermute | solution.py:33
  68.0 6.9 %collective-permute-done.9 = bf16[256,512]{1,0:T(8,128)(2,1)S(1)} collective-permute-done((bf16[256,512]{1,0:T(8,128)(2,1)S(1)}, bf16[256,512]{1,0:T(8,128)(2,1)S(1)}, u32[]{:S(2)}, u32[]{:S(2)}) %collective-permute-start.9) | collective-permute-done | bytes 262176 | tf_op jit(solution)/shard_map/ppermute | solution.py:33
  75.2 0.7 pad_maximum_fusion.4
  76.5 0.7 pad_maximum_fusion.3
  (58 shorter events, 5.4 us)
Async XLA Ops:
  1.3 1.2 %copy-start.10 = (bf16[128,1024]{1,0:T(8,128)(2,1)S(1)}, bf16[128,1024]{1,0:T(8,128)(2,1)}, u32[]{:S(2)}) copy-start(bf16[128,1024]{1,0:T(8,128)(2,1)} %param.7) | copy-start | bytes 786436
  1.3 1.8 %copy-start.1 = (bf16[128,2048]{1,0:T(8,128)(2,1)S(1)}, bf16[128,2048]{1,0:T(8,128)(2,1)}, u32[]{:S(2)}) copy-start(bf16[128,2048]{1,0:T(8,128)(2,1)} %g0.3) | copy-start | bytes 1572868
  2.4 1.1 %copy-start = (bf16[128,2048]{1,0:T(8,128)(2,1)S(1)}, bf16[128,2048]{1,0:T(8,128)(2,1)}, u32[]{:S(2)}) copy-start(bf16[128,2048]{1,0:T(8,128)(2,1)} %q0.3) | copy-start | bytes 1572868
  2.4 1.4 %collective-permute-start = (bf16[144,512]{1,0:T(8,128)(2,1)S(1)}, bf16[144,512]{1,0:T(8,128)(2,1)S(1)}, u32[]{:S(2)}, u32[]{:S(2)}) collective-permute-start(bf16[144,512]{1,0:T(8,128)(2,1)S(1)} %fusion.3), channel_id=1, source_target_pairs={{0,1},{1,0},{2,3},{3,2},{4,5},{5,4},{6,7},{7,6},{8,9},{9,8},{10,11... | collective-permute-start | bytes 442376 | tf_op jit(solution)/shard_map/ppermute | solution.py:27
  2.5 5.9 %collective-permute-start.4 = (bf16[128,512]{1,0:T(8,128)(2,1)S(1)}, bf16[128,512]{1,0:T(8,128)(2,1)S(1)}, u32[]{:S(2)}, u32[]{:S(2)}) collective-permute-start(bf16[128,512]{1,0:T(8,128)(2,1)S(1)} %get-tuple-element.30), channel_id=1, source_target_pairs={{0,1},{1,0},{2,3},{3,2},{4,5},{5,4},{6,7},{7,6},{8,9},{9,8},{10,11... | collective-permute-start | bytes 393224 | tf_op jit(solution)/shard_map/ppermute | solution.py:27
  4.5 11.4 %collective-permute-start.1 = (bf16[272,512]{1,0:T(8,128)(2,1)S(1)}, bf16[272,512]{1,0:T(8,128)(2,1)S(1)}, u32[]{:S(2)}, u32[]{:S(2)}) collective-permute-start(bf16[272,512]{1,0:T(8,128)(2,1)S(1)} %fusion.2.kc), channel_id=1, source_target_pairs={{0,2},{1,3},{2,4},{3,5},{4,6},{5,7},{6,8},{7,9},{8,10},{9,11},{10,... | collective-permute-start | bytes 835592 | tf_op jit(solution)/shard_map/ppermute | solution.py:33
  8.4 20.3 %collective-permute-start.3 = (bf16[256,1024]{1,0:T(8,128)(2,1)}, bf16[256,1024]{1,0:T(8,128)(2,1)S(1)}, u32[]{:S(2)}, u32[]{:S(2)}) collective-permute-start(bf16[256,1024]{1,0:T(8,128)(2,1)} %pad_maximum_fusion), channel_id=1, source_target_pairs={{0,1},{1,0},{2,3},{3,2},{4,5},{5,4},{6,7},{7,6},{8,9},{9,8},{10,11... | collective-permute-start | bytes 1572872 | tf_op jit(solution)/shard_map/ppermute | solution.py:27
  8.4 14.2 %collective-permute-start.5 = (bf16[256,512]{1,0:T(8,128)(2,1)S(1)}, bf16[256,512]{1,0:T(8,128)(2,1)S(1)}, u32[]{:S(2)}, u32[]{:S(2)}) collective-permute-start(bf16[256,512]{1,0:T(8,128)(2,1)S(1)} %pad_maximum_fusion.2.vc), channel_id=1, source_target_pairs={{0,2},{1,3},{2,4},{3,5},{4,6},{5,7},{6,8},{7,9},{8,10},{9,11},{10,... | collective-permute-start | bytes 786440 | tf_op jit(solution)/shard_map/ppermute | solution.py:33
  15.9 12.8 %collective-permute-start.2 = (bf16[272,512]{1,0:T(8,128)(2,1)S(1)}, bf16[272,512]{1,0:T(8,128)(2,1)S(1)}, u32[]{:S(2)}, u32[]{:S(2)}) collective-permute-start(bf16[272,512]{1,0:T(8,128)(2,1)S(1)} %collective-permute-done.1.sega.ka), channel_id=1, source_target_pairs={{0,2},{1,3},{2,4},{3,5},{4,6},{5,7},{6,8},{7,9},{8,10},{9,11},{10,... | collective-permute-start | bytes 835592 | tf_op jit(solution)/shard_map/ppermute | solution.py:33
  22.7 11.9 %copy-start.7 = (bf16[256,512]{1,0:T(8,128)(2,1)}, bf16[256,512]{1,0:T(8,128)(2,1)S(1)}, u32[]{:S(2)}) copy-start(bf16[256,512]{1,0:T(8,128)(2,1)S(1)} %collective-permute-done.5.va) | copy-start | bytes 786436
  22.7 14.6 %collective-permute-start.6 = (bf16[256,512]{1,0:T(8,128)(2,1)S(1)}, bf16[256,512]{1,0:T(8,128)(2,1)}, u32[]{:S(2)}, u32[]{:S(2)}) collective-permute-start(bf16[256,512]{1,0:T(8,128)(2,1)S(1)} %collective-permute-done.5.va), channel_id=1, source_target_pairs={{0,2},{1,3},{2,4},{3,5},{4,6},{5,7},{6,8},{7,9},{8,10},{9,11},{10,... | collective-permute-start | bytes 786440 | tf_op jit(solution)/shard_map/ppermute | solution.py:33
  34.6 0.8 %copy-start.4 = (f32[256,512]{1,0:T(8,128)}, f32[256,512]{1,0:T(8,128)S(1)}, u32[]{:S(2)}) copy-start(f32[256,512]{1,0:T(8,128)S(1)} %get-tuple-element.19) | copy-start | bytes 1572868
  35.4 15.9 %collective-permute-start.11 = (bf16[256,512]{1,0:T(8,128)(2,1)}, bf16[256,512]{1,0:T(8,128)(2,1)}, u32[]{:S(2)}, u32[]{:S(2)}) collective-permute-start(bf16[256,512]{1,0:T(8,128)(2,1)} %get-tuple-element.20), channel_id=1, source_target_pairs={{2,0},{3,1},{4,2},{5,3},{6,4},{7,5},{8,6},{9,7},{10,8},{11,9},{12,... | collective-permute-start | bytes 786440 | tf_op jit(solution)/shard_map/ppermute | solution.py:33
  37.3 1.0 %copy-start.8 = (bf16[256,512]{1,0:T(8,128)(2,1)S(1)}, bf16[256,512]{1,0:T(8,128)(2,1)}, u32[]{:S(2)}) copy-start(bf16[256,512]{1,0:T(8,128)(2,1)} %copy-done.7) | copy-start | bytes 786436
  47.0 0.8 %copy-start.2 = (f32[256,512]{1,0:T(8,128)}, f32[256,512]{1,0:T(8,128)S(1)}, u32[]{:S(2)}) copy-start(f32[256,512]{1,0:T(8,128)S(1)} %get-tuple-element.15) | copy-start | bytes 1572868
  47.8 0.8 %copy-start.5 = (f32[256,512]{1,0:T(8,128)}, f32[256,512]{1,0:T(8,128)S(1)}, u32[]{:S(2)}) copy-start(f32[256,512]{1,0:T(8,128)S(1)} %get-tuple-element.16) | copy-start | bytes 1572868
  49.3 13.7 %collective-permute-start.8 = (bf16[256,512]{1,0:T(8,128)(2,1)}, bf16[256,512]{1,0:T(8,128)(2,1)S(1)}, u32[]{:S(2)}, u32[]{:S(2)}) collective-permute-start(bf16[256,512]{1,0:T(8,128)(2,1)} %get-tuple-element.17), channel_id=1, source_target_pairs={{2,0},{3,1},{4,2},{5,3},{6,4},{7,5},{8,6},{9,7},{10,8},{11,9},{12,... | collective-permute-start | bytes 786440 | tf_op jit(solution)/shard_map/ppermute | solution.py:33
  51.2 13.8 %collective-permute-start.7 = (bf16[128,1024]{1,0:T(8,128)(2,1)}, bf16[128,1024]{1,0:T(8,128)(2,1)S(1)}, u32[]{:S(2)}, u32[]{:S(2)}) collective-permute-start(bf16[128,1024]{1,0:T(8,128)(2,1)} %copy-done.9), channel_id=1, source_target_pairs={{0,1},{1,0},{2,3},{3,2},{4,5},{5,4},{6,7},{7,6},{8,9},{9,8},{10,11... | collective-permute-start | bytes 786440 | tf_op jit(solution)/shard_map/ppermute | solution.py:27
  51.3 11.7 %copy-start.6 = (f32[256,512]{1,0:T(8,128)S(1)}, f32[256,512]{1,0:T(8,128)}, u32[]{:S(2)}) copy-start(f32[256,512]{1,0:T(8,128)} %copy-done.5) | copy-start | bytes 1572868
  52.6 15.3 %collective-permute-start.12 = (bf16[256,512]{1,0:T(8,128)(2,1)S(1)}, bf16[256,512]{1,0:T(8,128)(2,1)S(1)}, u32[]{:S(2)}, u32[]{:S(2)}) collective-permute-start(bf16[256,512]{1,0:T(8,128)(2,1)S(1)} %add_convert_fusion.1), channel_id=1, source_target_pairs={{2,0},{3,1},{4,2},{5,3},{6,4},{7,5},{8,6},{9,7},{10,8},{11,9},{12,... | collective-permute-start | bytes 786440 | tf_op jit(solution)/shard_map/ppermute | solution.py:33
  63.1 11.9 %collective-permute-start.9 = (bf16[256,512]{1,0:T(8,128)(2,1)S(1)}, bf16[256,512]{1,0:T(8,128)(2,1)S(1)}, u32[]{:S(2)}, u32[]{:S(2)}) collective-permute-start(bf16[256,512]{1,0:T(8,128)(2,1)S(1)} %add_convert_fusion.3), channel_id=1, source_target_pairs={{2,0},{3,1},{4,2},{5,3},{6,4},{7,5},{8,6},{9,7},{10,8},{11,9},{12,... | collective-permute-start | bytes 786440 | tf_op jit(solution)/shard_map/ppermute | solution.py:33
  67.9 7.1 %copy-start.3 = (f32[256,512]{1,0:T(8,128)S(1)}, f32[256,512]{1,0:T(8,128)}, u32[]{:S(2)}) copy-start(f32[256,512]{1,0:T(8,128)} %copy-done.2) | copy-start | bytes 1572868
  68.0 7.2 %collective-permute-start.13 = (bf16[128,512]{1,0:T(8,128)(2,1)S(1)}, bf16[128,512]{1,0:T(8,128)(2,1)S(1)}, u32[]{:S(2)}, u32[]{:S(2)}) collective-permute-start(bf16[128,512]{1,0:T(8,128)(2,1)S(1)} %slice.33), channel_id=1, source_target_pairs={{0,1},{1,0},{2,3},{3,2},{4,5},{5,4},{6,7},{7,6},{8,9},{9,8},{10,11... | collective-permute-start | bytes 393224 | tf_op jit(solution)/shard_map/ppermute | solution.py:27
  75.1 1.4 %collective-permute-start.10 = (bf16[128,512]{1,0:T(8,128)(2,1)S(1)}, bf16[128,512]{1,0:T(8,128)(2,1)S(1)}, u32[]{:S(2)}, u32[]{:S(2)}) collective-permute-start(bf16[128,512]{1,0:T(8,128)(2,1)S(1)} %slice.31), channel_id=1, source_target_pairs={{0,1},{1,0},{2,3},{3,2},{4,5},{5,4},{6,7},{7,6},{8,9},{9,8},{10,11... | collective-permute-start | bytes 393224 | tf_op jit(solution)/shard_map/ppermute | solution.py:27
  (2 other events, 1.4 us)

commit v2 on v1

v2 whole, which is shorter than its diff:
```python
import functools

import jax
import jax.numpy as jnp
from jax import lax
from jax.experimental import pallas as pl
from jax.experimental.pallas import tpu as pltpu
from jax.sharding import PartitionSpec as P

HEAD_DIM = 128
WINDOW = 512
SOFTCAP = 50.0
SCALE = 1.0 / 12.0
LOG2E = 1.4426950408889634
AXES = ("ctx", "fsdp")
NT = (((1,), (1,)), ((), ()))
NN = (((1,), (0,)), ((), ()))
SEG_ROWS = 16
FAR = 2


def dot(a, b, dims):
    return lax.dot_general(a, b, dims, preferred_element_type=jnp.float32)


def swap(x):
    n = lax.axis_size(AXES)
    return lax.ppermute(x, AXES, [(i, i ^ 1) for i in range(n)])


def hop(x, chips):
    n = lax.axis_size(AXES)
    by = 2 * chips
    return lax.ppermute(x, AXES, [(i, i + by) for i in range(n) if 0 <= i + by < n])


def rows_at(core, half, tok):
    return pl.ds(pl.multiple_of(lax.bitwise_xor(core, half) * tok, tok), tok)


def lanes_at(g):
    return pl.ds(pl.multiple_of(g * HEAD_DIM, HEAD_DIM), HEAD_DIM)


def block_of(core, pieces, b, g, tok):
    return pieces[b // 2][rows_at(core, b % 2, tok), lanes_at(g)]


def seen(lo, seg_ref, tok):
    ids = seg_ref[2 * tok : 2 * tok + 1, : 2 * tok].astype(jnp.float32)
    same = jnp.where(ids == lo[2:3, 0:1].astype(jnp.float32), 1.0, 0.0)
    return jnp.sum(same, axis=1, keepdims=True).astype(jnp.int32)


def first_keys(core, lo, count, half, tok):
    mine = jnp.where(core == half, lo[0:1], lo[1:2])
    mine = jnp.where(mine < 0, WINDOW - count, mine) - half * tok
    row = lax.broadcasted_iota(jnp.int32, (1, tok), 1)
    mine = jnp.maximum(mine, row + 1)
    return jnp.concatenate([mine, mine], 1)


def weights_of(key_rows, q_rows, lo, jj, last, tok):
    s = dot(key_rows, q_rows, NT)
    t = jnp.tanh(s * (SCALE / SOFTCAP))
    w = jnp.exp2(t * (SOFTCAP * LOG2E))
    pos = lax.broadcasted_iota(jnp.int32, s.shape, 0)
    ok = pos >= lo - jj * tok
    if last:
        col = lax.broadcasted_iota(jnp.int32, s.shape, 1)
        ok = ok & (pos <= jnp.where(col >= tok, col - tok, col))
    w = jnp.where(ok, w, 0.0)
    return w, w * (SCALE - t * t * SCALE)


def fold(x):
    return jnp.sum(x.reshape(x.shape[0] // 8, 8, x.shape[1]), axis=0)


def near_weights(tok, groups, core_ref, lo_ref, q, qx, ka, kc, qs, w_near, u_near, tot):
    core = core_ref[0]
    lo_all = lo_ref[...]
    count = seen(lo_all, ka, tok)
    los = [first_keys(core, lo_all, count, h, tok) for h in range(2)]
    blocks = WINDOW // tok + 1

    def step(g, _):
        for hd in range(2):
            at = (core * groups + g) * 2 + hd
            qs[g, core, pl.ds(hd * tok, tok), :] = q[:, lanes_at(at)]
            qs[g, 1 - core, pl.ds(hd * tok, tok), :] = qx[:tok, lanes_at(g * 2 + hd)]
        for h in range(2):
            q_rows = qs[g, h]
            total = jnp.zeros((8, 2 * tok), jnp.float32)
            for jj in range(FAR, blocks):
                k_blk = block_of(core, (None, ka, kc), h + jj, g, tok)
                w, u = weights_of(k_blk, q_rows, los[h], jj, jj == blocks - 1, tok)
                w_near[g, h, jj - FAR] = w
                u_near[g, h, jj - FAR] = u
                total = total + fold(w)
            tot[g, pl.ds(8 * h, 8), :] = total
        return 0

    lax.fori_loop(0, groups, step, 0)


def near_products(tok, groups, core_ref, go, gox, va, vc, w_near, gs, dp_near, term):
    core = core_ref[0]
    blocks = WINDOW // tok + 1

    def step(g, _):
        for hd in range(2):
            at = (core * groups + g) * 2 + hd
            gs[g, core, pl.ds(hd * tok, tok), :] = go[:, lanes_at(at)]
            gs[g, 1 - core, pl.ds(hd * tok, tok), :] = gox[tok:, lanes_at(g * 2 + hd)]
        for h in range(2):
            g_rows = gs[g, h]
            total = jnp.zeros((8, 2 * tok), jnp.float32)
            for jj in range(FAR, blocks):
                v_blk = block_of(core, (None, va, vc), h + jj, g, tok)
                dp = dot(v_blk, g_rows, NT)
                dp_near[g, h, jj - FAR] = dp
                total = total + fold(w_near[g, h, jj - FAR] * dp)
            term[g, pl.ds(8 * h, 8), :] = total
        return 0

    lax.fori_loop(0, groups, step, 0)


def far_values(tok, groups, core_ref, lo_ref, qs, gs, ka, kb, tot, dvb, w_far, u_far, inv):
    core = core_ref[0]
    lo_all = lo_ref[...]
    count = seen(lo_all, ka, tok) + seen(lo_all, kb, tok)
    los = [first_keys(core, lo_all, count, h, tok) for h in range(2)]

    def step(g, _):
        low = {}
        for h in range(2):
            q_rows = qs[g, h]
            total = tot[g, pl.ds(8 * h, 8), :]
            ws = []
            for jj in range(FAR):
                k_blk = block_of(core, (kb, ka), h + jj, g, tok)
                w, u = weights_of(k_blk, q_rows, los[h], jj, False, tok)
                w_far[g, h, jj] = w
                u_far[g, h, jj] = u
                total = total + fold(w)
                ws.append(w)
            one = 1.0 / jnp.sum(total, axis=0, keepdims=True)
            inv[g, pl.ds(8 * h, 8), :] = jnp.broadcast_to(one, (8, 2 * tok))
            for jj in range(FAR):
                if h + jj < FAR:
                    low[h, jj] = (ws[jj] * one).astype(jnp.bfloat16)
        for b in range(FAR):
            acc = None
            for h in range(2):
                if (h, b - h) in low:
                    part = dot(low[h, b - h], gs[g, h], NN)
                    acc = part if acc is None else acc + part
            dvb[rows_at(core, b % 2, tok), lanes_at(g)] = acc.astype(dvb.dtype)
        return 0

    lax.fori_loop(0, groups, step, 0)


def far_keys(tok, groups, core_ref, qs, gs, va, vb, w_far, u_far, inv, term, dkb, ds_far, row):
    core = core_ref[0]

    def step(g, _):
        for h in range(2):
            g_rows = gs[g, h]
            one = inv[g, pl.ds(8 * h, 1), :]
            total = term[g, pl.ds(8 * h, 8), :]
            dps = []
            for jj in range(FAR):
                v_blk = block_of(core, (vb, va), h + jj, g, tok)
                dp = dot(v_blk, g_rows, NT)
                total = total + fold(w_far[g, h, jj] * dp)
                dps.append(dp)
            mean = one * jnp.sum(total, axis=0, keepdims=True)
            row[g, pl.ds(8 * h, 8), :] = jnp.broadcast_to(mean, (8, 2 * tok))
            for jj in range(FAR):
                ds = (u_far[g, h, jj] * one) * (dps[jj] - mean)
                ds_far[g, h, jj] = ds.astype(jnp.bfloat16)
        for b in range(FAR):
            acc = None
            for h in range(2):
                if 0 <= b - h < FAR:
                    part = dot(ds_far[g, h, b - h], qs[g, h], NN)
                    acc = part if acc is None else acc + part
            dkb[rows_at(core, b % 2, tok), lanes_at(g)] = acc.astype(dkb.dtype)
        return 0

    lax.fori_loop(0, groups, step, 0)


def near_values(tok, groups, core_ref, gs, w_near, w_far, inv, dva, dvc):
    core = core_ref[0]
    blocks = WINDOW // tok + 1

    def step(g, _):
        for b in range(FAR, blocks + 1):
            acc = None
            for h in range(2):
                jj = b - h
                if jj >= blocks:
                    continue
                w = w_far[g, h, jj] if jj < FAR else w_near[g, h, jj - FAR]
                low = (w * inv[g, pl.ds(8 * h, 1), :]).astype(jnp.bfloat16)
                part = dot(low, gs[g, h], NN)
                acc = part if acc is None else acc + part
            out = (None, dva, dvc)[b // 2]
            out[rows_at(core, b % 2, tok), lanes_at(g)] = acc
        return 0

    lax.fori_loop(0, groups, step, 0)


def near_keys(tok, groups, core_ref, qs, kb, ka, kc, u_near, dp_near, ds_far, inv, row,
              dka, dkc, dq0, dq1, ds_s, dq_s):
    core = core_ref[0]
    blocks = WINDOW // tok + 1

    def step(g, _):
        for h in range(2):
            one = inv[g, pl.ds(8 * h, 1), :]
            mean = row[g, pl.ds(8 * h, 1), :]
            dq_t = jnp.zeros((HEAD_DIM, 2 * tok), jnp.float32)
            for jj in range(blocks):
                if jj < FAR:
                    ds = ds_far[g, h, jj]
                else:
                    ds = (u_near[g, h, jj - FAR] * one) * (dp_near[g, h, jj - FAR] - mean)
                    ds = ds.astype(jnp.bfloat16)
                    ds_s[h, jj - FAR] = ds
                k_blk = block_of(core, (kb, ka, kc), h + jj, g, tok)
                dq_t = dq_t + dot(k_blk.T, ds, NN)
            dq_s[lax.bitwise_xor(core, h)] = dq_t.T.astype(jnp.bfloat16)
        for r, dq in enumerate((dq0, dq1)):
            for hd in range(2):
                dq[:, lanes_at(2 * g + hd)] = dq_s[r, hd * tok : (hd + 1) * tok, :]
        for b in range(FAR, blocks + 1):
            acc = None
            for h in range(2):
                jj = b - h
                if jj >= blocks:
                    continue
                ds = ds_far[g, h, jj] if jj < FAR else ds_s[h, jj - FAR]
                part = dot(ds, qs[g, h], NN)
                acc = part if acc is None else acc + part
            out = (None, dka, dkc)[b // 2]
            out[rows_at(core, b % 2, tok), lanes_at(g)] = acc
        return 0

    lax.fori_loop(0, groups, step, 0)


def call(body, tok, groups, args, outs, scratch=()):
    vmem = pl.BlockSpec(memory_space=pltpu.VMEM)
    return pl.pallas_call(
        functools.partial(body, tok, groups),
        in_specs=[pl.BlockSpec(memory_space=pltpu.SMEM)] + [vmem] * (len(args) - 1),
        out_specs=[vmem] * len(outs),
        out_shape=[jax.ShapeDtypeStruct(s, d) for s, d in outs],
        scratch_shapes=list(scratch),
        compiler_params=pltpu.CompilerParams(vmem_limit_bytes=VMEM_LIMIT),
        name=body.__name__,
    )(*args)


VMEM_LIMIT = 24 * 1024 * 1024


def local(queries, keys, values, grad_out, segment):
    tok = queries.shape[0]
    kv_width = keys.shape[1]
    half = kv_width // 2
    groups = half // HEAD_DIM
    q_half = queries.shape[1] // 2
    bf16, f32 = jnp.bfloat16, jnp.float32
    core = lax.rem(lax.axis_index(AXES), 2)
    core_arr = core.reshape(1).astype(jnp.int32)

    def part(x, which, width):
        return lax.dynamic_slice(x, (0, which * width), (x.shape[0], width))

    seg_row = jnp.pad((segment + 1).astype(bf16)[None, :], ((0, SEG_ROWS - 1), (0, half - tok)))
    k_in = swap(jnp.concatenate([part(keys, 1 - core, half), seg_row], 0))
    v_in = swap(part(values, 1 - core, half))
    qg_in = swap(jnp.concatenate([part(queries, 1 - core, q_half), part(grad_out, 1 - core, q_half)], 0))
    seg_both = jnp.concatenate([(segment + 1).astype(bf16), k_in[tok, :tok]])
    both_row = jnp.pad(seg_both[None, :], ((0, SEG_ROWS - 1), (0, half - 2 * tok)))
    kc = jnp.concatenate([part(keys, core, half), k_in[:tok], both_row], 0)
    vc = jnp.concatenate([part(values, core, half), v_in], 0)
    ka = hop(kc, 1)
    va = hop(vc, 1)
    kb = hop(ka, 1)
    vb = hop(va, 1)

    seg_f = seg_both.astype(f32)
    seg0 = jnp.min(seg_f)
    before = jnp.sum((seg_f[:, None] < seg_f[None, :]).astype(jnp.int32), axis=0)
    starts = jnp.where(seg_f == seg0, -1, WINDOW + before).reshape(2, tok)
    lo = jnp.concatenate([starts, jnp.full((6, tok), seg0.astype(jnp.int32), jnp.int32)], 0)

    blocks = WINDOW // tok + 1
    near = (groups, 2, blocks - FAR, tok, 2 * tok)
    far = (groups, 2, FAR, tok, 2 * tok)
    rows = ((groups, 2, 2 * tok, HEAD_DIM), bf16)
    stat = ((groups, 16, 2 * tok), f32)
    kv_f = ((2 * tok, half), f32)
    kv_b = ((2 * tok, half), bf16)
    dq_o = ((tok, q_half), bf16)

    qs, w_near, u_near, tot = call(
        near_weights, tok, groups, (core_arr, lo, queries, qg_in, ka, kc),
        [rows, (near, f32), (near, f32), stat])
    gs, dp_near, term = call(
        near_products, tok, groups, (core_arr, grad_out, qg_in, va, vc, w_near),
        [rows, (near, f32), stat])
    dvb, w_far, u_far, inv = call(
        far_values, tok, groups, (core_arr, lo, qs, gs, ka, kb, tot),
        [kv_b, (far, f32), (far, f32), stat])
    cv = hop(dvb, -1)
    dkb, ds_far, row = call(
        far_keys, tok, groups, (core_arr, qs, gs, va, vb, w_far, u_far, inv, term),
        [kv_b, (far, bf16), stat])
    ck = hop(dkb, -1)
    dva, dvc = call(
        near_values, tok, groups, (core_arr, gs, w_near, w_far, inv), [kv_f, kv_f])
    dv = hop((dva + cv.astype(f32)).astype(bf16), -1)
    dka, dkc, dq0, dq1 = call(
        near_keys, tok, groups,
        (core_arr, qs, kb, ka, kc, u_near, dp_near, ds_far, inv, row),
        [kv_f, kv_f, dq_o, dq_o],
        [pltpu.VMEM((2, blocks - FAR, tok, 2 * tok), bf16), pltpu.VMEM((2, 2 * tok, HEAD_DIM), bf16)])
    dk = hop((dka + ck.astype(f32)).astype(bf16), -1)
    sum_v = dvc + dv.astype(f32)
    sum_k = dkc + dk.astype(f32)

    def settle(total):
        mine = total[:tok]
        other = swap(total[tok:].astype(bf16))
        return mine.astype(bf16), other

    def place(mine, other):
        first = jnp.where(core == 0, mine, other)
        second = jnp.where(core == 0, other, mine)
        return jnp.concatenate([first, second], 1)

    grad_q = place(dq0, swap(dq1))
    grad_k = place(*settle(sum_k))
    grad_v = place(*settle(sum_v))
    return grad_q, grad_k, grad_v


def solution(mesh):
    rows = P(AXES, None)
    return jax.shard_map(
        local,
        mesh=mesh,
        in_specs=(rows, rows, rows, rows, P(AXES)),
        out_specs=(rows, rows, rows),
        check_vma=False,
    )
```

time: 78 us -> 93.6 us (1.20)
  the two profiles are of different devices: /device:TPU:26 before, /device:TPU:13 now
where the time goes in v2:
time: 93.6 us; the launch traced here: 92.7 us
  starting transfers between devices  34 us (36%)
  local copies, waits for them, and re-layouts  20.2 us (22%)
  Pallas kernels  17.7 us (19%)
  waiting for transfers between devices  12.5 us (13%)
  other arithmetic  6.7 us (7%)
  between operations  1.62 us (2%)
    ppermute x8, starting transfers between devices, hop(): lax.ppermute(x, AXES, [(i, i + by) for i in range(n) if 0 <= i + by < n])  28 us
    pallas_call x6, Pallas kernels, call(): pl.pallas_call(functools.partial(body, tok, groups), in_specs=[pl.BlockSp...  17.7 us
    unnamed x36, local copies, waits for them, and re-layouts  17.1 us
    ppermute x8, waiting for transfers between devices, hop(): lax.ppermute(x, AXES, [(i, i + by) for i in range(n) if 0 <= i + by < n])  12.3 us
    ppermute x6, starting transfers between devices, swap(): return lax.ppermute(x, AXES, [(i, i ^ 1) for i in range(n)])  6.05 us
    dynamic_slice x3, local copies, waits for them, and re-layouts, part(): return lax.dynamic_slice(x, (0, which * width), (x.shape[0], width))  3.03 us
    concatenate x3, other arithmetic, place(): return jnp.concatenate([first, second], 1)  2.29 us
  transfers between devices with their start and end apart: 14, of which 5 were waited for; matrix products, arithmetic and copies ran while one was open for 8% of the time, Pallas kernels for 19%

profile of v2, /device:TPU:13, one launch (start us, length us, event | category | flops | bytes accessed | tf_op | source)
XLA Modules:
  0.0 92.7 jit_solution(8028162753520762214)
XLA Ops:
  5.9 3.2 %collective-permute-start.2 = (bf16[272,512]{1,0:T(8,128)(2,1)S(1)}, bf16[272,512]{1,0:T(8,128)(2,1)}, u32[]{:S(2)}, u32[]{:S(2)}) collective-permute-start(bf16[272,512]{1,0:T(8,128)(2,1)S(1)} %fusion.2.kc), channel_id=1, source_target_pairs={{0,2},{1,3},{2,4},{3,5},{4,6},{5,7},{6,8},{7,9},{8,10},{9,11},{10,... | collective-permute-start | bytes 835592 | tf_op jit(solution)/shard_map/ppermute | solution.py:34
  10.0 3.2 %collective-permute-start.5 = (bf16[256,512]{1,0:T(8,128)(2,1)S(1)}, bf16[256,512]{1,0:T(8,128)(2,1)}, u32[]{:S(2)}, u32[]{:S(2)}) collective-permute-start(bf16[256,512]{1,0:T(8,128)(2,1)S(1)} %pad_maximum_fusion.2.vc), channel_id=1, source_target_pairs={{0,2},{1,3},{2,4},{3,5},{4,6},{5,7},{6,8},{7,9},{8,10},{9,11},{10,... | collective-permute-start | bytes 786440 | tf_op jit(solution)/shard_map/ppermute | solution.py:34
  13.9 1.7 %collective-permute-done.2.ka = bf16[272,512]{1,0:T(8,128)(2,1)} collective-permute-done((bf16[272,512]{1,0:T(8,128)(2,1)S(1)}, bf16[272,512]{1,0:T(8,128)(2,1)}, u32[]{:S(2)}, u32[]{:S(2)}) %collective-permute-start.2) | collective-permute-done | bytes 278560 | tf_op jit(solution)/shard_map/ppermute | solution.py:34
  15.6 3.2 %collective-permute-start.3 = (bf16[272,512]{1,0:T(8,128)(2,1)}, bf16[272,512]{1,0:T(8,128)(2,1)}, u32[]{:S(2)}, u32[]{:S(2)}) collective-permute-start(bf16[272,512]{1,0:T(8,128)(2,1)} %collective-permute-done.2.ka), channel_id=1, source_target_pairs={{0,2},{1,3},{2,4},{3,5},{4,6},{5,7},{6,8},{7,9},{8,10},{9,11},{10,... | collective-permute-start | bytes 835592 | tf_op jit(solution)/shard_map/ppermute | solution.py:34
  18.9 2.3 %collective-permute-done.5.va = bf16[256,512]{1,0:T(8,128)(2,1)} collective-permute-done((bf16[256,512]{1,0:T(8,128)(2,1)S(1)}, bf16[256,512]{1,0:T(8,128)(2,1)}, u32[]{:S(2)}, u32[]{:S(2)}) %collective-permute-start.5) | collective-permute-done | bytes 262176 | tf_op jit(solution)/shard_map/ppermute | solution.py:34
  21.2 3.2 %collective-permute-start.6 = (bf16[256,512]{1,0:T(8,128)(2,1)}, bf16[256,512]{1,0:T(8,128)(2,1)}, u32[]{:S(2)}, u32[]{:S(2)}) collective-permute-start(bf16[256,512]{1,0:T(8,128)(2,1)} %collective-permute-done.5.va), channel_id=1, source_target_pairs={{0,2},{1,3},{2,4},{3,5},{4,6},{5,7},{6,8},{7,9},{8,10},{9,11},{10,... | collective-permute-start | bytes 786440 | tf_op jit(solution)/shard_map/ppermute | solution.py:34
  28.6 3.2 %near_weights.1 = (bf16[4,2,256,128]{3,2,1,0:T(8,128)(2,1)S(1)}, f32[4,2,3,128,256]{4,3,2,1,0:T(8,128)S(1)}, f32[4,2,3,128,256]{4,3,2,1,0:T(8,128)S(1)}, f32[4,16,256]{2,1,0:T(8,128)S(1)}) custom-call(s32[1]{0:T(128)} %bitcast.core_ref, s32[8,128]{1,0:T(8,128)S(1)} %concatenate.37.lo_ref, bf16[128,2048]{1,0:T(8,128)(2,1)S(1)} %copy-done.13, ...), custom_call_target="tpu_custom_call" | custom-call | tf_op jit(solution)/shard_map/near_weights/pallas_call | solution.py:260
  31.8 1.7 %copy-done.6 = f32[4,2,3,128,256]{4,3,2,1,0:T(8,128)} copy-done((f32[4,2,3,128,256]{4,3,2,1,0:T(8,128)}, f32[4,2,3,128,256]{4,3,2,1,0:T(8,128)S(1)}, u32[]{:S(2)}) %copy-start.6) | copy-done | bytes 3145752
  35.7 2.2 %near_products.1 = (bf16[4,2,256,128]{3,2,1,0:T(8,128)(2,1)S(1)}, f32[4,2,3,128,256]{4,3,2,1,0:T(8,128)S(1)}, f32[4,16,256]{2,1,0:T(8,128)S(1)}) custom-call(s32[1]{0:T(128)} %bitcast.core_ref, bf16[128,2048]{1,0:T(8,128)(2,1)S(1)} %copy-done.12, bf16[256,1024]{1,0:T(8,128)(2,1)S(1)} %copy-done.11, bf16[256,512]{1,0:T(8,128)(2,1)} %collective-permute-done.5.va, ...), custom_call_target="tpu_custom_call" | custom-call | tf_op jit(solution)/shard_map/near_products/pallas_call | solution.py:260
  37.9 1.6 %copy-done.8 = f32[4,2,3,128,256]{4,3,2,1,0:T(8,128)} copy-done((f32[4,2,3,128,256]{4,3,2,1,0:T(8,128)}, f32[4,2,3,128,256]{4,3,2,1,0:T(8,128)S(1)}, u32[]{:S(2)}) %copy-start.8) | copy-done | bytes 3145752
  39.5 4.3 %far_values.1 = (bf16[256,512]{1,0:T(8,128)(2,1)}, f32[4,2,2,128,256]{4,3,2,1,0:T(8,128)S(1)}, f32[4,2,2,128,256]{4,3,2,1,0:T(8,128)S(1)}, f32[4,16,256]{2,1,0:T(8,128)S(1)}) custom-call(s32[1]{0:T(128)} %bitcast.core_ref, s32[8,128]{1,0:T(8,128)S(1)} %concatenate.37.lo_ref, bf16[4,2,256,128]{3,2,1,0:T(8,128)(2,1)S(1)} %get-tuple-element.23.qs, ...), custom_call_target="tpu_custom_call" | custom-call | tf_op jit(solution)/shard_map/far_values/pallas_call | solution.py:260
  43.9 4.4 %collective-permute-start.11 = (bf16[256,512]{1,0:T(8,128)(2,1)}, bf16[256,512]{1,0:T(8,128)(2,1)}, u32[]{:S(2)}, u32[]{:S(2)}) collective-permute-start(bf16[256,512]{1,0:T(8,128)(2,1)} %get-tuple-element.42), channel_id=1, source_target_pairs={{2,0},{3,1},{4,2},{5,3},{6,4},{7,5},{8,6},{9,7},{10,8},{11,9},{12,... | collective-permute-start | bytes 786440 | tf_op jit(solution)/shard_map/ppermute | solution.py:34
  48.3 3.6 %far_keys.1 = (bf16[256,512]{1,0:T(8,128)(2,1)}, bf16[4,2,2,128,256]{4,3,2,1,0:T(8,128)(2,1)S(1)}, f32[4,16,256]{2,1,0:T(8,128)S(1)}) custom-call(s32[1]{0:T(128)} %bitcast.core_ref, bf16[4,2,256,128]{3,2,1,0:T(8,128)(2,1)S(1)} %get-tuple-element.23.qs, bf16[4,2,256,128]{3,2,1,0:T(8,128)(2,1)S(1)} %get-tuple-element.27.gs, ...), custom_call_target="tpu_custom_call" | custom-call | tf_op jit(solution)/shard_map/far_keys/pallas_call | solution.py:260
  51.9 1.4 %copy-done = f32[4,2,2,128,256]{4,3,2,1,0:T(8,128)} copy-done((f32[4,2,2,128,256]{4,3,2,1,0:T(8,128)}, f32[4,2,2,128,256]{4,3,2,1,0:T(8,128)S(1)}, u32[]{:S(2)}) %copy-start) | copy-done | bytes 2097176
  54.3 6.9 %collective-permute-start.8 = (bf16[256,512]{1,0:T(8,128)(2,1)}, bf16[256,512]{1,0:T(8,128)(2,1)}, u32[]{:S(2)}, u32[]{:S(2)}) collective-permute-start(bf16[256,512]{1,0:T(8,128)(2,1)} %get-tuple-element.39), channel_id=1, source_target_pairs={{2,0},{3,1},{4,2},{5,3},{6,4},{7,5},{8,6},{9,7},{10,8},{11,9},{12,... | collective-permute-start | bytes 786440 | tf_op jit(solution)/shard_map/ppermute | solution.py:34
  61.3 1.6 %copy-done.1 = f32[4,2,2,128,256]{4,3,2,1,0:T(8,128)S(1)} copy-done((f32[4,2,2,128,256]{4,3,2,1,0:T(8,128)S(1)}, f32[4,2,2,128,256]{4,3,2,1,0:T(8,128)}, u32[]{:S(2)}) %copy-start.1) | copy-done | bytes 2097176
  66.2 1.9 %copy-done.9 = f32[4,2,3,128,256]{4,3,2,1,0:T(8,128)S(1)} copy-done((f32[4,2,3,128,256]{4,3,2,1,0:T(8,128)S(1)}, f32[4,2,3,128,256]{4,3,2,1,0:T(8,128)}, u32[]{:S(2)}) %copy-start.9) | copy-done | bytes 3145752
  68.1 3.2 %near_keys.1 = (f32[256,512]{1,0:T(8,128)S(1)}, f32[256,512]{1,0:T(8,128)S(1)}, bf16[128,1024]{1,0:T(8,128)(2,1)S(1)}, bf16[128,1024]{1,0:T(8,128)(2,1)S(1)}) custom-call(s32[1]{0:T(128)} %bitcast.core_ref, bf16[4,2,256,128]{3,2,1,0:T(8,128)(2,1)S(1)} %copy-done.3, bf16[272,512]{1,0:T(8,128)(2,1)} %collective-permute-done.3.kb, ...), custom_call_target="tpu_custom_call" | custom-call | tf_op jit(solution)/shard_map/near_keys/pallas_call | solution.py:260
  71.3 2.3 %collective-permute-start.7 = (bf16[128,1024]{1,0:T(8,128)(2,1)S(1)}, bf16[128,1024]{1,0:T(8,128)(2,1)S(1)}, u32[]{:S(2)}, u32[]{:S(2)}) collective-permute-start(bf16[128,1024]{1,0:T(8,128)(2,1)S(1)} %get-tuple-element.36), channel_id=1, source_target_pairs={{0,1},{1,0},{2,3},{3,2},{4,5},{5,4},{6,7},{7,6},{8,9},{9,8},{10,11... | collective-permute-start | bytes 786440 | tf_op jit(solution)/shard_map/ppermute | solution.py:28
  74.6 1.9 %collective-permute-start.12 = (bf16[256,512]{1,0:T(8,128)(2,1)S(1)}, bf16[256,512]{1,0:T(8,128)(2,1)S(1)}, u32[]{:S(2)}, u32[]{:S(2)}) collective-permute-start(bf16[256,512]{1,0:T(8,128)(2,1)S(1)} %add_convert_fusion.1), channel_id=1, source_target_pairs={{2,0},{3,1},{4,2},{5,3},{6,4},{7,5},{8,6},{9,7},{10,8},{11,9},{12,... | collective-permute-start | bytes 786440 | tf_op jit(solution)/shard_map/ppermute | solution.py:34
  77.6 1.9 %collective-permute-start.9 = (bf16[256,512]{1,0:T(8,128)(2,1)S(1)}, bf16[256,512]{1,0:T(8,128)(2,1)S(1)}, u32[]{:S(2)}, u32[]{:S(2)}) collective-permute-start(bf16[256,512]{1,0:T(8,128)(2,1)S(1)} %add_convert_fusion.3), channel_id=1, source_target_pairs={{2,0},{3,1},{4,2},{5,3},{6,4},{7,5},{8,6},{9,7},{10,8},{11,9},{12,... | collective-permute-start | bytes 786440 | tf_op jit(solution)/shard_map/ppermute | solution.py:34
  80.4 4.0 %collective-permute-done.12 = bf16[256,512]{1,0:T(8,128)(2,1)S(1)} collective-permute-done((bf16[256,512]{1,0:T(8,128)(2,1)S(1)}, bf16[256,512]{1,0:T(8,128)(2,1)S(1)}, u32[]{:S(2)}, u32[]{:S(2)}) %collective-permute-start.12) | collective-permute-done | bytes 262176 | tf_op jit(solution)/shard_map/ppermute | solution.py:34
  84.5 1.3 %collective-permute-start.13 = (bf16[128,512]{1,0:T(8,128)(2,1)S(1)}, bf16[128,512]{1,0:T(8,128)(2,1)S(1)}, u32[]{:S(2)}, u32[]{:S(2)}) collective-permute-start(bf16[128,512]{1,0:T(8,128)(2,1)S(1)} %slice.33), channel_id=1, source_target_pairs={{0,1},{1,0},{2,3},{3,2},{4,5},{5,4},{6,7},{7,6},{8,9},{9,8},{10,11... | collective-permute-start | bytes 393224 | tf_op jit(solution)/shard_map/ppermute | solution.py:28
  85.8 4.3 %collective-permute-done.9 = bf16[256,512]{1,0:T(8,128)(2,1)S(1)} collective-permute-done((bf16[256,512]{1,0:T(8,128)(2,1)S(1)}, bf16[256,512]{1,0:T(8,128)(2,1)S(1)}, u32[]{:S(2)}, u32[]{:S(2)}) %collective-permute-start.9) | collective-permute-done | bytes 262176 | tf_op jit(solution)/shard_map/ppermute | solution.py:34
  (74 shorter events, 22.7 us)
Async XLA Ops:
  2.3 2.9 %collective-permute-start = (bf16[144,512]{1,0:T(8,128)(2,1)S(1)}, bf16[144,512]{1,0:T(8,128)(2,1)S(1)}, u32[]{:S(2)}, u32[]{:S(2)}) collective-permute-start(bf16[144,512]{1,0:T(8,128)(2,1)S(1)} %fusion.3), channel_id=1, source_target_pairs={{0,1},{1,0},{2,3},{3,2},{4,5},{5,4},{6,7},{7,6},{8,9},{9,8},{10,11... | collective-permute-start | bytes 442376 | tf_op jit(solution)/shard_map/ppermute | solution.py:28
  4.0 5.9 %collective-permute-start.4 = (bf16[128,512]{1,0:T(8,128)(2,1)S(1)}, bf16[128,512]{1,0:T(8,128)(2,1)S(1)}, u32[]{:S(2)}, u32[]{:S(2)}) collective-permute-start(bf16[128,512]{1,0:T(8,128)(2,1)S(1)} %get-tuple-element.52), channel_id=1, source_target_pairs={{0,1},{1,0},{2,3},{3,2},{4,5},{5,4},{6,7},{7,6},{8,9},{9,8},{10,11... | collective-permute-start | bytes 393224 | tf_op jit(solution)/shard_map/ppermute | solution.py:28
  5.9 9.7 %collective-permute-start.2 = (bf16[272,512]{1,0:T(8,128)(2,1)S(1)}, bf16[272,512]{1,0:T(8,128)(2,1)}, u32[]{:S(2)}, u32[]{:S(2)}) collective-permute-start(bf16[272,512]{1,0:T(8,128)(2,1)S(1)} %fusion.2.kc), channel_id=1, source_target_pairs={{0,2},{1,3},{2,4},{3,5},{4,6},{5,7},{6,8},{7,9},{8,10},{9,11},{10,... | collective-permute-start | bytes 835592 | tf_op jit(solution)/shard_map/ppermute | solution.py:34
  9.1 16.6 %collective-permute-start.1 = (bf16[256,1024]{1,0:T(8,128)(2,1)S(1)}, bf16[256,1024]{1,0:T(8,128)(2,1)S(1)}, u32[]{:S(2)}, u32[]{:S(2)}) collective-permute-start(bf16[256,1024]{1,0:T(8,128)(2,1)S(1)} %pad_maximum_fusion), channel_id=1, source_target_pairs={{0,1},{1,0},{2,3},{3,2},{4,5},{5,4},{6,7},{7,6},{8,9},{9,8},{10,11... | collective-permute-start | bytes 1572872 | tf_op jit(solution)/shard_map/ppermute | solution.py:28
  10.0 11.2 %collective-permute-start.5 = (bf16[256,512]{1,0:T(8,128)(2,1)S(1)}, bf16[256,512]{1,0:T(8,128)(2,1)}, u32[]{:S(2)}, u32[]{:S(2)}) collective-permute-start(bf16[256,512]{1,0:T(8,128)(2,1)S(1)} %pad_maximum_fusion.2.vc), channel_id=1, source_target_pairs={{0,2},{1,3},{2,4},{3,5},{4,6},{5,7},{6,8},{7,9},{8,10},{9,11},{10,... | collective-permute-start | bytes 786440 | tf_op jit(solution)/shard_map/ppermute | solution.py:34
  15.6 23.9 %collective-permute-start.3 = (bf16[272,512]{1,0:T(8,128)(2,1)}, bf16[272,512]{1,0:T(8,128)(2,1)}, u32[]{:S(2)}, u32[]{:S(2)}) collective-permute-start(bf16[272,512]{1,0:T(8,128)(2,1)} %collective-permute-done.2.ka), channel_id=1, source_target_pairs={{0,2},{1,3},{2,4},{3,5},{4,6},{5,7},{6,8},{7,9},{8,10},{9,11},{10,... | collective-permute-start | bytes 835592 | tf_op jit(solution)/shard_map/ppermute | solution.py:34
  21.2 27.0 %collective-permute-start.6 = (bf16[256,512]{1,0:T(8,128)(2,1)}, bf16[256,512]{1,0:T(8,128)(2,1)}, u32[]{:S(2)}, u32[]{:S(2)}) collective-permute-start(bf16[256,512]{1,0:T(8,128)(2,1)} %collective-permute-done.5.va), channel_id=1, source_target_pairs={{0,2},{1,3},{2,4},{3,5},{4,6},{5,7},{6,8},{7,9},{8,10},{9,11},{10,... | collective-permute-start | bytes 786440 | tf_op jit(solution)/shard_map/ppermute | solution.py:34
  31.8 1.7 %copy-start.6 = (f32[4,2,3,128,256]{4,3,2,1,0:T(8,128)}, f32[4,2,3,128,256]{4,3,2,1,0:T(8,128)S(1)}, u32[]{:S(2)}) copy-start(f32[4,2,3,128,256]{4,3,2,1,0:T(8,128)S(1)} %get-tuple-element.24.u_near) | copy-start | bytes 9437188
  33.5 14.8 %copy-start.2 = (bf16[4,2,256,128]{3,2,1,0:T(8,128)(2,1)}, bf16[4,2,256,128]{3,2,1,0:T(8,128)(2,1)S(1)}, u32[]{:S(2)}) copy-start(bf16[4,2,256,128]{3,2,1,0:T(8,128)(2,1)S(1)} %get-tuple-element.23.qs) | copy-start | bytes 1572868
  33.5 1.2 %copy-start.12 = (bf16[128,2048]{1,0:T(8,128)(2,1)S(1)}, bf16[128,2048]{1,0:T(8,128)(2,1)}, u32[]{:S(2)}) copy-start(bf16[128,2048]{1,0:T(8,128)(2,1)} %go.1) | copy-start | bytes 1572868
  37.9 1.6 %copy-start.8 = (f32[4,2,3,128,256]{4,3,2,1,0:T(8,128)}, f32[4,2,3,128,256]{4,3,2,1,0:T(8,128)S(1)}, u32[]{:S(2)}) copy-start(f32[4,2,3,128,256]{4,3,2,1,0:T(8,128)S(1)} %get-tuple-element.26.dp_near) | copy-start | bytes 9437188
  39.5 12.4 %copy-start.4 = (bf16[4,2,256,128]{3,2,1,0:T(8,128)(2,1)}, bf16[4,2,256,128]{3,2,1,0:T(8,128)(2,1)S(1)}, u32[]{:S(2)}) copy-start(bf16[4,2,256,128]{3,2,1,0:T(8,128)(2,1)S(1)} %get-tuple-element.27.gs) | copy-start | bytes 1572868
  43.9 29.7 %collective-permute-start.11 = (bf16[256,512]{1,0:T(8,128)(2,1)}, bf16[256,512]{1,0:T(8,128)(2,1)}, u32[]{:S(2)}, u32[]{:S(2)}) collective-permute-start(bf16[256,512]{1,0:T(8,128)(2,1)} %get-tuple-element.42), channel_id=1, source_target_pairs={{2,0},{3,1},{4,2},{5,3},{6,4},{7,5},{8,6},{9,7},{10,8},{11,9},{12,... | collective-permute-start | bytes 786440 | tf_op jit(solution)/shard_map/ppermute | solution.py:34
  51.9 1.4 %copy-start = (f32[4,2,2,128,256]{4,3,2,1,0:T(8,128)}, f32[4,2,2,128,256]{4,3,2,1,0:T(8,128)S(1)}, u32[]{:S(2)}) copy-start(f32[4,2,2,128,256]{4,3,2,1,0:T(8,128)S(1)} %get-tuple-element.29.w_far) | copy-start | bytes 6291460
  54.3 22.2 %collective-permute-start.8 = (bf16[256,512]{1,0:T(8,128)(2,1)}, bf16[256,512]{1,0:T(8,128)(2,1)}, u32[]{:S(2)}, u32[]{:S(2)}) collective-permute-start(bf16[256,512]{1,0:T(8,128)(2,1)} %get-tuple-element.39), channel_id=1, source_target_pairs={{2,0},{3,1},{4,2},{5,3},{6,4},{7,5},{8,6},{9,7},{10,8},{11,9},{12,... | collective-permute-start | bytes 786440 | tf_op jit(solution)/shard_map/ppermute | solution.py:34
  61.3 1.6 %copy-start.1 = (f32[4,2,2,128,256]{4,3,2,1,0:T(8,128)S(1)}, f32[4,2,2,128,256]{4,3,2,1,0:T(8,128)}, u32[]{:S(2)}) copy-start(f32[4,2,2,128,256]{4,3,2,1,0:T(8,128)} %copy-done) | copy-start | bytes 6291460
  63.9 2.1 %copy-start.7 = (f32[4,2,3,128,256]{4,3,2,1,0:T(8,128)S(1)}, f32[4,2,3,128,256]{4,3,2,1,0:T(8,128)}, u32[]{:S(2)}) copy-start(f32[4,2,3,128,256]{4,3,2,1,0:T(8,128)} %copy-done.6) | copy-start | bytes 9437188
  63.9 2.3 %copy-start.15 = (bf16[4,2,2,128,256]{4,3,2,1,0:T(8,128)(2,1)S(1)}, bf16[4,2,2,128,256]{4,3,2,1,0:T(8,128)(2,1)}, u32[]{:S(2)}) copy-start(bf16[4,2,2,128,256]{4,3,2,1,0:T(8,128)(2,1)} %copy-done.14) | copy-start | bytes 3145732
  66.2 1.9 %copy-start.9 = (f32[4,2,3,128,256]{4,3,2,1,0:T(8,128)S(1)}, f32[4,2,3,128,256]{4,3,2,1,0:T(8,128)}, u32[]{:S(2)}) copy-start(f32[4,2,3,128,256]{4,3,2,1,0:T(8,128)} %copy-done.8) | copy-start | bytes 9437188
  71.3 8.2 %collective-permute-start.7 = (bf16[128,1024]{1,0:T(8,128)(2,1)S(1)}, bf16[128,1024]{1,0:T(8,128)(2,1)S(1)}, u32[]{:S(2)}, u32[]{:S(2)}) collective-permute-start(bf16[128,1024]{1,0:T(8,128)(2,1)S(1)} %get-tuple-element.36), channel_id=1, source_target_pairs={{0,1},{1,0},{2,3},{3,2},{4,5},{5,4},{6,7},{7,6},{8,9},{9,8},{10,11... | collective-permute-start | bytes 786440 | tf_op jit(solution)/shard_map/ppermute | solution.py:28
  74.6 9.8 %collective-permute-start.12 = (bf16[256,512]{1,0:T(8,128)(2,1)S(1)}, bf16[256,512]{1,0:T(8,128)(2,1)S(1)}, u32[]{:S(2)}, u32[]{:S(2)}) collective-permute-start(bf16[256,512]{1,0:T(8,128)(2,1)S(1)} %add_convert_fusion.1), channel_id=1, source_target_pairs={{2,0},{3,1},{4,2},{5,3},{6,4},{7,5},{8,6},{9,7},{10,8},{11,9},{12,... | collective-permute-start | bytes 786440 | tf_op jit(solution)/shard_map/ppermute | solution.py:34
  77.6 12.5 %collective-permute-start.9 = (bf16[256,512]{1,0:T(8,128)(2,1)S(1)}, bf16[256,512]{1,0:T(8,128)(2,1)S(1)}, u32[]{:S(2)}, u32[]{:S(2)}) collective-permute-start(bf16[256,512]{1,0:T(8,128)(2,1)S(1)} %add_convert_fusion.3), channel_id=1, source_target_pairs={{2,0},{3,1},{4,2},{5,3},{6,4},{7,5},{8,6},{9,7},{10,8},{11,9},{12,... | collective-permute-start | bytes 786440 | tf_op jit(solution)/shard_map/ppermute | solution.py:34
  84.5 6.5 %collective-permute-start.13 = (bf16[128,512]{1,0:T(8,128)(2,1)S(1)}, bf16[128,512]{1,0:T(8,128)(2,1)S(1)}, u32[]{:S(2)}, u32[]{:S(2)}) collective-permute-start(bf16[128,512]{1,0:T(8,128)(2,1)S(1)} %slice.33), channel_id=1, source_target_pairs={{0,1},{1,0},{2,3},{3,2},{4,5},{5,4},{6,7},{7,6},{8,9},{9,8},{10,11... | collective-permute-start | bytes 393224 | tf_op jit(solution)/shard_map/ppermute | solution.py:28
  90.1 1.9 %collective-permute-start.10 = (bf16[128,512]{1,0:T(8,128)(2,1)S(1)}, bf16[128,512]{1,0:T(8,128)(2,1)S(1)}, u32[]{:S(2)}, u32[]{:S(2)}) collective-permute-start(bf16[128,512]{1,0:T(8,128)(2,1)S(1)} %slice.31), channel_id=1, source_target_pairs={{0,1},{1,0},{2,3},{3,2},{4,5},{5,4},{6,7},{7,6},{8,9},{9,8},{10,11... | collective-permute-start | bytes 393224 | tf_op jit(solution)/shard_map/ppermute | solution.py:28
  (8 other events, 7.7 us)

commit v3 on v2

v3 whole, which is shorter than its diff:
```python
import functools

import jax
import jax.numpy as jnp
from jax import lax
from jax.experimental import pallas as pl
from jax.experimental.pallas import tpu as pltpu
from jax.sharding import PartitionSpec as P

HEAD_DIM = 128
WINDOW = 512
SOFTCAP = 50.0
SCALE = 1.0 / 12.0
LOG2E = 1.4426950408889634
AXES = ("ctx", "fsdp")
NT = (((1,), (1,)), ((), ()))
NN = (((1,), (0,)), ((), ()))
SEG_ROWS = 16
FAR = 2


def dot(a, b, dims):
    return lax.dot_general(a, b, dims, preferred_element_type=jnp.float32)


def swap(x):
    n = lax.axis_size(AXES)
    return lax.ppermute(x, AXES, [(i, i ^ 1) for i in range(n)])


def hop(x, chips):
    n = lax.axis_size(AXES)
    by = 2 * chips
    return lax.ppermute(x, AXES, [(i, i + by) for i in range(n) if 0 <= i + by < n])


def cross(x, chips):
    n = lax.axis_size(AXES)
    by = 2 * chips
    return lax.ppermute(x, AXES, [(i, (i ^ 1) + by) for i in range(n) if 0 <= i + by < n])


def rows_at(core, half, tok):
    return pl.ds(pl.multiple_of(lax.bitwise_xor(core, half) * tok, tok), tok)


def lanes_at(g):
    return pl.ds(pl.multiple_of(g * HEAD_DIM, HEAD_DIM), HEAD_DIM)


def block_of(core, pieces, b, g, tok):
    return pieces[b // 2][rows_at(core, b % 2, tok), lanes_at(g)]


def seen(lo, seg_ref, tok):
    ids = seg_ref[2 * tok : 2 * tok + 1, : 2 * tok].astype(jnp.float32)
    same = jnp.where(ids == lo[2:3, 0:1].astype(jnp.float32), 1.0, 0.0)
    return jnp.sum(same, axis=1, keepdims=True).astype(jnp.int32)


def first_keys(core, lo, count, half, tok):
    mine = jnp.where(core == half, lo[0:1], lo[1:2])
    mine = jnp.where(mine < 0, WINDOW - count, mine) - half * tok
    row = lax.broadcasted_iota(jnp.int32, (1, tok), 1)
    mine = jnp.maximum(mine, row + 1)
    return jnp.concatenate([mine, mine], 1)


def keys_of(core, pieces, blocks, g, tok):
    return jnp.concatenate([block_of(core, pieces, b, g, tok) for b in blocks], 0)


def weights_of(s, lo, jj, last, tok):
    t = jnp.tanh(s * (SCALE / SOFTCAP))
    w = jnp.exp2(t * (SOFTCAP * LOG2E))
    pos = lax.broadcasted_iota(jnp.int32, s.shape, 0)
    ok = pos >= lo - jj * tok
    if last:
        col = lax.broadcasted_iota(jnp.int32, s.shape, 1)
        ok = ok & (pos <= jnp.where(col >= tok, col - tok, col))
    return t, jnp.where(ok, w, 0.0)


def slope(t):
    return SCALE - t * t * SCALE


def cut(x, i, tok):
    return x[i * tok : (i + 1) * tok]


def fold(x):
    return jnp.sum(x.reshape(x.shape[0] // 8, 8, x.shape[1]), axis=0)


def stack_heads(tok, groups, core_ref, q, go, qgx, qs, gs):
    core = core_ref[0]
    for g in range(groups):
        for hd in range(2):
            at = (core * groups + g) * 2 + hd
            here = pl.ds(hd * tok, tok)
            qs[g, core, here, :] = q[:, lanes_at(at)]
            gs[g, core, here, :] = go[:, lanes_at(at)]
            qs[g, 1 - core, here, :] = qgx[:tok, lanes_at(g * 2 + hd)]
            gs[g, 1 - core, here, :] = qgx[tok:, lanes_at(g * 2 + hd)]


def near_sums(tok, groups, core_ref, lo_ref, qs, gs, ka, kc, va, vc, tot, term):
    core = core_ref[0]
    lo_all = lo_ref[...]
    count = seen(lo_all, ka, tok)
    los = [first_keys(core, lo_all, count, h, tok) for h in range(2)]
    blocks = WINDOW // tok + 1

    def step(g, _):
        for h in range(2):
            near = range(h + FAR, h + blocks)
            s = dot(keys_of(core, (None, ka, kc), near, g, tok), qs[g, h], NT)
            dp = dot(keys_of(core, (None, va, vc), near, g, tok), gs[g, h], NT)
            total = jnp.zeros((8, 2 * tok), jnp.float32)
            mean = jnp.zeros((8, 2 * tok), jnp.float32)
            for jj in range(FAR, blocks):
                _, w = weights_of(cut(s, jj - FAR, tok), los[h], jj, jj == blocks - 1, tok)
                total = total + fold(w)
                mean = mean + fold(w * cut(dp, jj - FAR, tok))
            tot[g, pl.ds(8 * h, 8), :] = total
            term[g, pl.ds(8 * h, 8), :] = mean
        return 0

    lax.fori_loop(0, groups, step, 0, unroll=True)


def far_values(tok, groups, core_ref, lo_ref, qs, gs, ka, kb, tot, dvb, inv):
    core = core_ref[0]
    lo_all = lo_ref[...]
    count = seen(lo_all, ka, tok) + seen(lo_all, kb, tok)
    los = [first_keys(core, lo_all, count, h, tok) for h in range(2)]

    def step(g, _):
        accs = []
        for h in range(2):
            s = dot(keys_of(core, (kb, ka), range(h, h + FAR), g, tok), qs[g, h], NT)
            total = tot[g, pl.ds(8 * h, 8), :]
            ws = []
            for jj in range(FAR):
                _, w = weights_of(cut(s, jj, tok), los[h], jj, False, tok)
                total = total + fold(w)
                ws.append(w)
            one = 1.0 / jnp.sum(total, axis=0, keepdims=True)
            inv[g, pl.ds(8 * h, 8), :] = jnp.broadcast_to(one, (8, 2 * tok))
            low = jnp.concatenate([(w * one).astype(jnp.bfloat16) for w in ws[: FAR - h]], 0)
            accs.append(dot(low, gs[g, h], NN))
        spread(core, accs, 0, (dvb,), g, tok)
        return 0

    lax.fori_loop(0, groups, step, 0, unroll=True)


def spread(core, accs, start, outs, g, tok):
    first = (start, max(start, 1))
    for b in range(start, start + 2 * len(outs)):
        acc = None
        for h in range(2):
            i = b - first[h]
            if 0 <= i < accs[h].shape[0] // tok:
                piece = cut(accs[h], i, tok)
                acc = piece if acc is None else acc + piece
        out = outs[(b - start) // 2]
        out[rows_at(core, b % 2, tok), lanes_at(g)] = acc.astype(out.dtype)


def far_keys(tok, groups, core_ref, lo_ref, qs, gs, ka, kb, va, vb, inv, term, dkb, row):
    core = core_ref[0]
    lo_all = lo_ref[...]
    count = seen(lo_all, ka, tok) + seen(lo_all, kb, tok)
    los = [first_keys(core, lo_all, count, h, tok) for h in range(2)]

    def step(g, _):
        accs = []
        for h in range(2):
            s = dot(keys_of(core, (kb, ka), range(h, h + FAR), g, tok), qs[g, h], NT)
            dp = dot(keys_of(core, (vb, va), range(h, h + FAR), g, tok), gs[g, h], NT)
            one = inv[g, pl.ds(8 * h, 1), :]
            total = term[g, pl.ds(8 * h, 8), :]
            us = []
            for jj in range(FAR):
                t, w = weights_of(cut(s, jj, tok), los[h], jj, False, tok)
                total = total + fold(w * cut(dp, jj, tok))
                us.append(w * slope(t))
            mean = one * jnp.sum(total, axis=0, keepdims=True)
            row[g, pl.ds(8 * h, 8), :] = jnp.broadcast_to(mean, (8, 2 * tok))
            low = [((us[jj] * one) * (cut(dp, jj, tok) - mean)).astype(jnp.bfloat16) for jj in range(FAR - h)]
            accs.append(dot(jnp.concatenate(low, 0), qs[g, h], NN))
        spread(core, accs, 0, (dkb,), g, tok)
        return 0

    lax.fori_loop(0, groups, step, 0, unroll=True)


def near_grads(tok, groups, core_ref, lo_ref, qs, gs, kb, ka, kc, vb, va, vc, inv, row,
               dva, dvc, dka, dkc, dq0, dq1, dq_s):
    core = core_ref[0]
    lo_all = lo_ref[...]
    count = seen(lo_all, ka, tok) + seen(lo_all, kb, tok)
    los = [first_keys(core, lo_all, count, h, tok) for h in range(2)]
    blocks = WINDOW // tok + 1

    def step(g, _):
        dvs, dks = [], []
        for h in range(2):
            k_rows = keys_of(core, (kb, ka, kc), range(h, h + blocks), g, tok)
            v_rows = keys_of(core, (vb, va, vc), range(h, h + blocks), g, tok)
            s = dot(k_rows, qs[g, h], NT)
            dp = dot(v_rows, gs[g, h], NT)
            one = inv[g, pl.ds(8 * h, 1), :]
            mean = row[g, pl.ds(8 * h, 1), :]
            low, dlow = [], []
            for jj in range(blocks):
                t, w = weights_of(cut(s, jj, tok), los[h], jj, jj == blocks - 1, tok)
                p = w * one
                low.append(p.astype(jnp.bfloat16))
                ds = p * slope(t) * (cut(dp, jj, tok) - mean)
                dlow.append(ds.astype(jnp.bfloat16))
            dvs.append(dot(jnp.concatenate(low[FAR - h :], 0), gs[g, h], NN))
            dks.append(dot(jnp.concatenate(dlow[FAR - h :], 0), qs[g, h], NN))
            dq_t = dot(k_rows.T, jnp.concatenate(dlow, 0), NN)
            dq_s[g, lax.bitwise_xor(core, h)] = dq_t.T.astype(jnp.bfloat16)
        spread(core, dvs, FAR, (dva, dvc), g, tok)
        spread(core, dks, FAR, (dka, dkc), g, tok)
        for r, dq in enumerate((dq0, dq1)):
            for hd in range(2):
                dq[:, lanes_at(2 * g + hd)] = dq_s[g, r, hd * tok : (hd + 1) * tok, :]
        return 0

    lax.fori_loop(0, groups, step, 0, unroll=True)


def call(body, tok, groups, args, outs, scratch=()):
    vmem = pl.BlockSpec(memory_space=pltpu.VMEM)
    return pl.pallas_call(
        functools.partial(body, tok, groups),
        in_specs=[pl.BlockSpec(memory_space=pltpu.SMEM)] + [vmem] * (len(args) - 1),
        out_specs=[vmem] * len(outs),
        out_shape=[jax.ShapeDtypeStruct(s, d) for s, d in outs],
        scratch_shapes=list(scratch),
        compiler_params=pltpu.CompilerParams(vmem_limit_bytes=VMEM_LIMIT),
        name=body.__name__,
    )(*args)


VMEM_LIMIT = 4 * 1024 * 1024


def local(queries, keys, values, grad_out, segment):
    tok = queries.shape[0]
    kv_width = keys.shape[1]
    half = kv_width // 2
    groups = half // HEAD_DIM
    q_half = queries.shape[1] // 2
    bf16, f32 = jnp.bfloat16, jnp.float32
    core = lax.rem(lax.axis_index(AXES), 2)
    core_arr = core.reshape(1).astype(jnp.int32)

    def part(x, which, width):
        return lax.dynamic_slice(x, (0, which * width), (x.shape[0], width))

    seg_own = (segment + 1).astype(bf16)[None, :]
    seg_row = jnp.pad(seg_own, ((0, SEG_ROWS - 1), (0, half - tok)))
    own_row = jnp.pad(seg_own, ((0, SEG_ROWS - 1), (tok, half - 2 * tok)))
    k_out = jnp.concatenate([part(keys, 1 - core, half), seg_row], 0)
    k_in = swap(k_out)
    kc = jnp.concatenate([part(keys, core, half), k_in[:tok], k_in[tok:] + own_row], 0)
    values, _ = lax.optimization_barrier((values, kc))
    v_in = swap(part(values, 1 - core, half))
    vc = jnp.concatenate([part(values, core, half), v_in], 0)
    ka = hop(kc, 1)
    va = hop(vc, 1)
    queries, grad_out, _ = lax.optimization_barrier((queries, grad_out, kc))
    qg_in = swap(jnp.concatenate([part(queries, 1 - core, q_half), part(grad_out, 1 - core, q_half)], 0))

    seg_f = jnp.concatenate([seg_own[0], k_in[tok, :tok]]).astype(f32)
    seg0 = jnp.min(seg_f)
    before = jnp.sum((seg_f[:, None] < seg_f[None, :]).astype(jnp.int32), axis=0)
    starts = jnp.where(seg_f == seg0, -1, WINDOW + before).reshape(2, tok)
    lo = jnp.concatenate([starts, jnp.full((6, tok), seg0.astype(jnp.int32), jnp.int32)], 0)

    rows = ((groups, 2, 2 * tok, HEAD_DIM), bf16)
    stat = ((groups, 16, 2 * tok), f32)
    kv_f = ((2 * tok, half), f32)
    kv_b = ((2 * tok, half), bf16)
    dq_o = ((tok, q_half), bf16)

    qs, gs = call(stack_heads, tok, groups, (core_arr, queries, grad_out, qg_in), [rows, rows])
    va, qs, gs, lo = lax.optimization_barrier((va, qs, gs, lo))
    kb = hop(ka, 1)
    vb = hop(va, 1)
    tot, term = call(
        near_sums, tok, groups, (core_arr, lo, qs, gs, ka, kc, va, vc), [stat, stat])
    dvb, inv = call(
        far_values, tok, groups, (core_arr, lo, qs, gs, ka, kb, tot), [kv_b, stat])
    cv = hop(dvb, -1)
    dkb, row = call(
        far_keys, tok, groups, (core_arr, lo, qs, gs, ka, kb, va, vb, inv, term), [kv_b, stat])
    ck = hop(dkb, -1)
    dva, dvc, dka, dkc, dq0, dq1 = call(
        near_grads, tok, groups, (core_arr, lo, qs, gs, kb, ka, kc, vb, va, vc, inv, row),
        [kv_f, kv_f, kv_f, kv_f, dq_o, dq_o],
        [pltpu.VMEM((groups, 2, 2 * tok, HEAD_DIM), bf16)])
    dv = hop((dva + cv.astype(f32)).astype(bf16), -1)
    dk_out = (dka + ck.astype(f32)).astype(bf16)
    dk_same = hop(dk_out[:tok], -1)
    dk_cross = cross(dk_out[tok:], -1)
    def place(mine, other):
        first = jnp.where(core == 0, mine, other)
        second = jnp.where(core == 0, other, mine)
        return jnp.concatenate([first, second], 1)

    grad_q = place(dq0, swap(dq1))
    sum_v = dvc + dv.astype(f32)
    grad_v = place(sum_v[:tok].astype(bf16), swap(sum_v[tok:].astype(bf16)))
    other_k = swap(dkc[tok:])
    same = (dkc[:tok] + dk_same.astype(f32)).astype(bf16)
    other = (other_k + dk_cross.astype(f32)).astype(bf16)
    grad_k = place(same, other)
    return grad_q, grad_k, grad_v


def solution(mesh):
    rows = P(AXES, None)
    return jax.shard_map(
        local,
        mesh=mesh,
        in_specs=(rows, rows, rows, rows, P(AXES)),
        out_specs=(rows, rows, rows),
        check_vma=False,
    )
```

time: 93.6 us -> 67.2 us (0.72)
  the two profiles are of different devices: /device:TPU:13 before, /device:TPU:26 now
where the time goes in v3:
time: 67.2 us; the launch traced here: 66.1 us
  starting transfers between devices  28.3 us (42%)
  waiting for transfers between devices  15.1 us (22%)
  Pallas kernels  9.27 us (14%)
  other arithmetic  6.03 us (9%)
  local copies, waits for them, and re-layouts  5.74 us (9%)
  between operations  1.67 us (2%)
    ppermute x8, starting transfers between devices, hop(): lax.ppermute(x, AXES, [(i, i + by) for i in range(n) if 0 <= i + by < n])  25.5 us
    ppermute x8, waiting for transfers between devices, hop(): lax.ppermute(x, AXES, [(i, i + by) for i in range(n) if 0 <= i + by < n])  10.4 us
    pallas_call x5, Pallas kernels, call(): pl.pallas_call(functools.partial(body, tok, groups), in_specs=[pl.BlockSp...  9.27 us
    unnamed x14, local copies, waits for them, and re-layouts  3.94 us
    ppermute x1, waiting for transfers between devices, cross(): lax.ppermute(x, AXES, [(i, (i ^ 1) + by) for i in range(n) if 0 <= i + by...  2.63 us
    concatenate x3, other arithmetic, place(): return jnp.concatenate([first, second], 1)  2.29 us
    ppermute x6, waiting for transfers between devices, swap(): return lax.ppermute(x, AXES, [(i, i ^ 1) for i in range(n)])  2 us
    ppermute x1, starting transfers between devices, cross(): lax.ppermute(x, AXES, [(i, (i ^ 1) + by) for i in range(n) if 0 <= i + by...  1.92 us
  transfers between devices with their start and end apart: 15, of which 8 were waited for; matrix products, arithmetic and copies ran while one was open for 9% of the time, Pallas kernels for 14%

profile of v3, /device:TPU:26, one launch (start us, length us, event | category | flops | bytes accessed | tf_op | source)
XLA Modules:
  0.0 66.1 jit_solution(2470002067686022786)
XLA Ops:
  1.3 1.0 %constant_dynamic-slice_fusion.5 = (bf16[128,512]{1,0:T(8,128)(2,1)S(1)}, bf16[128,512]{1,0:T(8,128)(2,1)S(1)}) fusion(bf16[128,1024]{1,0:T(8,128)(2,1)} %param.6, s32[]{:T(128)S(6)} %select_n.53, s32[]{:T(128)S(6)} %select_n.54), kind=kLoop, calls=%fused_computation.28 | loop fusion | bytes 524296 | tf_op jit(solution)/shard_map/dynamic_slice | solution.py:265
  2.4 1.4 %collective-permute-done = bf16[144,512]{1,0:T(8,128)(2,1)S(1)} collective-permute-done((bf16[144,512]{1,0:T(8,128)(2,1)S(1)}, bf16[144,512]{1,0:T(8,128)(2,1)S(1)}, u32[]{:S(2)}, u32[]{:S(2)}) %collective-permute-start) | collective-permute-done | bytes 147488 | tf_op jit(solution)/shard_map/ppermute | solution.py:28
  4.5 3.1 %collective-permute-start.4 = (bf16[272,512]{1,0:T(8,128)(2,1)S(1)}, bf16[272,512]{1,0:T(8,128)(2,1)S(1)}, u32[]{:S(2)}, u32[]{:S(2)}) collective-permute-start(bf16[272,512]{1,0:T(8,128)(2,1)S(1)} %pad_maximum_fusion.2.kc), channel_id=1, source_target_pairs={{0,2},{1,3},{2,4},{3,5},{4,6},{5,7},{6,8},{7,9},{8,10},{9,11},{10,... | collective-permute-start | bytes 835592 | tf_op jit(solution)/shard_map/ppermute | solution.py:34
  10.0 3.5 %collective-permute-start.2 = (bf16[256,512]{1,0:T(8,128)(2,1)S(1)}, bf16[256,512]{1,0:T(8,128)(2,1)S(1)}, u32[]{:S(2)}, u32[]{:S(2)}) collective-permute-start(bf16[256,512]{1,0:T(8,128)(2,1)S(1)} %pad_maximum_fusion.3.vc), channel_id=1, source_target_pairs={{0,2},{1,3},{2,4},{3,5},{4,6},{5,7},{6,8},{7,9},{8,10},{9,11},{10,... | collective-permute-start | bytes 786440 | tf_op jit(solution)/shard_map/ppermute | solution.py:34
  13.5 1.9 %collective-permute-done.4.ka = bf16[272,512]{1,0:T(8,128)(2,1)S(1)} collective-permute-done((bf16[272,512]{1,0:T(8,128)(2,1)S(1)}, bf16[272,512]{1,0:T(8,128)(2,1)S(1)}, u32[]{:S(2)}, u32[]{:S(2)}) %collective-permute-start.4) | collective-permute-done | bytes 278560 | tf_op jit(solution)/shard_map/ppermute | solution.py:34
  15.4 6.3 %collective-permute-start.5 = (bf16[272,512]{1,0:T(8,128)(2,1)S(1)}, bf16[272,512]{1,0:T(8,128)(2,1)S(1)}, u32[]{:S(2)}, u32[]{:S(2)}) collective-permute-start(bf16[272,512]{1,0:T(8,128)(2,1)S(1)} %collective-permute-done.4.ka), channel_id=1, source_target_pairs={{0,2},{1,3},{2,4},{3,5},{4,6},{5,7},{6,8},{7,9},{8,10},{9,11},{10,... | collective-permute-start | bytes 835592 | tf_op jit(solution)/shard_map/ppermute | solution.py:34
  24.6 1.0 %copy-done.3 = bf16[256,1024]{1,0:T(8,128)(2,1)S(1)} copy-done((bf16[256,1024]{1,0:T(8,128)(2,1)S(1)}, bf16[256,1024]{1,0:T(8,128)(2,1)}, u32[]{:S(2)}) %copy-start.3) | copy-done | bytes 524312
  25.8 1.9 %collective-permute-start.6 = (bf16[256,512]{1,0:T(8,128)(2,1)S(1)}, bf16[256,512]{1,0:T(8,128)(2,1)S(1)}, u32[]{:S(2)}, u32[]{:S(2)}) collective-permute-start(bf16[256,512]{1,0:T(8,128)(2,1)S(1)} %collective-permute-done.2.va), channel_id=1, source_target_pairs={{0,2},{1,3},{2,4},{3,5},{4,6},{5,7},{6,8},{7,9},{8,10},{9,11},{10,... | collective-permute-start | bytes 786440 | tf_op jit(solution)/shard_map/ppermute | solution.py:34
  27.7 1.1 %near_sums.1 = (f32[4,16,256]{2,1,0:T(8,128)S(1)}, f32[4,16,256]{2,1,0:T(8,128)S(1)}) custom-call(s32[1]{0:T(128)} %bitcast.core_ref, s32[8,128]{1,0:T(8,128)S(1)} %concatenate.40.lo_ref, bf16[4,2,256,128]{3,2,1,0:T(8,128)(2,1)S(1)} %get-tuple-element.30.qs, bf16[4,2,256,128]{3,2,1,0:T(8,128)(2,1)S(1)} %get-tuple-element.31.gs, ...), custom_call_target="tpu_custom_call" | custom-call | tf_op jit(solution)/shard_map/near_sums/pallas_call | solution.py:240
  28.9 1.7 %far_values.1 = (bf16[256,512]{1,0:T(8,128)(2,1)S(1)}, f32[4,16,256]{2,1,0:T(8,128)S(1)}) custom-call(s32[1]{0:T(128)} %bitcast.core_ref, s32[8,128]{1,0:T(8,128)S(1)} %concatenate.40.lo_ref, bf16[4,2,256,128]{3,2,1,0:T(8,128)(2,1)S(1)} %get-tuple-element.30.qs, bf16[4,2,256,128]{3,2,1,0:T(8,128)(2,1)S(1)} %get-tuple-element.31.gs, ...), custom_call_target="tpu_custom_call" | custom-call | tf_op jit(solution)/shard_map/far_values/pallas_call | solution.py:240
  30.6 3.9 %collective-permute-start.12 = (bf16[256,512]{1,0:T(8,128)(2,1)S(1)}, bf16[256,512]{1,0:T(8,128)(2,1)}, u32[]{:S(2)}, u32[]{:S(2)}) collective-permute-start(bf16[256,512]{1,0:T(8,128)(2,1)S(1)} %get-tuple-element.44), channel_id=1, source_target_pairs={{2,0},{3,1},{4,2},{5,3},{6,4},{7,5},{8,6},{9,7},{10,8},{11,9},{12,... | collective-permute-start | bytes 786440 | tf_op jit(solution)/shard_map/ppermute | solution.py:34
  35.0 2.3 %far_keys.1 = (bf16[256,512]{1,0:T(8,128)(2,1)S(1)}, f32[4,16,256]{2,1,0:T(8,128)S(1)}) custom-call(s32[1]{0:T(128)} %bitcast.core_ref, s32[8,128]{1,0:T(8,128)S(1)} %concatenate.40.lo_ref, bf16[4,2,256,128]{3,2,1,0:T(8,128)(2,1)S(1)} %get-tuple-element.30.qs, bf16[4,2,256,128]{3,2,1,0:T(8,128)(2,1)S(1)} %get-tuple-element.31.gs, ...), custom_call_target="tpu_custom_call" | custom-call | tf_op jit(solution)/shard_map/far_keys/pallas_call | solution.py:240
  37.3 1.9 %collective-permute-start.8 = (bf16[256,512]{1,0:T(8,128)(2,1)S(1)}, bf16[256,512]{1,0:T(8,128)(2,1)}, u32[]{:S(2)}, u32[]{:S(2)}) collective-permute-start(bf16[256,512]{1,0:T(8,128)(2,1)S(1)} %get-tuple-element.41), channel_id=1, source_target_pairs={{2,0},{3,1},{4,2},{5,3},{6,4},{7,5},{8,6},{9,7},{10,8},{11,9},{12,... | collective-permute-start | bytes 786440 | tf_op jit(solution)/shard_map/ppermute | solution.py:34
  39.2 3.9 %near_grads.1 = (f32[256,512]{1,0:T(8,128)S(1)}, f32[256,512]{1,0:T(8,128)S(1)}, f32[256,512]{1,0:T(8,128)S(1)}, f32[256,512]{1,0:T(8,128)S(1)}, bf16[128,1024]{...) custom-call(s32[1]{0:T(128)} %bitcast.core_ref, s32[8,128]{1,0:T(8,128)S(1)} %concatenate.40.lo_ref, ...), custom_call_target="tpu_custom_call" | custom-call | tf_op jit(solution)/shard_map/near_grads/pallas_call | solution.py:240
  43.8 1.0 %add_convert_fusion.1 = bf16[256,512]{1,0:T(8,128)(2,1)S(1)} fusion(f32[256,512]{1,0:T(8,128)S(1)} %get-tuple-element.43, bf16[256,512]{1,0:T(8,128)(2,1)} %collective-permute-done.12), kind=kLoop, calls=%fused_computation.3 | loop fusion | flops 393216 | bytes 1048576 | tf_op jit(solution)/shard_map/convert_element_type | solution.py:309
  44.8 2.1 %collective-permute-start.13 = (bf16[256,512]{1,0:T(8,128)(2,1)S(1)}, bf16[256,512]{1,0:T(8,128)(2,1)S(1)}, u32[]{:S(2)}, u32[]{:S(2)}) collective-permute-start(bf16[256,512]{1,0:T(8,128)(2,1)S(1)} %add_convert_fusion.1), channel_id=1, source_target_pairs={{2,0},{3,1},{4,2},{5,3},{6,4},{7,5},{8,6},{9,7},{10,8},{11,9},{12,... | collective-permute-start | bytes 786440 | tf_op jit(solution)/shard_map/ppermute | solution.py:34
  46.9 2.3 %collective-permute-done.8 = bf16[256,512]{1,0:T(8,128)(2,1)} collective-permute-done((bf16[256,512]{1,0:T(8,128)(2,1)S(1)}, bf16[256,512]{1,0:T(8,128)(2,1)}, u32[]{:S(2)}, u32[]{:S(2)}) %collective-permute-start.8) | collective-permute-done | bytes 262176 | tf_op jit(solution)/shard_map/ppermute | solution.py:34
  49.3 1.0 %add_convert_fusion.2 = bf16[256,512]{1,0:T(8,128)(2,1)S(1)} fusion(f32[256,512]{1,0:T(8,128)S(1)} %get-tuple-element.40, bf16[256,512]{1,0:T(8,128)(2,1)} %collective-permute-done.8), kind=kLoop, calls=%fused_computation.4 | loop fusion | flops 393216 | bytes 1048576 | tf_op jit(solution)/shard_map/convert_element_type | solution.py:310
  50.3 1.9 %collective-permute-start.11 = (bf16[128,512]{1,0:T(8,128)(2,1)S(1)}, bf16[128,512]{1,0:T(8,128)(2,1)S(1)}, u32[]{:S(2)}, u32[]{:S(2)}) collective-permute-start(bf16[128,512]{1,0:T(8,128)(2,1)S(1)} %get-tuple-element.52), channel_id=1, source_target_pairs={{2,1},{3,0},{4,3},{5,2},{6,5},{7,4},{8,7},{9,6},{10,9},{11,8},{12,... | collective-permute-start | bytes 393224 | tf_op jit(solution)/shard_map/ppermute | solution.py:40
  52.3 2.8 %collective-permute-start.9 = (bf16[128,512]{1,0:T(8,128)(2,1)S(1)}, bf16[128,512]{1,0:T(8,128)(2,1)S(1)}, u32[]{:S(2)}, u32[]{:S(2)}) collective-permute-start(bf16[128,512]{1,0:T(8,128)(2,1)S(1)} %get-tuple-element.51), channel_id=1, source_target_pairs={{2,0},{3,1},{4,2},{5,3},{6,4},{7,5},{8,6},{9,7},{10,8},{11,9},{12,... | collective-permute-start | bytes 393224 | tf_op jit(solution)/shard_map/ppermute | solution.py:34
  55.1 0.8 %pad_maximum_fusion.1 = bf16[128,2048]{1,0:T(8,128)(2,1)} fusion(bf16[128,1024]{1,0:T(8,128)(2,1)S(1)} %get-tuple-element.48, bf16[128,1024]{1,0:T(8,128)(2,1)S(1)} %get-tuple-element.47), kind=kLoop, calls=%fused_computation.1 | loop fusion | flops 1048576 | bytes 1048576 | tf_op jit(solution)/shard_map/concatenate | solution.py:316
  55.9 2.9 %collective-permute-done.13 = bf16[256,512]{1,0:T(8,128)(2,1)S(1)} collective-permute-done((bf16[256,512]{1,0:T(8,128)(2,1)S(1)}, bf16[256,512]{1,0:T(8,128)(2,1)S(1)}, u32[]{:S(2)}, u32[]{:S(2)}) %collective-permute-start.13) | collective-permute-done | bytes 262176 | tf_op jit(solution)/shard_map/ppermute | solution.py:34
  59.1 2.6 %collective-permute-done.11 = bf16[128,512]{1,0:T(8,128)(2,1)S(1)} collective-permute-done((bf16[128,512]{1,0:T(8,128)(2,1)S(1)}, bf16[128,512]{1,0:T(8,128)(2,1)S(1)}, u32[]{:S(2)}, u32[]{:S(2)}) %collective-permute-start.11) | collective-permute-done | bytes 131104 | tf_op jit(solution)/shard_map/ppermute | solution.py:40
  61.7 2.8 %collective-permute-done.9 = bf16[128,512]{1,0:T(8,128)(2,1)S(1)} collective-permute-done((bf16[128,512]{1,0:T(8,128)(2,1)S(1)}, bf16[128,512]{1,0:T(8,128)(2,1)S(1)}, u32[]{:S(2)}, u32[]{:S(2)}) %collective-permute-start.9) | collective-permute-done | bytes 131104 | tf_op jit(solution)/shard_map/ppermute | solution.py:34
  (53 shorter events, 9.0 us)
Async XLA Ops:
  0.6 0.7 copy-start.6
  2.3 5.2 %copy-start = (bf16[128,2048]{1,0:T(8,128)(2,1)S(1)}, bf16[128,2048]{1,0:T(8,128)(2,1)}, u32[]{:S(2)}) copy-start(bf16[128,2048]{1,0:T(8,128)(2,1)} %q) | copy-start | bytes 1572868
  2.3 5.2 %copy-start.1 = (bf16[128,2048]{1,0:T(8,128)(2,1)S(1)}, bf16[128,2048]{1,0:T(8,128)(2,1)}, u32[]{:S(2)}) copy-start(bf16[128,2048]{1,0:T(8,128)(2,1)} %go) | copy-start | bytes 1572868
  2.3 1.4 %collective-permute-start = (bf16[144,512]{1,0:T(8,128)(2,1)S(1)}, bf16[144,512]{1,0:T(8,128)(2,1)S(1)}, u32[]{:S(2)}, u32[]{:S(2)}) collective-permute-start(bf16[144,512]{1,0:T(8,128)(2,1)S(1)} %fusion.1), channel_id=1, source_target_pairs={{0,1},{1,0},{2,3},{3,2},{4,5},{5,4},{6,7},{7,6},{8,9},{9,8},{10,11... | collective-permute-start | bytes 442376 | tf_op jit(solution)/shard_map/ppermute | solution.py:28
  3.8 0.7 %copy-start.5 = (bf16[144,512]{1,0:T(8,128)(2,1)}, bf16[144,512]{1,0:T(8,128)(2,1)S(1)}, u32[]{:S(2)}) copy-start(bf16[144,512]{1,0:T(8,128)(2,1)S(1)} %collective-permute-done) | copy-start | bytes 442372
  4.5 10.9 %collective-permute-start.4 = (bf16[272,512]{1,0:T(8,128)(2,1)S(1)}, bf16[272,512]{1,0:T(8,128)(2,1)S(1)}, u32[]{:S(2)}, u32[]{:S(2)}) collective-permute-start(bf16[272,512]{1,0:T(8,128)(2,1)S(1)} %pad_maximum_fusion.2.kc), channel_id=1, source_target_pairs={{0,2},{1,3},{2,4},{3,5},{4,6},{5,7},{6,8},{7,9},{8,10},{9,11},{10,... | collective-permute-start | bytes 835592 | tf_op jit(solution)/shard_map/ppermute | solution.py:34
  7.6 1.0 %copy-start.4 = (bf16[128,1024]{1,0:T(8,128)(2,1)S(1)}, bf16[128,1024]{1,0:T(8,128)(2,1)}, u32[]{:S(2)}) copy-start(bf16[128,1024]{1,0:T(8,128)(2,1)} %param.7) | copy-start | bytes 786436
  7.7 16.1 %collective-permute-start.3 = (bf16[256,1024]{1,0:T(8,128)(2,1)S(1)}, bf16[256,1024]{1,0:T(8,128)(2,1)S(1)}, u32[]{:S(2)}, u32[]{:S(2)}) collective-permute-start(bf16[256,1024]{1,0:T(8,128)(2,1)S(1)} %pad_maximum_fusion), channel_id=1, source_target_pairs={{0,1},{1,0},{2,3},{3,2},{4,5},{5,4},{6,7},{7,6},{8,9},{9,8},{10,11... | collective-permute-start | bytes 1572872 | tf_op jit(solution)/shard_map/ppermute | solution.py:28
  8.6 1.4 %collective-permute-start.1 = (bf16[128,512]{1,0:T(8,128)(2,1)S(1)}, bf16[128,512]{1,0:T(8,128)(2,1)S(1)}, u32[]{:S(2)}, u32[]{:S(2)}) collective-permute-start(bf16[128,512]{1,0:T(8,128)(2,1)S(1)} %get-tuple-element.54), channel_id=1, source_target_pairs={{0,1},{1,0},{2,3},{3,2},{4,5},{5,4},{6,7},{7,6},{8,9},{9,8},{10,11... | collective-permute-start | bytes 393224 | tf_op jit(solution)/shard_map/ppermute | solution.py:28
  10.0 15.8 %collective-permute-start.2 = (bf16[256,512]{1,0:T(8,128)(2,1)S(1)}, bf16[256,512]{1,0:T(8,128)(2,1)S(1)}, u32[]{:S(2)}, u32[]{:S(2)}) collective-permute-start(bf16[256,512]{1,0:T(8,128)(2,1)S(1)} %pad_maximum_fusion.3.vc), channel_id=1, source_target_pairs={{0,2},{1,3},{2,4},{3,5},{4,6},{5,7},{6,8},{7,9},{8,10},{9,11},{10,... | collective-permute-start | bytes 786440 | tf_op jit(solution)/shard_map/ppermute | solution.py:34
  15.4 13.5 %collective-permute-start.5 = (bf16[272,512]{1,0:T(8,128)(2,1)S(1)}, bf16[272,512]{1,0:T(8,128)(2,1)S(1)}, u32[]{:S(2)}, u32[]{:S(2)}) collective-permute-start(bf16[272,512]{1,0:T(8,128)(2,1)S(1)} %collective-permute-done.4.ka), channel_id=1, source_target_pairs={{0,2},{1,3},{2,4},{3,5},{4,6},{5,7},{6,8},{7,9},{8,10},{9,11},{10,... | collective-permute-start | bytes 835592 | tf_op jit(solution)/shard_map/ppermute | solution.py:34
  23.8 0.8 %copy-start.2 = (bf16[256,1024]{1,0:T(8,128)(2,1)}, bf16[256,1024]{1,0:T(8,128)(2,1)S(1)}, u32[]{:S(2)}) copy-start(bf16[256,1024]{1,0:T(8,128)(2,1)S(1)} %collective-permute-done.3.qgx) | copy-start | bytes 1572868
  24.6 1.0 %copy-start.3 = (bf16[256,1024]{1,0:T(8,128)(2,1)S(1)}, bf16[256,1024]{1,0:T(8,128)(2,1)}, u32[]{:S(2)}) copy-start(bf16[256,1024]{1,0:T(8,128)(2,1)} %copy-done.2) | copy-start | bytes 1572868
  25.8 9.1 %collective-permute-start.6 = (bf16[256,512]{1,0:T(8,128)(2,1)S(1)}, bf16[256,512]{1,0:T(8,128)(2,1)S(1)}, u32[]{:S(2)}, u32[]{:S(2)}) collective-permute-start(bf16[256,512]{1,0:T(8,128)(2,1)S(1)} %collective-permute-done.2.va), channel_id=1, source_target_pairs={{0,2},{1,3},{2,4},{3,5},{4,6},{5,7},{6,8},{7,9},{8,10},{9,11},{10,... | collective-permute-start | bytes 786440 | tf_op jit(solution)/shard_map/ppermute | solution.py:34
  30.6 13.2 %collective-permute-start.12 = (bf16[256,512]{1,0:T(8,128)(2,1)S(1)}, bf16[256,512]{1,0:T(8,128)(2,1)}, u32[]{:S(2)}, u32[]{:S(2)}) collective-permute-start(bf16[256,512]{1,0:T(8,128)(2,1)S(1)} %get-tuple-element.44), channel_id=1, source_target_pairs={{2,0},{3,1},{4,2},{5,3},{6,4},{7,5},{8,6},{9,7},{10,8},{11,9},{12,... | collective-permute-start | bytes 786440 | tf_op jit(solution)/shard_map/ppermute | solution.py:34
  37.3 12.0 %collective-permute-start.8 = (bf16[256,512]{1,0:T(8,128)(2,1)S(1)}, bf16[256,512]{1,0:T(8,128)(2,1)}, u32[]{:S(2)}, u32[]{:S(2)}) collective-permute-start(bf16[256,512]{1,0:T(8,128)(2,1)S(1)} %get-tuple-element.41), channel_id=1, source_target_pairs={{2,0},{3,1},{4,2},{5,3},{6,4},{7,5},{8,6},{9,7},{10,8},{11,9},{12,... | collective-permute-start | bytes 786440 | tf_op jit(solution)/shard_map/ppermute | solution.py:34
  43.2 15.8 %collective-permute-start.10 = (f32[128,512]{1,0:T(8,128)S(1)}, f32[128,512]{1,0:T(8,128)S(1)}, u32[]{:S(2)}, u32[]{:S(2)}) collective-permute-start(f32[128,512]{1,0:T(8,128)S(1)} %slice.34), channel_id=1, source_target_pairs={{0,1},{1,0},{2,3},{3,2},{4,5},{5,4},{6,7},{7,6},{8,9},{9,8},{10,11... | collective-permute-start | bytes 786440 | tf_op jit(solution)/shard_map/ppermute | solution.py:28
  43.3 11.8 %collective-permute-start.7 = (bf16[128,1024]{1,0:T(8,128)(2,1)S(1)}, bf16[128,1024]{1,0:T(8,128)(2,1)S(1)}, u32[]{:S(2)}, u32[]{:S(2)}) collective-permute-start(bf16[128,1024]{1,0:T(8,128)(2,1)S(1)} %get-tuple-element.38), channel_id=1, source_target_pairs={{0,1},{1,0},{2,3},{3,2},{4,5},{5,4},{6,7},{7,6},{8,9},{9,8},{10,11... | collective-permute-start | bytes 786440 | tf_op jit(solution)/shard_map/ppermute | solution.py:28
  44.8 14.1 %collective-permute-start.13 = (bf16[256,512]{1,0:T(8,128)(2,1)S(1)}, bf16[256,512]{1,0:T(8,128)(2,1)S(1)}, u32[]{:S(2)}, u32[]{:S(2)}) collective-permute-start(bf16[256,512]{1,0:T(8,128)(2,1)S(1)} %add_convert_fusion.1), channel_id=1, source_target_pairs={{2,0},{3,1},{4,2},{5,3},{6,4},{7,5},{8,6},{9,7},{10,8},{11,9},{12,... | collective-permute-start | bytes 786440 | tf_op jit(solution)/shard_map/ppermute | solution.py:34
  50.3 11.3 %collective-permute-start.11 = (bf16[128,512]{1,0:T(8,128)(2,1)S(1)}, bf16[128,512]{1,0:T(8,128)(2,1)S(1)}, u32[]{:S(2)}, u32[]{:S(2)}) collective-permute-start(bf16[128,512]{1,0:T(8,128)(2,1)S(1)} %get-tuple-element.52), channel_id=1, source_target_pairs={{2,1},{3,0},{4,3},{5,2},{6,5},{7,4},{8,7},{9,6},{10,9},{11,8},{12,... | collective-permute-start | bytes 393224 | tf_op jit(solution)/shard_map/ppermute | solution.py:40
  52.3 12.2 %collective-permute-start.9 = (bf16[128,512]{1,0:T(8,128)(2,1)S(1)}, bf16[128,512]{1,0:T(8,128)(2,1)S(1)}, u32[]{:S(2)}, u32[]{:S(2)}) collective-permute-start(bf16[128,512]{1,0:T(8,128)(2,1)S(1)} %get-tuple-element.51), channel_id=1, source_target_pairs={{2,0},{3,1},{4,2},{5,3},{6,4},{7,5},{8,6},{9,7},{10,8},{11,9},{12,... | collective-permute-start | bytes 393224 | tf_op jit(solution)/shard_map/ppermute | solution.py:34
  59.0 6.3 %collective-permute-start.14 = (bf16[128,512]{1,0:T(8,128)(2,1)S(1)}, bf16[128,512]{1,0:T(8,128)(2,1)S(1)}, u32[]{:S(2)}, u32[]{:S(2)}) collective-permute-start(bf16[128,512]{1,0:T(8,128)(2,1)S(1)} %slice.44), channel_id=1, source_target_pairs={{0,1},{1,0},{2,3},{3,2},{4,5},{5,4},{6,7},{7,6},{8,9},{9,8},{10,11... | collective-permute-start | bytes 393224 | tf_op jit(solution)/shard_map/ppermute | solution.py:28

commit v4 on v3

--- a/solution.py
+++ b/solution.py
@@ -40,6 +40,16 @@
     return lax.ppermute(x, AXES, [(i, (i ^ 1) + by) for i in range(n) if 0 <= i + by < n])
 
 
+def forward(x):
+    n, row = lax.axis_size(AXES), lax.axis_size("fsdp")
+    return lax.ppermute(x, AXES, [(i, i + 2) for i in range(n) if i % row < row - 2])
+
+
+def ahead(x):
+    n, row = lax.axis_size(AXES), lax.axis_size("fsdp")
+    return lax.ppermute(x, AXES, [(i, i + 4) for i in range(n - 4) if row - 4 <= i % row < row - 2])
+
+
 def rows_at(core, half, tok):
     return pl.ds(pl.multiple_of(lax.bitwise_xor(core, half) * tok, tok), tok)
 
@@ -49,7 +59,9 @@
 
 
 def block_of(core, pieces, b, g, tok):
-    return pieces[b // 2][rows_at(core, b % 2, tok), lanes_at(g)]
+    parts = pieces[b // 2]
+    at = (rows_at(core, b % 2, tok), lanes_at(g))
+    return parts[0][at] + parts[1][at] if isinstance(parts, tuple) else parts[at]
 
 
 def seen(lo, seg_ref, tok):
@@ -93,8 +105,16 @@
     return jnp.sum(x.reshape(x.shape[0] // 8, 8, x.shape[1]), axis=0)
 
 
-def stack_heads(tok, groups, core_ref, q, go, qgx, qs, gs):
-    core = core_ref[0]
+def stack_heads(tok, groups, core_ref, q, go, qgx, kc, qs, gs, lo):
+    core = core_ref[0]
+    ids = kc[2 * tok : 2 * tok + 1, : 2 * tok].astype(jnp.float32)
+    column = jnp.broadcast_to(ids, (8, 2 * tok)).T[:, 0:1]
+    before = jnp.sum(jnp.where(column < ids, 1.0, 0.0), axis=0, keepdims=True)
+    first = jnp.min(ids, axis=1, keepdims=True)
+    starts = jnp.where(ids == first, -1.0, WINDOW + before).astype(jnp.int32)
+    lo[0:1, :] = starts[:, :tok]
+    lo[1:2, :] = starts[:, tok:]
+    lo[2:8, :] = jnp.broadcast_to(first.astype(jnp.int32), (6, tok))
     for g in range(groups):
         for hd in range(2):
             at = (core * groups + g) * 2 + hd
@@ -130,16 +150,16 @@
     lax.fori_loop(0, groups, step, 0, unroll=True)
 
 
-def far_values(tok, groups, core_ref, lo_ref, qs, gs, ka, kb, tot, dvb, inv):
+def far_values(tok, groups, core_ref, lo_ref, qs, gs, ka, kb, wk, tot, dvb, inv):
     core = core_ref[0]
     lo_all = lo_ref[...]
-    count = seen(lo_all, ka, tok) + seen(lo_all, kb, tok)
+    count = seen(lo_all, ka, tok) + seen(lo_all, kb, tok) + seen(lo_all, wk, tok)
     los = [first_keys(core, lo_all, count, h, tok) for h in range(2)]
 
     def step(g, _):
         accs = []
         for h in range(2):
-            s = dot(keys_of(core, (kb, ka), range(h, h + FAR), g, tok), qs[g, h], NT)
+            s = dot(keys_of(core, ((kb, wk), ka), range(h, h + FAR), g, tok), qs[g, h], NT)
             total = tot[g, pl.ds(8 * h, 8), :]
             ws = []
             for jj in range(FAR):
@@ -169,17 +189,17 @@
         out[rows_at(core, b % 2, tok), lanes_at(g)] = acc.astype(out.dtype)
 
 
-def far_keys(tok, groups, core_ref, lo_ref, qs, gs, ka, kb, va, vb, inv, term, dkb, row):
+def far_keys(tok, groups, core_ref, lo_ref, qs, gs, ka, kb, wk, va, vb, wv, inv, term, dkb, row):
     core = core_ref[0]
     lo_all = lo_ref[...]
-    count = seen(lo_all, ka, tok) + seen(lo_all, kb, tok)
+    count = seen(lo_all, ka, tok) + seen(lo_all, kb, tok) + seen(lo_all, wk, tok)
     los = [first_keys(core, lo_all, count, h, tok) for h in range(2)]
 
     def step(g, _):
         accs = []
         for h in range(2):
-            s = dot(keys_of(core, (kb, ka), range(h, h + FAR), g, tok), qs[g, h], NT)
-            dp = dot(keys_of(core, (vb, va), range(h, h + FAR), g, tok), gs[g, h], NT)
+            s = dot(keys_of(core, ((kb, wk), ka), range(h, h + FAR), g, tok), qs[g, h], NT)
+            dp = dot(keys_of(core, ((vb, wv), va), range(h, h + FAR), g, tok), gs[g, h], NT)
             one = inv[g, pl.ds(8 * h, 1), :]
             total = term[g, pl.ds(8 * h, 8), :]
             us = []
@@ -197,19 +217,19 @@
     lax.fori_loop(0, groups, step, 0, unroll=True)
 
 
-def near_grads(tok, groups, core_ref, lo_ref, qs, gs, kb, ka, kc, vb, va, vc, inv, row,
+def near_grads(tok, groups, core_ref, lo_ref, qs, gs, kb, wk, ka, kc, vb, wv, va, vc, inv, row,
                dva, dvc, dka, dkc, dq0, dq1, dq_s):
     core = core_ref[0]
     lo_all = lo_ref[...]
-    count = seen(lo_all, ka, tok) + seen(lo_all, kb, tok)
+    count = seen(lo_all, ka, tok) + seen(lo_all, kb, tok) + seen(lo_all, wk, tok)
     los = [first_keys(core, lo_all, count, h, tok) for h in range(2)]
     blocks = WINDOW // tok + 1
 
     def step(g, _):
         dvs, dks = [], []
         for h in range(2):
-            k_rows = keys_of(core, (kb, ka, kc), range(h, h + blocks), g, tok)
-            v_rows = keys_of(core, (vb, va, vc), range(h, h + blocks), g, tok)
+            k_rows = keys_of(core, ((kb, wk), ka, kc), range(h, h + blocks), g, tok)
+            v_rows = keys_of(core, ((vb, wv), va, vc), range(h, h + blocks), g, tok)
             s = dot(k_rows, qs[g, h], NT)
             dp = dot(v_rows, gs[g, h], NT)
             one = inv[g, pl.ds(8 * h, 1), :]
@@ -265,24 +285,17 @@
         return lax.dynamic_slice(x, (0, which * width), (x.shape[0], width))
 
     seg_own = (segment + 1).astype(bf16)[None, :]
-    seg_row = jnp.pad(seg_own, ((0, SEG_ROWS - 1), (0, half - tok)))
-    own_row = jnp.pad(seg_own, ((0, SEG_ROWS - 1), (tok, half - 2 * tok)))
-    k_out = jnp.concatenate([part(keys, 1 - core, half), seg_row], 0)
-    k_in = swap(k_out)
+    seg_row = jnp.pad(seg_own, ((0, SEG_ROWS - 1), (tok, half - 2 * tok)))
+    own_row = jnp.pad(seg_own, ((0, SEG_ROWS - 1), (0, half - tok)))
+    k_in = swap(jnp.concatenate([part(keys, 1 - core, half), seg_row], 0))
     kc = jnp.concatenate([part(keys, core, half), k_in[:tok], k_in[tok:] + own_row], 0)
     values, _ = lax.optimization_barrier((values, kc))
     v_in = swap(part(values, 1 - core, half))
-    vc = jnp.concatenate([part(values, core, half), v_in], 0)
+    vc = jnp.concatenate([part(values, core, half), v_in, jnp.zeros((16, half), bf16)], 0)
     ka = hop(kc, 1)
     va = hop(vc, 1)
     queries, grad_out, _ = lax.optimization_barrier((queries, grad_out, kc))
     qg_in = swap(jnp.concatenate([part(queries, 1 - core, q_half), part(grad_out, 1 - core, q_half)], 0))
-
-    seg_f = jnp.concatenate([seg_own[0], k_in[tok, :tok]]).astype(f32)
-    seg0 = jnp.min(seg_f)
-    before = jnp.sum((seg_f[:, None] < seg_f[None, :]).astype(jnp.int32), axis=0)
-    starts = jnp.where(seg_f == seg0, -1, WINDOW + before).reshape(2, tok)
-    lo = jnp.concatenate([starts, jnp.full((6, tok), seg0.astype(jnp.int32), jnp.int32)], 0)
 
     rows = ((groups, 2, 2 * tok, HEAD_DIM), bf16)
     stat = ((groups, 16, 2 * tok), f32)
@@ -290,20 +303,24 @@
     kv_b = ((2 * tok, half), bf16)
     dq_o = ((tok, q_half), bf16)
 
-    qs, gs = call(stack_heads, tok, groups, (core_arr, queries, grad_out, qg_in), [rows, rows])
+    qs, gs, lo = call(
+        stack_heads, tok, groups, (core_arr, queries, grad_out, qg_in, kc),
+        [rows, rows, ((8, tok), jnp.int32)])
     va, qs, gs, lo = lax.optimization_barrier((va, qs, gs, lo))
-    kb = hop(ka, 1)
-    vb = hop(va, 1)
+    wk = ahead(kc)
+    wv = ahead(vc)
+    kb = forward(ka)
+    vb = forward(va)
     tot, term = call(
         near_sums, tok, groups, (core_arr, lo, qs, gs, ka, kc, va, vc), [stat, stat])
     dvb, inv = call(
-        far_values, tok, groups, (core_arr, lo, qs, gs, ka, kb, tot), [kv_b, stat])
+        far_values, tok, groups, (core_arr, lo, qs, gs, ka, kb, wk, tot), [kv_b, stat])
     cv = hop(dvb, -1)
     dkb, row = call(
-        far_keys, tok, groups, (core_arr, lo, qs, gs, ka, kb, va, vb, inv, term), [kv_b, stat])
+        far_keys, tok, groups, (core_arr, lo, qs, gs, ka, kb, wk, va, vb, wv, inv, term), [kv_b, stat])
     ck = hop(dkb, -1)
     dva, dvc, dka, dkc, dq0, dq1 = call(
-        near_grads, tok, groups, (core_arr, lo, qs, gs, kb, ka, kc, vb, va, vc, inv, row),
+        near_grads, tok, groups, (core_arr, lo, qs, gs, kb, wk, ka, kc, vb, wv, va, vc, inv, row),
         [kv_f, kv_f, kv_f, kv_f, dq_o, dq_o],
         [pltpu.VMEM((groups, 2, 2 * tok, HEAD_DIM), bf16)])
     dv = hop((dva + cv.astype(f32)).astype(bf16), -1)
@@ -319,6 +336,7 @@
     sum_v = dvc + dv.astype(f32)
     grad_v = place(sum_v[:tok].astype(bf16), swap(sum_v[tok:].astype(bf16)))
     other_k = swap(dkc[tok:])
+    dk_cross, grad_v = lax.optimization_barrier((dk_cross, grad_v))
     same = (dkc[:tok] + dk_same.astype(f32)).astype(bf16)
     other = (other_k + dk_cross.astype(f32)).astype(bf16)
     grad_k = place(same, other)

time: 67.2 us -> 65 us (0.967)
  waiting for transfers between devices: 15.1 us -> 21.7 us
  starting transfers between devices: 28.3 us -> 24.3 us
  local copies, waits for them, and re-layouts: 5.74 us -> 1.79 us
  Pallas kernels: 9.27 us -> 10.9 us
  other arithmetic: 6.03 us -> 4.74 us
    ppermute x8 -> x6, starting transfers between devices: 25.5 us -> 17.2 us  [hop(): lax.ppermute(x, AXES, [(i, i + by) for i in range(n) if 0 <= i + by < n])]
    ppermute x0 -> x4, waiting for transfers between devices: none -> 4.33 us  [the longest x2 4.33 us: forward(): lax.ppermute(x, AXES, [(i, i + 2) for i in range(n) if i % row < row - 2])]
    ppermute x0 -> x4, starting transfers between devices: none -> 3.92 us  [the longest x2 2.56 us: forward(): lax.ppermute(x, AXES, [(i, i + 2) for i in range(n) if i % row < row - 2])]
    ppermute x8 -> x6, waiting for transfers between devices: 10.4 us -> 14.3 us  [hop(): lax.ppermute(x, AXES, [(i, i + by) for i in range(n) if 0 <= i + by < n])]
    unnamed x14 -> x8, local copies, waits for them, and re-layouts: 3.94 us -> 0.66 us
    ppermute x1, waiting for transfers between devices: 2.63 us -> 0.54 us  [cross(): lax.ppermute(x, AXES, [(i, (i ^ 1) + by) for i in range(n) if 0 <= i + by...]
    pallas_call x5, Pallas kernels: 9.27 us -> 10.9 us  [call(): pl.pallas_call(functools.partial(body, tok, groups), in_specs=[pl.BlockSp...]
    squeeze x1 -> x0, local copies, waits for them, and re-layouts: 0.69 us -> none  [local(): seg_f = jnp.concatenate([seg_own[0], k_in[tok, :tok]]).astype(f32)]
  transfers between devices with their start and end apart: 15 -> 17, of which waited for: 8 -> 11; matrix products, arithmetic and copies ran while one was open for 9% -> 6% of each run, Pallas kernels for 14% -> 17%
where the time goes in v4:
time: 65 us; the launch traced here: 64.5 us
  starting transfers between devices  24.3 us (37%)
  waiting for transfers between devices  21.7 us (33%)
  Pallas kernels  10.9 us (17%)
  other arithmetic  4.74 us (7%)
  local copies, waits for them, and re-layouts  1.79 us (3%)
  between operations  1 us (2%)
    ppermute x6, starting transfers between devices, hop(): lax.ppermute(x, AXES, [(i, i + by) for i in range(n) if 0 <= i + by < n])  17.2 us
    ppermute x6, waiting for transfers between devices, hop(): lax.ppermute(x, AXES, [(i, i + by) for i in range(n) if 0 <= i + by < n])  14.3 us
    pallas_call x5, Pallas kernels, call(): pl.pallas_call(functools.partial(body, tok, groups), in_specs=[pl.BlockSp...  10.9 us
    ppermute x2, waiting for transfers between devices, forward(): lax.ppermute(x, AXES, [(i, i + 2) for i in range(n) if i % row < row - 2])  4.33 us
    ppermute x2, starting transfers between devices, forward(): lax.ppermute(x, AXES, [(i, i + 2) for i in range(n) if i % row < row - 2])  2.56 us
    ppermute x6, waiting for transfers between devices, swap(): return lax.ppermute(x, AXES, [(i, i ^ 1) for i in range(n)])  2.53 us
    concatenate x3, other arithmetic, place(): return jnp.concatenate([first, second], 1)  2.29 us
    ppermute x1, starting transfers between devices, cross(): lax.ppermute(x, AXES, [(i, (i ^ 1) + by) for i in range(n) if 0 <= i + by...  1.92 us
  transfers between devices with their start and end apart: 17, of which 11 were waited for; matrix products, arithmetic and copies ran while one was open for 6% of the time, Pallas kernels for 17%

profile of v4, /device:TPU:26, one launch (start us, length us, event | category | flops | bytes accessed | tf_op | source)
XLA Modules:
  0.0 64.5 jit_solution(3500413538791344858)
XLA Ops:
  1.3 1.0 %constant_dynamic-slice_fusion.5 = (bf16[128,512]{1,0:T(8,128)(2,1)S(1)}, bf16[128,512]{1,0:T(8,128)(2,1)S(1)}) fusion(bf16[128,1024]{1,0:T(8,128)(2,1)} %param.6, s32[]{:T(128)S(6)} %select_n.45, s32[]{:T(128)S(6)} %select_n.46), kind=kLoop, calls=%fused_computation.26 | loop fusion | bytes 524296 | tf_op jit(solution)/shard_map/dynamic_slice | solution.py:285
  2.4 1.4 %collective-permute-done = bf16[144,512]{1,0:T(8,128)(2,1)S(1)} collective-permute-done((bf16[144,512]{1,0:T(8,128)(2,1)S(1)}, bf16[144,512]{1,0:T(8,128)(2,1)S(1)}, u32[]{:S(2)}, u32[]{:S(2)}) %collective-permute-start) | collective-permute-done | bytes 147488 | tf_op jit(solution)/shard_map/ppermute | solution.py:28
  3.8 3.2 %collective-permute-start.4 = (bf16[272,512]{1,0:T(8,128)(2,1)S(1)}, bf16[272,512]{1,0:T(8,128)(2,1)S(1)}, u32[]{:S(2)}, u32[]{:S(2)}) collective-permute-start(bf16[272,512]{1,0:T(8,128)(2,1)S(1)} %pad_maximum_fusion.2.kc), channel_id=1, source_target_pairs={{0,2},{1,3},{2,4},{3,5},{4,6},{5,7},{6,8},{7,9},{8,10},{9,11},{10,... | collective-permute-start | bytes 835592 | tf_op jit(solution)/shard_map/ppermute | solution.py:34
  8.6 3.5 %collective-permute-start.2 = (bf16[272,512]{1,0:T(8,128)(2,1)S(1)}, bf16[272,512]{1,0:T(8,128)(2,1)S(1)}, u32[]{:S(2)}, u32[]{:S(2)}) collective-permute-start(bf16[272,512]{1,0:T(8,128)(2,1)S(1)} %maximum_maximum_fusion.vc), channel_id=1, source_target_pairs={{0,2},{1,3},{2,4},{3,5},{4,6},{5,7},{6,8},{7,9},{8,10},{9,11},{10,... | collective-permute-start | bytes 835592 | tf_op jit(solution)/shard_map/ppermute | solution.py:34
  12.8 2.6 %collective-permute-done.4.ka = bf16[272,512]{1,0:T(8,128)(2,1)S(1)} collective-permute-done((bf16[272,512]{1,0:T(8,128)(2,1)S(1)}, bf16[272,512]{1,0:T(8,128)(2,1)S(1)}, u32[]{:S(2)}, u32[]{:S(2)}) %collective-permute-start.4) | collective-permute-done | bytes 278560 | tf_op jit(solution)/shard_map/ppermute | solution.py:34
  15.4 1.3 %collective-permute-start.5 = (bf16[272,512]{1,0:T(8,128)(2,1)S(1)}, bf16[272,512]{1,0:T(8,128)(2,1)S(1)}, u32[]{:S(2)}, u32[]{:S(2)}) collective-permute-start(bf16[272,512]{1,0:T(8,128)(2,1)S(1)} %collective-permute-done.4.ka), channel_id=1, source_target_pairs={{0,2},{1,3},{2,4},{3,5},{4,6},{5,7},{8,10},{9,11},{10,12},{11,13},... | collective-permute-start | bytes 835592 | tf_op jit(solution)/shard_map/ppermute | solution.py:45
  17.7 3.6 %collective-permute-done.2.va = bf16[272,512]{1,0:T(8,128)(2,1)S(1)} collective-permute-done((bf16[272,512]{1,0:T(8,128)(2,1)S(1)}, bf16[272,512]{1,0:T(8,128)(2,1)S(1)}, u32[]{:S(2)}, u32[]{:S(2)}) %collective-permute-start.2) | collective-permute-done | bytes 278560 | tf_op jit(solution)/shard_map/ppermute | solution.py:34
  21.3 1.3 %collective-permute-start.7 = (bf16[272,512]{1,0:T(8,128)(2,1)S(1)}, bf16[272,512]{1,0:T(8,128)(2,1)S(1)}, u32[]{:S(2)}, u32[]{:S(2)}) collective-permute-start(bf16[272,512]{1,0:T(8,128)(2,1)S(1)} %collective-permute-done.2.va), channel_id=1, source_target_pairs={{0,2},{1,3},{2,4},{3,5},{4,6},{5,7},{8,10},{9,11},{10,12},{11,13},... | collective-permute-start | bytes 835592 | tf_op jit(solution)/shard_map/ppermute | solution.py:45
  22.6 1.1 %near_sums.1 = (f32[4,16,256]{2,1,0:T(8,128)S(1)}, f32[4,16,256]{2,1,0:T(8,128)S(1)}) custom-call(s32[1]{0:T(128)} %bitcast.core_ref, s32[8,128]{1,0:T(8,128)S(1)} %get-tuple-element.33.lo_ref, bf16[4,2,256,128]{3,2,1,0:T(8,128)(2,1)S(1)} %get-tuple-element.34.qs, bf16[4,2,256,128]{3,2,1,0:T(8,128)(2,1)S(1)} %get-tuple-element.35.gs, ...), custom_call_target="tpu_custom_call" | custom-call | tf_op jit(solution)/shard_map/near_sums/pallas_call | solution.py:260
  23.7 3.5 %collective-permute-done.5.kb = bf16[272,512]{1,0:T(8,128)(2,1)S(1)} collective-permute-done((bf16[272,512]{1,0:T(8,128)(2,1)S(1)}, bf16[272,512]{1,0:T(8,128)(2,1)S(1)}, u32[]{:S(2)}, u32[]{:S(2)}) %collective-permute-start.5) | collective-permute-done | bytes 278560 | tf_op jit(solution)/shard_map/ppermute | solution.py:45
  27.3 2.4 %far_values.1 = (bf16[256,512]{1,0:T(8,128)(2,1)}, f32[4,16,256]{2,1,0:T(8,128)S(1)}) custom-call(s32[1]{0:T(128)} %bitcast.core_ref, s32[8,128]{1,0:T(8,128)S(1)} %get-tuple-element.33.lo_ref, bf16[4,2,256,128]{3,2,1,0:T(8,128)(2,1)S(1)} %get-tuple-element.34.qs, bf16[4,2,256,128]{3,2,1,0:T(8,128)(2,1)S(1)} %get-tuple-element.35.gs, ...), custom_call_target="tpu_custom_call" | custom-call | tf_op jit(solution)/shard_map/far_values/pallas_call | solution.py:260
  29.7 2.0 %collective-permute-start.14 = (bf16[256,512]{1,0:T(8,128)(2,1)}, bf16[256,512]{1,0:T(8,128)(2,1)}, u32[]{:S(2)}, u32[]{:S(2)}) collective-permute-start(bf16[256,512]{1,0:T(8,128)(2,1)} %get-tuple-element.48), channel_id=1, source_target_pairs={{2,0},{3,1},{4,2},{5,3},{6,4},{7,5},{8,6},{9,7},{10,8},{11,9},{12,... | collective-permute-start | bytes 786440 | tf_op jit(solution)/shard_map/ppermute | solution.py:34
  32.5 3.1 %far_keys.1 = (bf16[256,512]{1,0:T(8,128)(2,1)}, f32[4,16,256]{2,1,0:T(8,128)S(1)}) custom-call(s32[1]{0:T(128)} %bitcast.core_ref, s32[8,128]{1,0:T(8,128)S(1)} %get-tuple-element.33.lo_ref, bf16[4,2,256,128]{3,2,1,0:T(8,128)(2,1)S(1)} %get-tuple-element.34.qs, bf16[4,2,256,128]{3,2,1,0:T(8,128)(2,1)S(1)} %get-tuple-element.35.gs, ...), custom_call_target="tpu_custom_call" | custom-call | tf_op jit(solution)/shard_map/far_keys/pallas_call | solution.py:260
  35.5 3.1 %collective-permute-start.10 = (bf16[256,512]{1,0:T(8,128)(2,1)}, bf16[256,512]{1,0:T(8,128)(2,1)}, u32[]{:S(2)}, u32[]{:S(2)}) collective-permute-start(bf16[256,512]{1,0:T(8,128)(2,1)} %get-tuple-element.45), channel_id=1, source_target_pairs={{2,0},{3,1},{4,2},{5,3},{6,4},{7,5},{8,6},{9,7},{10,8},{11,9},{12,... | collective-permute-start | bytes 786440 | tf_op jit(solution)/shard_map/ppermute | solution.py:34
  38.7 3.9 %near_grads.1 = (f32[256,512]{1,0:T(8,128)S(1)}, f32[256,512]{1,0:T(8,128)S(1)}, f32[256,512]{1,0:T(8,128)S(1)}, f32[256,512]{1,0:T(8,128)S(1)}, bf16[128,1024]{...) custom-call(s32[1]{0:T(128)} %bitcast.core_ref, s32[8,128]{1,0:T(8,128)S(1)} %get-tuple-element.33.lo_ref, ...), custom_call_target="tpu_custom_call" | custom-call | tf_op jit(solution)/shard_map/near_grads/pallas_call | solution.py:260
  43.2 1.0 %add_convert_fusion.1 = bf16[256,512]{1,0:T(8,128)(2,1)S(1)} fusion(f32[256,512]{1,0:T(8,128)S(1)} %get-tuple-element.47, bf16[256,512]{1,0:T(8,128)(2,1)} %collective-permute-done.14), kind=kLoop, calls=%fused_computation.3 | loop fusion | flops 393216 | bytes 1048576 | tf_op jit(solution)/shard_map/convert_element_type | solution.py:326
  44.3 3.2 %collective-permute-start.15 = (bf16[256,512]{1,0:T(8,128)(2,1)S(1)}, bf16[256,512]{1,0:T(8,128)(2,1)S(1)}, u32[]{:S(2)}, u32[]{:S(2)}) collective-permute-start(bf16[256,512]{1,0:T(8,128)(2,1)S(1)} %add_convert_fusion.1), channel_id=1, source_target_pairs={{2,0},{3,1},{4,2},{5,3},{6,4},{7,5},{8,6},{9,7},{10,8},{11,9},{12,... | collective-permute-start | bytes 786440 | tf_op jit(solution)/shard_map/ppermute | solution.py:34
  47.4 1.5 %collective-permute-done.10 = bf16[256,512]{1,0:T(8,128)(2,1)} collective-permute-done((bf16[256,512]{1,0:T(8,128)(2,1)}, bf16[256,512]{1,0:T(8,128)(2,1)}, u32[]{:S(2)}, u32[]{:S(2)}) %collective-permute-start.10) | collective-permute-done | bytes 262176 | tf_op jit(solution)/shard_map/ppermute | solution.py:34
  49.0 1.0 %add_convert_fusion.2 = bf16[256,512]{1,0:T(8,128)(2,1)S(1)} fusion(f32[256,512]{1,0:T(8,128)S(1)} %get-tuple-element.44, bf16[256,512]{1,0:T(8,128)(2,1)} %collective-permute-done.10), kind=kLoop, calls=%fused_computation.4 | loop fusion | flops 393216 | bytes 1048576 | tf_op jit(solution)/shard_map/convert_element_type | solution.py:327
  50.0 1.9 %collective-permute-start.13 = (bf16[128,512]{1,0:T(8,128)(2,1)S(1)}, bf16[128,512]{1,0:T(8,128)(2,1)S(1)}, u32[]{:S(2)}, u32[]{:S(2)}) collective-permute-start(bf16[128,512]{1,0:T(8,128)(2,1)S(1)} %get-tuple-element.58), channel_id=1, source_target_pairs={{2,1},{3,0},{4,3},{5,2},{6,5},{7,4},{8,7},{9,6},{10,9},{11,8},{12,... | collective-permute-start | bytes 393224 | tf_op jit(solution)/shard_map/ppermute | solution.py:40
  52.0 2.2 %collective-permute-start.11 = (bf16[128,512]{1,0:T(8,128)(2,1)S(1)}, bf16[128,512]{1,0:T(8,128)(2,1)S(1)}, u32[]{:S(2)}, u32[]{:S(2)}) collective-permute-start(bf16[128,512]{1,0:T(8,128)(2,1)S(1)} %get-tuple-element.57), channel_id=1, source_target_pairs={{2,0},{3,1},{4,2},{5,3},{6,4},{7,5},{8,6},{9,7},{10,8},{11,9},{12,... | collective-permute-start | bytes 393224 | tf_op jit(solution)/shard_map/ppermute | solution.py:34
  54.2 3.8 %collective-permute-done.15 = bf16[256,512]{1,0:T(8,128)(2,1)S(1)} collective-permute-done((bf16[256,512]{1,0:T(8,128)(2,1)S(1)}, bf16[256,512]{1,0:T(8,128)(2,1)S(1)}, u32[]{:S(2)}, u32[]{:S(2)}) %collective-permute-start.15) | collective-permute-done | bytes 262176 | tf_op jit(solution)/shard_map/ppermute | solution.py:34
  58.2 0.8 %pad_maximum_fusion.1 = bf16[128,2048]{1,0:T(8,128)(2,1)} fusion(bf16[128,1024]{1,0:T(8,128)(2,1)S(1)} %get-tuple-element.54, bf16[128,1024]{1,0:T(8,128)(2,1)S(1)} %get-tuple-element.53), kind=kLoop, calls=%fused_computation.1 | loop fusion | flops 1048576 | bytes 1048576 | tf_op jit(solution)/shard_map/concatenate | solution.py:333
  60.9 2.8 %collective-permute-done.11 = bf16[128,512]{1,0:T(8,128)(2,1)S(1)} collective-permute-done((bf16[128,512]{1,0:T(8,128)(2,1)S(1)}, bf16[128,512]{1,0:T(8,128)(2,1)S(1)}, u32[]{:S(2)}, u32[]{:S(2)}) %collective-permute-start.11) | collective-permute-done | bytes 131104 | tf_op jit(solution)/shard_map/ppermute | solution.py:34
  (47 shorter events, 8.2 us)
Async XLA Ops:
  0.6 0.7 %copy-start.3 = (s32[128]{0:T(128)S(1)}, s32[128]{0:T(128)}, u32[]{:S(2)}) copy-start(s32[128]{0:T(128)} %param.9) | copy-start | bytes 1540
  2.3 1.4 %collective-permute-start = (bf16[144,512]{1,0:T(8,128)(2,1)S(1)}, bf16[144,512]{1,0:T(8,128)(2,1)S(1)}, u32[]{:S(2)}, u32[]{:S(2)}) collective-permute-start(bf16[144,512]{1,0:T(8,128)(2,1)S(1)} %fusion.1), channel_id=1, source_target_pairs={{0,1},{1,0},{2,3},{3,2},{4,5},{5,4},{6,7},{7,6},{8,9},{9,8},{10,11... | collective-permute-start | bytes 442376 | tf_op jit(solution)/shard_map/ppermute | solution.py:28
  3.7 3.3 %copy-start.2 = (bf16[128,1024]{1,0:T(8,128)(2,1)S(1)}, bf16[128,1024]{1,0:T(8,128)(2,1)}, u32[]{:S(2)}) copy-start(bf16[128,1024]{1,0:T(8,128)(2,1)} %param.7) | copy-start | bytes 786436
  3.8 3.4 %copy-start = (bf16[128,2048]{1,0:T(8,128)(2,1)S(1)}, bf16[128,2048]{1,0:T(8,128)(2,1)}, u32[]{:S(2)}) copy-start(bf16[128,2048]{1,0:T(8,128)(2,1)} %q) | copy-start | bytes 1572868
  3.8 3.4 %copy-start.1 = (bf16[128,2048]{1,0:T(8,128)(2,1)S(1)}, bf16[128,2048]{1,0:T(8,128)(2,1)}, u32[]{:S(2)}) copy-start(bf16[128,2048]{1,0:T(8,128)(2,1)} %go) | copy-start | bytes 1572868
  3.8 11.5 %collective-permute-start.4 = (bf16[272,512]{1,0:T(8,128)(2,1)S(1)}, bf16[272,512]{1,0:T(8,128)(2,1)S(1)}, u32[]{:S(2)}, u32[]{:S(2)}) collective-permute-start(bf16[272,512]{1,0:T(8,128)(2,1)S(1)} %pad_maximum_fusion.2.kc), channel_id=1, source_target_pairs={{0,2},{1,3},{2,4},{3,5},{4,6},{5,7},{6,8},{7,9},{8,10},{9,11},{10,... | collective-permute-start | bytes 835592 | tf_op jit(solution)/shard_map/ppermute | solution.py:34
  7.1 1.4 %collective-permute-start.1 = (bf16[128,512]{1,0:T(8,128)(2,1)S(1)}, bf16[128,512]{1,0:T(8,128)(2,1)S(1)}, u32[]{:S(2)}, u32[]{:S(2)}) collective-permute-start(bf16[128,512]{1,0:T(8,128)(2,1)S(1)} %get-tuple-element.60), channel_id=1, source_target_pairs={{0,1},{1,0},{2,3},{3,2},{4,5},{5,4},{6,7},{7,6},{8,9},{9,8},{10,11... | collective-permute-start | bytes 393224 | tf_op jit(solution)/shard_map/ppermute | solution.py:28
  7.3 10.1 %collective-permute-start.3 = (bf16[256,1024]{1,0:T(8,128)(2,1)S(1)}, bf16[256,1024]{1,0:T(8,128)(2,1)S(1)}, u32[]{:S(2)}, u32[]{:S(2)}) collective-permute-start(bf16[256,1024]{1,0:T(8,128)(2,1)S(1)} %pad_maximum_fusion), channel_id=1, source_target_pairs={{0,1},{1,0},{2,3},{3,2},{4,5},{5,4},{6,7},{7,6},{8,9},{9,8},{10,11... | collective-permute-start | bytes 1572872 | tf_op jit(solution)/shard_map/ppermute | solution.py:28
  8.6 12.7 %collective-permute-start.2 = (bf16[272,512]{1,0:T(8,128)(2,1)S(1)}, bf16[272,512]{1,0:T(8,128)(2,1)S(1)}, u32[]{:S(2)}, u32[]{:S(2)}) collective-permute-start(bf16[272,512]{1,0:T(8,128)(2,1)S(1)} %maximum_maximum_fusion.vc), channel_id=1, source_target_pairs={{0,2},{1,3},{2,4},{3,5},{4,6},{5,7},{6,8},{7,9},{8,10},{9,11},{10,... | collective-permute-start | bytes 835592 | tf_op jit(solution)/shard_map/ppermute | solution.py:34
  12.1 11.6 %collective-permute-start.6 = (bf16[272,512]{1,0:T(8,128)(2,1)S(1)}, bf16[272,512]{1,0:T(8,128)(2,1)S(1)}, u32[]{:S(2)}, u32[]{:S(2)}) collective-permute-start(bf16[272,512]{1,0:T(8,128)(2,1)S(1)} %pad_maximum_fusion.2.kc), channel_id=1, source_target_pairs={{4,8},{5,9},{12,16},{13,17},{20,24},{21,25}} | collective-permute-start | bytes 835592 | tf_op jit(solution)/shard_map/ppermute | solution.py:50
  15.4 11.9 %collective-permute-start.5 = (bf16[272,512]{1,0:T(8,128)(2,1)S(1)}, bf16[272,512]{1,0:T(8,128)(2,1)S(1)}, u32[]{:S(2)}, u32[]{:S(2)}) collective-permute-start(bf16[272,512]{1,0:T(8,128)(2,1)S(1)} %collective-permute-done.4.ka), channel_id=1, source_target_pairs={{0,2},{1,3},{2,4},{3,5},{4,6},{5,7},{8,10},{9,11},{10,12},{11,13},... | collective-permute-start | bytes 835592 | tf_op jit(solution)/shard_map/ppermute | solution.py:45
  16.6 15.0 %collective-permute-start.8 = (bf16[272,512]{1,0:T(8,128)(2,1)S(1)}, bf16[272,512]{1,0:T(8,128)(2,1)S(1)}, u32[]{:S(2)}, u32[]{:S(2)}) collective-permute-start(bf16[272,512]{1,0:T(8,128)(2,1)S(1)} %maximum_maximum_fusion.vc), channel_id=1, source_target_pairs={{4,8},{5,9},{12,16},{13,17},{20,24},{21,25}} | collective-permute-start | bytes 835592 | tf_op jit(solution)/shard_map/ppermute | solution.py:50
  21.3 11.1 %collective-permute-start.7 = (bf16[272,512]{1,0:T(8,128)(2,1)S(1)}, bf16[272,512]{1,0:T(8,128)(2,1)S(1)}, u32[]{:S(2)}, u32[]{:S(2)}) collective-permute-start(bf16[272,512]{1,0:T(8,128)(2,1)S(1)} %collective-permute-done.2.va), channel_id=1, source_target_pairs={{0,2},{1,3},{2,4},{3,5},{4,6},{5,7},{8,10},{9,11},{10,12},{11,13},... | collective-permute-start | bytes 835592 | tf_op jit(solution)/shard_map/ppermute | solution.py:45
  29.7 13.5 %collective-permute-start.14 = (bf16[256,512]{1,0:T(8,128)(2,1)}, bf16[256,512]{1,0:T(8,128)(2,1)}, u32[]{:S(2)}, u32[]{:S(2)}) collective-permute-start(bf16[256,512]{1,0:T(8,128)(2,1)} %get-tuple-element.48), channel_id=1, source_target_pairs={{2,0},{3,1},{4,2},{5,3},{6,4},{7,5},{8,6},{9,7},{10,8},{11,9},{12,... | collective-permute-start | bytes 786440 | tf_op jit(solution)/shard_map/ppermute | solution.py:34
  35.5 13.4 %collective-permute-start.10 = (bf16[256,512]{1,0:T(8,128)(2,1)}, bf16[256,512]{1,0:T(8,128)(2,1)}, u32[]{:S(2)}, u32[]{:S(2)}) collective-permute-start(bf16[256,512]{1,0:T(8,128)(2,1)} %get-tuple-element.45), channel_id=1, source_target_pairs={{2,0},{3,1},{4,2},{5,3},{6,4},{7,5},{8,6},{9,7},{10,8},{11,9},{12,... | collective-permute-start | bytes 786440 | tf_op jit(solution)/shard_map/ppermute | solution.py:34
  42.7 18.2 %collective-permute-start.12 = (f32[128,512]{1,0:T(8,128)S(1)}, f32[128,512]{1,0:T(8,128)S(1)}, u32[]{:S(2)}, u32[]{:S(2)}) collective-permute-start(f32[128,512]{1,0:T(8,128)S(1)} %slice.30), channel_id=1, source_target_pairs={{0,1},{1,0},{2,3},{3,2},{4,5},{5,4},{6,7},{7,6},{8,9},{9,8},{10,11... | collective-permute-start | bytes 786440 | tf_op jit(solution)/shard_map/ppermute | solution.py:28
  42.7 11.4 %collective-permute-start.9 = (bf16[128,1024]{1,0:T(8,128)(2,1)S(1)}, bf16[128,1024]{1,0:T(8,128)(2,1)S(1)}, u32[]{:S(2)}, u32[]{:S(2)}) collective-permute-start(bf16[128,1024]{1,0:T(8,128)(2,1)S(1)} %get-tuple-element.42), channel_id=1, source_target_pairs={{0,1},{1,0},{2,3},{3,2},{4,5},{5,4},{6,7},{7,6},{8,9},{9,8},{10,11... | collective-permute-start | bytes 786440 | tf_op jit(solution)/shard_map/ppermute | solution.py:28
  44.3 13.8 %collective-permute-start.15 = (bf16[256,512]{1,0:T(8,128)(2,1)S(1)}, bf16[256,512]{1,0:T(8,128)(2,1)S(1)}, u32[]{:S(2)}, u32[]{:S(2)}) collective-permute-start(bf16[256,512]{1,0:T(8,128)(2,1)S(1)} %add_convert_fusion.1), channel_id=1, source_target_pairs={{2,0},{3,1},{4,2},{5,3},{6,4},{7,5},{8,6},{9,7},{10,8},{11,9},{12,... | collective-permute-start | bytes 786440 | tf_op jit(solution)/shard_map/ppermute | solution.py:34
  50.0 10.8 %collective-permute-start.13 = (bf16[128,512]{1,0:T(8,128)(2,1)S(1)}, bf16[128,512]{1,0:T(8,128)(2,1)S(1)}, u32[]{:S(2)}, u32[]{:S(2)}) collective-permute-start(bf16[128,512]{1,0:T(8,128)(2,1)S(1)} %get-tuple-element.58), channel_id=1, source_target_pairs={{2,1},{3,0},{4,3},{5,2},{6,5},{7,4},{8,7},{9,6},{10,9},{11,8},{12,... | collective-permute-start | bytes 393224 | tf_op jit(solution)/shard_map/ppermute | solution.py:40
  52.0 11.7 %collective-permute-start.11 = (bf16[128,512]{1,0:T(8,128)(2,1)S(1)}, bf16[128,512]{1,0:T(8,128)(2,1)S(1)}, u32[]{:S(2)}, u32[]{:S(2)}) collective-permute-start(bf16[128,512]{1,0:T(8,128)(2,1)S(1)} %get-tuple-element.57), channel_id=1, source_target_pairs={{2,0},{3,1},{4,2},{5,3},{6,4},{7,5},{8,6},{9,7},{10,8},{11,9},{12,... | collective-permute-start | bytes 393224 | tf_op jit(solution)/shard_map/ppermute | solution.py:34
  58.2 1.4 %collective-permute-start.16 = (bf16[128,512]{1,0:T(8,128)(2,1)S(1)}, bf16[128,512]{1,0:T(8,128)(2,1)S(1)}, u32[]{:S(2)}, u32[]{:S(2)}) collective-permute-start(bf16[128,512]{1,0:T(8,128)(2,1)S(1)} %slice.39), channel_id=1, source_target_pairs={{0,1},{1,0},{2,3},{3,2},{4,5},{5,4},{6,7},{7,6},{8,9},{9,8},{10,11... | collective-permute-start | bytes 393224 | tf_op jit(solution)/shard_map/ppermute | solution.py:28

commit v5 on v4

--- a/solution.py
+++ b/solution.py
@@ -255,6 +255,10 @@
     lax.fori_loop(0, groups, step, 0, unroll=True)
 
 
+def merge(tok, groups, core_ref, mine, came, out):
+    out[...] = (mine[...] + came[...].astype(jnp.float32)).astype(out.dtype)
+
+
 def call(body, tok, groups, args, outs, scratch=()):
     vmem = pl.BlockSpec(memory_space=pltpu.VMEM)
     return pl.pallas_call(
@@ -289,12 +293,11 @@
     own_row = jnp.pad(seg_own, ((0, SEG_ROWS - 1), (0, half - tok)))
     k_in = swap(jnp.concatenate([part(keys, 1 - core, half), seg_row], 0))
     kc = jnp.concatenate([part(keys, core, half), k_in[:tok], k_in[tok:] + own_row], 0)
-    values, _ = lax.optimization_barrier((values, kc))
     v_in = swap(part(values, 1 - core, half))
-    vc = jnp.concatenate([part(values, core, half), v_in, jnp.zeros((16, half), bf16)], 0)
+    vc = jnp.concatenate([part(values, core, half), v_in, jnp.zeros((SEG_ROWS, half), bf16)], 0)
     ka = hop(kc, 1)
     va = hop(vc, 1)
-    queries, grad_out, _ = lax.optimization_barrier((queries, grad_out, kc))
+    queries, grad_out, _ = lax.optimization_barrier((queries, grad_out, v_in))
     qg_in = swap(jnp.concatenate([part(queries, 1 - core, q_half), part(grad_out, 1 - core, q_half)], 0))
 
     rows = ((groups, 2, 2 * tok, HEAD_DIM), bf16)
@@ -323,8 +326,10 @@
         near_grads, tok, groups, (core_arr, lo, qs, gs, kb, wk, ka, kc, vb, wv, va, vc, inv, row),
         [kv_f, kv_f, kv_f, kv_f, dq_o, dq_o],
         [pltpu.VMEM((groups, 2, 2 * tok, HEAD_DIM), bf16)])
-    dv = hop((dva + cv.astype(f32)).astype(bf16), -1)
-    dk_out = (dka + ck.astype(f32)).astype(bf16)
+    (dv_out,) = call(merge, tok, groups, (core_arr, dva, cv), [kv_b])
+    dv = hop(dv_out, -1)
+    (dk_out,) = call(merge, tok, groups, (core_arr, dka, ck), [kv_b])
+    dkc, dq1, _ = lax.optimization_barrier((dkc, dq1, dv_out))
     dk_same = hop(dk_out[:tok], -1)
     dk_cross = cross(dk_out[tok:], -1)
     def place(mine, other):

time: 65 us -> 62.3 us (0.958)
  other arithmetic: 4.74 us -> 2.71 us
  waiting for transfers between devices: 21.7 us -> 23.7 us
  Pallas kernels: 10.9 us -> 9.71 us
  starting transfers between devices: 24.3 us -> 23.5 us
    convert_element_type x2 -> x0, other arithmetic: 2.06 us -> none  [the longest x1 1.03 us: local(): dv = hop((dva + cv.astype(f32)).astype(bf16), -1)]
    ppermute x6, waiting for transfers between devices: 14.3 us -> 16.1 us  [hop(): lax.ppermute(x, AXES, [(i, i + by) for i in range(n) if 0 <= i + by < n])]
    ppermute x6, waiting for transfers between devices: 2.53 us -> 1.13 us  [swap(): return lax.ppermute(x, AXES, [(i, i ^ 1) for i in range(n)])]
    pallas_call x5 -> x7, Pallas kernels: 10.9 us -> 9.71 us  [call(): pl.pallas_call(functools.partial(body, tok, groups), in_specs=[pl.BlockSp...]
    ppermute x6, starting transfers between devices: 17.2 us -> 16.2 us  [hop(): lax.ppermute(x, AXES, [(i, i + by) for i in range(n) if 0 <= i + by < n])]
    ppermute x1, waiting for transfers between devices: 0.54 us -> 1.35 us  [cross(): lax.ppermute(x, AXES, [(i, (i ^ 1) + by) for i in range(n) if 0 <= i + by...]
    ppermute x2, waiting for transfers between devices: 4.33 us -> 5.09 us  [forward(): lax.ppermute(x, AXES, [(i, i + 2) for i in range(n) if i % row < row - 2])]
  transfers between devices with their start and end apart: 17 -> 17, of which waited for: 11 -> 10; matrix products, arithmetic and copies ran while one was open for 6% -> 3% of each run, Pallas kernels for 17% -> 16%
where the time goes in v5:
time: 62.3 us; the launch traced here: 61.9 us
  waiting for transfers between devices  23.7 us (38%)
  starting transfers between devices  23.5 us (38%)
  Pallas kernels  9.71 us (16%)
  other arithmetic  2.71 us (4%)
  local copies, waits for them, and re-layouts  1.22 us (2%)
  between operations  1.01 us (2%)
    ppermute x6, starting transfers between devices, hop(): lax.ppermute(x, AXES, [(i, i + by) for i in range(n) if 0 <= i + by < n])  16.2 us
    ppermute x6, waiting for transfers between devices, hop(): lax.ppermute(x, AXES, [(i, i + by) for i in range(n) if 0 <= i + by < n])  16.1 us
    pallas_call x7, Pallas kernels, call(): pl.pallas_call(functools.partial(body, tok, groups), in_specs=[pl.BlockSp...  9.71 us
    ppermute x2, waiting for transfers between devices, forward(): lax.ppermute(x, AXES, [(i, i + 2) for i in range(n) if i % row < row - 2])  5.09 us
    ppermute x2, starting transfers between devices, forward(): lax.ppermute(x, AXES, [(i, i + 2) for i in range(n) if i % row < row - 2])  2.56 us
    concatenate x3, other arithmetic, place(): return jnp.concatenate([first, second], 1)  2.29 us
    ppermute x1, starting transfers between devices, cross(): lax.ppermute(x, AXES, [(i, (i ^ 1) + by) for i in range(n) if 0 <= i + by...  1.92 us
    ppermute x6, starting transfers between devices, swap(): return lax.ppermute(x, AXES, [(i, i ^ 1) for i in range(n)])  1.46 us
  transfers between devices with their start and end apart: 17, of which 10 were waited for; matrix products, arithmetic and copies ran while one was open for 3% of the time, Pallas kernels for 16%

profile of v5, /device:TPU:26, one launch (start us, length us, event | category | flops | bytes accessed | tf_op | source)
XLA Modules:
  0.0 61.9 jit_solution(2370553020390713371)
XLA Ops:
  0.7 1.1 %constant_dynamic-slice_fusion.5 = (bf16[128,512]{1,0:T(8,128)(2,1)S(1)}, bf16[128,512]{1,0:T(8,128)(2,1)S(1)}) fusion(bf16[128,1024]{1,0:T(8,128)(2,1)} %param.7, s32[]{:T(128)S(6)} %select_n.45, s32[]{:T(128)S(6)} %select_n.46), kind=kLoop, calls=%fused_computation.24 | loop fusion | bytes 524296 | tf_op jit(solution)/shard_map/dynamic_slice | solution.py:289
  3.5 3.1 %collective-permute-start.4 = (bf16[272,512]{1,0:T(8,128)(2,1)S(1)}, bf16[272,512]{1,0:T(8,128)(2,1)S(1)}, u32[]{:S(2)}, u32[]{:S(2)}) collective-permute-start(bf16[272,512]{1,0:T(8,128)(2,1)S(1)} %pad_maximum_fusion.2.kc), channel_id=1, source_target_pairs={{0,2},{1,3},{2,4},{3,5},{4,6},{5,7},{6,8},{7,9},{8,10},{9,11},{10,... | collective-permute-start | bytes 835592 | tf_op jit(solution)/shard_map/ppermute | solution.py:34
  6.7 3.5 %collective-permute-start.1 = (bf16[272,512]{1,0:T(8,128)(2,1)S(1)}, bf16[272,512]{1,0:T(8,128)(2,1)S(1)}, u32[]{:S(2)}, u32[]{:S(2)}) collective-permute-start(bf16[272,512]{1,0:T(8,128)(2,1)S(1)} %maximum_maximum_fusion.vc), channel_id=1, source_target_pairs={{0,2},{1,3},{2,4},{3,5},{4,6},{5,7},{6,8},{7,9},{8,10},{9,11},{10,... | collective-permute-start | bytes 835592 | tf_op jit(solution)/shard_map/ppermute | solution.py:34
  10.9 4.0 %collective-permute-done.4.ka = bf16[272,512]{1,0:T(8,128)(2,1)S(1)} collective-permute-done((bf16[272,512]{1,0:T(8,128)(2,1)S(1)}, bf16[272,512]{1,0:T(8,128)(2,1)S(1)}, u32[]{:S(2)}, u32[]{:S(2)}) %collective-permute-start.4) | collective-permute-done | bytes 278560 | tf_op jit(solution)/shard_map/ppermute | solution.py:34
  14.9 1.3 %collective-permute-start.5 = (bf16[272,512]{1,0:T(8,128)(2,1)S(1)}, bf16[272,512]{1,0:T(8,128)(2,1)S(1)}, u32[]{:S(2)}, u32[]{:S(2)}) collective-permute-start(bf16[272,512]{1,0:T(8,128)(2,1)S(1)} %collective-permute-done.4.ka), channel_id=1, source_target_pairs={{0,2},{1,3},{2,4},{3,5},{4,6},{5,7},{8,10},{9,11},{10,12},{11,13},... | collective-permute-start | bytes 835592 | tf_op jit(solution)/shard_map/ppermute | solution.py:45
  17.3 3.6 %collective-permute-done.1.va = bf16[272,512]{1,0:T(8,128)(2,1)S(1)} collective-permute-done((bf16[272,512]{1,0:T(8,128)(2,1)S(1)}, bf16[272,512]{1,0:T(8,128)(2,1)S(1)}, u32[]{:S(2)}, u32[]{:S(2)}) %collective-permute-start.1) | collective-permute-done | bytes 278560 | tf_op jit(solution)/shard_map/ppermute | solution.py:34
  20.9 1.3 %collective-permute-start.7 = (bf16[272,512]{1,0:T(8,128)(2,1)S(1)}, bf16[272,512]{1,0:T(8,128)(2,1)S(1)}, u32[]{:S(2)}, u32[]{:S(2)}) collective-permute-start(bf16[272,512]{1,0:T(8,128)(2,1)S(1)} %collective-permute-done.1.va), channel_id=1, source_target_pairs={{0,2},{1,3},{2,4},{3,5},{4,6},{5,7},{8,10},{9,11},{10,12},{11,13},... | collective-permute-start | bytes 835592 | tf_op jit(solution)/shard_map/ppermute | solution.py:45
  22.2 1.1 %near_sums.1 = (f32[4,16,256]{2,1,0:T(8,128)S(1)}, f32[4,16,256]{2,1,0:T(8,128)S(1)}) custom-call(s32[1]{0:T(128)} %bitcast.core_ref, s32[8,128]{1,0:T(8,128)S(1)} %get-tuple-element.33.lo_ref, bf16[4,2,256,128]{3,2,1,0:T(8,128)(2,1)S(1)} %get-tuple-element.34.qs, bf16[4,2,256,128]{3,2,1,0:T(8,128)(2,1)S(1)} %get-tuple-element.35.gs, ...), custom_call_target="tpu_custom_call" | custom-call | tf_op jit(solution)/shard_map/near_sums/pallas_call | solution.py:264
  23.3 3.5 %collective-permute-done.5.kb = bf16[272,512]{1,0:T(8,128)(2,1)S(1)} collective-permute-done((bf16[272,512]{1,0:T(8,128)(2,1)S(1)}, bf16[272,512]{1,0:T(8,128)(2,1)S(1)}, u32[]{:S(2)}, u32[]{:S(2)}) %collective-permute-start.5) | collective-permute-done | bytes 278560 | tf_op jit(solution)/shard_map/ppermute | solution.py:45
  26.9 1.7 %far_values.1 = (bf16[256,512]{1,0:T(8,128)(2,1)S(1)}, f32[4,16,256]{2,1,0:T(8,128)S(1)}) custom-call(s32[1]{0:T(128)} %bitcast.core_ref, s32[8,128]{1,0:T(8,128)S(1)} %get-tuple-element.33.lo_ref, bf16[4,2,256,128]{3,2,1,0:T(8,128)(2,1)S(1)} %get-tuple-element.34.qs, bf16[4,2,256,128]{3,2,1,0:T(8,128)(2,1)S(1)} %get-tuple-element.35.gs, ...), custom_call_target="tpu_custom_call" | custom-call | tf_op jit(solution)/shard_map/far_values/pallas_call | solution.py:264
  28.6 2.1 %collective-permute-start.9 = (bf16[256,512]{1,0:T(8,128)(2,1)S(1)}, bf16[256,512]{1,0:T(8,128)(2,1)S(1)}, u32[]{:S(2)}, u32[]{:S(2)}) collective-permute-start(bf16[256,512]{1,0:T(8,128)(2,1)S(1)} %get-tuple-element.45), channel_id=1, source_target_pairs={{2,0},{3,1},{4,2},{5,3},{6,4},{7,5},{8,6},{9,7},{10,8},{11,9},{12,... | collective-permute-start | bytes 786440 | tf_op jit(solution)/shard_map/ppermute | solution.py:34
  30.7 1.6 %collective-permute-done.7.vb = bf16[272,512]{1,0:T(8,128)(2,1)S(1)} collective-permute-done((bf16[272,512]{1,0:T(8,128)(2,1)S(1)}, bf16[272,512]{1,0:T(8,128)(2,1)S(1)}, u32[]{:S(2)}, u32[]{:S(2)}) %collective-permute-start.7) | collective-permute-done | bytes 278560 | tf_op jit(solution)/shard_map/ppermute | solution.py:45
  32.3 2.4 %far_keys.1 = (bf16[256,512]{1,0:T(8,128)(2,1)S(1)}, f32[4,16,256]{2,1,0:T(8,128)S(1)}) custom-call(s32[1]{0:T(128)} %bitcast.core_ref, s32[8,128]{1,0:T(8,128)S(1)} %get-tuple-element.33.lo_ref, bf16[4,2,256,128]{3,2,1,0:T(8,128)(2,1)S(1)} %get-tuple-element.34.qs, bf16[4,2,256,128]{3,2,1,0:T(8,128)(2,1)S(1)} %get-tuple-element.35.gs, ...), custom_call_target="tpu_custom_call" | custom-call | tf_op jit(solution)/shard_map/far_keys/pallas_call | solution.py:264
  34.7 2.7 %collective-permute-start.11 = (bf16[256,512]{1,0:T(8,128)(2,1)S(1)}, bf16[256,512]{1,0:T(8,128)(2,1)S(1)}, u32[]{:S(2)}, u32[]{:S(2)}) collective-permute-start(bf16[256,512]{1,0:T(8,128)(2,1)S(1)} %get-tuple-element.49), channel_id=1, source_target_pairs={{2,0},{3,1},{4,2},{5,3},{6,4},{7,5},{8,6},{9,7},{10,8},{11,9},{12,... | collective-permute-start | bytes 786440 | tf_op jit(solution)/shard_map/ppermute | solution.py:34
  37.3 4.0 %near_grads.1 = (f32[256,512]{1,0:T(8,128)S(1)}, f32[256,512]{1,0:T(8,128)S(1)}, f32[256,512]{1,0:T(8,128)S(1)}, f32[256,512]{1,0:T(8,128)S(1)}, bf16[128,1024]{...) custom-call(s32[1]{0:T(128)} %bitcast.core_ref, s32[8,128]{1,0:T(8,128)S(1)} %get-tuple-element.33.lo_ref, ...), custom_call_target="tpu_custom_call" | custom-call | tf_op jit(solution)/shard_map/near_grads/pallas_call | solution.py:264
  41.4 3.0 %collective-permute-start.15 = (bf16[256,512]{1,0:T(8,128)(2,1)S(1)}, bf16[256,512]{1,0:T(8,128)(2,1)S(1)}, u32[]{:S(2)}, u32[]{:S(2)}) collective-permute-start(bf16[256,512]{1,0:T(8,128)(2,1)S(1)} %merge.2), channel_id=1, source_target_pairs={{2,0},{3,1},{4,2},{5,3},{6,4},{7,5},{8,6},{9,7},{10,8},{11,9},{12,... | collective-permute-start | bytes 786440 | tf_op jit(solution)/shard_map/ppermute | solution.py:34
  45.0 2.8 %collective-permute-done.11.came = bf16[256,512]{1,0:T(8,128)(2,1)S(1)} collective-permute-done((bf16[256,512]{1,0:T(8,128)(2,1)S(1)}, bf16[256,512]{1,0:T(8,128)(2,1)S(1)}, u32[]{:S(2)}, u32[]{:S(2)}) %collective-permute-start.11) | collective-permute-done | bytes 262176 | tf_op jit(solution)/shard_map/ppermute | solution.py:34
  47.9 1.9 %collective-permute-start.14 = (bf16[128,512]{1,0:T(8,128)(2,1)S(1)}, bf16[128,512]{1,0:T(8,128)(2,1)S(1)}, u32[]{:S(2)}, u32[]{:S(2)}) collective-permute-start(bf16[128,512]{1,0:T(8,128)(2,1)S(1)} %get-tuple-element.60), channel_id=1, source_target_pairs={{2,1},{3,0},{4,3},{5,2},{6,5},{7,4},{8,7},{9,6},{10,9},{11,8},{12,... | collective-permute-start | bytes 393224 | tf_op jit(solution)/shard_map/ppermute | solution.py:40
  49.8 1.9 %collective-permute-start.12 = (bf16[128,512]{1,0:T(8,128)(2,1)S(1)}, bf16[128,512]{1,0:T(8,128)(2,1)S(1)}, u32[]{:S(2)}, u32[]{:S(2)}) collective-permute-start(bf16[128,512]{1,0:T(8,128)(2,1)S(1)} %get-tuple-element.59), channel_id=1, source_target_pairs={{2,0},{3,1},{4,2},{5,3},{6,4},{7,5},{8,6},{9,7},{10,8},{11,9},{12,... | collective-permute-start | bytes 393224 | tf_op jit(solution)/shard_map/ppermute | solution.py:34
  51.7 2.5 %collective-permute-done.15 = bf16[256,512]{1,0:T(8,128)(2,1)S(1)} collective-permute-done((bf16[256,512]{1,0:T(8,128)(2,1)S(1)}, bf16[256,512]{1,0:T(8,128)(2,1)S(1)}, u32[]{:S(2)}, u32[]{:S(2)}) %collective-permute-start.15) | collective-permute-done | bytes 262176 | tf_op jit(solution)/shard_map/ppermute | solution.py:34
  54.5 0.8 %pad_maximum_fusion.1 = bf16[128,2048]{1,0:T(8,128)(2,1)} fusion(bf16[128,1024]{1,0:T(8,128)(2,1)S(1)} %get-tuple-element.56, bf16[128,1024]{1,0:T(8,128)(2,1)S(1)} %get-tuple-element.55), kind=kLoop, calls=%fused_computation.1 | loop fusion | flops 1048576 | bytes 1048576 | tf_op jit(solution)/shard_map/concatenate | solution.py:338
  55.8 0.7 %pad_maximum_fusion.3 = bf16[128,1024]{1,0:T(8,128)(2,1)} fusion(bf16[128,512]{1,0:T(8,128)(2,1)S(1)} %get-tuple-element.58, bf16[128,512]{1,0:T(8,128)(2,1)S(1)} %get-tuple-element.57), kind=kLoop, calls=%fused_computation.7 | loop fusion | flops 524288 | bytes 524288 | tf_op jit(solution)/shard_map/concatenate | solution.py:338
  56.5 1.4 %collective-permute-done.14 = bf16[128,512]{1,0:T(8,128)(2,1)S(1)} collective-permute-done((bf16[128,512]{1,0:T(8,128)(2,1)S(1)}, bf16[128,512]{1,0:T(8,128)(2,1)S(1)}, u32[]{:S(2)}, u32[]{:S(2)}) %collective-permute-start.14) | collective-permute-done | bytes 131104 | tf_op jit(solution)/shard_map/ppermute | solution.py:40
  57.8 3.2 %collective-permute-done.12 = bf16[128,512]{1,0:T(8,128)(2,1)S(1)} collective-permute-done((bf16[128,512]{1,0:T(8,128)(2,1)S(1)}, bf16[128,512]{1,0:T(8,128)(2,1)S(1)}, u32[]{:S(2)}, u32[]{:S(2)}) %collective-permute-start.12) | collective-permute-done | bytes 131104 | tf_op jit(solution)/shard_map/ppermute | solution.py:34
  (47 shorter events, 5.8 us)
Async XLA Ops:
  0.6 1.2 %copy-start.3 = (s32[128]{0:T(128)S(1)}, s32[128]{0:T(128)}, u32[]{:S(2)}) copy-start(s32[128]{0:T(128)} %param.9) | copy-start | bytes 1540
  0.7 1.2 %copy-start.2 = (bf16[128,1024]{1,0:T(8,128)(2,1)S(1)}, bf16[128,1024]{1,0:T(8,128)(2,1)}, u32[]{:S(2)}) copy-start(bf16[128,1024]{1,0:T(8,128)(2,1)} %param.6) | copy-start | bytes 786436
  0.7 2.5 %copy-start.1 = (bf16[128,2048]{1,0:T(8,128)(2,1)S(1)}, bf16[128,2048]{1,0:T(8,128)(2,1)}, u32[]{:S(2)}) copy-start(bf16[128,2048]{1,0:T(8,128)(2,1)} %go) | copy-start | bytes 1572868
  1.7 1.4 %copy-start = (bf16[128,2048]{1,0:T(8,128)(2,1)S(1)}, bf16[128,2048]{1,0:T(8,128)(2,1)}, u32[]{:S(2)}) copy-start(bf16[128,2048]{1,0:T(8,128)(2,1)} %q) | copy-start | bytes 1572868
  1.8 1.4 %collective-permute-start = (bf16[128,512]{1,0:T(8,128)(2,1)S(1)}, bf16[128,512]{1,0:T(8,128)(2,1)S(1)}, u32[]{:S(2)}, u32[]{:S(2)}) collective-permute-start(bf16[128,512]{1,0:T(8,128)(2,1)S(1)} %get-tuple-element.64), channel_id=1, source_target_pairs={{0,1},{1,0},{2,3},{3,2},{4,5},{5,4},{6,7},{7,6},{8,9},{9,8},{10,11... | collective-permute-start | bytes 393224 | tf_op jit(solution)/shard_map/ppermute | solution.py:28
  1.9 1.6 %collective-permute-start.3 = (bf16[144,512]{1,0:T(8,128)(2,1)S(1)}, bf16[144,512]{1,0:T(8,128)(2,1)S(1)}, u32[]{:S(2)}, u32[]{:S(2)}) collective-permute-start(bf16[144,512]{1,0:T(8,128)(2,1)S(1)} %fusion.1), channel_id=1, source_target_pairs={{0,1},{1,0},{2,3},{3,2},{4,5},{5,4},{6,7},{7,6},{8,9},{9,8},{10,11... | collective-permute-start | bytes 442376 | tf_op jit(solution)/shard_map/ppermute | solution.py:28
  3.3 13.6 %collective-permute-start.2 = (bf16[256,1024]{1,0:T(8,128)(2,1)S(1)}, bf16[256,1024]{1,0:T(8,128)(2,1)S(1)}, u32[]{:S(2)}, u32[]{:S(2)}) collective-permute-start(bf16[256,1024]{1,0:T(8,128)(2,1)S(1)} %pad_maximum_fusion), channel_id=1, source_target_pairs={{0,1},{1,0},{2,3},{3,2},{4,5},{5,4},{6,7},{7,6},{8,9},{9,8},{10,11... | collective-permute-start | bytes 1572872 | tf_op jit(solution)/shard_map/ppermute | solution.py:28
  3.5 11.4 %collective-permute-start.4 = (bf16[272,512]{1,0:T(8,128)(2,1)S(1)}, bf16[272,512]{1,0:T(8,128)(2,1)S(1)}, u32[]{:S(2)}, u32[]{:S(2)}) collective-permute-start(bf16[272,512]{1,0:T(8,128)(2,1)S(1)} %pad_maximum_fusion.2.kc), channel_id=1, source_target_pairs={{0,2},{1,3},{2,4},{3,5},{4,6},{5,7},{6,8},{7,9},{8,10},{9,11},{10,... | collective-permute-start | bytes 835592 | tf_op jit(solution)/shard_map/ppermute | solution.py:34
  6.7 14.2 %collective-permute-start.1 = (bf16[272,512]{1,0:T(8,128)(2,1)S(1)}, bf16[272,512]{1,0:T(8,128)(2,1)S(1)}, u32[]{:S(2)}, u32[]{:S(2)}) collective-permute-start(bf16[272,512]{1,0:T(8,128)(2,1)S(1)} %maximum_maximum_fusion.vc), channel_id=1, source_target_pairs={{0,2},{1,3},{2,4},{3,5},{4,6},{5,7},{6,8},{7,9},{8,10},{9,11},{10,... | collective-permute-start | bytes 835592 | tf_op jit(solution)/shard_map/ppermute | solution.py:34
  10.2 13.1 %collective-permute-start.6 = (bf16[272,512]{1,0:T(8,128)(2,1)S(1)}, bf16[272,512]{1,0:T(8,128)(2,1)S(1)}, u32[]{:S(2)}, u32[]{:S(2)}) collective-permute-start(bf16[272,512]{1,0:T(8,128)(2,1)S(1)} %pad_maximum_fusion.2.kc), channel_id=1, source_target_pairs={{4,8},{5,9},{12,16},{13,17},{20,24},{21,25}} | collective-permute-start | bytes 835592 | tf_op jit(solution)/shard_map/ppermute | solution.py:50
  14.9 11.9 %collective-permute-start.5 = (bf16[272,512]{1,0:T(8,128)(2,1)S(1)}, bf16[272,512]{1,0:T(8,128)(2,1)S(1)}, u32[]{:S(2)}, u32[]{:S(2)}) collective-permute-start(bf16[272,512]{1,0:T(8,128)(2,1)S(1)} %collective-permute-done.4.ka), channel_id=1, source_target_pairs={{0,2},{1,3},{2,4},{3,5},{4,6},{5,7},{8,10},{9,11},{10,12},{11,13},... | collective-permute-start | bytes 835592 | tf_op jit(solution)/shard_map/ppermute | solution.py:45
  16.2 14.5 %collective-permute-start.8 = (bf16[272,512]{1,0:T(8,128)(2,1)S(1)}, bf16[272,512]{1,0:T(8,128)(2,1)S(1)}, u32[]{:S(2)}, u32[]{:S(2)}) collective-permute-start(bf16[272,512]{1,0:T(8,128)(2,1)S(1)} %maximum_maximum_fusion.vc), channel_id=1, source_target_pairs={{4,8},{5,9},{12,16},{13,17},{20,24},{21,25}} | collective-permute-start | bytes 835592 | tf_op jit(solution)/shard_map/ppermute | solution.py:50
  20.9 11.4 %collective-permute-start.7 = (bf16[272,512]{1,0:T(8,128)(2,1)S(1)}, bf16[272,512]{1,0:T(8,128)(2,1)S(1)}, u32[]{:S(2)}, u32[]{:S(2)}) collective-permute-start(bf16[272,512]{1,0:T(8,128)(2,1)S(1)} %collective-permute-done.1.va), channel_id=1, source_target_pairs={{0,2},{1,3},{2,4},{3,5},{4,6},{5,7},{8,10},{9,11},{10,12},{11,13},... | collective-permute-start | bytes 835592 | tf_op jit(solution)/shard_map/ppermute | solution.py:45
  28.6 12.8 %collective-permute-start.9 = (bf16[256,512]{1,0:T(8,128)(2,1)S(1)}, bf16[256,512]{1,0:T(8,128)(2,1)S(1)}, u32[]{:S(2)}, u32[]{:S(2)}) collective-permute-start(bf16[256,512]{1,0:T(8,128)(2,1)S(1)} %get-tuple-element.45), channel_id=1, source_target_pairs={{2,0},{3,1},{4,2},{5,3},{6,4},{7,5},{8,6},{9,7},{10,8},{11,9},{12,... | collective-permute-start | bytes 786440 | tf_op jit(solution)/shard_map/ppermute | solution.py:34
  34.7 13.1 %collective-permute-start.11 = (bf16[256,512]{1,0:T(8,128)(2,1)S(1)}, bf16[256,512]{1,0:T(8,128)(2,1)S(1)}, u32[]{:S(2)}, u32[]{:S(2)}) collective-permute-start(bf16[256,512]{1,0:T(8,128)(2,1)S(1)} %get-tuple-element.49), channel_id=1, source_target_pairs={{2,0},{3,1},{4,2},{5,3},{6,4},{7,5},{8,6},{9,7},{10,8},{11,9},{12,... | collective-permute-start | bytes 786440 | tf_op jit(solution)/shard_map/ppermute | solution.py:34
  41.4 12.8 %collective-permute-start.15 = (bf16[256,512]{1,0:T(8,128)(2,1)S(1)}, bf16[256,512]{1,0:T(8,128)(2,1)S(1)}, u32[]{:S(2)}, u32[]{:S(2)}) collective-permute-start(bf16[256,512]{1,0:T(8,128)(2,1)S(1)} %merge.2), channel_id=1, source_target_pairs={{2,0},{3,1},{4,2},{5,3},{6,4},{7,5},{8,6},{9,7},{10,8},{11,9},{12,... | collective-permute-start | bytes 786440 | tf_op jit(solution)/shard_map/ppermute | solution.py:34
  44.4 13.4 %collective-permute-start.13 = (f32[128,512]{1,0:T(8,128)S(1)}, f32[128,512]{1,0:T(8,128)S(1)}, u32[]{:S(2)}, u32[]{:S(2)}) collective-permute-start(f32[128,512]{1,0:T(8,128)S(1)} %slice.30), channel_id=1, source_target_pairs={{0,1},{1,0},{2,3},{3,2},{4,5},{5,4},{6,7},{7,6},{8,9},{9,8},{10,11... | collective-permute-start | bytes 786440 | tf_op jit(solution)/shard_map/ppermute | solution.py:28
  44.5 9.9 %collective-permute-start.10 = (bf16[128,1024]{1,0:T(8,128)(2,1)S(1)}, bf16[128,1024]{1,0:T(8,128)(2,1)S(1)}, u32[]{:S(2)}, u32[]{:S(2)}) collective-permute-start(bf16[128,1024]{1,0:T(8,128)(2,1)S(1)} %get-tuple-element.46), channel_id=1, source_target_pairs={{0,1},{1,0},{2,3},{3,2},{4,5},{5,4},{6,7},{7,6},{8,9},{9,8},{10,11... | collective-permute-start | bytes 786440 | tf_op jit(solution)/shard_map/ppermute | solution.py:28
  47.9 10.0 %collective-permute-start.14 = (bf16[128,512]{1,0:T(8,128)(2,1)S(1)}, bf16[128,512]{1,0:T(8,128)(2,1)S(1)}, u32[]{:S(2)}, u32[]{:S(2)}) collective-permute-start(bf16[128,512]{1,0:T(8,128)(2,1)S(1)} %get-tuple-element.60), channel_id=1, source_target_pairs={{2,1},{3,0},{4,3},{5,2},{6,5},{7,4},{8,7},{9,6},{10,9},{11,8},{12,... | collective-permute-start | bytes 393224 | tf_op jit(solution)/shard_map/ppermute | solution.py:40
  49.8 11.3 %collective-permute-start.12 = (bf16[128,512]{1,0:T(8,128)(2,1)S(1)}, bf16[128,512]{1,0:T(8,128)(2,1)S(1)}, u32[]{:S(2)}, u32[]{:S(2)}) collective-permute-start(bf16[128,512]{1,0:T(8,128)(2,1)S(1)} %get-tuple-element.59), channel_id=1, source_target_pairs={{2,0},{3,1},{4,2},{5,3},{6,4},{7,5},{8,6},{9,7},{10,8},{11,9},{12,... | collective-permute-start | bytes 393224 | tf_op jit(solution)/shard_map/ppermute | solution.py:34
  54.3 1.4 %collective-permute-start.16 = (bf16[128,512]{1,0:T(8,128)(2,1)S(1)}, bf16[128,512]{1,0:T(8,128)(2,1)S(1)}, u32[]{:S(2)}, u32[]{:S(2)}) collective-permute-start(bf16[128,512]{1,0:T(8,128)(2,1)S(1)} %slice.39), channel_id=1, source_target_pairs={{0,1},{1,0},{2,3},{3,2},{4,5},{5,4},{6,7},{7,6},{8,9},{9,8},{10,11... | collective-permute-start | bytes 393224 | tf_op jit(solution)/shard_map/ppermute | solution.py:28

commit v6 on v5

--- a/solution.py
+++ b/solution.py
@@ -15,7 +15,7 @@
 AXES = ("ctx", "fsdp")
 NT = (((1,), (1,)), ((), ()))
 NN = (((1,), (0,)), ((), ()))
-SEG_ROWS = 16
+SEG_ROWS = 8
 FAR = 2
 
 

time: 62.3 us -> 61.6 us (0.989)
  waiting for transfers between devices: 23.7 us -> 22.5 us
    ppermute x2, waiting for transfers between devices: 5.09 us -> 4.39 us  [forward(): lax.ppermute(x, AXES, [(i, i + 2) for i in range(n) if i % row < row - 2])]
where the time goes in v6:
time: 61.6 us; the launch traced here: 61.2 us
  starting transfers between devices  24 us (39%)
  waiting for transfers between devices  22.5 us (37%)
  Pallas kernels  9.76 us (16%)
  other arithmetic  2.71 us (4%)
  local copies, waits for them, and re-layouts  1.22 us (2%)
  between operations  1.01 us (2%)
    ppermute x6, starting transfers between devices, hop(): lax.ppermute(x, AXES, [(i, i + by) for i in range(n) if 0 <= i + by < n])  16.7 us
    ppermute x6, waiting for transfers between devices, hop(): lax.ppermute(x, AXES, [(i, i + by) for i in range(n) if 0 <= i + by < n])  15.6 us
    pallas_call x7, Pallas kernels, call(): pl.pallas_call(functools.partial(body, tok, groups), in_specs=[pl.BlockSp...  9.76 us
    ppermute x2, waiting for transfers between devices, forward(): lax.ppermute(x, AXES, [(i, i + 2) for i in range(n) if i % row < row - 2])  4.39 us
    ppermute x2, starting transfers between devices, forward(): lax.ppermute(x, AXES, [(i, i + 2) for i in range(n) if i % row < row - 2])  2.56 us
    concatenate x3, other arithmetic, place(): return jnp.concatenate([first, second], 1)  2.29 us
    ppermute x1, starting transfers between devices, cross(): lax.ppermute(x, AXES, [(i, (i ^ 1) + by) for i in range(n) if 0 <= i + by...  1.92 us
    ppermute x6, starting transfers between devices, swap(): return lax.ppermute(x, AXES, [(i, i ^ 1) for i in range(n)])  1.46 us
  transfers between devices with their start and end apart: 17, of which 10 were waited for; matrix products, arithmetic and copies ran while one was open for 3% of the time, Pallas kernels for 16%

profile of v6, /device:TPU:26, one launch (start us, length us, event | category | flops | bytes accessed | tf_op | source)
XLA Modules:
  0.0 61.2 jit_solution(841652037167101500)
XLA Ops:
  0.7 1.1 %constant_dynamic-slice_fusion.5 = (bf16[128,512]{1,0:T(8,128)(2,1)S(1)}, bf16[128,512]{1,0:T(8,128)(2,1)S(1)}) fusion(bf16[128,1024]{1,0:T(8,128)(2,1)} %param.7, s32[]{:T(128)S(6)} %select_n.45, s32[]{:T(128)S(6)} %select_n.46), kind=kLoop, calls=%fused_computation.24 | loop fusion | bytes 524296 | tf_op jit(solution)/shard_map/dynamic_slice | solution.py:289
  3.5 3.1 %collective-permute-start.4 = (bf16[264,512]{1,0:T(8,128)(2,1)S(1)}, bf16[264,512]{1,0:T(8,128)(2,1)S(1)}, u32[]{:S(2)}, u32[]{:S(2)}) collective-permute-start(bf16[264,512]{1,0:T(8,128)(2,1)S(1)} %pad_maximum_fusion.2.kc), channel_id=1, source_target_pairs={{0,2},{1,3},{2,4},{3,5},{4,6},{5,7},{6,8},{7,9},{8,10},{9,11},{10,... | collective-permute-start | bytes 811016 | tf_op jit(solution)/shard_map/ppermute | solution.py:34
  6.7 3.5 %collective-permute-start.1 = (bf16[264,512]{1,0:T(8,128)(2,1)S(1)}, bf16[264,512]{1,0:T(8,128)(2,1)S(1)}, u32[]{:S(2)}, u32[]{:S(2)}) collective-permute-start(bf16[264,512]{1,0:T(8,128)(2,1)S(1)} %maximum_maximum_fusion.vc), channel_id=1, source_target_pairs={{0,2},{1,3},{2,4},{3,5},{4,6},{5,7},{6,8},{7,9},{8,10},{9,11},{10,... | collective-permute-start | bytes 811016 | tf_op jit(solution)/shard_map/ppermute | solution.py:34
  10.9 3.8 %collective-permute-done.4.ka = bf16[264,512]{1,0:T(8,128)(2,1)S(1)} collective-permute-done((bf16[264,512]{1,0:T(8,128)(2,1)S(1)}, bf16[264,512]{1,0:T(8,128)(2,1)S(1)}, u32[]{:S(2)}, u32[]{:S(2)}) %collective-permute-start.4) | collective-permute-done | bytes 270368 | tf_op jit(solution)/shard_map/ppermute | solution.py:34
  14.7 1.3 %collective-permute-start.5 = (bf16[264,512]{1,0:T(8,128)(2,1)S(1)}, bf16[264,512]{1,0:T(8,128)(2,1)S(1)}, u32[]{:S(2)}, u32[]{:S(2)}) collective-permute-start(bf16[264,512]{1,0:T(8,128)(2,1)S(1)} %collective-permute-done.4.ka), channel_id=1, source_target_pairs={{0,2},{1,3},{2,4},{3,5},{4,6},{5,7},{8,10},{9,11},{10,12},{11,13},... | collective-permute-start | bytes 811016 | tf_op jit(solution)/shard_map/ppermute | solution.py:45
  17.1 3.4 %collective-permute-done.1.va = bf16[264,512]{1,0:T(8,128)(2,1)S(1)} collective-permute-done((bf16[264,512]{1,0:T(8,128)(2,1)S(1)}, bf16[264,512]{1,0:T(8,128)(2,1)S(1)}, u32[]{:S(2)}, u32[]{:S(2)}) %collective-permute-start.1) | collective-permute-done | bytes 270368 | tf_op jit(solution)/shard_map/ppermute | solution.py:34
  20.5 1.3 %collective-permute-start.7 = (bf16[264,512]{1,0:T(8,128)(2,1)S(1)}, bf16[264,512]{1,0:T(8,128)(2,1)S(1)}, u32[]{:S(2)}, u32[]{:S(2)}) collective-permute-start(bf16[264,512]{1,0:T(8,128)(2,1)S(1)} %collective-permute-done.1.va), channel_id=1, source_target_pairs={{0,2},{1,3},{2,4},{3,5},{4,6},{5,7},{8,10},{9,11},{10,12},{11,13},... | collective-permute-start | bytes 811016 | tf_op jit(solution)/shard_map/ppermute | solution.py:45
  21.8 1.1 %near_sums.1 = (f32[4,16,256]{2,1,0:T(8,128)S(1)}, f32[4,16,256]{2,1,0:T(8,128)S(1)}) custom-call(s32[1]{0:T(128)} %bitcast.core_ref, s32[8,128]{1,0:T(8,128)S(1)} %get-tuple-element.33.lo_ref, bf16[4,2,256,128]{3,2,1,0:T(8,128)(2,1)S(1)} %get-tuple-element.34.qs, bf16[4,2,256,128]{3,2,1,0:T(8,128)(2,1)S(1)} %get-tuple-element.35.gs, ...), custom_call_target="tpu_custom_call" | custom-call | tf_op jit(solution)/shard_map/near_sums/pallas_call | solution.py:264
  23.0 3.3 %collective-permute-done.5.kb = bf16[264,512]{1,0:T(8,128)(2,1)S(1)} collective-permute-done((bf16[264,512]{1,0:T(8,128)(2,1)S(1)}, bf16[264,512]{1,0:T(8,128)(2,1)S(1)}, u32[]{:S(2)}, u32[]{:S(2)}) %collective-permute-start.5) | collective-permute-done | bytes 270368 | tf_op jit(solution)/shard_map/ppermute | solution.py:45
  26.3 1.7 %far_values.1 = (bf16[256,512]{1,0:T(8,128)(2,1)S(1)}, f32[4,16,256]{2,1,0:T(8,128)S(1)}) custom-call(s32[1]{0:T(128)} %bitcast.core_ref, s32[8,128]{1,0:T(8,128)S(1)} %get-tuple-element.33.lo_ref, bf16[4,2,256,128]{3,2,1,0:T(8,128)(2,1)S(1)} %get-tuple-element.34.qs, bf16[4,2,256,128]{3,2,1,0:T(8,128)(2,1)S(1)} %get-tuple-element.35.gs, ...), custom_call_target="tpu_custom_call" | custom-call | tf_op jit(solution)/shard_map/far_values/pallas_call | solution.py:264
  28.0 2.4 %collective-permute-start.9 = (bf16[256,512]{1,0:T(8,128)(2,1)S(1)}, bf16[256,512]{1,0:T(8,128)(2,1)S(1)}, u32[]{:S(2)}, u32[]{:S(2)}) collective-permute-start(bf16[256,512]{1,0:T(8,128)(2,1)S(1)} %get-tuple-element.45), channel_id=1, source_target_pairs={{2,0},{3,1},{4,2},{5,3},{6,4},{7,5},{8,6},{9,7},{10,8},{11,9},{12,... | collective-permute-start | bytes 786440 | tf_op jit(solution)/shard_map/ppermute | solution.py:34
  30.5 1.1 %collective-permute-done.7.vb = bf16[264,512]{1,0:T(8,128)(2,1)S(1)} collective-permute-done((bf16[264,512]{1,0:T(8,128)(2,1)S(1)}, bf16[264,512]{1,0:T(8,128)(2,1)S(1)}, u32[]{:S(2)}, u32[]{:S(2)}) %collective-permute-start.7) | collective-permute-done | bytes 270368 | tf_op jit(solution)/shard_map/ppermute | solution.py:45
  31.6 2.4 %far_keys.1 = (bf16[256,512]{1,0:T(8,128)(2,1)S(1)}, f32[4,16,256]{2,1,0:T(8,128)S(1)}) custom-call(s32[1]{0:T(128)} %bitcast.core_ref, s32[8,128]{1,0:T(8,128)S(1)} %get-tuple-element.33.lo_ref, bf16[4,2,256,128]{3,2,1,0:T(8,128)(2,1)S(1)} %get-tuple-element.34.qs, bf16[4,2,256,128]{3,2,1,0:T(8,128)(2,1)S(1)} %get-tuple-element.35.gs, ...), custom_call_target="tpu_custom_call" | custom-call | tf_op jit(solution)/shard_map/far_keys/pallas_call | solution.py:264
  34.0 3.0 %collective-permute-start.11 = (bf16[256,512]{1,0:T(8,128)(2,1)S(1)}, bf16[256,512]{1,0:T(8,128)(2,1)S(1)}, u32[]{:S(2)}, u32[]{:S(2)}) collective-permute-start(bf16[256,512]{1,0:T(8,128)(2,1)S(1)} %get-tuple-element.49), channel_id=1, source_target_pairs={{2,0},{3,1},{4,2},{5,3},{6,4},{7,5},{8,6},{9,7},{10,8},{11,9},{12,... | collective-permute-start | bytes 786440 | tf_op jit(solution)/shard_map/ppermute | solution.py:34
  37.0 4.0 %near_grads.1 = (f32[256,512]{1,0:T(8,128)S(1)}, f32[256,512]{1,0:T(8,128)S(1)}, f32[256,512]{1,0:T(8,128)S(1)}, f32[256,512]{1,0:T(8,128)S(1)}, bf16[128,1024]{...) custom-call(s32[1]{0:T(128)} %bitcast.core_ref, s32[8,128]{1,0:T(8,128)S(1)} %get-tuple-element.33.lo_ref, ...), custom_call_target="tpu_custom_call" | custom-call | tf_op jit(solution)/shard_map/near_grads/pallas_call | solution.py:264
  41.1 2.8 %collective-permute-start.15 = (bf16[256,512]{1,0:T(8,128)(2,1)S(1)}, bf16[256,512]{1,0:T(8,128)(2,1)S(1)}, u32[]{:S(2)}, u32[]{:S(2)}) collective-permute-start(bf16[256,512]{1,0:T(8,128)(2,1)S(1)} %merge.2), channel_id=1, source_target_pairs={{2,0},{3,1},{4,2},{5,3},{6,4},{7,5},{8,6},{9,7},{10,8},{11,9},{12,... | collective-permute-start | bytes 786440 | tf_op jit(solution)/shard_map/ppermute | solution.py:34
  44.5 2.6 %collective-permute-done.11.came = bf16[256,512]{1,0:T(8,128)(2,1)S(1)} collective-permute-done((bf16[256,512]{1,0:T(8,128)(2,1)S(1)}, bf16[256,512]{1,0:T(8,128)(2,1)S(1)}, u32[]{:S(2)}, u32[]{:S(2)}) %collective-permute-start.11) | collective-permute-done | bytes 262176 | tf_op jit(solution)/shard_map/ppermute | solution.py:34
  47.2 1.9 %collective-permute-start.14 = (bf16[128,512]{1,0:T(8,128)(2,1)S(1)}, bf16[128,512]{1,0:T(8,128)(2,1)S(1)}, u32[]{:S(2)}, u32[]{:S(2)}) collective-permute-start(bf16[128,512]{1,0:T(8,128)(2,1)S(1)} %get-tuple-element.60), channel_id=1, source_target_pairs={{2,1},{3,0},{4,3},{5,2},{6,5},{7,4},{8,7},{9,6},{10,9},{11,8},{12,... | collective-permute-start | bytes 393224 | tf_op jit(solution)/shard_map/ppermute | solution.py:40
  49.1 1.9 %collective-permute-start.12 = (bf16[128,512]{1,0:T(8,128)(2,1)S(1)}, bf16[128,512]{1,0:T(8,128)(2,1)S(1)}, u32[]{:S(2)}, u32[]{:S(2)}) collective-permute-start(bf16[128,512]{1,0:T(8,128)(2,1)S(1)} %get-tuple-element.59), channel_id=1, source_target_pairs={{2,0},{3,1},{4,2},{5,3},{6,4},{7,5},{8,6},{9,7},{10,8},{11,9},{12,... | collective-permute-start | bytes 393224 | tf_op jit(solution)/shard_map/ppermute | solution.py:34
  51.0 2.5 %collective-permute-done.15 = bf16[256,512]{1,0:T(8,128)(2,1)S(1)} collective-permute-done((bf16[256,512]{1,0:T(8,128)(2,1)S(1)}, bf16[256,512]{1,0:T(8,128)(2,1)S(1)}, u32[]{:S(2)}, u32[]{:S(2)}) %collective-permute-start.15) | collective-permute-done | bytes 262176 | tf_op jit(solution)/shard_map/ppermute | solution.py:34
  53.8 0.8 %pad_maximum_fusion.1 = bf16[128,2048]{1,0:T(8,128)(2,1)} fusion(bf16[128,1024]{1,0:T(8,128)(2,1)S(1)} %get-tuple-element.56, bf16[128,1024]{1,0:T(8,128)(2,1)S(1)} %get-tuple-element.55), kind=kLoop, calls=%fused_computation.1 | loop fusion | flops 1048576 | bytes 1048576 | tf_op jit(solution)/shard_map/concatenate | solution.py:338
  55.1 0.7 %pad_maximum_fusion.3 = bf16[128,1024]{1,0:T(8,128)(2,1)} fusion(bf16[128,512]{1,0:T(8,128)(2,1)S(1)} %get-tuple-element.58, bf16[128,512]{1,0:T(8,128)(2,1)S(1)} %get-tuple-element.57), kind=kLoop, calls=%fused_computation.7 | loop fusion | flops 524288 | bytes 524288 | tf_op jit(solution)/shard_map/concatenate | solution.py:338
  55.8 1.3 %collective-permute-done.14 = bf16[128,512]{1,0:T(8,128)(2,1)S(1)} collective-permute-done((bf16[128,512]{1,0:T(8,128)(2,1)S(1)}, bf16[128,512]{1,0:T(8,128)(2,1)S(1)}, u32[]{:S(2)}, u32[]{:S(2)}) %collective-permute-start.14) | collective-permute-done | bytes 131104 | tf_op jit(solution)/shard_map/ppermute | solution.py:40
  57.2 3.2 %collective-permute-done.12 = bf16[128,512]{1,0:T(8,128)(2,1)S(1)} collective-permute-done((bf16[128,512]{1,0:T(8,128)(2,1)S(1)}, bf16[128,512]{1,0:T(8,128)(2,1)S(1)}, u32[]{:S(2)}, u32[]{:S(2)}) %collective-permute-start.12) | collective-permute-done | bytes 131104 | tf_op jit(solution)/shard_map/ppermute | solution.py:34
  (47 shorter events, 5.7 us)
Async XLA Ops:
  0.6 1.2 %copy-start.3 = (s32[128]{0:T(128)S(1)}, s32[128]{0:T(128)}, u32[]{:S(2)}) copy-start(s32[128]{0:T(128)} %param.9) | copy-start | bytes 1540
  0.7 1.2 %copy-start.2 = (bf16[128,1024]{1,0:T(8,128)(2,1)S(1)}, bf16[128,1024]{1,0:T(8,128)(2,1)}, u32[]{:S(2)}) copy-start(bf16[128,1024]{1,0:T(8,128)(2,1)} %param.6) | copy-start | bytes 786436
  0.7 2.5 %copy-start.1 = (bf16[128,2048]{1,0:T(8,128)(2,1)S(1)}, bf16[128,2048]{1,0:T(8,128)(2,1)}, u32[]{:S(2)}) copy-start(bf16[128,2048]{1,0:T(8,128)(2,1)} %go) | copy-start | bytes 1572868
  1.7 1.4 %copy-start = (bf16[128,2048]{1,0:T(8,128)(2,1)S(1)}, bf16[128,2048]{1,0:T(8,128)(2,1)}, u32[]{:S(2)}) copy-start(bf16[128,2048]{1,0:T(8,128)(2,1)} %q) | copy-start | bytes 1572868
  1.8 1.4 %collective-permute-start = (bf16[128,512]{1,0:T(8,128)(2,1)S(1)}, bf16[128,512]{1,0:T(8,128)(2,1)S(1)}, u32[]{:S(2)}, u32[]{:S(2)}) collective-permute-start(bf16[128,512]{1,0:T(8,128)(2,1)S(1)} %get-tuple-element.64), channel_id=1, source_target_pairs={{0,1},{1,0},{2,3},{3,2},{4,5},{5,4},{6,7},{7,6},{8,9},{9,8},{10,11... | collective-permute-start | bytes 393224 | tf_op jit(solution)/shard_map/ppermute | solution.py:28
  1.9 1.6 %collective-permute-start.3 = (bf16[136,512]{1,0:T(8,128)(2,1)S(1)}, bf16[136,512]{1,0:T(8,128)(2,1)S(1)}, u32[]{:S(2)}, u32[]{:S(2)}) collective-permute-start(bf16[136,512]{1,0:T(8,128)(2,1)S(1)} %fusion.1), channel_id=1, source_target_pairs={{0,1},{1,0},{2,3},{3,2},{4,5},{5,4},{6,7},{7,6},{8,9},{9,8},{10,11... | collective-permute-start | bytes 417800 | tf_op jit(solution)/shard_map/ppermute | solution.py:28
  3.3 13.5 %collective-permute-start.2 = (bf16[256,1024]{1,0:T(8,128)(2,1)S(1)}, bf16[256,1024]{1,0:T(8,128)(2,1)S(1)}, u32[]{:S(2)}, u32[]{:S(2)}) collective-permute-start(bf16[256,1024]{1,0:T(8,128)(2,1)S(1)} %pad_maximum_fusion), channel_id=1, source_target_pairs={{0,1},{1,0},{2,3},{3,2},{4,5},{5,4},{6,7},{7,6},{8,9},{9,8},{10,11... | collective-permute-start | bytes 1572872 | tf_op jit(solution)/shard_map/ppermute | solution.py:28
  3.5 11.2 %collective-permute-start.4 = (bf16[264,512]{1,0:T(8,128)(2,1)S(1)}, bf16[264,512]{1,0:T(8,128)(2,1)S(1)}, u32[]{:S(2)}, u32[]{:S(2)}) collective-permute-start(bf16[264,512]{1,0:T(8,128)(2,1)S(1)} %pad_maximum_fusion.2.kc), channel_id=1, source_target_pairs={{0,2},{1,3},{2,4},{3,5},{4,6},{5,7},{6,8},{7,9},{8,10},{9,11},{10,... | collective-permute-start | bytes 811016 | tf_op jit(solution)/shard_map/ppermute | solution.py:34
  6.7 13.8 %collective-permute-start.1 = (bf16[264,512]{1,0:T(8,128)(2,1)S(1)}, bf16[264,512]{1,0:T(8,128)(2,1)S(1)}, u32[]{:S(2)}, u32[]{:S(2)}) collective-permute-start(bf16[264,512]{1,0:T(8,128)(2,1)S(1)} %maximum_maximum_fusion.vc), channel_id=1, source_target_pairs={{0,2},{1,3},{2,4},{3,5},{4,6},{5,7},{6,8},{7,9},{8,10},{9,11},{10,... | collective-permute-start | bytes 811016 | tf_op jit(solution)/shard_map/ppermute | solution.py:34
  10.2 12.8 %collective-permute-start.6 = (bf16[264,512]{1,0:T(8,128)(2,1)S(1)}, bf16[264,512]{1,0:T(8,128)(2,1)S(1)}, u32[]{:S(2)}, u32[]{:S(2)}) collective-permute-start(bf16[264,512]{1,0:T(8,128)(2,1)S(1)} %pad_maximum_fusion.2.kc), channel_id=1, source_target_pairs={{4,8},{5,9},{12,16},{13,17},{20,24},{21,25}} | collective-permute-start | bytes 811016 | tf_op jit(solution)/shard_map/ppermute | solution.py:50
  14.7 11.6 %collective-permute-start.5 = (bf16[264,512]{1,0:T(8,128)(2,1)S(1)}, bf16[264,512]{1,0:T(8,128)(2,1)S(1)}, u32[]{:S(2)}, u32[]{:S(2)}) collective-permute-start(bf16[264,512]{1,0:T(8,128)(2,1)S(1)} %collective-permute-done.4.ka), channel_id=1, source_target_pairs={{0,2},{1,3},{2,4},{3,5},{4,6},{5,7},{8,10},{9,11},{10,12},{11,13},... | collective-permute-start | bytes 811016 | tf_op jit(solution)/shard_map/ppermute | solution.py:45
  16.0 14.5 %collective-permute-start.8 = (bf16[264,512]{1,0:T(8,128)(2,1)S(1)}, bf16[264,512]{1,0:T(8,128)(2,1)S(1)}, u32[]{:S(2)}, u32[]{:S(2)}) collective-permute-start(bf16[264,512]{1,0:T(8,128)(2,1)S(1)} %maximum_maximum_fusion.vc), channel_id=1, source_target_pairs={{4,8},{5,9},{12,16},{13,17},{20,24},{21,25}} | collective-permute-start | bytes 811016 | tf_op jit(solution)/shard_map/ppermute | solution.py:50
  20.5 11.0 %collective-permute-start.7 = (bf16[264,512]{1,0:T(8,128)(2,1)S(1)}, bf16[264,512]{1,0:T(8,128)(2,1)S(1)}, u32[]{:S(2)}, u32[]{:S(2)}) collective-permute-start(bf16[264,512]{1,0:T(8,128)(2,1)S(1)} %collective-permute-done.1.va), channel_id=1, source_target_pairs={{0,2},{1,3},{2,4},{3,5},{4,6},{5,7},{8,10},{9,11},{10,12},{11,13},... | collective-permute-start | bytes 811016 | tf_op jit(solution)/shard_map/ppermute | solution.py:45
  28.0 13.0 %collective-permute-start.9 = (bf16[256,512]{1,0:T(8,128)(2,1)S(1)}, bf16[256,512]{1,0:T(8,128)(2,1)S(1)}, u32[]{:S(2)}, u32[]{:S(2)}) collective-permute-start(bf16[256,512]{1,0:T(8,128)(2,1)S(1)} %get-tuple-element.45), channel_id=1, source_target_pairs={{2,0},{3,1},{4,2},{5,3},{6,4},{7,5},{8,6},{9,7},{10,8},{11,9},{12,... | collective-permute-start | bytes 786440 | tf_op jit(solution)/shard_map/ppermute | solution.py:34
  34.0 13.1 %collective-permute-start.11 = (bf16[256,512]{1,0:T(8,128)(2,1)S(1)}, bf16[256,512]{1,0:T(8,128)(2,1)S(1)}, u32[]{:S(2)}, u32[]{:S(2)}) collective-permute-start(bf16[256,512]{1,0:T(8,128)(2,1)S(1)} %get-tuple-element.49), channel_id=1, source_target_pairs={{2,0},{3,1},{4,2},{5,3},{6,4},{7,5},{8,6},{9,7},{10,8},{11,9},{12,... | collective-permute-start | bytes 786440 | tf_op jit(solution)/shard_map/ppermute | solution.py:34
  41.1 12.5 %collective-permute-start.15 = (bf16[256,512]{1,0:T(8,128)(2,1)S(1)}, bf16[256,512]{1,0:T(8,128)(2,1)S(1)}, u32[]{:S(2)}, u32[]{:S(2)}) collective-permute-start(bf16[256,512]{1,0:T(8,128)(2,1)S(1)} %merge.2), channel_id=1, source_target_pairs={{2,0},{3,1},{4,2},{5,3},{6,4},{7,5},{8,6},{9,7},{10,8},{11,9},{12,... | collective-permute-start | bytes 786440 | tf_op jit(solution)/shard_map/ppermute | solution.py:34
  43.9 13.2 %collective-permute-start.13 = (f32[128,512]{1,0:T(8,128)S(1)}, f32[128,512]{1,0:T(8,128)S(1)}, u32[]{:S(2)}, u32[]{:S(2)}) collective-permute-start(f32[128,512]{1,0:T(8,128)S(1)} %slice.30), channel_id=1, source_target_pairs={{0,1},{1,0},{2,3},{3,2},{4,5},{5,4},{6,7},{7,6},{8,9},{9,8},{10,11... | collective-permute-start | bytes 786440 | tf_op jit(solution)/shard_map/ppermute | solution.py:28
  44.0 9.7 %collective-permute-start.10 = (bf16[128,1024]{1,0:T(8,128)(2,1)S(1)}, bf16[128,1024]{1,0:T(8,128)(2,1)S(1)}, u32[]{:S(2)}, u32[]{:S(2)}) collective-permute-start(bf16[128,1024]{1,0:T(8,128)(2,1)S(1)} %get-tuple-element.46), channel_id=1, source_target_pairs={{0,1},{1,0},{2,3},{3,2},{4,5},{5,4},{6,7},{7,6},{8,9},{9,8},{10,11... | collective-permute-start | bytes 786440 | tf_op jit(solution)/shard_map/ppermute | solution.py:28
  47.2 10.0 %collective-permute-start.14 = (bf16[128,512]{1,0:T(8,128)(2,1)S(1)}, bf16[128,512]{1,0:T(8,128)(2,1)S(1)}, u32[]{:S(2)}, u32[]{:S(2)}) collective-permute-start(bf16[128,512]{1,0:T(8,128)(2,1)S(1)} %get-tuple-element.60), channel_id=1, source_target_pairs={{2,1},{3,0},{4,3},{5,2},{6,5},{7,4},{8,7},{9,6},{10,9},{11,8},{12,... | collective-permute-start | bytes 393224 | tf_op jit(solution)/shard_map/ppermute | solution.py:40
  49.1 11.3 %collective-permute-start.12 = (bf16[128,512]{1,0:T(8,128)(2,1)S(1)}, bf16[128,512]{1,0:T(8,128)(2,1)S(1)}, u32[]{:S(2)}, u32[]{:S(2)}) collective-permute-start(bf16[128,512]{1,0:T(8,128)(2,1)S(1)} %get-tuple-element.59), channel_id=1, source_target_pairs={{2,0},{3,1},{4,2},{5,3},{6,4},{7,5},{8,6},{9,7},{10,8},{11,9},{12,... | collective-permute-start | bytes 393224 | tf_op jit(solution)/shard_map/ppermute | solution.py:34
  53.7 1.4 %collective-permute-start.16 = (bf16[128,512]{1,0:T(8,128)(2,1)S(1)}, bf16[128,512]{1,0:T(8,128)(2,1)S(1)}, u32[]{:S(2)}, u32[]{:S(2)}) collective-permute-start(bf16[128,512]{1,0:T(8,128)(2,1)S(1)} %slice.39), channel_id=1, source_target_pairs={{0,1},{1,0},{2,3},{3,2},{4,5},{5,4},{6,7},{7,6},{8,9},{9,8},{10,11... | collective-permute-start | bytes 393224 | tf_op jit(solution)/shard_map/ppermute | solution.py:28

commit v7 on v6

--- a/solution.py
+++ b/solution.py
@@ -150,30 +150,47 @@
     lax.fori_loop(0, groups, step, 0, unroll=True)
 
 
+def in_turn(groups, products, weigh, finish):
+    units = [(g, h) for g in range(groups) for h in range(2)]
+    ready, waiting = products(*units[0]), None
+    for i, (g, h) in enumerate(units):
+        ahead_of = products(*units[i + 1]) if i + 1 < len(units) else None
+        held = weigh(g, h, ready)
+        if waiting is not None:
+            finish(*waiting)
+        ready, waiting = ahead_of, (g, h, held)
+    finish(*waiting)
+
+
 def far_values(tok, groups, core_ref, lo_ref, qs, gs, ka, kb, wk, tot, dvb, inv):
     core = core_ref[0]
     lo_all = lo_ref[...]
     count = seen(lo_all, ka, tok) + seen(lo_all, kb, tok) + seen(lo_all, wk, tok)
     los = [first_keys(core, lo_all, count, h, tok) for h in range(2)]
-
-    def step(g, _):
-        accs = []
-        for h in range(2):
-            s = dot(keys_of(core, ((kb, wk), ka), range(h, h + FAR), g, tok), qs[g, h], NT)
-            total = tot[g, pl.ds(8 * h, 8), :]
-            ws = []
-            for jj in range(FAR):
-                _, w = weights_of(cut(s, jj, tok), los[h], jj, False, tok)
-                total = total + fold(w)
-                ws.append(w)
-            one = 1.0 / jnp.sum(total, axis=0, keepdims=True)
-            inv[g, pl.ds(8 * h, 8), :] = jnp.broadcast_to(one, (8, 2 * tok))
-            low = jnp.concatenate([(w * one).astype(jnp.bfloat16) for w in ws[: FAR - h]], 0)
-            accs.append(dot(low, gs[g, h], NN))
-        spread(core, accs, 0, (dvb,), g, tok)
-        return 0
-
-    lax.fori_loop(0, groups, step, 0, unroll=True)
+    accs = {}
+
+    def products(g, h):
+        return dot(keys_of(core, ((kb, wk), ka), range(h, h + FAR), g, tok), qs[g, h], NT)
+
+    def weigh(g, h, s):
+        total = tot[g, pl.ds(8 * h, 8), :]
+        ws = []
+        for jj in range(FAR):
+            _, w = weights_of(cut(s, jj, tok), los[h], jj, False, tok)
+            total = total + fold(w)
+            ws.append(w)
+        return total, ws
+
+    def finish(g, h, held):
+        total, ws = held
+        one = 1.0 / jnp.sum(total, axis=0, keepdims=True)
+        inv[g, pl.ds(8 * h, 8), :] = jnp.broadcast_to(one, (8, 2 * tok))
+        low = jnp.concatenate([(w * one).astype(jnp.bfloat16) for w in ws[: FAR - h]], 0)
+        accs[h] = dot(low, gs[g, h], NN)
+        if h == 1:
+            spread(core, accs, 0, (dvb,), g, tok)
+
+    in_turn(groups, products, weigh, finish)
 
 
 def spread(core, accs, start, outs, g, tok):
@@ -194,27 +211,36 @@
     lo_all = lo_ref[...]
     count = seen(lo_all, ka, tok) + seen(lo_all, kb, tok) + seen(lo_all, wk, tok)
     los = [first_keys(core, lo_all, count, h, tok) for h in range(2)]
-
-    def step(g, _):
-        accs = []
-        for h in range(2):
-            s = dot(keys_of(core, ((kb, wk), ka), range(h, h + FAR), g, tok), qs[g, h], NT)
-            dp = dot(keys_of(core, ((vb, wv), va), range(h, h + FAR), g, tok), gs[g, h], NT)
-            one = inv[g, pl.ds(8 * h, 1), :]
-            total = term[g, pl.ds(8 * h, 8), :]
-            us = []
-            for jj in range(FAR):
-                t, w = weights_of(cut(s, jj, tok), los[h], jj, False, tok)
-                total = total + fold(w * cut(dp, jj, tok))
-                us.append(w * slope(t))
-            mean = one * jnp.sum(total, axis=0, keepdims=True)
-            row[g, pl.ds(8 * h, 8), :] = jnp.broadcast_to(mean, (8, 2 * tok))
-            low = [((us[jj] * one) * (cut(dp, jj, tok) - mean)).astype(jnp.bfloat16) for jj in range(FAR - h)]
-            accs.append(dot(jnp.concatenate(low, 0), qs[g, h], NN))
-        spread(core, accs, 0, (dkb,), g, tok)
-        return 0
-
-    lax.fori_loop(0, groups, step, 0, unroll=True)
+    accs = {}
+
+    def products(g, h):
+        blocks = range(h, h + FAR)
+        return (
+            dot(keys_of(core, ((kb, wk), ka), blocks, g, tok), qs[g, h], NT),
+            dot(keys_of(core, ((vb, wv), va), blocks, g, tok), gs[g, h], NT),
+        )
+
+    def weigh(g, h, ready):
+        s, dp = ready
+        total = term[g, pl.ds(8 * h, 8), :]
+        us = []
+        for jj in range(FAR):
+            t, w = weights_of(cut(s, jj, tok), los[h], jj, False, tok)
+            total = total + fold(w * cut(dp, jj, tok))
+            us.append(w * slope(t))
+        return total, us, dp
+
+    def finish(g, h, held):
+        total, us, dp = held
+        one = inv[g, pl.ds(8 * h, 1), :]
+        mean = one * jnp.sum(total, axis=0, keepdims=True)
+        row[g, pl.ds(8 * h, 8), :] = jnp.broadcast_to(mean, (8, 2 * tok))
+        low = [((us[jj] * one) * (cut(dp, jj, tok) - mean)).astype(jnp.bfloat16) for jj in range(FAR - h)]
+        accs[h] = dot(jnp.concatenate(low, 0), qs[g, h], NN)
+        if h == 1:
+            spread(core, accs, 0, (dkb,), g, tok)
+
+    in_turn(groups, products, weigh, finish)
 
 
 def near_grads(tok, groups, core_ref, lo_ref, qs, gs, kb, wk, ka, kc, vb, wv, va, vc, inv, row,
@@ -272,7 +298,7 @@
     )(*args)
 
 
-VMEM_LIMIT = 4 * 1024 * 1024
+VMEM_LIMIT = 16 * 1024 * 1024
 
 
 def local(queries, keys, values, grad_out, segment):

time: 61.6 us -> 60.8 us (0.987)
  Pallas kernels: 9.76 us -> 8.33 us
  waiting for transfers between devices: 22.5 us -> 23.6 us
    pallas_call x7, Pallas kernels: 9.76 us -> 8.33 us  [call(): pl.pallas_call(functools.partial(body, tok, groups), in_specs=[pl.BlockSp...]
  transfers between devices with their start and end apart: 17 -> 17, of which waited for: 10 -> 10; matrix products, arithmetic and copies ran while one was open for 3% -> 3% of each run, Pallas kernels for 16% -> 14%
where the time goes in v7:
time: 60.8 us; the launch traced here: 60.4 us
  waiting for transfers between devices  23.6 us (39%)
  starting transfers between devices  23.5 us (39%)
  Pallas kernels  8.33 us (14%)
  other arithmetic  2.72 us (4%)
  local copies, waits for them, and re-layouts  1.22 us (2%)
  between operations  1.01 us (2%)
    ppermute x6, starting transfers between devices, hop(): lax.ppermute(x, AXES, [(i, i + by) for i in range(n) if 0 <= i + by < n])  16.2 us
    ppermute x6, waiting for transfers between devices, hop(): lax.ppermute(x, AXES, [(i, i + by) for i in range(n) if 0 <= i + by < n])  16.1 us
    pallas_call x7, Pallas kernels, call(): pl.pallas_call(functools.partial(body, tok, groups), in_specs=[pl.BlockSp...  8.33 us
    ppermute x2, waiting for transfers between devices, forward(): lax.ppermute(x, AXES, [(i, i + 2) for i in range(n) if i % row < row - 2])  4.98 us
    ppermute x2, starting transfers between devices, forward(): lax.ppermute(x, AXES, [(i, i + 2) for i in range(n) if i % row < row - 2])  2.56 us
    concatenate x3, other arithmetic, place(): return jnp.concatenate([first, second], 1)  2.29 us
    ppermute x1, starting transfers between devices, cross(): lax.ppermute(x, AXES, [(i, (i ^ 1) + by) for i in range(n) if 0 <= i + by...  1.92 us
    ppermute x6, starting transfers between devices, swap(): return lax.ppermute(x, AXES, [(i, i ^ 1) for i in range(n)])  1.46 us
  transfers between devices with their start and end apart: 17, of which 10 were waited for; matrix products, arithmetic and copies ran while one was open for 3% of the time, Pallas kernels for 14%

profile of v7, /device:TPU:26, one launch (start us, length us, event | category | flops | bytes accessed | tf_op | source)
XLA Modules:
  0.0 60.4 jit_solution(8499369110453529187)
XLA Ops:
  0.7 1.1 %constant_dynamic-slice_fusion.5 = (bf16[128,512]{1,0:T(8,128)(2,1)S(1)}, bf16[128,512]{1,0:T(8,128)(2,1)S(1)}) fusion(bf16[128,1024]{1,0:T(8,128)(2,1)} %param.7, s32[]{:T(128)S(6)} %select_n.45, s32[]{:T(128)S(6)} %select_n.46), kind=kLoop, calls=%fused_computation.24 | loop fusion | bytes 524296 | tf_op jit(solution)/shard_map/dynamic_slice | solution.py:315
  3.5 3.1 %collective-permute-start.4 = (bf16[264,512]{1,0:T(8,128)(2,1)S(1)}, bf16[264,512]{1,0:T(8,128)(2,1)S(1)}, u32[]{:S(2)}, u32[]{:S(2)}) collective-permute-start(bf16[264,512]{1,0:T(8,128)(2,1)S(1)} %pad_maximum_fusion.2.kc), channel_id=1, source_target_pairs={{0,2},{1,3},{2,4},{3,5},{4,6},{5,7},{6,8},{7,9},{8,10},{9,11},{10,... | collective-permute-start | bytes 811016 | tf_op jit(solution)/shard_map/ppermute | solution.py:34
  6.7 3.5 %collective-permute-start.1 = (bf16[264,512]{1,0:T(8,128)(2,1)S(1)}, bf16[264,512]{1,0:T(8,128)(2,1)S(1)}, u32[]{:S(2)}, u32[]{:S(2)}) collective-permute-start(bf16[264,512]{1,0:T(8,128)(2,1)S(1)} %maximum_maximum_fusion.vc), channel_id=1, source_target_pairs={{0,2},{1,3},{2,4},{3,5},{4,6},{5,7},{6,8},{7,9},{8,10},{9,11},{10,... | collective-permute-start | bytes 811016 | tf_op jit(solution)/shard_map/ppermute | solution.py:34
  10.9 3.8 %collective-permute-done.4.ka = bf16[264,512]{1,0:T(8,128)(2,1)S(1)} collective-permute-done((bf16[264,512]{1,0:T(8,128)(2,1)S(1)}, bf16[264,512]{1,0:T(8,128)(2,1)S(1)}, u32[]{:S(2)}, u32[]{:S(2)}) %collective-permute-start.4) | collective-permute-done | bytes 270368 | tf_op jit(solution)/shard_map/ppermute | solution.py:34
  14.7 1.3 %collective-permute-start.5 = (bf16[264,512]{1,0:T(8,128)(2,1)S(1)}, bf16[264,512]{1,0:T(8,128)(2,1)S(1)}, u32[]{:S(2)}, u32[]{:S(2)}) collective-permute-start(bf16[264,512]{1,0:T(8,128)(2,1)S(1)} %collective-permute-done.4.ka), channel_id=1, source_target_pairs={{0,2},{1,3},{2,4},{3,5},{4,6},{5,7},{8,10},{9,11},{10,12},{11,13},... | collective-permute-start | bytes 811016 | tf_op jit(solution)/shard_map/ppermute | solution.py:45
  17.1 3.4 %collective-permute-done.1.va = bf16[264,512]{1,0:T(8,128)(2,1)S(1)} collective-permute-done((bf16[264,512]{1,0:T(8,128)(2,1)S(1)}, bf16[264,512]{1,0:T(8,128)(2,1)S(1)}, u32[]{:S(2)}, u32[]{:S(2)}) %collective-permute-start.1) | collective-permute-done | bytes 270368 | tf_op jit(solution)/shard_map/ppermute | solution.py:34
  20.5 1.3 %collective-permute-start.7 = (bf16[264,512]{1,0:T(8,128)(2,1)S(1)}, bf16[264,512]{1,0:T(8,128)(2,1)S(1)}, u32[]{:S(2)}, u32[]{:S(2)}) collective-permute-start(bf16[264,512]{1,0:T(8,128)(2,1)S(1)} %collective-permute-done.1.va), channel_id=1, source_target_pairs={{0,2},{1,3},{2,4},{3,5},{4,6},{5,7},{8,10},{9,11},{10,12},{11,13},... | collective-permute-start | bytes 811016 | tf_op jit(solution)/shard_map/ppermute | solution.py:45
  21.8 1.1 %near_sums.1 = (f32[4,16,256]{2,1,0:T(8,128)S(1)}, f32[4,16,256]{2,1,0:T(8,128)S(1)}) custom-call(s32[1]{0:T(128)} %bitcast.core_ref, s32[8,128]{1,0:T(8,128)S(1)} %get-tuple-element.33.lo_ref, bf16[4,2,256,128]{3,2,1,0:T(8,128)(2,1)S(1)} %get-tuple-element.34.qs, bf16[4,2,256,128]{3,2,1,0:T(8,128)(2,1)S(1)} %get-tuple-element.35.gs, ...), custom_call_target="tpu_custom_call" | custom-call | tf_op jit(solution)/shard_map/near_sums/pallas_call | solution.py:290
  23.0 3.4 %collective-permute-done.5.kb = bf16[264,512]{1,0:T(8,128)(2,1)S(1)} collective-permute-done((bf16[264,512]{1,0:T(8,128)(2,1)S(1)}, bf16[264,512]{1,0:T(8,128)(2,1)S(1)}, u32[]{:S(2)}, u32[]{:S(2)}) %collective-permute-start.5) | collective-permute-done | bytes 270368 | tf_op jit(solution)/shard_map/ppermute | solution.py:45
  26.3 1.1 %far_values.1 = (bf16[256,512]{1,0:T(8,128)(2,1)S(1)}, f32[4,16,256]{2,1,0:T(8,128)S(1)}) custom-call(s32[1]{0:T(128)} %bitcast.core_ref, s32[8,128]{1,0:T(8,128)S(1)} %get-tuple-element.33.lo_ref, bf16[4,2,256,128]{3,2,1,0:T(8,128)(2,1)S(1)} %get-tuple-element.34.qs, bf16[4,2,256,128]{3,2,1,0:T(8,128)(2,1)S(1)} %get-tuple-element.35.gs, ...), custom_call_target="tpu_custom_call" | custom-call | tf_op jit(solution)/shard_map/far_values/pallas_call | solution.py:290
  27.5 2.5 %collective-permute-start.9 = (bf16[256,512]{1,0:T(8,128)(2,1)S(1)}, bf16[256,512]{1,0:T(8,128)(2,1)S(1)}, u32[]{:S(2)}, u32[]{:S(2)}) collective-permute-start(bf16[256,512]{1,0:T(8,128)(2,1)S(1)} %get-tuple-element.45), channel_id=1, source_target_pairs={{2,0},{3,1},{4,2},{5,3},{6,4},{7,5},{8,6},{9,7},{10,8},{11,9},{12,... | collective-permute-start | bytes 786440 | tf_op jit(solution)/shard_map/ppermute | solution.py:34
  29.9 1.6 %collective-permute-done.7.vb = bf16[264,512]{1,0:T(8,128)(2,1)S(1)} collective-permute-done((bf16[264,512]{1,0:T(8,128)(2,1)S(1)}, bf16[264,512]{1,0:T(8,128)(2,1)S(1)}, u32[]{:S(2)}, u32[]{:S(2)}) %collective-permute-start.7) | collective-permute-done | bytes 270368 | tf_op jit(solution)/shard_map/ppermute | solution.py:45
  31.6 1.6 %far_keys.1 = (bf16[256,512]{1,0:T(8,128)(2,1)S(1)}, f32[4,16,256]{2,1,0:T(8,128)S(1)}) custom-call(s32[1]{0:T(128)} %bitcast.core_ref, s32[8,128]{1,0:T(8,128)S(1)} %get-tuple-element.33.lo_ref, bf16[4,2,256,128]{3,2,1,0:T(8,128)(2,1)S(1)} %get-tuple-element.34.qs, bf16[4,2,256,128]{3,2,1,0:T(8,128)(2,1)S(1)} %get-tuple-element.35.gs, ...), custom_call_target="tpu_custom_call" | custom-call | tf_op jit(solution)/shard_map/far_keys/pallas_call | solution.py:290
  33.2 3.1 %collective-permute-start.11 = (bf16[256,512]{1,0:T(8,128)(2,1)S(1)}, bf16[256,512]{1,0:T(8,128)(2,1)S(1)}, u32[]{:S(2)}, u32[]{:S(2)}) collective-permute-start(bf16[256,512]{1,0:T(8,128)(2,1)S(1)} %get-tuple-element.49), channel_id=1, source_target_pairs={{2,0},{3,1},{4,2},{5,3},{6,4},{7,5},{8,6},{9,7},{10,8},{11,9},{12,... | collective-permute-start | bytes 786440 | tf_op jit(solution)/shard_map/ppermute | solution.py:34
  36.2 4.0 %near_grads.1 = (f32[256,512]{1,0:T(8,128)S(1)}, f32[256,512]{1,0:T(8,128)S(1)}, f32[256,512]{1,0:T(8,128)S(1)}, f32[256,512]{1,0:T(8,128)S(1)}, bf16[128,1024]{...) custom-call(s32[1]{0:T(128)} %bitcast.core_ref, s32[8,128]{1,0:T(8,128)S(1)} %get-tuple-element.33.lo_ref, ...), custom_call_target="tpu_custom_call" | custom-call | tf_op jit(solution)/shard_map/near_grads/pallas_call | solution.py:290
  40.3 2.2 %collective-permute-start.15 = (bf16[256,512]{1,0:T(8,128)(2,1)S(1)}, bf16[256,512]{1,0:T(8,128)(2,1)S(1)}, u32[]{:S(2)}, u32[]{:S(2)}) collective-permute-start(bf16[256,512]{1,0:T(8,128)(2,1)S(1)} %merge.2), channel_id=1, source_target_pairs={{2,0},{3,1},{4,2},{5,3},{6,4},{7,5},{8,6},{9,7},{10,8},{11,9},{12,... | collective-permute-start | bytes 786440 | tf_op jit(solution)/shard_map/ppermute | solution.py:34
  43.1 3.2 %collective-permute-done.11.came = bf16[256,512]{1,0:T(8,128)(2,1)S(1)} collective-permute-done((bf16[256,512]{1,0:T(8,128)(2,1)S(1)}, bf16[256,512]{1,0:T(8,128)(2,1)S(1)}, u32[]{:S(2)}, u32[]{:S(2)}) %collective-permute-start.11) | collective-permute-done | bytes 262176 | tf_op jit(solution)/shard_map/ppermute | solution.py:34
  46.4 1.9 %collective-permute-start.14 = (bf16[128,512]{1,0:T(8,128)(2,1)S(1)}, bf16[128,512]{1,0:T(8,128)(2,1)S(1)}, u32[]{:S(2)}, u32[]{:S(2)}) collective-permute-start(bf16[128,512]{1,0:T(8,128)(2,1)S(1)} %get-tuple-element.60), channel_id=1, source_target_pairs={{2,1},{3,0},{4,3},{5,2},{6,5},{7,4},{8,7},{9,6},{10,9},{11,8},{12,... | collective-permute-start | bytes 393224 | tf_op jit(solution)/shard_map/ppermute | solution.py:40
  48.3 1.9 %collective-permute-start.12 = (bf16[128,512]{1,0:T(8,128)(2,1)S(1)}, bf16[128,512]{1,0:T(8,128)(2,1)S(1)}, u32[]{:S(2)}, u32[]{:S(2)}) collective-permute-start(bf16[128,512]{1,0:T(8,128)(2,1)S(1)} %get-tuple-element.59), channel_id=1, source_target_pairs={{2,0},{3,1},{4,2},{5,3},{6,4},{7,5},{8,6},{9,7},{10,8},{11,9},{12,... | collective-permute-start | bytes 393224 | tf_op jit(solution)/shard_map/ppermute | solution.py:34
  50.2 2.5 %collective-permute-done.15 = bf16[256,512]{1,0:T(8,128)(2,1)S(1)} collective-permute-done((bf16[256,512]{1,0:T(8,128)(2,1)S(1)}, bf16[256,512]{1,0:T(8,128)(2,1)S(1)}, u32[]{:S(2)}, u32[]{:S(2)}) %collective-permute-start.15) | collective-permute-done | bytes 262176 | tf_op jit(solution)/shard_map/ppermute | solution.py:34
  52.9 0.8 %pad_maximum_fusion.1 = bf16[128,2048]{1,0:T(8,128)(2,1)} fusion(bf16[128,1024]{1,0:T(8,128)(2,1)S(1)} %get-tuple-element.56, bf16[128,1024]{1,0:T(8,128)(2,1)S(1)} %get-tuple-element.55), kind=kLoop, calls=%fused_computation.1 | loop fusion | flops 1048576 | bytes 1048576 | tf_op jit(solution)/shard_map/concatenate | solution.py:364
  55.0 1.4 %collective-permute-done.14 = bf16[128,512]{1,0:T(8,128)(2,1)S(1)} collective-permute-done((bf16[128,512]{1,0:T(8,128)(2,1)S(1)}, bf16[128,512]{1,0:T(8,128)(2,1)S(1)}, u32[]{:S(2)}, u32[]{:S(2)}) %collective-permute-start.14) | collective-permute-done | bytes 131104 | tf_op jit(solution)/shard_map/ppermute | solution.py:40
  56.3 3.2 %collective-permute-done.12 = bf16[128,512]{1,0:T(8,128)(2,1)S(1)} collective-permute-done((bf16[128,512]{1,0:T(8,128)(2,1)S(1)}, bf16[128,512]{1,0:T(8,128)(2,1)S(1)}, u32[]{:S(2)}, u32[]{:S(2)}) %collective-permute-start.12) | collective-permute-done | bytes 131104 | tf_op jit(solution)/shard_map/ppermute | solution.py:34
  59.7 0.7 %pad_maximum_fusion.4 = bf16[128,1024]{1,0:T(8,128)(2,1)} fusion(bf16[128,512]{1,0:T(8,128)(2,1)S(1)} %get-tuple-element.54, bf16[128,512]{1,0:T(8,128)(2,1)S(1)} %get-tuple-element.53), kind=kLoop, calls=%fused_computation.8 | loop fusion | flops 524288 | bytes 524288 | tf_op jit(solution)/shard_map/concatenate | solution.py:364
  (47 shorter events, 5.8 us)
Async XLA Ops:
  0.6 1.2 %copy-start.3 = (s32[128]{0:T(128)S(1)}, s32[128]{0:T(128)}, u32[]{:S(2)}) copy-start(s32[128]{0:T(128)} %param.9) | copy-start | bytes 1540
  0.7 1.2 %copy-start.2 = (bf16[128,1024]{1,0:T(8,128)(2,1)S(1)}, bf16[128,1024]{1,0:T(8,128)(2,1)}, u32[]{:S(2)}) copy-start(bf16[128,1024]{1,0:T(8,128)(2,1)} %param.6) | copy-start | bytes 786436
  0.7 2.5 %copy-start.1 = (bf16[128,2048]{1,0:T(8,128)(2,1)S(1)}, bf16[128,2048]{1,0:T(8,128)(2,1)}, u32[]{:S(2)}) copy-start(bf16[128,2048]{1,0:T(8,128)(2,1)} %go) | copy-start | bytes 1572868
  1.7 1.4 %copy-start = (bf16[128,2048]{1,0:T(8,128)(2,1)S(1)}, bf16[128,2048]{1,0:T(8,128)(2,1)}, u32[]{:S(2)}) copy-start(bf16[128,2048]{1,0:T(8,128)(2,1)} %q) | copy-start | bytes 1572868
  1.8 1.4 %collective-permute-start = (bf16[128,512]{1,0:T(8,128)(2,1)S(1)}, bf16[128,512]{1,0:T(8,128)(2,1)S(1)}, u32[]{:S(2)}, u32[]{:S(2)}) collective-permute-start(bf16[128,512]{1,0:T(8,128)(2,1)S(1)} %get-tuple-element.64), channel_id=1, source_target_pairs={{0,1},{1,0},{2,3},{3,2},{4,5},{5,4},{6,7},{7,6},{8,9},{9,8},{10,11... | collective-permute-start | bytes 393224 | tf_op jit(solution)/shard_map/ppermute | solution.py:28
  1.9 1.6 %collective-permute-start.3 = (bf16[136,512]{1,0:T(8,128)(2,1)S(1)}, bf16[136,512]{1,0:T(8,128)(2,1)S(1)}, u32[]{:S(2)}, u32[]{:S(2)}) collective-permute-start(bf16[136,512]{1,0:T(8,128)(2,1)S(1)} %fusion.1), channel_id=1, source_target_pairs={{0,1},{1,0},{2,3},{3,2},{4,5},{5,4},{6,7},{7,6},{8,9},{9,8},{10,11... | collective-permute-start | bytes 417800 | tf_op jit(solution)/shard_map/ppermute | solution.py:28
  3.3 13.5 %collective-permute-start.2 = (bf16[256,1024]{1,0:T(8,128)(2,1)S(1)}, bf16[256,1024]{1,0:T(8,128)(2,1)S(1)}, u32[]{:S(2)}, u32[]{:S(2)}) collective-permute-start(bf16[256,1024]{1,0:T(8,128)(2,1)S(1)} %pad_maximum_fusion), channel_id=1, source_target_pairs={{0,1},{1,0},{2,3},{3,2},{4,5},{5,4},{6,7},{7,6},{8,9},{9,8},{10,11... | collective-permute-start | bytes 1572872 | tf_op jit(solution)/shard_map/ppermute | solution.py:28
  3.5 11.2 %collective-permute-start.4 = (bf16[264,512]{1,0:T(8,128)(2,1)S(1)}, bf16[264,512]{1,0:T(8,128)(2,1)S(1)}, u32[]{:S(2)}, u32[]{:S(2)}) collective-permute-start(bf16[264,512]{1,0:T(8,128)(2,1)S(1)} %pad_maximum_fusion.2.kc), channel_id=1, source_target_pairs={{0,2},{1,3},{2,4},{3,5},{4,6},{5,7},{6,8},{7,9},{8,10},{9,11},{10,... | collective-permute-start | bytes 811016 | tf_op jit(solution)/shard_map/ppermute | solution.py:34
  6.7 13.8 %collective-permute-start.1 = (bf16[264,512]{1,0:T(8,128)(2,1)S(1)}, bf16[264,512]{1,0:T(8,128)(2,1)S(1)}, u32[]{:S(2)}, u32[]{:S(2)}) collective-permute-start(bf16[264,512]{1,0:T(8,128)(2,1)S(1)} %maximum_maximum_fusion.vc), channel_id=1, source_target_pairs={{0,2},{1,3},{2,4},{3,5},{4,6},{5,7},{6,8},{7,9},{8,10},{9,11},{10,... | collective-permute-start | bytes 811016 | tf_op jit(solution)/shard_map/ppermute | solution.py:34
  10.2 12.7 %collective-permute-start.6 = (bf16[264,512]{1,0:T(8,128)(2,1)S(1)}, bf16[264,512]{1,0:T(8,128)(2,1)S(1)}, u32[]{:S(2)}, u32[]{:S(2)}) collective-permute-start(bf16[264,512]{1,0:T(8,128)(2,1)S(1)} %pad_maximum_fusion.2.kc), channel_id=1, source_target_pairs={{4,8},{5,9},{12,16},{13,17},{20,24},{21,25}} | collective-permute-start | bytes 811016 | tf_op jit(solution)/shard_map/ppermute | solution.py:50
  14.7 11.6 %collective-permute-start.5 = (bf16[264,512]{1,0:T(8,128)(2,1)S(1)}, bf16[264,512]{1,0:T(8,128)(2,1)S(1)}, u32[]{:S(2)}, u32[]{:S(2)}) collective-permute-start(bf16[264,512]{1,0:T(8,128)(2,1)S(1)} %collective-permute-done.4.ka), channel_id=1, source_target_pairs={{0,2},{1,3},{2,4},{3,5},{4,6},{5,7},{8,10},{9,11},{10,12},{11,13},... | collective-permute-start | bytes 811016 | tf_op jit(solution)/shard_map/ppermute | solution.py:45
  16.0 13.9 %collective-permute-start.8 = (bf16[264,512]{1,0:T(8,128)(2,1)S(1)}, bf16[264,512]{1,0:T(8,128)(2,1)S(1)}, u32[]{:S(2)}, u32[]{:S(2)}) collective-permute-start(bf16[264,512]{1,0:T(8,128)(2,1)S(1)} %maximum_maximum_fusion.vc), channel_id=1, source_target_pairs={{4,8},{5,9},{12,16},{13,17},{20,24},{21,25}} | collective-permute-start | bytes 811016 | tf_op jit(solution)/shard_map/ppermute | solution.py:50
  20.5 11.0 %collective-permute-start.7 = (bf16[264,512]{1,0:T(8,128)(2,1)S(1)}, bf16[264,512]{1,0:T(8,128)(2,1)S(1)}, u32[]{:S(2)}, u32[]{:S(2)}) collective-permute-start(bf16[264,512]{1,0:T(8,128)(2,1)S(1)} %collective-permute-done.1.va), channel_id=1, source_target_pairs={{0,2},{1,3},{2,4},{3,5},{4,6},{5,7},{8,10},{9,11},{10,12},{11,13},... | collective-permute-start | bytes 811016 | tf_op jit(solution)/shard_map/ppermute | solution.py:45
  27.5 12.7 %collective-permute-start.9 = (bf16[256,512]{1,0:T(8,128)(2,1)S(1)}, bf16[256,512]{1,0:T(8,128)(2,1)S(1)}, u32[]{:S(2)}, u32[]{:S(2)}) collective-permute-start(bf16[256,512]{1,0:T(8,128)(2,1)S(1)} %get-tuple-element.45), channel_id=1, source_target_pairs={{2,0},{3,1},{4,2},{5,3},{6,4},{7,5},{8,6},{9,7},{10,8},{11,9},{12,... | collective-permute-start | bytes 786440 | tf_op jit(solution)/shard_map/ppermute | solution.py:34
  33.2 13.1 %collective-permute-start.11 = (bf16[256,512]{1,0:T(8,128)(2,1)S(1)}, bf16[256,512]{1,0:T(8,128)(2,1)S(1)}, u32[]{:S(2)}, u32[]{:S(2)}) collective-permute-start(bf16[256,512]{1,0:T(8,128)(2,1)S(1)} %get-tuple-element.49), channel_id=1, source_target_pairs={{2,0},{3,1},{4,2},{5,3},{6,4},{7,5},{8,6},{9,7},{10,8},{11,9},{12,... | collective-permute-start | bytes 786440 | tf_op jit(solution)/shard_map/ppermute | solution.py:34
  40.3 12.4 %collective-permute-start.15 = (bf16[256,512]{1,0:T(8,128)(2,1)S(1)}, bf16[256,512]{1,0:T(8,128)(2,1)S(1)}, u32[]{:S(2)}, u32[]{:S(2)}) collective-permute-start(bf16[256,512]{1,0:T(8,128)(2,1)S(1)} %merge.2), channel_id=1, source_target_pairs={{2,0},{3,1},{4,2},{5,3},{6,4},{7,5},{8,6},{9,7},{10,8},{11,9},{12,... | collective-permute-start | bytes 786440 | tf_op jit(solution)/shard_map/ppermute | solution.py:34
  42.5 13.8 %collective-permute-start.13 = (f32[128,512]{1,0:T(8,128)S(1)}, f32[128,512]{1,0:T(8,128)S(1)}, u32[]{:S(2)}, u32[]{:S(2)}) collective-permute-start(f32[128,512]{1,0:T(8,128)S(1)} %slice.30), channel_id=1, source_target_pairs={{0,1},{1,0},{2,3},{3,2},{4,5},{5,4},{6,7},{7,6},{8,9},{9,8},{10,11... | collective-permute-start | bytes 786440 | tf_op jit(solution)/shard_map/ppermute | solution.py:28
  42.6 10.3 %collective-permute-start.10 = (bf16[128,1024]{1,0:T(8,128)(2,1)S(1)}, bf16[128,1024]{1,0:T(8,128)(2,1)S(1)}, u32[]{:S(2)}, u32[]{:S(2)}) collective-permute-start(bf16[128,1024]{1,0:T(8,128)(2,1)S(1)} %get-tuple-element.46), channel_id=1, source_target_pairs={{0,1},{1,0},{2,3},{3,2},{4,5},{5,4},{6,7},{7,6},{8,9},{9,8},{10,11... | collective-permute-start | bytes 786440 | tf_op jit(solution)/shard_map/ppermute | solution.py:28
  46.4 10.0 %collective-permute-start.14 = (bf16[128,512]{1,0:T(8,128)(2,1)S(1)}, bf16[128,512]{1,0:T(8,128)(2,1)S(1)}, u32[]{:S(2)}, u32[]{:S(2)}) collective-permute-start(bf16[128,512]{1,0:T(8,128)(2,1)S(1)} %get-tuple-element.60), channel_id=1, source_target_pairs={{2,1},{3,0},{4,3},{5,2},{6,5},{7,4},{8,7},{9,6},{10,9},{11,8},{12,... | collective-permute-start | bytes 393224 | tf_op jit(solution)/shard_map/ppermute | solution.py:40
  48.3 11.3 %collective-permute-start.12 = (bf16[128,512]{1,0:T(8,128)(2,1)S(1)}, bf16[128,512]{1,0:T(8,128)(2,1)S(1)}, u32[]{:S(2)}, u32[]{:S(2)}) collective-permute-start(bf16[128,512]{1,0:T(8,128)(2,1)S(1)} %get-tuple-element.59), channel_id=1, source_target_pairs={{2,0},{3,1},{4,2},{5,3},{6,4},{7,5},{8,6},{9,7},{10,8},{11,9},{12,... | collective-permute-start | bytes 393224 | tf_op jit(solution)/shard_map/ppermute | solution.py:34
  52.8 1.4 %collective-permute-start.16 = (bf16[128,512]{1,0:T(8,128)(2,1)S(1)}, bf16[128,512]{1,0:T(8,128)(2,1)S(1)}, u32[]{:S(2)}, u32[]{:S(2)}) collective-permute-start(bf16[128,512]{1,0:T(8,128)(2,1)S(1)} %slice.39), channel_id=1, source_target_pairs={{0,1},{1,0},{2,3},{3,2},{4,5},{5,4},{6,7},{7,6},{8,9},{9,8},{10,11... | collective-permute-start | bytes 393224 | tf_op jit(solution)/shard_map/ppermute | solution.py:28

commit v8 on v7

--- a/solution.py
+++ b/solution.py
@@ -314,16 +314,16 @@
     def part(x, which, width):
         return lax.dynamic_slice(x, (0, which * width), (x.shape[0], width))
 
-    seg_own = (segment + 1).astype(bf16)[None, :]
-    seg_row = jnp.pad(seg_own, ((0, SEG_ROWS - 1), (tok, half - 2 * tok)))
-    own_row = jnp.pad(seg_own, ((0, SEG_ROWS - 1), (0, half - tok)))
-    k_in = swap(jnp.concatenate([part(keys, 1 - core, half), seg_row], 0))
-    kc = jnp.concatenate([part(keys, core, half), k_in[:tok], k_in[tok:] + own_row], 0)
-    v_in = swap(part(values, 1 - core, half))
-    vc = jnp.concatenate([part(values, core, half), v_in, jnp.zeros((SEG_ROWS, half), bf16)], 0)
+    k_in = swap(keys)
+    seg_in = swap(segment)
+    ids = jnp.concatenate([segment, seg_in]) + 1
+    seg_rows = jnp.pad(ids.astype(bf16)[None, :], ((0, SEG_ROWS - 1), (0, half - 2 * tok)))
+    kc = jnp.concatenate([part(keys, core, half), part(k_in, core, half), seg_rows], 0)
+    v_in = swap(values)
+    vc = jnp.concatenate([part(values, core, half), part(v_in, core, half), jnp.zeros((SEG_ROWS, half), bf16)], 0)
     ka = hop(kc, 1)
     va = hop(vc, 1)
-    queries, grad_out, _ = lax.optimization_barrier((queries, grad_out, v_in))
+    queries, grad_out, _ = lax.optimization_barrier((queries, grad_out, kc))
     qg_in = swap(jnp.concatenate([part(queries, 1 - core, q_half), part(grad_out, 1 - core, q_half)], 0))
 
     rows = ((groups, 2, 2 * tok, HEAD_DIM), bf16)

time: 60.8 us -> 59.9 us (0.985)
  waiting for transfers between devices: 23.6 us -> 22.9 us
    ppermute x6 -> x7, starting transfers between devices: 1.46 us -> 1.39 us  [swap(): return lax.ppermute(x, AXES, [(i, i ^ 1) for i in range(n)])]
  transfers between devices with their start and end apart: 17 -> 18, of which waited for: 10 -> 10; matrix products, arithmetic and copies ran while one was open for 3% -> 5% of each run, Pallas kernels for 14% -> 14%
where the time goes in v8:
time: 59.9 us; the launch traced here: 59.5 us
  starting transfers between devices  23.4 us (39%)
  waiting for transfers between devices  22.9 us (38%)
  Pallas kernels  8.32 us (14%)
  other arithmetic  2.7 us (5%)
  local copies, waits for them, and re-layouts  1.1 us (2%)
  between operations  1.01 us (2%)
    ppermute x6, starting transfers between devices, hop(): lax.ppermute(x, AXES, [(i, i + by) for i in range(n) if 0 <= i + by < n])  16.2 us
    ppermute x6, waiting for transfers between devices, hop(): lax.ppermute(x, AXES, [(i, i + by) for i in range(n) if 0 <= i + by < n])  15.9 us
    pallas_call x7, Pallas kernels, call(): pl.pallas_call(functools.partial(body, tok, groups), in_specs=[pl.BlockSp...  8.32 us
    ppermute x2, waiting for transfers between devices, forward(): lax.ppermute(x, AXES, [(i, i + 2) for i in range(n) if i % row < row - 2])  5.02 us
    ppermute x2, starting transfers between devices, forward(): lax.ppermute(x, AXES, [(i, i + 2) for i in range(n) if i % row < row - 2])  2.56 us
    concatenate x3, other arithmetic, place(): return jnp.concatenate([first, second], 1)  2.29 us
    ppermute x1, starting transfers between devices, cross(): lax.ppermute(x, AXES, [(i, (i ^ 1) + by) for i in range(n) if 0 <= i + by...  1.92 us
    ppermute x1, waiting for transfers between devices, cross(): lax.ppermute(x, AXES, [(i, (i ^ 1) + by) for i in range(n) if 0 <= i + by...  1.4 us
  transfers between devices with their start and end apart: 18, of which 10 were waited for; matrix products, arithmetic and copies ran while one was open for 5% of the time, Pallas kernels for 14%

profile of v8, /device:TPU:26, one launch (start us, length us, event | category | flops | bytes accessed | tf_op | source)
XLA Modules:
  0.0 59.5 jit_solution(14123796548871432465)
XLA Ops:
  1.3 0.9 %constant_dynamic-slice_fusion.3 = bf16[128,512]{1,0:T(8,128)(2,1)S(1)} fusion(bf16[128,1024]{1,0:T(8,128)(2,1)} %param.6, s32[]{:T(128)S(6)} %select_n.43), kind=kLoop, calls=%fused_computation.20 | loop fusion | bytes 262148 | tf_op jit(solution)/shard_map/dynamic_slice | solution.py:315
  2.5 3.2 %collective-permute-start.5 = (bf16[264,512]{1,0:T(8,128)(2,1)S(1)}, bf16[264,512]{1,0:T(8,128)(2,1)S(1)}, u32[]{:S(2)}, u32[]{:S(2)}) collective-permute-start(bf16[264,512]{1,0:T(8,128)(2,1)S(1)} %fusion.1.kc), channel_id=1, source_target_pairs={{0,2},{1,3},{2,4},{3,5},{4,6},{5,7},{6,8},{7,9},{8,10},{9,11},{10,... | collective-permute-start | bytes 811016 | tf_op jit(solution)/shard_map/ppermute | solution.py:34
  6.1 3.5 %collective-permute-start.1 = (bf16[264,512]{1,0:T(8,128)(2,1)S(1)}, bf16[264,512]{1,0:T(8,128)(2,1)S(1)}, u32[]{:S(2)}, u32[]{:S(2)}) collective-permute-start(bf16[264,512]{1,0:T(8,128)(2,1)S(1)} %maximum_maximum_fusion.vc), channel_id=1, source_target_pairs={{0,2},{1,3},{2,4},{3,5},{4,6},{5,7},{6,8},{7,9},{8,10},{9,11},{10,... | collective-permute-start | bytes 811016 | tf_op jit(solution)/shard_map/ppermute | solution.py:34
  10.3 3.6 %collective-permute-done.5.ka = bf16[264,512]{1,0:T(8,128)(2,1)S(1)} collective-permute-done((bf16[264,512]{1,0:T(8,128)(2,1)S(1)}, bf16[264,512]{1,0:T(8,128)(2,1)S(1)}, u32[]{:S(2)}, u32[]{:S(2)}) %collective-permute-start.5) | collective-permute-done | bytes 270368 | tf_op jit(solution)/shard_map/ppermute | solution.py:34
  13.9 1.3 %collective-permute-start.6 = (bf16[264,512]{1,0:T(8,128)(2,1)S(1)}, bf16[264,512]{1,0:T(8,128)(2,1)S(1)}, u32[]{:S(2)}, u32[]{:S(2)}) collective-permute-start(bf16[264,512]{1,0:T(8,128)(2,1)S(1)} %collective-permute-done.5.ka), channel_id=1, source_target_pairs={{0,2},{1,3},{2,4},{3,5},{4,6},{5,7},{8,10},{9,11},{10,12},{11,13},... | collective-permute-start | bytes 811016 | tf_op jit(solution)/shard_map/ppermute | solution.py:45
  16.3 3.4 %collective-permute-done.1.va = bf16[264,512]{1,0:T(8,128)(2,1)S(1)} collective-permute-done((bf16[264,512]{1,0:T(8,128)(2,1)S(1)}, bf16[264,512]{1,0:T(8,128)(2,1)S(1)}, u32[]{:S(2)}, u32[]{:S(2)}) %collective-permute-start.1) | collective-permute-done | bytes 270368 | tf_op jit(solution)/shard_map/ppermute | solution.py:34
  19.7 1.3 %collective-permute-start.8 = (bf16[264,512]{1,0:T(8,128)(2,1)S(1)}, bf16[264,512]{1,0:T(8,128)(2,1)S(1)}, u32[]{:S(2)}, u32[]{:S(2)}) collective-permute-start(bf16[264,512]{1,0:T(8,128)(2,1)S(1)} %collective-permute-done.1.va), channel_id=1, source_target_pairs={{0,2},{1,3},{2,4},{3,5},{4,6},{5,7},{8,10},{9,11},{10,12},{11,13},... | collective-permute-start | bytes 811016 | tf_op jit(solution)/shard_map/ppermute | solution.py:45
  20.9 1.1 %near_sums.1 = (f32[4,16,256]{2,1,0:T(8,128)S(1)}, f32[4,16,256]{2,1,0:T(8,128)S(1)}) custom-call(s32[1]{0:T(128)} %bitcast.core_ref, s32[8,128]{1,0:T(8,128)S(1)} %get-tuple-element.33.lo_ref, bf16[4,2,256,128]{3,2,1,0:T(8,128)(2,1)S(1)} %get-tuple-element.34.qs, bf16[4,2,256,128]{3,2,1,0:T(8,128)(2,1)S(1)} %get-tuple-element.35.gs, ...), custom_call_target="tpu_custom_call" | custom-call | tf_op jit(solution)/shard_map/near_sums/pallas_call | solution.py:290
  22.1 3.4 %collective-permute-done.6.kb = bf16[264,512]{1,0:T(8,128)(2,1)S(1)} collective-permute-done((bf16[264,512]{1,0:T(8,128)(2,1)S(1)}, bf16[264,512]{1,0:T(8,128)(2,1)S(1)}, u32[]{:S(2)}, u32[]{:S(2)}) %collective-permute-start.6) | collective-permute-done | bytes 270368 | tf_op jit(solution)/shard_map/ppermute | solution.py:45
  25.4 1.1 %far_values.1 = (bf16[256,512]{1,0:T(8,128)(2,1)S(1)}, f32[4,16,256]{2,1,0:T(8,128)S(1)}) custom-call(s32[1]{0:T(128)} %bitcast.core_ref, s32[8,128]{1,0:T(8,128)S(1)} %get-tuple-element.33.lo_ref, bf16[4,2,256,128]{3,2,1,0:T(8,128)(2,1)S(1)} %get-tuple-element.34.qs, bf16[4,2,256,128]{3,2,1,0:T(8,128)(2,1)S(1)} %get-tuple-element.35.gs, ...), custom_call_target="tpu_custom_call" | custom-call | tf_op jit(solution)/shard_map/far_values/pallas_call | solution.py:290
  26.6 2.4 %collective-permute-start.10 = (bf16[256,512]{1,0:T(8,128)(2,1)S(1)}, bf16[256,512]{1,0:T(8,128)(2,1)S(1)}, u32[]{:S(2)}, u32[]{:S(2)}) collective-permute-start(bf16[256,512]{1,0:T(8,128)(2,1)S(1)} %get-tuple-element.45), channel_id=1, source_target_pairs={{2,0},{3,1},{4,2},{5,3},{6,4},{7,5},{8,6},{9,7},{10,8},{11,9},{12,... | collective-permute-start | bytes 786440 | tf_op jit(solution)/shard_map/ppermute | solution.py:34
  29.0 1.6 %collective-permute-done.8.vb = bf16[264,512]{1,0:T(8,128)(2,1)S(1)} collective-permute-done((bf16[264,512]{1,0:T(8,128)(2,1)S(1)}, bf16[264,512]{1,0:T(8,128)(2,1)S(1)}, u32[]{:S(2)}, u32[]{:S(2)}) %collective-permute-start.8) | collective-permute-done | bytes 270368 | tf_op jit(solution)/shard_map/ppermute | solution.py:45
  30.6 1.6 %far_keys.1 = (bf16[256,512]{1,0:T(8,128)(2,1)S(1)}, f32[4,16,256]{2,1,0:T(8,128)S(1)}) custom-call(s32[1]{0:T(128)} %bitcast.core_ref, s32[8,128]{1,0:T(8,128)S(1)} %get-tuple-element.33.lo_ref, bf16[4,2,256,128]{3,2,1,0:T(8,128)(2,1)S(1)} %get-tuple-element.34.qs, bf16[4,2,256,128]{3,2,1,0:T(8,128)(2,1)S(1)} %get-tuple-element.35.gs, ...), custom_call_target="tpu_custom_call" | custom-call | tf_op jit(solution)/shard_map/far_keys/pallas_call | solution.py:290
  32.2 3.0 %collective-permute-start.12 = (bf16[256,512]{1,0:T(8,128)(2,1)S(1)}, bf16[256,512]{1,0:T(8,128)(2,1)S(1)}, u32[]{:S(2)}, u32[]{:S(2)}) collective-permute-start(bf16[256,512]{1,0:T(8,128)(2,1)S(1)} %get-tuple-element.49), channel_id=1, source_target_pairs={{2,0},{3,1},{4,2},{5,3},{6,4},{7,5},{8,6},{9,7},{10,8},{11,9},{12,... | collective-permute-start | bytes 786440 | tf_op jit(solution)/shard_map/ppermute | solution.py:34
  35.3 4.0 %near_grads.1 = (f32[256,512]{1,0:T(8,128)S(1)}, f32[256,512]{1,0:T(8,128)S(1)}, f32[256,512]{1,0:T(8,128)S(1)}, f32[256,512]{1,0:T(8,128)S(1)}, bf16[128,1024]{...) custom-call(s32[1]{0:T(128)} %bitcast.core_ref, s32[8,128]{1,0:T(8,128)S(1)} %get-tuple-element.33.lo_ref, ...), custom_call_target="tpu_custom_call" | custom-call | tf_op jit(solution)/shard_map/near_grads/pallas_call | solution.py:290
  39.3 2.2 %collective-permute-start.16 = (bf16[256,512]{1,0:T(8,128)(2,1)S(1)}, bf16[256,512]{1,0:T(8,128)(2,1)S(1)}, u32[]{:S(2)}, u32[]{:S(2)}) collective-permute-start(bf16[256,512]{1,0:T(8,128)(2,1)S(1)} %merge.2), channel_id=1, source_target_pairs={{2,0},{3,1},{4,2},{5,3},{6,4},{7,5},{8,6},{9,7},{10,8},{11,9},{12,... | collective-permute-start | bytes 786440 | tf_op jit(solution)/shard_map/ppermute | solution.py:34
  42.1 3.3 %collective-permute-done.12.came = bf16[256,512]{1,0:T(8,128)(2,1)S(1)} collective-permute-done((bf16[256,512]{1,0:T(8,128)(2,1)S(1)}, bf16[256,512]{1,0:T(8,128)(2,1)S(1)}, u32[]{:S(2)}, u32[]{:S(2)}) %collective-permute-start.12) | collective-permute-done | bytes 262176 | tf_op jit(solution)/shard_map/ppermute | solution.py:34
  45.5 1.9 %collective-permute-start.15 = (bf16[128,512]{1,0:T(8,128)(2,1)S(1)}, bf16[128,512]{1,0:T(8,128)(2,1)S(1)}, u32[]{:S(2)}, u32[]{:S(2)}) collective-permute-start(bf16[128,512]{1,0:T(8,128)(2,1)S(1)} %get-tuple-element.60), channel_id=1, source_target_pairs={{2,1},{3,0},{4,3},{5,2},{6,5},{7,4},{8,7},{9,6},{10,9},{11,8},{12,... | collective-permute-start | bytes 393224 | tf_op jit(solution)/shard_map/ppermute | solution.py:40
  47.4 1.9 %collective-permute-start.13 = (bf16[128,512]{1,0:T(8,128)(2,1)S(1)}, bf16[128,512]{1,0:T(8,128)(2,1)S(1)}, u32[]{:S(2)}, u32[]{:S(2)}) collective-permute-start(bf16[128,512]{1,0:T(8,128)(2,1)S(1)} %get-tuple-element.59), channel_id=1, source_target_pairs={{2,0},{3,1},{4,2},{5,3},{6,4},{7,5},{8,6},{9,7},{10,8},{11,9},{12,... | collective-permute-start | bytes 393224 | tf_op jit(solution)/shard_map/ppermute | solution.py:34
  49.3 2.5 %collective-permute-done.16 = bf16[256,512]{1,0:T(8,128)(2,1)S(1)} collective-permute-done((bf16[256,512]{1,0:T(8,128)(2,1)S(1)}, bf16[256,512]{1,0:T(8,128)(2,1)S(1)}, u32[]{:S(2)}, u32[]{:S(2)}) %collective-permute-start.16) | collective-permute-done | bytes 262176 | tf_op jit(solution)/shard_map/ppermute | solution.py:34
  52.1 0.8 %pad_maximum_fusion.1 = bf16[128,2048]{1,0:T(8,128)(2,1)} fusion(bf16[128,1024]{1,0:T(8,128)(2,1)S(1)} %get-tuple-element.56, bf16[128,1024]{1,0:T(8,128)(2,1)S(1)} %get-tuple-element.55), kind=kLoop, calls=%fused_computation.3 | loop fusion | flops 1048576 | bytes 1048576 | tf_op jit(solution)/shard_map/concatenate | solution.py:364
  53.3 0.7 %pad_maximum_fusion.2 = bf16[128,1024]{1,0:T(8,128)(2,1)} fusion(bf16[128,512]{1,0:T(8,128)(2,1)S(1)} %get-tuple-element.58, bf16[128,512]{1,0:T(8,128)(2,1)S(1)} %get-tuple-element.57), kind=kLoop, calls=%fused_computation.7 | loop fusion | flops 524288 | bytes 524288 | tf_op jit(solution)/shard_map/concatenate | solution.py:364
  54.1 1.4 %collective-permute-done.15 = bf16[128,512]{1,0:T(8,128)(2,1)S(1)} collective-permute-done((bf16[128,512]{1,0:T(8,128)(2,1)S(1)}, bf16[128,512]{1,0:T(8,128)(2,1)S(1)}, u32[]{:S(2)}, u32[]{:S(2)}) %collective-permute-start.15) | collective-permute-done | bytes 131104 | tf_op jit(solution)/shard_map/ppermute | solution.py:40
  55.5 3.2 %collective-permute-done.13 = bf16[128,512]{1,0:T(8,128)(2,1)S(1)} collective-permute-done((bf16[128,512]{1,0:T(8,128)(2,1)S(1)}, bf16[128,512]{1,0:T(8,128)(2,1)S(1)}, u32[]{:S(2)}, u32[]{:S(2)}) %collective-permute-start.13) | collective-permute-done | bytes 131104 | tf_op jit(solution)/shard_map/ppermute | solution.py:34
  (48 shorter events, 5.1 us)
Async XLA Ops:
  0.6 1.6 %copy-start.2 = (bf16[128,1024]{1,0:T(8,128)(2,1)S(1)}, bf16[128,1024]{1,0:T(8,128)(2,1)}, u32[]{:S(2)}) copy-start(bf16[128,1024]{1,0:T(8,128)(2,1)} %param.7) | copy-start | bytes 786436
  0.6 1.8 %collective-permute-start.2 = (bf16[128,1024]{1,0:T(8,128)(2,1)}, bf16[128,1024]{1,0:T(8,128)(2,1)S(1)}, u32[]{:S(2)}, u32[]{:S(2)}) collective-permute-start(bf16[128,1024]{1,0:T(8,128)(2,1)} %param.6), channel_id=1, source_target_pairs={{0,1},{1,0},{2,3},{3,2},{4,5},{5,4},{6,7},{7,6},{8,9},{9,8},{10,11... | collective-permute-start | bytes 786440 | tf_op jit(solution)/shard_map/ppermute | solution.py:28
  0.7 1.7 %collective-permute-start.3 = (s32[128]{0:T(128)}, s32[128]{0:T(128)S(1)}, u32[]{:S(2)}, u32[]{:S(2)}) collective-permute-start(s32[128]{0:T(128)} %param.9), channel_id=1, source_target_pairs={{0,1},{1,0},{2,3},{3,2},{4,5},{5,4},{6,7},{7,6},{8,9},{9,8},{10,11... | collective-permute-start | bytes 1544 | tf_op jit(solution)/shard_map/ppermute | solution.py:28
  1.2 4.7 %collective-permute-start = (bf16[128,1024]{1,0:T(8,128)(2,1)}, bf16[128,1024]{1,0:T(8,128)(2,1)S(1)}, u32[]{:S(2)}, u32[]{:S(2)}) collective-permute-start(bf16[128,1024]{1,0:T(8,128)(2,1)} %param.7), channel_id=1, source_target_pairs={{0,1},{1,0},{2,3},{3,2},{4,5},{5,4},{6,7},{7,6},{8,9},{9,8},{10,11... | collective-permute-start | bytes 786440 | tf_op jit(solution)/shard_map/ppermute | solution.py:28
  1.3 1.2 %copy-start.3 = (s32[128]{0:T(128)S(1)}, s32[128]{0:T(128)}, u32[]{:S(2)}) copy-start(s32[128]{0:T(128)} %param.9) | copy-start | bytes 1540
  2.2 3.5 %copy-start = (bf16[128,2048]{1,0:T(8,128)(2,1)S(1)}, bf16[128,2048]{1,0:T(8,128)(2,1)}, u32[]{:S(2)}) copy-start(bf16[128,2048]{1,0:T(8,128)(2,1)} %q) | copy-start | bytes 1572868
  2.2 3.5 %copy-start.1 = (bf16[128,2048]{1,0:T(8,128)(2,1)S(1)}, bf16[128,2048]{1,0:T(8,128)(2,1)}, u32[]{:S(2)}) copy-start(bf16[128,2048]{1,0:T(8,128)(2,1)} %go) | copy-start | bytes 1572868
  2.5 11.3 %collective-permute-start.5 = (bf16[264,512]{1,0:T(8,128)(2,1)S(1)}, bf16[264,512]{1,0:T(8,128)(2,1)S(1)}, u32[]{:S(2)}, u32[]{:S(2)}) collective-permute-start(bf16[264,512]{1,0:T(8,128)(2,1)S(1)} %fusion.1.kc), channel_id=1, source_target_pairs={{0,2},{1,3},{2,4},{3,5},{4,6},{5,7},{6,8},{7,9},{8,10},{9,11},{10,... | collective-permute-start | bytes 811016 | tf_op jit(solution)/shard_map/ppermute | solution.py:34
  5.8 10.0 %collective-permute-start.4 = (bf16[256,1024]{1,0:T(8,128)(2,1)S(1)}, bf16[256,1024]{1,0:T(8,128)(2,1)S(1)}, u32[]{:S(2)}, u32[]{:S(2)}) collective-permute-start(bf16[256,1024]{1,0:T(8,128)(2,1)S(1)} %pad_maximum_fusion), channel_id=1, source_target_pairs={{0,1},{1,0},{2,3},{3,2},{4,5},{5,4},{6,7},{7,6},{8,9},{9,8},{10,11... | collective-permute-start | bytes 1572872 | tf_op jit(solution)/shard_map/ppermute | solution.py:28
  6.1 13.6 %collective-permute-start.1 = (bf16[264,512]{1,0:T(8,128)(2,1)S(1)}, bf16[264,512]{1,0:T(8,128)(2,1)S(1)}, u32[]{:S(2)}, u32[]{:S(2)}) collective-permute-start(bf16[264,512]{1,0:T(8,128)(2,1)S(1)} %maximum_maximum_fusion.vc), channel_id=1, source_target_pairs={{0,2},{1,3},{2,4},{3,5},{4,6},{5,7},{6,8},{7,9},{8,10},{9,11},{10,... | collective-permute-start | bytes 811016 | tf_op jit(solution)/shard_map/ppermute | solution.py:34
  9.6 12.5 %collective-permute-start.7 = (bf16[264,512]{1,0:T(8,128)(2,1)S(1)}, bf16[264,512]{1,0:T(8,128)(2,1)S(1)}, u32[]{:S(2)}, u32[]{:S(2)}) collective-permute-start(bf16[264,512]{1,0:T(8,128)(2,1)S(1)} %fusion.1.kc), channel_id=1, source_target_pairs={{4,8},{5,9},{12,16},{13,17},{20,24},{21,25}} | collective-permute-start | bytes 811016 | tf_op jit(solution)/shard_map/ppermute | solution.py:50
  13.9 11.6 %collective-permute-start.6 = (bf16[264,512]{1,0:T(8,128)(2,1)S(1)}, bf16[264,512]{1,0:T(8,128)(2,1)S(1)}, u32[]{:S(2)}, u32[]{:S(2)}) collective-permute-start(bf16[264,512]{1,0:T(8,128)(2,1)S(1)} %collective-permute-done.5.ka), channel_id=1, source_target_pairs={{0,2},{1,3},{2,4},{3,5},{4,6},{5,7},{8,10},{9,11},{10,12},{11,13},... | collective-permute-start | bytes 811016 | tf_op jit(solution)/shard_map/ppermute | solution.py:45
  15.1 13.8 %collective-permute-start.9 = (bf16[264,512]{1,0:T(8,128)(2,1)S(1)}, bf16[264,512]{1,0:T(8,128)(2,1)S(1)}, u32[]{:S(2)}, u32[]{:S(2)}) collective-permute-start(bf16[264,512]{1,0:T(8,128)(2,1)S(1)} %maximum_maximum_fusion.vc), channel_id=1, source_target_pairs={{4,8},{5,9},{12,16},{13,17},{20,24},{21,25}} | collective-permute-start | bytes 811016 | tf_op jit(solution)/shard_map/ppermute | solution.py:50
  19.7 11.0 %collective-permute-start.8 = (bf16[264,512]{1,0:T(8,128)(2,1)S(1)}, bf16[264,512]{1,0:T(8,128)(2,1)S(1)}, u32[]{:S(2)}, u32[]{:S(2)}) collective-permute-start(bf16[264,512]{1,0:T(8,128)(2,1)S(1)} %collective-permute-done.1.va), channel_id=1, source_target_pairs={{0,2},{1,3},{2,4},{3,5},{4,6},{5,7},{8,10},{9,11},{10,12},{11,13},... | collective-permute-start | bytes 811016 | tf_op jit(solution)/shard_map/ppermute | solution.py:45
  26.6 12.7 %collective-permute-start.10 = (bf16[256,512]{1,0:T(8,128)(2,1)S(1)}, bf16[256,512]{1,0:T(8,128)(2,1)S(1)}, u32[]{:S(2)}, u32[]{:S(2)}) collective-permute-start(bf16[256,512]{1,0:T(8,128)(2,1)S(1)} %get-tuple-element.45), channel_id=1, source_target_pairs={{2,0},{3,1},{4,2},{5,3},{6,4},{7,5},{8,6},{9,7},{10,8},{11,9},{12,... | collective-permute-start | bytes 786440 | tf_op jit(solution)/shard_map/ppermute | solution.py:34
  32.2 13.2 %collective-permute-start.12 = (bf16[256,512]{1,0:T(8,128)(2,1)S(1)}, bf16[256,512]{1,0:T(8,128)(2,1)S(1)}, u32[]{:S(2)}, u32[]{:S(2)}) collective-permute-start(bf16[256,512]{1,0:T(8,128)(2,1)S(1)} %get-tuple-element.49), channel_id=1, source_target_pairs={{2,0},{3,1},{4,2},{5,3},{6,4},{7,5},{8,6},{9,7},{10,8},{11,9},{12,... | collective-permute-start | bytes 786440 | tf_op jit(solution)/shard_map/ppermute | solution.py:34
  39.3 12.5 %collective-permute-start.16 = (bf16[256,512]{1,0:T(8,128)(2,1)S(1)}, bf16[256,512]{1,0:T(8,128)(2,1)S(1)}, u32[]{:S(2)}, u32[]{:S(2)}) collective-permute-start(bf16[256,512]{1,0:T(8,128)(2,1)S(1)} %merge.2), channel_id=1, source_target_pairs={{2,0},{3,1},{4,2},{5,3},{6,4},{7,5},{8,6},{9,7},{10,8},{11,9},{12,... | collective-permute-start | bytes 786440 | tf_op jit(solution)/shard_map/ppermute | solution.py:34
  41.6 13.9 %collective-permute-start.14 = (f32[128,512]{1,0:T(8,128)S(1)}, f32[128,512]{1,0:T(8,128)S(1)}, u32[]{:S(2)}, u32[]{:S(2)}) collective-permute-start(f32[128,512]{1,0:T(8,128)S(1)} %slice.22), channel_id=1, source_target_pairs={{0,1},{1,0},{2,3},{3,2},{4,5},{5,4},{6,7},{7,6},{8,9},{9,8},{10,11... | collective-permute-start | bytes 786440 | tf_op jit(solution)/shard_map/ppermute | solution.py:28
  41.6 10.3 %collective-permute-start.11 = (bf16[128,1024]{1,0:T(8,128)(2,1)S(1)}, bf16[128,1024]{1,0:T(8,128)(2,1)S(1)}, u32[]{:S(2)}, u32[]{:S(2)}) collective-permute-start(bf16[128,1024]{1,0:T(8,128)(2,1)S(1)} %get-tuple-element.46), channel_id=1, source_target_pairs={{0,1},{1,0},{2,3},{3,2},{4,5},{5,4},{6,7},{7,6},{8,9},{9,8},{10,11... | collective-permute-start | bytes 786440 | tf_op jit(solution)/shard_map/ppermute | solution.py:28
  45.5 10.0 %collective-permute-start.15 = (bf16[128,512]{1,0:T(8,128)(2,1)S(1)}, bf16[128,512]{1,0:T(8,128)(2,1)S(1)}, u32[]{:S(2)}, u32[]{:S(2)}) collective-permute-start(bf16[128,512]{1,0:T(8,128)(2,1)S(1)} %get-tuple-element.60), channel_id=1, source_target_pairs={{2,1},{3,0},{4,3},{5,2},{6,5},{7,4},{8,7},{9,6},{10,9},{11,8},{12,... | collective-permute-start | bytes 393224 | tf_op jit(solution)/shard_map/ppermute | solution.py:40
  47.4 11.3 %collective-permute-start.13 = (bf16[128,512]{1,0:T(8,128)(2,1)S(1)}, bf16[128,512]{1,0:T(8,128)(2,1)S(1)}, u32[]{:S(2)}, u32[]{:S(2)}) collective-permute-start(bf16[128,512]{1,0:T(8,128)(2,1)S(1)} %get-tuple-element.59), channel_id=1, source_target_pairs={{2,0},{3,1},{4,2},{5,3},{6,4},{7,5},{8,6},{9,7},{10,8},{11,9},{12,... | collective-permute-start | bytes 393224 | tf_op jit(solution)/shard_map/ppermute | solution.py:34
  51.9 1.4 %collective-permute-start.17 = (bf16[128,512]{1,0:T(8,128)(2,1)S(1)}, bf16[128,512]{1,0:T(8,128)(2,1)S(1)}, u32[]{:S(2)}, u32[]{:S(2)}) collective-permute-start(bf16[128,512]{1,0:T(8,128)(2,1)S(1)} %slice.29), channel_id=1, source_target_pairs={{0,1},{1,0},{2,3},{3,2},{4,5},{5,4},{6,7},{7,6},{8,9},{9,8},{10,11... | collective-permute-start | bytes 393224 | tf_op jit(solution)/shard_map/ppermute | solution.py:28

commit v9 on v8

--- a/solution.py
+++ b/solution.py
@@ -320,7 +320,8 @@
     seg_rows = jnp.pad(ids.astype(bf16)[None, :], ((0, SEG_ROWS - 1), (0, half - 2 * tok)))
     kc = jnp.concatenate([part(keys, core, half), part(k_in, core, half), seg_rows], 0)
     v_in = swap(values)
-    vc = jnp.concatenate([part(values, core, half), part(v_in, core, half), jnp.zeros((SEG_ROWS, half), bf16)], 0)
+    values, _ = lax.optimization_barrier((values, kc))
+    vc = jnp.concatenate([part(values, core, half), part(v_in, core, half)], 0)
     ka = hop(kc, 1)
     va = hop(vc, 1)
     queries, grad_out, _ = lax.optimization_barrier((queries, grad_out, kc))

time: 59.9 us -> 59.4 us (level)
  waiting for transfers between devices: 22.9 us -> 21.2 us
  local copies, waits for them, and re-layouts: 1.1 us -> 1.96 us
    ppermute x6, waiting for transfers between devices: 15.9 us -> 14.8 us  [hop(): lax.ppermute(x, AXES, [(i, i + by) for i in range(n) if 0 <= i + by < n])]
    unnamed x8, local copies, waits for them, and re-layouts: 0.02 us -> 0.81 us
where the time goes in v9:
time: 59.4 us; the launch traced here: 59 us
  starting transfers between devices  23.9 us (40%)
  waiting for transfers between devices  21.2 us (36%)
  Pallas kernels  8.34 us (14%)
  other arithmetic  2.61 us (4%)
  local copies, waits for them, and re-layouts  1.96 us (3%)
  between operations  0.98 us (2%)
    ppermute x6, starting transfers between devices, hop(): lax.ppermute(x, AXES, [(i, i + by) for i in range(n) if 0 <= i + by < n])  16.7 us
    ppermute x6, waiting for transfers between devices, hop(): lax.ppermute(x, AXES, [(i, i + by) for i in range(n) if 0 <= i + by < n])  14.8 us
    pallas_call x7, Pallas kernels, call(): pl.pallas_call(functools.partial(body, tok, groups), in_specs=[pl.BlockSp...  8.34 us
    ppermute x2, waiting for transfers between devices, forward(): lax.ppermute(x, AXES, [(i, i + 2) for i in range(n) if i % row < row - 2])  4.44 us
    ppermute x2, starting transfers between devices, forward(): lax.ppermute(x, AXES, [(i, i + 2) for i in range(n) if i % row < row - 2])  2.56 us
    concatenate x3, other arithmetic, place(): return jnp.concatenate([first, second], 1)  2.29 us
    ppermute x1, starting transfers between devices, cross(): lax.ppermute(x, AXES, [(i, (i ^ 1) + by) for i in range(n) if 0 <= i + by...  1.92 us
    ppermute x7, starting transfers between devices, swap(): return lax.ppermute(x, AXES, [(i, i ^ 1) for i in range(n)])  1.38 us
  transfers between devices with their start and end apart: 18, of which 10 were waited for; matrix products, arithmetic and copies ran while one was open for 5% of the time, Pallas kernels for 14%

profile of v9, /device:TPU:26, one launch (start us, length us, event | category | flops | bytes accessed | tf_op | source)
XLA Modules:
  0.0 59.0 jit_solution(16280042381784365284)
XLA Ops:
  1.3 1.0 %constant_dynamic-slice_fusion.5 = bf16[128,512]{1,0:T(8,128)(2,1)S(1)} fusion(bf16[128,1024]{1,0:T(8,128)(2,1)} %param.6, s32[]{:T(128)S(6)} %select_n.43), kind=kLoop, calls=%fused_computation.22 | loop fusion | bytes 262148 | tf_op jit(solution)/shard_map/dynamic_slice | solution.py:315
  2.5 3.1 %collective-permute-start.5 = (bf16[264,512]{1,0:T(8,128)(2,1)S(1)}, bf16[264,512]{1,0:T(8,128)(2,1)S(1)}, u32[]{:S(2)}, u32[]{:S(2)}) collective-permute-start(bf16[264,512]{1,0:T(8,128)(2,1)S(1)} %fusion.1.kc), channel_id=1, source_target_pairs={{0,2},{1,3},{2,4},{3,5},{4,6},{5,7},{6,8},{7,9},{8,10},{9,11},{10,... | collective-permute-start | bytes 811016 | tf_op jit(solution)/shard_map/ppermute | solution.py:34
  5.8 0.8 %copy-done.2 = bf16[128,1024]{1,0:T(8,128)(2,1)S(1)} copy-done((bf16[128,1024]{1,0:T(8,128)(2,1)S(1)}, bf16[128,1024]{1,0:T(8,128)(2,1)}, u32[]{:S(2)}) %copy-start.2) | copy-done | bytes 262168
  6.7 3.5 %collective-permute-start.3 = (bf16[256,512]{1,0:T(8,128)(2,1)S(1)}, bf16[256,512]{1,0:T(8,128)(2,1)S(1)}, u32[]{:S(2)}, u32[]{:S(2)}) collective-permute-start(bf16[256,512]{1,0:T(8,128)(2,1)S(1)} %pad_maximum_fusion.2.vc), channel_id=1, source_target_pairs={{0,2},{1,3},{2,4},{3,5},{4,6},{5,7},{6,8},{7,9},{8,10},{9,11},{10,... | collective-permute-start | bytes 786440 | tf_op jit(solution)/shard_map/ppermute | solution.py:34
  10.9 2.8 %collective-permute-done.5.ka = bf16[264,512]{1,0:T(8,128)(2,1)S(1)} collective-permute-done((bf16[264,512]{1,0:T(8,128)(2,1)S(1)}, bf16[264,512]{1,0:T(8,128)(2,1)S(1)}, u32[]{:S(2)}, u32[]{:S(2)}) %collective-permute-start.5) | collective-permute-done | bytes 270368 | tf_op jit(solution)/shard_map/ppermute | solution.py:34
  13.7 1.3 %collective-permute-start.6 = (bf16[264,512]{1,0:T(8,128)(2,1)S(1)}, bf16[264,512]{1,0:T(8,128)(2,1)S(1)}, u32[]{:S(2)}, u32[]{:S(2)}) collective-permute-start(bf16[264,512]{1,0:T(8,128)(2,1)S(1)} %collective-permute-done.5.ka), channel_id=1, source_target_pairs={{0,2},{1,3},{2,4},{3,5},{4,6},{5,7},{8,10},{9,11},{10,12},{11,13},... | collective-permute-start | bytes 811016 | tf_op jit(solution)/shard_map/ppermute | solution.py:45
  16.1 3.2 %collective-permute-done.3.va = bf16[256,512]{1,0:T(8,128)(2,1)S(1)} collective-permute-done((bf16[256,512]{1,0:T(8,128)(2,1)S(1)}, bf16[256,512]{1,0:T(8,128)(2,1)S(1)}, u32[]{:S(2)}, u32[]{:S(2)}) %collective-permute-start.3) | collective-permute-done | bytes 262176 | tf_op jit(solution)/shard_map/ppermute | solution.py:34
  19.3 1.3 %collective-permute-start.8 = (bf16[256,512]{1,0:T(8,128)(2,1)S(1)}, bf16[256,512]{1,0:T(8,128)(2,1)S(1)}, u32[]{:S(2)}, u32[]{:S(2)}) collective-permute-start(bf16[256,512]{1,0:T(8,128)(2,1)S(1)} %collective-permute-done.3.va), channel_id=1, source_target_pairs={{0,2},{1,3},{2,4},{3,5},{4,6},{5,7},{8,10},{9,11},{10,12},{11,13},... | collective-permute-start | bytes 786440 | tf_op jit(solution)/shard_map/ppermute | solution.py:45
  20.6 1.1 %near_sums.1 = (f32[4,16,256]{2,1,0:T(8,128)S(1)}, f32[4,16,256]{2,1,0:T(8,128)S(1)}) custom-call(s32[1]{0:T(128)} %bitcast.core_ref, s32[8,128]{1,0:T(8,128)S(1)} %get-tuple-element.35.lo_ref, bf16[4,2,256,128]{3,2,1,0:T(8,128)(2,1)S(1)} %get-tuple-element.36.qs, bf16[4,2,256,128]{3,2,1,0:T(8,128)(2,1)S(1)} %get-tuple-element.37.gs, ...), custom_call_target="tpu_custom_call" | custom-call | tf_op jit(solution)/shard_map/near_sums/pallas_call | solution.py:290
  21.8 3.1 %collective-permute-done.6.kb = bf16[264,512]{1,0:T(8,128)(2,1)S(1)} collective-permute-done((bf16[264,512]{1,0:T(8,128)(2,1)S(1)}, bf16[264,512]{1,0:T(8,128)(2,1)S(1)}, u32[]{:S(2)}, u32[]{:S(2)}) %collective-permute-start.6) | collective-permute-done | bytes 270368 | tf_op jit(solution)/shard_map/ppermute | solution.py:45
  24.9 1.1 %far_values.1 = (bf16[256,512]{1,0:T(8,128)(2,1)S(1)}, f32[4,16,256]{2,1,0:T(8,128)S(1)}) custom-call(s32[1]{0:T(128)} %bitcast.core_ref, s32[8,128]{1,0:T(8,128)S(1)} %get-tuple-element.35.lo_ref, bf16[4,2,256,128]{3,2,1,0:T(8,128)(2,1)S(1)} %get-tuple-element.36.qs, bf16[4,2,256,128]{3,2,1,0:T(8,128)(2,1)S(1)} %get-tuple-element.37.gs, ...), custom_call_target="tpu_custom_call" | custom-call | tf_op jit(solution)/shard_map/far_values/pallas_call | solution.py:290
  26.0 2.8 %collective-permute-start.10 = (bf16[256,512]{1,0:T(8,128)(2,1)S(1)}, bf16[256,512]{1,0:T(8,128)(2,1)S(1)}, u32[]{:S(2)}, u32[]{:S(2)}) collective-permute-start(bf16[256,512]{1,0:T(8,128)(2,1)S(1)} %get-tuple-element.47), channel_id=1, source_target_pairs={{2,0},{3,1},{4,2},{5,3},{6,4},{7,5},{8,6},{9,7},{10,8},{11,9},{12,... | collective-permute-start | bytes 786440 | tf_op jit(solution)/shard_map/ppermute | solution.py:34
  28.8 1.3 %collective-permute-done.8.vb = bf16[256,512]{1,0:T(8,128)(2,1)S(1)} collective-permute-done((bf16[256,512]{1,0:T(8,128)(2,1)S(1)}, bf16[256,512]{1,0:T(8,128)(2,1)S(1)}, u32[]{:S(2)}, u32[]{:S(2)}) %collective-permute-start.8) | collective-permute-done | bytes 262176 | tf_op jit(solution)/shard_map/ppermute | solution.py:45
  30.1 1.6 %far_keys.1 = (bf16[256,512]{1,0:T(8,128)(2,1)S(1)}, f32[4,16,256]{2,1,0:T(8,128)S(1)}) custom-call(s32[1]{0:T(128)} %bitcast.core_ref, s32[8,128]{1,0:T(8,128)S(1)} %get-tuple-element.35.lo_ref, bf16[4,2,256,128]{3,2,1,0:T(8,128)(2,1)S(1)} %get-tuple-element.36.qs, bf16[4,2,256,128]{3,2,1,0:T(8,128)(2,1)S(1)} %get-tuple-element.37.gs, ...), custom_call_target="tpu_custom_call" | custom-call | tf_op jit(solution)/shard_map/far_keys/pallas_call | solution.py:290
  31.7 3.2 %collective-permute-start.12 = (bf16[256,512]{1,0:T(8,128)(2,1)S(1)}, bf16[256,512]{1,0:T(8,128)(2,1)S(1)}, u32[]{:S(2)}, u32[]{:S(2)}) collective-permute-start(bf16[256,512]{1,0:T(8,128)(2,1)S(1)} %get-tuple-element.51), channel_id=1, source_target_pairs={{2,0},{3,1},{4,2},{5,3},{6,4},{7,5},{8,6},{9,7},{10,8},{11,9},{12,... | collective-permute-start | bytes 786440 | tf_op jit(solution)/shard_map/ppermute | solution.py:34
  34.9 4.0 %near_grads.1 = (f32[256,512]{1,0:T(8,128)S(1)}, f32[256,512]{1,0:T(8,128)S(1)}, f32[256,512]{1,0:T(8,128)S(1)}, f32[256,512]{1,0:T(8,128)S(1)}, bf16[128,1024]{...) custom-call(s32[1]{0:T(128)} %bitcast.core_ref, s32[8,128]{1,0:T(8,128)S(1)} %get-tuple-element.35.lo_ref, ...), custom_call_target="tpu_custom_call" | custom-call | tf_op jit(solution)/shard_map/near_grads/pallas_call | solution.py:290
  39.0 2.2 %collective-permute-start.16 = (bf16[256,512]{1,0:T(8,128)(2,1)S(1)}, bf16[256,512]{1,0:T(8,128)(2,1)S(1)}, u32[]{:S(2)}, u32[]{:S(2)}) collective-permute-start(bf16[256,512]{1,0:T(8,128)(2,1)S(1)} %merge.2), channel_id=1, source_target_pairs={{2,0},{3,1},{4,2},{5,3},{6,4},{7,5},{8,6},{9,7},{10,8},{11,9},{12,... | collective-permute-start | bytes 786440 | tf_op jit(solution)/shard_map/ppermute | solution.py:34
  41.9 3.0 %collective-permute-done.12.came = bf16[256,512]{1,0:T(8,128)(2,1)S(1)} collective-permute-done((bf16[256,512]{1,0:T(8,128)(2,1)S(1)}, bf16[256,512]{1,0:T(8,128)(2,1)S(1)}, u32[]{:S(2)}, u32[]{:S(2)}) %collective-permute-start.12) | collective-permute-done | bytes 262176 | tf_op jit(solution)/shard_map/ppermute | solution.py:34
  45.0 1.9 %collective-permute-start.15 = (bf16[128,512]{1,0:T(8,128)(2,1)S(1)}, bf16[128,512]{1,0:T(8,128)(2,1)S(1)}, u32[]{:S(2)}, u32[]{:S(2)}) collective-permute-start(bf16[128,512]{1,0:T(8,128)(2,1)S(1)} %get-tuple-element.62), channel_id=1, source_target_pairs={{2,1},{3,0},{4,3},{5,2},{6,5},{7,4},{8,7},{9,6},{10,9},{11,8},{12,... | collective-permute-start | bytes 393224 | tf_op jit(solution)/shard_map/ppermute | solution.py:40
  46.9 1.9 %collective-permute-start.13 = (bf16[128,512]{1,0:T(8,128)(2,1)S(1)}, bf16[128,512]{1,0:T(8,128)(2,1)S(1)}, u32[]{:S(2)}, u32[]{:S(2)}) collective-permute-start(bf16[128,512]{1,0:T(8,128)(2,1)S(1)} %get-tuple-element.61), channel_id=1, source_target_pairs={{2,0},{3,1},{4,2},{5,3},{6,4},{7,5},{8,6},{9,7},{10,8},{11,9},{12,... | collective-permute-start | bytes 393224 | tf_op jit(solution)/shard_map/ppermute | solution.py:34
  48.8 2.5 %collective-permute-done.16 = bf16[256,512]{1,0:T(8,128)(2,1)S(1)} collective-permute-done((bf16[256,512]{1,0:T(8,128)(2,1)S(1)}, bf16[256,512]{1,0:T(8,128)(2,1)S(1)}, u32[]{:S(2)}, u32[]{:S(2)}) %collective-permute-start.16) | collective-permute-done | bytes 262176 | tf_op jit(solution)/shard_map/ppermute | solution.py:34
  51.5 0.8 %pad_maximum_fusion.1 = bf16[128,2048]{1,0:T(8,128)(2,1)} fusion(bf16[128,1024]{1,0:T(8,128)(2,1)S(1)} %get-tuple-element.58, bf16[128,1024]{1,0:T(8,128)(2,1)S(1)} %get-tuple-element.57), kind=kLoop, calls=%fused_computation.3 | loop fusion | flops 1048576 | bytes 1048576 | tf_op jit(solution)/shard_map/concatenate | solution.py:365
  53.6 1.4 %collective-permute-done.15 = bf16[128,512]{1,0:T(8,128)(2,1)S(1)} collective-permute-done((bf16[128,512]{1,0:T(8,128)(2,1)S(1)}, bf16[128,512]{1,0:T(8,128)(2,1)S(1)}, u32[]{:S(2)}, u32[]{:S(2)}) %collective-permute-start.15) | collective-permute-done | bytes 131104 | tf_op jit(solution)/shard_map/ppermute | solution.py:40
  54.9 3.2 %collective-permute-done.13 = bf16[128,512]{1,0:T(8,128)(2,1)S(1)} collective-permute-done((bf16[128,512]{1,0:T(8,128)(2,1)S(1)}, bf16[128,512]{1,0:T(8,128)(2,1)S(1)}, u32[]{:S(2)}, u32[]{:S(2)}) %collective-permute-start.13) | collective-permute-done | bytes 131104 | tf_op jit(solution)/shard_map/ppermute | solution.py:34
  (46 shorter events, 5.8 us)
Async XLA Ops:
  0.6 1.8 %collective-permute-start = (bf16[128,1024]{1,0:T(8,128)(2,1)}, bf16[128,1024]{1,0:T(8,128)(2,1)S(1)}, u32[]{:S(2)}, u32[]{:S(2)}) collective-permute-start(bf16[128,1024]{1,0:T(8,128)(2,1)} %param.6), channel_id=1, source_target_pairs={{0,1},{1,0},{2,3},{3,2},{4,5},{5,4},{6,7},{7,6},{8,9},{9,8},{10,11... | collective-permute-start | bytes 786440 | tf_op jit(solution)/shard_map/ppermute | solution.py:28
  0.7 1.7 %collective-permute-start.1 = (s32[128]{0:T(128)}, s32[128]{0:T(128)S(1)}, u32[]{:S(2)}, u32[]{:S(2)}) collective-permute-start(s32[128]{0:T(128)} %param.9), channel_id=1, source_target_pairs={{0,1},{1,0},{2,3},{3,2},{4,5},{5,4},{6,7},{7,6},{8,9},{9,8},{10,11... | collective-permute-start | bytes 1544 | tf_op jit(solution)/shard_map/ppermute | solution.py:28
  1.2 5.4 %collective-permute-start.2 = (bf16[128,1024]{1,0:T(8,128)(2,1)}, bf16[128,1024]{1,0:T(8,128)(2,1)S(1)}, u32[]{:S(2)}, u32[]{:S(2)}) collective-permute-start(bf16[128,1024]{1,0:T(8,128)(2,1)} %param.7), channel_id=1, source_target_pairs={{0,1},{1,0},{2,3},{3,2},{4,5},{5,4},{6,7},{7,6},{8,9},{9,8},{10,11... | collective-permute-start | bytes 786440 | tf_op jit(solution)/shard_map/ppermute | solution.py:28
  1.3 1.2 %copy-start.3 = (s32[128]{0:T(128)S(1)}, s32[128]{0:T(128)}, u32[]{:S(2)}) copy-start(s32[128]{0:T(128)} %param.9) | copy-start | bytes 1540
  1.3 4.3 %copy-start = (bf16[128,2048]{1,0:T(8,128)(2,1)S(1)}, bf16[128,2048]{1,0:T(8,128)(2,1)}, u32[]{:S(2)}) copy-start(bf16[128,2048]{1,0:T(8,128)(2,1)} %q) | copy-start | bytes 1572868
  1.3 4.3 %copy-start.1 = (bf16[128,2048]{1,0:T(8,128)(2,1)S(1)}, bf16[128,2048]{1,0:T(8,128)(2,1)}, u32[]{:S(2)}) copy-start(bf16[128,2048]{1,0:T(8,128)(2,1)} %go) | copy-start | bytes 1572868
  2.5 11.2 %collective-permute-start.5 = (bf16[264,512]{1,0:T(8,128)(2,1)S(1)}, bf16[264,512]{1,0:T(8,128)(2,1)S(1)}, u32[]{:S(2)}, u32[]{:S(2)}) collective-permute-start(bf16[264,512]{1,0:T(8,128)(2,1)S(1)} %fusion.1.kc), channel_id=1, source_target_pairs={{0,2},{1,3},{2,4},{3,5},{4,6},{5,7},{6,8},{7,9},{8,10},{9,11},{10,... | collective-permute-start | bytes 811016 | tf_op jit(solution)/shard_map/ppermute | solution.py:34
  5.7 1.0 %copy-start.2 = (bf16[128,1024]{1,0:T(8,128)(2,1)S(1)}, bf16[128,1024]{1,0:T(8,128)(2,1)}, u32[]{:S(2)}) copy-start(bf16[128,1024]{1,0:T(8,128)(2,1)} %param.7) | copy-start | bytes 786436
  5.7 10.0 %collective-permute-start.4 = (bf16[256,1024]{1,0:T(8,128)(2,1)S(1)}, bf16[256,1024]{1,0:T(8,128)(2,1)S(1)}, u32[]{:S(2)}, u32[]{:S(2)}) collective-permute-start(bf16[256,1024]{1,0:T(8,128)(2,1)S(1)} %pad_maximum_fusion), channel_id=1, source_target_pairs={{0,1},{1,0},{2,3},{3,2},{4,5},{5,4},{6,7},{7,6},{8,9},{9,8},{10,11... | collective-permute-start | bytes 1572872 | tf_op jit(solution)/shard_map/ppermute | solution.py:28
  6.7 12.6 %collective-permute-start.3 = (bf16[256,512]{1,0:T(8,128)(2,1)S(1)}, bf16[256,512]{1,0:T(8,128)(2,1)S(1)}, u32[]{:S(2)}, u32[]{:S(2)}) collective-permute-start(bf16[256,512]{1,0:T(8,128)(2,1)S(1)} %pad_maximum_fusion.2.vc), channel_id=1, source_target_pairs={{0,2},{1,3},{2,4},{3,5},{4,6},{5,7},{6,8},{7,9},{8,10},{9,11},{10,... | collective-permute-start | bytes 786440 | tf_op jit(solution)/shard_map/ppermute | solution.py:34
  10.2 11.6 %collective-permute-start.7 = (bf16[264,512]{1,0:T(8,128)(2,1)S(1)}, bf16[264,512]{1,0:T(8,128)(2,1)S(1)}, u32[]{:S(2)}, u32[]{:S(2)}) collective-permute-start(bf16[264,512]{1,0:T(8,128)(2,1)S(1)} %fusion.1.kc), channel_id=1, source_target_pairs={{4,8},{5,9},{12,16},{13,17},{20,24},{21,25}} | collective-permute-start | bytes 811016 | tf_op jit(solution)/shard_map/ppermute | solution.py:50
  13.7 11.2 %collective-permute-start.6 = (bf16[264,512]{1,0:T(8,128)(2,1)S(1)}, bf16[264,512]{1,0:T(8,128)(2,1)S(1)}, u32[]{:S(2)}, u32[]{:S(2)}) collective-permute-start(bf16[264,512]{1,0:T(8,128)(2,1)S(1)} %collective-permute-done.5.ka), channel_id=1, source_target_pairs={{0,2},{1,3},{2,4},{3,5},{4,6},{5,7},{8,10},{9,11},{10,12},{11,13},... | collective-permute-start | bytes 811016 | tf_op jit(solution)/shard_map/ppermute | solution.py:45
  15.0 13.8 %collective-permute-start.9 = (bf16[256,512]{1,0:T(8,128)(2,1)S(1)}, bf16[256,512]{1,0:T(8,128)(2,1)S(1)}, u32[]{:S(2)}, u32[]{:S(2)}) collective-permute-start(bf16[256,512]{1,0:T(8,128)(2,1)S(1)} %pad_maximum_fusion.2.vc), channel_id=1, source_target_pairs={{4,8},{5,9},{12,16},{13,17},{20,24},{21,25}} | collective-permute-start | bytes 786440 | tf_op jit(solution)/shard_map/ppermute | solution.py:50
  19.3 10.8 %collective-permute-start.8 = (bf16[256,512]{1,0:T(8,128)(2,1)S(1)}, bf16[256,512]{1,0:T(8,128)(2,1)S(1)}, u32[]{:S(2)}, u32[]{:S(2)}) collective-permute-start(bf16[256,512]{1,0:T(8,128)(2,1)S(1)} %collective-permute-done.3.va), channel_id=1, source_target_pairs={{0,2},{1,3},{2,4},{3,5},{4,6},{5,7},{8,10},{9,11},{10,12},{11,13},... | collective-permute-start | bytes 786440 | tf_op jit(solution)/shard_map/ppermute | solution.py:45
  26.0 12.9 %collective-permute-start.10 = (bf16[256,512]{1,0:T(8,128)(2,1)S(1)}, bf16[256,512]{1,0:T(8,128)(2,1)S(1)}, u32[]{:S(2)}, u32[]{:S(2)}) collective-permute-start(bf16[256,512]{1,0:T(8,128)(2,1)S(1)} %get-tuple-element.47), channel_id=1, source_target_pairs={{2,0},{3,1},{4,2},{5,3},{6,4},{7,5},{8,6},{9,7},{10,8},{11,9},{12,... | collective-permute-start | bytes 786440 | tf_op jit(solution)/shard_map/ppermute | solution.py:34
  31.7 13.1 %collective-permute-start.12 = (bf16[256,512]{1,0:T(8,128)(2,1)S(1)}, bf16[256,512]{1,0:T(8,128)(2,1)S(1)}, u32[]{:S(2)}, u32[]{:S(2)}) collective-permute-start(bf16[256,512]{1,0:T(8,128)(2,1)S(1)} %get-tuple-element.51), channel_id=1, source_target_pairs={{2,0},{3,1},{4,2},{5,3},{6,4},{7,5},{8,6},{9,7},{10,8},{11,9},{12,... | collective-permute-start | bytes 786440 | tf_op jit(solution)/shard_map/ppermute | solution.py:34
  39.0 12.3 %collective-permute-start.16 = (bf16[256,512]{1,0:T(8,128)(2,1)S(1)}, bf16[256,512]{1,0:T(8,128)(2,1)S(1)}, u32[]{:S(2)}, u32[]{:S(2)}) collective-permute-start(bf16[256,512]{1,0:T(8,128)(2,1)S(1)} %merge.2), channel_id=1, source_target_pairs={{2,0},{3,1},{4,2},{5,3},{6,4},{7,5},{8,6},{9,7},{10,8},{11,9},{12,... | collective-permute-start | bytes 786440 | tf_op jit(solution)/shard_map/ppermute | solution.py:34
  41.3 13.7 %collective-permute-start.14 = (f32[128,512]{1,0:T(8,128)S(1)}, f32[128,512]{1,0:T(8,128)S(1)}, u32[]{:S(2)}, u32[]{:S(2)}) collective-permute-start(f32[128,512]{1,0:T(8,128)S(1)} %slice.22), channel_id=1, source_target_pairs={{0,1},{1,0},{2,3},{3,2},{4,5},{5,4},{6,7},{7,6},{8,9},{9,8},{10,11... | collective-permute-start | bytes 786440 | tf_op jit(solution)/shard_map/ppermute | solution.py:28
  41.4 10.1 %collective-permute-start.11 = (bf16[128,1024]{1,0:T(8,128)(2,1)S(1)}, bf16[128,1024]{1,0:T(8,128)(2,1)S(1)}, u32[]{:S(2)}, u32[]{:S(2)}) collective-permute-start(bf16[128,1024]{1,0:T(8,128)(2,1)S(1)} %get-tuple-element.48), channel_id=1, source_target_pairs={{0,1},{1,0},{2,3},{3,2},{4,5},{5,4},{6,7},{7,6},{8,9},{9,8},{10,11... | collective-permute-start | bytes 786440 | tf_op jit(solution)/shard_map/ppermute | solution.py:28
  45.0 10.0 %collective-permute-start.15 = (bf16[128,512]{1,0:T(8,128)(2,1)S(1)}, bf16[128,512]{1,0:T(8,128)(2,1)S(1)}, u32[]{:S(2)}, u32[]{:S(2)}) collective-permute-start(bf16[128,512]{1,0:T(8,128)(2,1)S(1)} %get-tuple-element.62), channel_id=1, source_target_pairs={{2,1},{3,0},{4,3},{5,2},{6,5},{7,4},{8,7},{9,6},{10,9},{11,8},{12,... | collective-permute-start | bytes 393224 | tf_op jit(solution)/shard_map/ppermute | solution.py:40
  46.9 11.3 %collective-permute-start.13 = (bf16[128,512]{1,0:T(8,128)(2,1)S(1)}, bf16[128,512]{1,0:T(8,128)(2,1)S(1)}, u32[]{:S(2)}, u32[]{:S(2)}) collective-permute-start(bf16[128,512]{1,0:T(8,128)(2,1)S(1)} %get-tuple-element.61), channel_id=1, source_target_pairs={{2,0},{3,1},{4,2},{5,3},{6,4},{7,5},{8,6},{9,7},{10,8},{11,9},{12,... | collective-permute-start | bytes 393224 | tf_op jit(solution)/shard_map/ppermute | solution.py:34
  51.4 1.4 %collective-permute-start.17 = (bf16[128,512]{1,0:T(8,128)(2,1)S(1)}, bf16[128,512]{1,0:T(8,128)(2,1)S(1)}, u32[]{:S(2)}, u32[]{:S(2)}) collective-permute-start(bf16[128,512]{1,0:T(8,128)(2,1)S(1)} %slice.29), channel_id=1, source_target_pairs={{0,1},{1,0},{2,3},{3,2},{4,5},{5,4},{6,7},{7,6},{8,9},{9,8},{10,11... | collective-permute-start | bytes 393224 | tf_op jit(solution)/shard_map/ppermute | solution.py:28

commit v10 on v9

--- a/solution.py
+++ b/solution.py
@@ -132,22 +132,28 @@
     los = [first_keys(core, lo_all, count, h, tok) for h in range(2)]
     blocks = WINDOW // tok + 1
 
-    def step(g, _):
-        for h in range(2):
-            near = range(h + FAR, h + blocks)
-            s = dot(keys_of(core, (None, ka, kc), near, g, tok), qs[g, h], NT)
-            dp = dot(keys_of(core, (None, va, vc), near, g, tok), gs[g, h], NT)
-            total = jnp.zeros((8, 2 * tok), jnp.float32)
-            mean = jnp.zeros((8, 2 * tok), jnp.float32)
-            for jj in range(FAR, blocks):
-                _, w = weights_of(cut(s, jj - FAR, tok), los[h], jj, jj == blocks - 1, tok)
-                total = total + fold(w)
-                mean = mean + fold(w * cut(dp, jj - FAR, tok))
-            tot[g, pl.ds(8 * h, 8), :] = total
-            term[g, pl.ds(8 * h, 8), :] = mean
-        return 0
-
-    lax.fori_loop(0, groups, step, 0, unroll=True)
+    def products(g, h):
+        near = range(h + FAR, h + blocks)
+        return (
+            dot(keys_of(core, (None, ka, kc), near, g, tok), qs[g, h], NT),
+            dot(keys_of(core, (None, va, vc), near, g, tok), gs[g, h], NT),
+        )
+
+    def weigh(g, h, ready):
+        s, dp = ready
+        total = jnp.zeros((8, 2 * tok), jnp.float32)
+        mean = jnp.zeros((8, 2 * tok), jnp.float32)
+        for jj in range(FAR, blocks):
+            _, w = weights_of(cut(s, jj - FAR, tok), los[h], jj, jj == blocks - 1, tok)
+            total = total + fold(w)
+            mean = mean + fold(w * cut(dp, jj - FAR, tok))
+        return total, mean
+
+    def finish(g, h, held):
+        tot[g, pl.ds(8 * h, 8), :] = held[0]
+        term[g, pl.ds(8 * h, 8), :] = held[1]
+
+    in_turn(groups, products, weigh, finish)
 
 
 def in_turn(groups, products, weigh, finish):

time: 59.4 us -> 59.4 us (level)
  no operation moved by 1% of the time
where the time goes in v10:
time: 59.4 us; the launch traced here: 59 us
  starting transfers between devices  23.9 us (40%)
  waiting for transfers between devices  21.2 us (36%)
  Pallas kernels  8.34 us (14%)
  other arithmetic  2.61 us (4%)
  local copies, waits for them, and re-layouts  1.96 us (3%)
  between operations  0.98 us (2%)
    ppermute x6, starting transfers between devices, hop(): lax.ppermute(x, AXES, [(i, i + by) for i in range(n) if 0 <= i + by < n])  16.7 us
    ppermute x6, waiting for transfers between devices, hop(): lax.ppermute(x, AXES, [(i, i + by) for i in range(n) if 0 <= i + by < n])  14.8 us
    pallas_call x7, Pallas kernels, call(): pl.pallas_call(functools.partial(body, tok, groups), in_specs=[pl.BlockSp...  8.34 us
    ppermute x2, waiting for transfers between devices, forward(): lax.ppermute(x, AXES, [(i, i + 2) for i in range(n) if i % row < row - 2])  4.44 us
    ppermute x2, starting transfers between devices, forward(): lax.ppermute(x, AXES, [(i, i + 2) for i in range(n) if i % row < row - 2])  2.56 us
    concatenate x3, other arithmetic, place(): return jnp.concatenate([first, second], 1)  2.29 us
    ppermute x1, starting transfers between devices, cross(): lax.ppermute(x, AXES, [(i, (i ^ 1) + by) for i in range(n) if 0 <= i + by...  1.92 us
    ppermute x7, starting transfers between devices, swap(): return lax.ppermute(x, AXES, [(i, i ^ 1) for i in range(n)])  1.38 us
  transfers between devices with their start and end apart: 18, of which 10 were waited for; matrix products, arithmetic and copies ran while one was open for 5% of the time, Pallas kernels for 14%

profile of v10, /device:TPU:26, one launch (start us, length us, event | category | flops | bytes accessed | tf_op | source)
XLA Modules:
  0.0 59.0 jit_solution(328251705275111589)
XLA Ops:
  1.3 1.0 %constant_dynamic-slice_fusion.5 = bf16[128,512]{1,0:T(8,128)(2,1)S(1)} fusion(bf16[128,1024]{1,0:T(8,128)(2,1)} %param.6, s32[]{:T(128)S(6)} %select_n.43), kind=kLoop, calls=%fused_computation.22 | loop fusion | bytes 262148 | tf_op jit(solution)/shard_map/dynamic_slice | solution.py:321
  2.5 3.1 %collective-permute-start.5 = (bf16[264,512]{1,0:T(8,128)(2,1)S(1)}, bf16[264,512]{1,0:T(8,128)(2,1)S(1)}, u32[]{:S(2)}, u32[]{:S(2)}) collective-permute-start(bf16[264,512]{1,0:T(8,128)(2,1)S(1)} %fusion.1.kc), channel_id=1, source_target_pairs={{0,2},{1,3},{2,4},{3,5},{4,6},{5,7},{6,8},{7,9},{8,10},{9,11},{10,... | collective-permute-start | bytes 811016 | tf_op jit(solution)/shard_map/ppermute | solution.py:34
  5.8 0.8 %copy-done.2 = bf16[128,1024]{1,0:T(8,128)(2,1)S(1)} copy-done((bf16[128,1024]{1,0:T(8,128)(2,1)S(1)}, bf16[128,1024]{1,0:T(8,128)(2,1)}, u32[]{:S(2)}) %copy-start.2) | copy-done | bytes 262168
  6.7 3.5 %collective-permute-start.3 = (bf16[256,512]{1,0:T(8,128)(2,1)S(1)}, bf16[256,512]{1,0:T(8,128)(2,1)S(1)}, u32[]{:S(2)}, u32[]{:S(2)}) collective-permute-start(bf16[256,512]{1,0:T(8,128)(2,1)S(1)} %pad_maximum_fusion.2.vc), channel_id=1, source_target_pairs={{0,2},{1,3},{2,4},{3,5},{4,6},{5,7},{6,8},{7,9},{8,10},{9,11},{10,... | collective-permute-start | bytes 786440 | tf_op jit(solution)/shard_map/ppermute | solution.py:34
  10.9 2.8 %collective-permute-done.5.ka = bf16[264,512]{1,0:T(8,128)(2,1)S(1)} collective-permute-done((bf16[264,512]{1,0:T(8,128)(2,1)S(1)}, bf16[264,512]{1,0:T(8,128)(2,1)S(1)}, u32[]{:S(2)}, u32[]{:S(2)}) %collective-permute-start.5) | collective-permute-done | bytes 270368 | tf_op jit(solution)/shard_map/ppermute | solution.py:34
  13.7 1.3 %collective-permute-start.6 = (bf16[264,512]{1,0:T(8,128)(2,1)S(1)}, bf16[264,512]{1,0:T(8,128)(2,1)S(1)}, u32[]{:S(2)}, u32[]{:S(2)}) collective-permute-start(bf16[264,512]{1,0:T(8,128)(2,1)S(1)} %collective-permute-done.5.ka), channel_id=1, source_target_pairs={{0,2},{1,3},{2,4},{3,5},{4,6},{5,7},{8,10},{9,11},{10,12},{11,13},... | collective-permute-start | bytes 811016 | tf_op jit(solution)/shard_map/ppermute | solution.py:45
  16.1 3.2 %collective-permute-done.3.va = bf16[256,512]{1,0:T(8,128)(2,1)S(1)} collective-permute-done((bf16[256,512]{1,0:T(8,128)(2,1)S(1)}, bf16[256,512]{1,0:T(8,128)(2,1)S(1)}, u32[]{:S(2)}, u32[]{:S(2)}) %collective-permute-start.3) | collective-permute-done | bytes 262176 | tf_op jit(solution)/shard_map/ppermute | solution.py:34
  19.3 1.3 %collective-permute-start.8 = (bf16[256,512]{1,0:T(8,128)(2,1)S(1)}, bf16[256,512]{1,0:T(8,128)(2,1)S(1)}, u32[]{:S(2)}, u32[]{:S(2)}) collective-permute-start(bf16[256,512]{1,0:T(8,128)(2,1)S(1)} %collective-permute-done.3.va), channel_id=1, source_target_pairs={{0,2},{1,3},{2,4},{3,5},{4,6},{5,7},{8,10},{9,11},{10,12},{11,13},... | collective-permute-start | bytes 786440 | tf_op jit(solution)/shard_map/ppermute | solution.py:45
  20.6 1.1 %near_sums.1 = (f32[4,16,256]{2,1,0:T(8,128)S(1)}, f32[4,16,256]{2,1,0:T(8,128)S(1)}) custom-call(s32[1]{0:T(128)} %bitcast.core_ref, s32[8,128]{1,0:T(8,128)S(1)} %get-tuple-element.35.lo_ref, bf16[4,2,256,128]{3,2,1,0:T(8,128)(2,1)S(1)} %get-tuple-element.36.qs, bf16[4,2,256,128]{3,2,1,0:T(8,128)(2,1)S(1)} %get-tuple-element.37.gs, ...), custom_call_target="tpu_custom_call" | custom-call | tf_op jit(solution)/shard_map/near_sums/pallas_call | solution.py:296
  21.8 3.1 %collective-permute-done.6.kb = bf16[264,512]{1,0:T(8,128)(2,1)S(1)} collective-permute-done((bf16[264,512]{1,0:T(8,128)(2,1)S(1)}, bf16[264,512]{1,0:T(8,128)(2,1)S(1)}, u32[]{:S(2)}, u32[]{:S(2)}) %collective-permute-start.6) | collective-permute-done | bytes 270368 | tf_op jit(solution)/shard_map/ppermute | solution.py:45
  24.9 1.1 %far_values.1 = (bf16[256,512]{1,0:T(8,128)(2,1)S(1)}, f32[4,16,256]{2,1,0:T(8,128)S(1)}) custom-call(s32[1]{0:T(128)} %bitcast.core_ref, s32[8,128]{1,0:T(8,128)S(1)} %get-tuple-element.35.lo_ref, bf16[4,2,256,128]{3,2,1,0:T(8,128)(2,1)S(1)} %get-tuple-element.36.qs, bf16[4,2,256,128]{3,2,1,0:T(8,128)(2,1)S(1)} %get-tuple-element.37.gs, ...), custom_call_target="tpu_custom_call" | custom-call | tf_op jit(solution)/shard_map/far_values/pallas_call | solution.py:296
  26.0 2.8 %collective-permute-start.10 = (bf16[256,512]{1,0:T(8,128)(2,1)S(1)}, bf16[256,512]{1,0:T(8,128)(2,1)S(1)}, u32[]{:S(2)}, u32[]{:S(2)}) collective-permute-start(bf16[256,512]{1,0:T(8,128)(2,1)S(1)} %get-tuple-element.47), channel_id=1, source_target_pairs={{2,0},{3,1},{4,2},{5,3},{6,4},{7,5},{8,6},{9,7},{10,8},{11,9},{12,... | collective-permute-start | bytes 786440 | tf_op jit(solution)/shard_map/ppermute | solution.py:34
  28.8 1.3 %collective-permute-done.8.vb = bf16[256,512]{1,0:T(8,128)(2,1)S(1)} collective-permute-done((bf16[256,512]{1,0:T(8,128)(2,1)S(1)}, bf16[256,512]{1,0:T(8,128)(2,1)S(1)}, u32[]{:S(2)}, u32[]{:S(2)}) %collective-permute-start.8) | collective-permute-done | bytes 262176 | tf_op jit(solution)/shard_map/ppermute | solution.py:45
  30.1 1.6 %far_keys.1 = (bf16[256,512]{1,0:T(8,128)(2,1)S(1)}, f32[4,16,256]{2,1,0:T(8,128)S(1)}) custom-call(s32[1]{0:T(128)} %bitcast.core_ref, s32[8,128]{1,0:T(8,128)S(1)} %get-tuple-element.35.lo_ref, bf16[4,2,256,128]{3,2,1,0:T(8,128)(2,1)S(1)} %get-tuple-element.36.qs, bf16[4,2,256,128]{3,2,1,0:T(8,128)(2,1)S(1)} %get-tuple-element.37.gs, ...), custom_call_target="tpu_custom_call" | custom-call | tf_op jit(solution)/shard_map/far_keys/pallas_call | solution.py:296
  31.7 3.2 %collective-permute-start.12 = (bf16[256,512]{1,0:T(8,128)(2,1)S(1)}, bf16[256,512]{1,0:T(8,128)(2,1)S(1)}, u32[]{:S(2)}, u32[]{:S(2)}) collective-permute-start(bf16[256,512]{1,0:T(8,128)(2,1)S(1)} %get-tuple-element.51), channel_id=1, source_target_pairs={{2,0},{3,1},{4,2},{5,3},{6,4},{7,5},{8,6},{9,7},{10,8},{11,9},{12,... | collective-permute-start | bytes 786440 | tf_op jit(solution)/shard_map/ppermute | solution.py:34
  34.9 4.0 %near_grads.1 = (f32[256,512]{1,0:T(8,128)S(1)}, f32[256,512]{1,0:T(8,128)S(1)}, f32[256,512]{1,0:T(8,128)S(1)}, f32[256,512]{1,0:T(8,128)S(1)}, bf16[128,1024]{...) custom-call(s32[1]{0:T(128)} %bitcast.core_ref, s32[8,128]{1,0:T(8,128)S(1)} %get-tuple-element.35.lo_ref, ...), custom_call_target="tpu_custom_call" | custom-call | tf_op jit(solution)/shard_map/near_grads/pallas_call | solution.py:296
  39.0 2.2 %collective-permute-start.16 = (bf16[256,512]{1,0:T(8,128)(2,1)S(1)}, bf16[256,512]{1,0:T(8,128)(2,1)S(1)}, u32[]{:S(2)}, u32[]{:S(2)}) collective-permute-start(bf16[256,512]{1,0:T(8,128)(2,1)S(1)} %merge.2), channel_id=1, source_target_pairs={{2,0},{3,1},{4,2},{5,3},{6,4},{7,5},{8,6},{9,7},{10,8},{11,9},{12,... | collective-permute-start | bytes 786440 | tf_op jit(solution)/shard_map/ppermute | solution.py:34
  41.9 3.0 %collective-permute-done.12.came = bf16[256,512]{1,0:T(8,128)(2,1)S(1)} collective-permute-done((bf16[256,512]{1,0:T(8,128)(2,1)S(1)}, bf16[256,512]{1,0:T(8,128)(2,1)S(1)}, u32[]{:S(2)}, u32[]{:S(2)}) %collective-permute-start.12) | collective-permute-done | bytes 262176 | tf_op jit(solution)/shard_map/ppermute | solution.py:34
  45.0 1.9 %collective-permute-start.15 = (bf16[128,512]{1,0:T(8,128)(2,1)S(1)}, bf16[128,512]{1,0:T(8,128)(2,1)S(1)}, u32[]{:S(2)}, u32[]{:S(2)}) collective-permute-start(bf16[128,512]{1,0:T(8,128)(2,1)S(1)} %get-tuple-element.62), channel_id=1, source_target_pairs={{2,1},{3,0},{4,3},{5,2},{6,5},{7,4},{8,7},{9,6},{10,9},{11,8},{12,... | collective-permute-start | bytes 393224 | tf_op jit(solution)/shard_map/ppermute | solution.py:40
  46.9 1.9 %collective-permute-start.13 = (bf16[128,512]{1,0:T(8,128)(2,1)S(1)}, bf16[128,512]{1,0:T(8,128)(2,1)S(1)}, u32[]{:S(2)}, u32[]{:S(2)}) collective-permute-start(bf16[128,512]{1,0:T(8,128)(2,1)S(1)} %get-tuple-element.61), channel_id=1, source_target_pairs={{2,0},{3,1},{4,2},{5,3},{6,4},{7,5},{8,6},{9,7},{10,8},{11,9},{12,... | collective-permute-start | bytes 393224 | tf_op jit(solution)/shard_map/ppermute | solution.py:34
  48.8 2.5 %collective-permute-done.16 = bf16[256,512]{1,0:T(8,128)(2,1)S(1)} collective-permute-done((bf16[256,512]{1,0:T(8,128)(2,1)S(1)}, bf16[256,512]{1,0:T(8,128)(2,1)S(1)}, u32[]{:S(2)}, u32[]{:S(2)}) %collective-permute-start.16) | collective-permute-done | bytes 262176 | tf_op jit(solution)/shard_map/ppermute | solution.py:34
  51.5 0.8 %pad_maximum_fusion.1 = bf16[128,2048]{1,0:T(8,128)(2,1)} fusion(bf16[128,1024]{1,0:T(8,128)(2,1)S(1)} %get-tuple-element.58, bf16[128,1024]{1,0:T(8,128)(2,1)S(1)} %get-tuple-element.57), kind=kLoop, calls=%fused_computation.3 | loop fusion | flops 1048576 | bytes 1048576 | tf_op jit(solution)/shard_map/concatenate | solution.py:371
  53.6 1.4 %collective-permute-done.15 = bf16[128,512]{1,0:T(8,128)(2,1)S(1)} collective-permute-done((bf16[128,512]{1,0:T(8,128)(2,1)S(1)}, bf16[128,512]{1,0:T(8,128)(2,1)S(1)}, u32[]{:S(2)}, u32[]{:S(2)}) %collective-permute-start.15) | collective-permute-done | bytes 131104 | tf_op jit(solution)/shard_map/ppermute | solution.py:40
  54.9 3.2 %collective-permute-done.13 = bf16[128,512]{1,0:T(8,128)(2,1)S(1)} collective-permute-done((bf16[128,512]{1,0:T(8,128)(2,1)S(1)}, bf16[128,512]{1,0:T(8,128)(2,1)S(1)}, u32[]{:S(2)}, u32[]{:S(2)}) %collective-permute-start.13) | collective-permute-done | bytes 131104 | tf_op jit(solution)/shard_map/ppermute | solution.py:34
  (46 shorter events, 5.8 us)
Async XLA Ops:
  0.6 1.8 %collective-permute-start = (bf16[128,1024]{1,0:T(8,128)(2,1)}, bf16[128,1024]{1,0:T(8,128)(2,1)S(1)}, u32[]{:S(2)}, u32[]{:S(2)}) collective-permute-start(bf16[128,1024]{1,0:T(8,128)(2,1)} %param.6), channel_id=1, source_target_pairs={{0,1},{1,0},{2,3},{3,2},{4,5},{5,4},{6,7},{7,6},{8,9},{9,8},{10,11... | collective-permute-start | bytes 786440 | tf_op jit(solution)/shard_map/ppermute | solution.py:28
  0.7 1.7 %collective-permute-start.1 = (s32[128]{0:T(128)}, s32[128]{0:T(128)S(1)}, u32[]{:S(2)}, u32[]{:S(2)}) collective-permute-start(s32[128]{0:T(128)} %param.9), channel_id=1, source_target_pairs={{0,1},{1,0},{2,3},{3,2},{4,5},{5,4},{6,7},{7,6},{8,9},{9,8},{10,11... | collective-permute-start | bytes 1544 | tf_op jit(solution)/shard_map/ppermute | solution.py:28
  1.2 5.4 %collective-permute-start.2 = (bf16[128,1024]{1,0:T(8,128)(2,1)}, bf16[128,1024]{1,0:T(8,128)(2,1)S(1)}, u32[]{:S(2)}, u32[]{:S(2)}) collective-permute-start(bf16[128,1024]{1,0:T(8,128)(2,1)} %param.7), channel_id=1, source_target_pairs={{0,1},{1,0},{2,3},{3,2},{4,5},{5,4},{6,7},{7,6},{8,9},{9,8},{10,11... | collective-permute-start | bytes 786440 | tf_op jit(solution)/shard_map/ppermute | solution.py:28
  1.3 1.2 %copy-start.3 = (s32[128]{0:T(128)S(1)}, s32[128]{0:T(128)}, u32[]{:S(2)}) copy-start(s32[128]{0:T(128)} %param.9) | copy-start | bytes 1540
  1.3 4.3 %copy-start = (bf16[128,2048]{1,0:T(8,128)(2,1)S(1)}, bf16[128,2048]{1,0:T(8,128)(2,1)}, u32[]{:S(2)}) copy-start(bf16[128,2048]{1,0:T(8,128)(2,1)} %q) | copy-start | bytes 1572868
  1.3 4.3 %copy-start.1 = (bf16[128,2048]{1,0:T(8,128)(2,1)S(1)}, bf16[128,2048]{1,0:T(8,128)(2,1)}, u32[]{:S(2)}) copy-start(bf16[128,2048]{1,0:T(8,128)(2,1)} %go) | copy-start | bytes 1572868
  2.5 11.2 %collective-permute-start.5 = (bf16[264,512]{1,0:T(8,128)(2,1)S(1)}, bf16[264,512]{1,0:T(8,128)(2,1)S(1)}, u32[]{:S(2)}, u32[]{:S(2)}) collective-permute-start(bf16[264,512]{1,0:T(8,128)(2,1)S(1)} %fusion.1.kc), channel_id=1, source_target_pairs={{0,2},{1,3},{2,4},{3,5},{4,6},{5,7},{6,8},{7,9},{8,10},{9,11},{10,... | collective-permute-start | bytes 811016 | tf_op jit(solution)/shard_map/ppermute | solution.py:34
  5.7 1.0 %copy-start.2 = (bf16[128,1024]{1,0:T(8,128)(2,1)S(1)}, bf16[128,1024]{1,0:T(8,128)(2,1)}, u32[]{:S(2)}) copy-start(bf16[128,1024]{1,0:T(8,128)(2,1)} %param.7) | copy-start | bytes 786436
  5.7 10.0 %collective-permute-start.4 = (bf16[256,1024]{1,0:T(8,128)(2,1)S(1)}, bf16[256,1024]{1,0:T(8,128)(2,1)S(1)}, u32[]{:S(2)}, u32[]{:S(2)}) collective-permute-start(bf16[256,1024]{1,0:T(8,128)(2,1)S(1)} %pad_maximum_fusion), channel_id=1, source_target_pairs={{0,1},{1,0},{2,3},{3,2},{4,5},{5,4},{6,7},{7,6},{8,9},{9,8},{10,11... | collective-permute-start | bytes 1572872 | tf_op jit(solution)/shard_map/ppermute | solution.py:28
  6.7 12.6 %collective-permute-start.3 = (bf16[256,512]{1,0:T(8,128)(2,1)S(1)}, bf16[256,512]{1,0:T(8,128)(2,1)S(1)}, u32[]{:S(2)}, u32[]{:S(2)}) collective-permute-start(bf16[256,512]{1,0:T(8,128)(2,1)S(1)} %pad_maximum_fusion.2.vc), channel_id=1, source_target_pairs={{0,2},{1,3},{2,4},{3,5},{4,6},{5,7},{6,8},{7,9},{8,10},{9,11},{10,... | collective-permute-start | bytes 786440 | tf_op jit(solution)/shard_map/ppermute | solution.py:34
  10.2 11.6 %collective-permute-start.7 = (bf16[264,512]{1,0:T(8,128)(2,1)S(1)}, bf16[264,512]{1,0:T(8,128)(2,1)S(1)}, u32[]{:S(2)}, u32[]{:S(2)}) collective-permute-start(bf16[264,512]{1,0:T(8,128)(2,1)S(1)} %fusion.1.kc), channel_id=1, source_target_pairs={{4,8},{5,9},{12,16},{13,17},{20,24},{21,25}} | collective-permute-start | bytes 811016 | tf_op jit(solution)/shard_map/ppermute | solution.py:50
  13.7 11.2 %collective-permute-start.6 = (bf16[264,512]{1,0:T(8,128)(2,1)S(1)}, bf16[264,512]{1,0:T(8,128)(2,1)S(1)}, u32[]{:S(2)}, u32[]{:S(2)}) collective-permute-start(bf16[264,512]{1,0:T(8,128)(2,1)S(1)} %collective-permute-done.5.ka), channel_id=1, source_target_pairs={{0,2},{1,3},{2,4},{3,5},{4,6},{5,7},{8,10},{9,11},{10,12},{11,13},... | collective-permute-start | bytes 811016 | tf_op jit(solution)/shard_map/ppermute | solution.py:45
  15.0 13.8 %collective-permute-start.9 = (bf16[256,512]{1,0:T(8,128)(2,1)S(1)}, bf16[256,512]{1,0:T(8,128)(2,1)S(1)}, u32[]{:S(2)}, u32[]{:S(2)}) collective-permute-start(bf16[256,512]{1,0:T(8,128)(2,1)S(1)} %pad_maximum_fusion.2.vc), channel_id=1, source_target_pairs={{4,8},{5,9},{12,16},{13,17},{20,24},{21,25}} | collective-permute-start | bytes 786440 | tf_op jit(solution)/shard_map/ppermute | solution.py:50
  19.3 10.8 %collective-permute-start.8 = (bf16[256,512]{1,0:T(8,128)(2,1)S(1)}, bf16[256,512]{1,0:T(8,128)(2,1)S(1)}, u32[]{:S(2)}, u32[]{:S(2)}) collective-permute-start(bf16[256,512]{1,0:T(8,128)(2,1)S(1)} %collective-permute-done.3.va), channel_id=1, source_target_pairs={{0,2},{1,3},{2,4},{3,5},{4,6},{5,7},{8,10},{9,11},{10,12},{11,13},... | collective-permute-start | bytes 786440 | tf_op jit(solution)/shard_map/ppermute | solution.py:45
  26.0 12.9 %collective-permute-start.10 = (bf16[256,512]{1,0:T(8,128)(2,1)S(1)}, bf16[256,512]{1,0:T(8,128)(2,1)S(1)}, u32[]{:S(2)}, u32[]{:S(2)}) collective-permute-start(bf16[256,512]{1,0:T(8,128)(2,1)S(1)} %get-tuple-element.47), channel_id=1, source_target_pairs={{2,0},{3,1},{4,2},{5,3},{6,4},{7,5},{8,6},{9,7},{10,8},{11,9},{12,... | collective-permute-start | bytes 786440 | tf_op jit(solution)/shard_map/ppermute | solution.py:34
  31.7 13.1 %collective-permute-start.12 = (bf16[256,512]{1,0:T(8,128)(2,1)S(1)}, bf16[256,512]{1,0:T(8,128)(2,1)S(1)}, u32[]{:S(2)}, u32[]{:S(2)}) collective-permute-start(bf16[256,512]{1,0:T(8,128)(2,1)S(1)} %get-tuple-element.51), channel_id=1, source_target_pairs={{2,0},{3,1},{4,2},{5,3},{6,4},{7,5},{8,6},{9,7},{10,8},{11,9},{12,... | collective-permute-start | bytes 786440 | tf_op jit(solution)/shard_map/ppermute | solution.py:34
  39.0 12.3 %collective-permute-start.16 = (bf16[256,512]{1,0:T(8,128)(2,1)S(1)}, bf16[256,512]{1,0:T(8,128)(2,1)S(1)}, u32[]{:S(2)}, u32[]{:S(2)}) collective-permute-start(bf16[256,512]{1,0:T(8,128)(2,1)S(1)} %merge.2), channel_id=1, source_target_pairs={{2,0},{3,1},{4,2},{5,3},{6,4},{7,5},{8,6},{9,7},{10,8},{11,9},{12,... | collective-permute-start | bytes 786440 | tf_op jit(solution)/shard_map/ppermute | solution.py:34
  41.3 13.7 %collective-permute-start.14 = (f32[128,512]{1,0:T(8,128)S(1)}, f32[128,512]{1,0:T(8,128)S(1)}, u32[]{:S(2)}, u32[]{:S(2)}) collective-permute-start(f32[128,512]{1,0:T(8,128)S(1)} %slice.22), channel_id=1, source_target_pairs={{0,1},{1,0},{2,3},{3,2},{4,5},{5,4},{6,7},{7,6},{8,9},{9,8},{10,11... | collective-permute-start | bytes 786440 | tf_op jit(solution)/shard_map/ppermute | solution.py:28
  41.4 10.1 %collective-permute-start.11 = (bf16[128,1024]{1,0:T(8,128)(2,1)S(1)}, bf16[128,1024]{1,0:T(8,128)(2,1)S(1)}, u32[]{:S(2)}, u32[]{:S(2)}) collective-permute-start(bf16[128,1024]{1,0:T(8,128)(2,1)S(1)} %get-tuple-element.48), channel_id=1, source_target_pairs={{0,1},{1,0},{2,3},{3,2},{4,5},{5,4},{6,7},{7,6},{8,9},{9,8},{10,11... | collective-permute-start | bytes 786440 | tf_op jit(solution)/shard_map/ppermute | solution.py:28
  45.0 10.0 %collective-permute-start.15 = (bf16[128,512]{1,0:T(8,128)(2,1)S(1)}, bf16[128,512]{1,0:T(8,128)(2,1)S(1)}, u32[]{:S(2)}, u32[]{:S(2)}) collective-permute-start(bf16[128,512]{1,0:T(8,128)(2,1)S(1)} %get-tuple-element.62), channel_id=1, source_target_pairs={{2,1},{3,0},{4,3},{5,2},{6,5},{7,4},{8,7},{9,6},{10,9},{11,8},{12,... | collective-permute-start | bytes 393224 | tf_op jit(solution)/shard_map/ppermute | solution.py:40
  46.9 11.3 %collective-permute-start.13 = (bf16[128,512]{1,0:T(8,128)(2,1)S(1)}, bf16[128,512]{1,0:T(8,128)(2,1)S(1)}, u32[]{:S(2)}, u32[]{:S(2)}) collective-permute-start(bf16[128,512]{1,0:T(8,128)(2,1)S(1)} %get-tuple-element.61), channel_id=1, source_target_pairs={{2,0},{3,1},{4,2},{5,3},{6,4},{7,5},{8,6},{9,7},{10,8},{11,9},{12,... | collective-permute-start | bytes 393224 | tf_op jit(solution)/shard_map/ppermute | solution.py:34
  51.4 1.4 %collective-permute-start.17 = (bf16[128,512]{1,0:T(8,128)(2,1)S(1)}, bf16[128,512]{1,0:T(8,128)(2,1)S(1)}, u32[]{:S(2)}, u32[]{:S(2)}) collective-permute-start(bf16[128,512]{1,0:T(8,128)(2,1)S(1)} %slice.29), channel_id=1, source_target_pairs={{0,1},{1,0},{2,3},{3,2},{4,5},{5,4},{6,7},{7,6},{8,9},{9,8},{10,11... | collective-permute-start | bytes 393224 | tf_op jit(solution)/shard_map/ppermute | solution.py:28

commit v11 on v10

--- a/solution.py
+++ b/solution.py
@@ -291,6 +291,12 @@
     out[...] = (mine[...] + came[...].astype(jnp.float32)).astype(out.dtype)
 
 
+def merge_halves(tok, groups, core_ref, mine, came, own, other):
+    for r, out in enumerate((own, other)):
+        rows = pl.ds(r * tok, tok)
+        out[...] = (mine[rows, :] + came[rows, :].astype(jnp.float32)).astype(out.dtype)
+
+
 def call(body, tok, groups, args, outs, scratch=()):
     vmem = pl.BlockSpec(memory_space=pltpu.VMEM)
     return pl.pallas_call(
@@ -361,10 +367,10 @@
         [pltpu.VMEM((groups, 2, 2 * tok, HEAD_DIM), bf16)])
     (dv_out,) = call(merge, tok, groups, (core_arr, dva, cv), [kv_b])
     dv = hop(dv_out, -1)
-    (dk_out,) = call(merge, tok, groups, (core_arr, dka, ck), [kv_b])
+    dk_own, dk_other = call(merge_halves, tok, groups, (core_arr, dka, ck), [((tok, half), bf16)] * 2)
     dkc, dq1, _ = lax.optimization_barrier((dkc, dq1, dv_out))
-    dk_same = hop(dk_out[:tok], -1)
-    dk_cross = cross(dk_out[tok:], -1)
+    dk_same = hop(dk_own, -1)
+    dk_cross = cross(dk_other, -1)
     def place(mine, other):
         first = jnp.where(core == 0, mine, other)
         second = jnp.where(core == 0, other, mine)

time: 59.4 us -> 66 us (1.11)
  starting transfers between devices: 23.9 us -> 29.9 us
    ppermute x6, starting transfers between devices: 16.7 us -> 22.6 us  [hop(): lax.ppermute(x, AXES, [(i, i + by) for i in range(n) if 0 <= i + by < n])]
    ppermute x6, waiting for transfers between devices: 14.8 us -> 19.1 us  [hop(): lax.ppermute(x, AXES, [(i, i + by) for i in range(n) if 0 <= i + by < n])]
    ppermute x2, waiting for transfers between devices: 4.44 us -> 0.73 us  [forward(): lax.ppermute(x, AXES, [(i, i + 2) for i in range(n) if i % row < row - 2])]
  transfers between devices with their start and end apart: 18 -> 18, of which waited for: 10 -> 10; matrix products, arithmetic and copies ran while one was open for 5% -> 4% of each run, Pallas kernels for 14% -> 13%
where the time goes in v11:
time: 66 us; the launch traced here: 65.5 us
  starting transfers between devices  29.9 us (45%)
  waiting for transfers between devices  21.8 us (33%)
  Pallas kernels  8.35 us (13%)
  other arithmetic  2.58 us (4%)
  local copies, waits for them, and re-layouts  1.94 us (3%)
  between operations  0.98 us (1%)
    ppermute x6, starting transfers between devices, hop(): lax.ppermute(x, AXES, [(i, i + by) for i in range(n) if 0 <= i + by < n])  22.6 us
    ppermute x6, waiting for transfers between devices, hop(): lax.ppermute(x, AXES, [(i, i + by) for i in range(n) if 0 <= i + by < n])  19.1 us
    pallas_call x7, Pallas kernels, call(): pl.pallas_call(functools.partial(body, tok, groups), in_specs=[pl.BlockSp...  8.35 us
    ppermute x2, starting transfers between devices, forward(): lax.ppermute(x, AXES, [(i, i + 2) for i in range(n) if i % row < row - 2])  2.56 us
    concatenate x3, other arithmetic, place(): return jnp.concatenate([first, second], 1)  2.29 us
    ppermute x1, starting transfers between devices, cross(): lax.ppermute(x, AXES, [(i, (i ^ 1) + by) for i in range(n) if 0 <= i + by...  1.92 us
    ppermute x7, starting transfers between devices, swap(): return lax.ppermute(x, AXES, [(i, i ^ 1) for i in range(n)])  1.44 us
    ppermute x1, waiting for transfers between devices, cross(): lax.ppermute(x, AXES, [(i, (i ^ 1) + by) for i in range(n) if 0 <= i + by...  1.37 us
  transfers between devices with their start and end apart: 18, of which 10 were waited for; matrix products, arithmetic and copies ran while one was open for 4% of the time, Pallas kernels for 13%

profile of v11, /device:TPU:26, one launch (start us, length us, event | category | flops | bytes accessed | tf_op | source)
XLA Modules:
  0.0 65.5 jit_solution(3710253546138743720)
XLA Ops:
  1.3 1.0 %constant_dynamic-slice_fusion.5 = bf16[128,512]{1,0:T(8,128)(2,1)S(1)} fusion(bf16[128,1024]{1,0:T(8,128)(2,1)} %param.6, s32[]{:T(128)S(6)} %select_n.43), kind=kLoop, calls=%fused_computation.22 | loop fusion | bytes 262148 | tf_op jit(solution)/shard_map/dynamic_slice | solution.py:327
  2.5 3.1 %collective-permute-start.5 = (bf16[264,512]{1,0:T(8,128)(2,1)S(1)}, bf16[264,512]{1,0:T(8,128)(2,1)S(1)}, u32[]{:S(2)}, u32[]{:S(2)}) collective-permute-start(bf16[264,512]{1,0:T(8,128)(2,1)S(1)} %fusion.1.kc), channel_id=1, source_target_pairs={{0,2},{1,3},{2,4},{3,5},{4,6},{5,7},{6,8},{7,9},{8,10},{9,11},{10,... | collective-permute-start | bytes 811016 | tf_op jit(solution)/shard_map/ppermute | solution.py:34
  6.5 0.8 %copy-done.2 = bf16[128,1024]{1,0:T(8,128)(2,1)S(1)} copy-done((bf16[128,1024]{1,0:T(8,128)(2,1)S(1)}, bf16[128,1024]{1,0:T(8,128)(2,1)}, u32[]{:S(2)}) %copy-start.2) | copy-done | bytes 262168
  7.3 5.8 %collective-permute-done.5.ka = bf16[264,512]{1,0:T(8,128)(2,1)S(1)} collective-permute-done((bf16[264,512]{1,0:T(8,128)(2,1)S(1)}, bf16[264,512]{1,0:T(8,128)(2,1)S(1)}, u32[]{:S(2)}, u32[]{:S(2)}) %collective-permute-start.5) | collective-permute-done | bytes 270368 | tf_op jit(solution)/shard_map/ppermute | solution.py:34
  13.1 1.3 %collective-permute-start.6 = (bf16[264,512]{1,0:T(8,128)(2,1)S(1)}, bf16[264,512]{1,0:T(8,128)(2,1)S(1)}, u32[]{:S(2)}, u32[]{:S(2)}) collective-permute-start(bf16[264,512]{1,0:T(8,128)(2,1)S(1)} %collective-permute-done.5.ka), channel_id=1, source_target_pairs={{0,2},{1,3},{2,4},{3,5},{4,6},{5,7},{8,10},{9,11},{10,12},{11,13},... | collective-permute-start | bytes 811016 | tf_op jit(solution)/shard_map/ppermute | solution.py:45
  14.4 6.8 %collective-permute-start.3 = (bf16[256,512]{1,0:T(8,128)(2,1)S(1)}, bf16[256,512]{1,0:T(8,128)(2,1)S(1)}, u32[]{:S(2)}, u32[]{:S(2)}) collective-permute-start(bf16[256,512]{1,0:T(8,128)(2,1)S(1)} %pad_maximum_fusion.2.vc), channel_id=1, source_target_pairs={{0,2},{1,3},{2,4},{3,5},{4,6},{5,7},{6,8},{7,9},{8,10},{9,11},{10,... | collective-permute-start | bytes 786440 | tf_op jit(solution)/shard_map/ppermute | solution.py:34
  22.3 6.2 %collective-permute-done.3.va = bf16[256,512]{1,0:T(8,128)(2,1)S(1)} collective-permute-done((bf16[256,512]{1,0:T(8,128)(2,1)S(1)}, bf16[256,512]{1,0:T(8,128)(2,1)S(1)}, u32[]{:S(2)}, u32[]{:S(2)}) %collective-permute-start.3) | collective-permute-done | bytes 262176 | tf_op jit(solution)/shard_map/ppermute | solution.py:34
  28.5 1.3 %collective-permute-start.8 = (bf16[256,512]{1,0:T(8,128)(2,1)S(1)}, bf16[256,512]{1,0:T(8,128)(2,1)S(1)}, u32[]{:S(2)}, u32[]{:S(2)}) collective-permute-start(bf16[256,512]{1,0:T(8,128)(2,1)S(1)} %collective-permute-done.3.va), channel_id=1, source_target_pairs={{0,2},{1,3},{2,4},{3,5},{4,6},{5,7},{8,10},{9,11},{10,12},{11,13},... | collective-permute-start | bytes 786440 | tf_op jit(solution)/shard_map/ppermute | solution.py:45
  29.8 1.1 %near_sums.1 = (f32[4,16,256]{2,1,0:T(8,128)S(1)}, f32[4,16,256]{2,1,0:T(8,128)S(1)}) custom-call(s32[1]{0:T(128)} %bitcast.core_ref, s32[8,128]{1,0:T(8,128)S(1)} %get-tuple-element.37.lo_ref, bf16[4,2,256,128]{3,2,1,0:T(8,128)(2,1)S(1)} %get-tuple-element.38.qs, bf16[4,2,256,128]{3,2,1,0:T(8,128)(2,1)S(1)} %get-tuple-element.39.gs, ...), custom_call_target="tpu_custom_call" | custom-call | tf_op jit(solution)/shard_map/near_sums/pallas_call | solution.py:302
  30.9 1.1 %far_values.1 = (bf16[256,512]{1,0:T(8,128)(2,1)S(1)}, f32[4,16,256]{2,1,0:T(8,128)S(1)}) custom-call(s32[1]{0:T(128)} %bitcast.core_ref, s32[8,128]{1,0:T(8,128)S(1)} %get-tuple-element.37.lo_ref, bf16[4,2,256,128]{3,2,1,0:T(8,128)(2,1)S(1)} %get-tuple-element.38.qs, bf16[4,2,256,128]{3,2,1,0:T(8,128)(2,1)S(1)} %get-tuple-element.39.gs, ...), custom_call_target="tpu_custom_call" | custom-call | tf_op jit(solution)/shard_map/far_values/pallas_call | solution.py:302
  32.1 4.5 %collective-permute-start.10 = (bf16[256,512]{1,0:T(8,128)(2,1)S(1)}, bf16[256,512]{1,0:T(8,128)(2,1)S(1)}, u32[]{:S(2)}, u32[]{:S(2)}) collective-permute-start(bf16[256,512]{1,0:T(8,128)(2,1)S(1)} %get-tuple-element.49), channel_id=1, source_target_pairs={{2,0},{3,1},{4,2},{5,3},{6,4},{7,5},{8,6},{9,7},{10,8},{11,9},{12,... | collective-permute-start | bytes 786440 | tf_op jit(solution)/shard_map/ppermute | solution.py:34
  37.4 1.6 %far_keys.1 = (bf16[256,512]{1,0:T(8,128)(2,1)S(1)}, f32[4,16,256]{2,1,0:T(8,128)S(1)}) custom-call(s32[1]{0:T(128)} %bitcast.core_ref, s32[8,128]{1,0:T(8,128)S(1)} %get-tuple-element.37.lo_ref, bf16[4,2,256,128]{3,2,1,0:T(8,128)(2,1)S(1)} %get-tuple-element.38.qs, bf16[4,2,256,128]{3,2,1,0:T(8,128)(2,1)S(1)} %get-tuple-element.39.gs, ...), custom_call_target="tpu_custom_call" | custom-call | tf_op jit(solution)/shard_map/far_keys/pallas_call | solution.py:302
  39.0 2.2 %collective-permute-start.12 = (bf16[256,512]{1,0:T(8,128)(2,1)S(1)}, bf16[256,512]{1,0:T(8,128)(2,1)S(1)}, u32[]{:S(2)}, u32[]{:S(2)}) collective-permute-start(bf16[256,512]{1,0:T(8,128)(2,1)S(1)} %get-tuple-element.53), channel_id=1, source_target_pairs={{2,0},{3,1},{4,2},{5,3},{6,4},{7,5},{8,6},{9,7},{10,8},{11,9},{12,... | collective-permute-start | bytes 786440 | tf_op jit(solution)/shard_map/ppermute | solution.py:34
  41.2 4.0 %near_grads.1 = (f32[256,512]{1,0:T(8,128)S(1)}, f32[256,512]{1,0:T(8,128)S(1)}, f32[256,512]{1,0:T(8,128)S(1)}, f32[256,512]{1,0:T(8,128)S(1)}, bf16[128,1024]{...) custom-call(s32[1]{0:T(128)} %bitcast.core_ref, s32[8,128]{1,0:T(8,128)S(1)} %get-tuple-element.37.lo_ref, ...), custom_call_target="tpu_custom_call" | custom-call | tf_op jit(solution)/shard_map/near_grads/pallas_call | solution.py:302
  45.2 1.1 %collective-permute-done.10.came = bf16[256,512]{1,0:T(8,128)(2,1)S(1)} collective-permute-done((bf16[256,512]{1,0:T(8,128)(2,1)S(1)}, bf16[256,512]{1,0:T(8,128)(2,1)S(1)}, u32[]{:S(2)}, u32[]{:S(2)}) %collective-permute-start.10) | collective-permute-done | bytes 262176 | tf_op jit(solution)/shard_map/ppermute | solution.py:34
  46.4 3.3 %collective-permute-start.16 = (bf16[256,512]{1,0:T(8,128)(2,1)S(1)}, bf16[256,512]{1,0:T(8,128)(2,1)S(1)}, u32[]{:S(2)}, u32[]{:S(2)}) collective-permute-start(bf16[256,512]{1,0:T(8,128)(2,1)S(1)} %merge.1), channel_id=1, source_target_pairs={{2,0},{3,1},{4,2},{5,3},{6,4},{7,5},{8,6},{9,7},{10,8},{11,9},{12,... | collective-permute-start | bytes 786440 | tf_op jit(solution)/shard_map/ppermute | solution.py:34
  50.4 0.7 %collective-permute-done.12.came = bf16[256,512]{1,0:T(8,128)(2,1)S(1)} collective-permute-done((bf16[256,512]{1,0:T(8,128)(2,1)S(1)}, bf16[256,512]{1,0:T(8,128)(2,1)S(1)}, u32[]{:S(2)}, u32[]{:S(2)}) %collective-permute-start.12) | collective-permute-done | bytes 262176 | tf_op jit(solution)/shard_map/ppermute | solution.py:34
  51.2 1.9 %collective-permute-start.15 = (bf16[128,512]{1,0:T(8,128)(2,1)S(1)}, bf16[128,512]{1,0:T(8,128)(2,1)S(1)}, u32[]{:S(2)}, u32[]{:S(2)}) collective-permute-start(bf16[128,512]{1,0:T(8,128)(2,1)S(1)} %get-tuple-element.55), channel_id=1, source_target_pairs={{2,1},{3,0},{4,3},{5,2},{6,5},{7,4},{8,7},{9,6},{10,9},{11,8},{12,... | collective-permute-start | bytes 393224 | tf_op jit(solution)/shard_map/ppermute | solution.py:40
  53.1 2.7 %collective-permute-start.13 = (bf16[128,512]{1,0:T(8,128)(2,1)S(1)}, bf16[128,512]{1,0:T(8,128)(2,1)S(1)}, u32[]{:S(2)}, u32[]{:S(2)}) collective-permute-start(bf16[128,512]{1,0:T(8,128)(2,1)S(1)} %get-tuple-element.54), channel_id=1, source_target_pairs={{2,0},{3,1},{4,2},{5,3},{6,4},{7,5},{8,6},{9,7},{10,8},{11,9},{12,... | collective-permute-start | bytes 393224 | tf_op jit(solution)/shard_map/ppermute | solution.py:34
  55.8 2.5 %collective-permute-done.16 = bf16[256,512]{1,0:T(8,128)(2,1)S(1)} collective-permute-done((bf16[256,512]{1,0:T(8,128)(2,1)S(1)}, bf16[256,512]{1,0:T(8,128)(2,1)S(1)}, u32[]{:S(2)}, u32[]{:S(2)}) %collective-permute-start.16) | collective-permute-done | bytes 262176 | tf_op jit(solution)/shard_map/ppermute | solution.py:34
  58.5 0.8 %pad_maximum_fusion.1 = bf16[128,2048]{1,0:T(8,128)(2,1)} fusion(bf16[128,1024]{1,0:T(8,128)(2,1)S(1)} %get-tuple-element.62, bf16[128,1024]{1,0:T(8,128)(2,1)S(1)} %get-tuple-element.61), kind=kLoop, calls=%fused_computation.3 | loop fusion | flops 1048576 | bytes 1048576 | tf_op jit(solution)/shard_map/concatenate | solution.py:377
  59.8 0.7 %pad_maximum_fusion.3 = bf16[128,1024]{1,0:T(8,128)(2,1)} fusion(bf16[128,512]{1,0:T(8,128)(2,1)S(1)} %get-tuple-element.64, bf16[128,512]{1,0:T(8,128)(2,1)S(1)} %get-tuple-element.63), kind=kLoop, calls=%fused_computation.7 | loop fusion | flops 524288 | bytes 524288 | tf_op jit(solution)/shard_map/concatenate | solution.py:377
  60.6 1.4 %collective-permute-done.15 = bf16[128,512]{1,0:T(8,128)(2,1)S(1)} collective-permute-done((bf16[128,512]{1,0:T(8,128)(2,1)S(1)}, bf16[128,512]{1,0:T(8,128)(2,1)S(1)}, u32[]{:S(2)}, u32[]{:S(2)}) %collective-permute-start.15) | collective-permute-done | bytes 131104 | tf_op jit(solution)/shard_map/ppermute | solution.py:40
  61.9 2.8 %collective-permute-done.13 = bf16[128,512]{1,0:T(8,128)(2,1)S(1)} collective-permute-done((bf16[128,512]{1,0:T(8,128)(2,1)S(1)}, bf16[128,512]{1,0:T(8,128)(2,1)S(1)}, u32[]{:S(2)}, u32[]{:S(2)}) %collective-permute-start.13) | collective-permute-done | bytes 131104 | tf_op jit(solution)/shard_map/ppermute | solution.py:34
  (45 shorter events, 5.8 us)
Async XLA Ops:
  0.6 1.8 %collective-permute-start = (bf16[128,1024]{1,0:T(8,128)(2,1)}, bf16[128,1024]{1,0:T(8,128)(2,1)S(1)}, u32[]{:S(2)}, u32[]{:S(2)}) collective-permute-start(bf16[128,1024]{1,0:T(8,128)(2,1)} %param.6), channel_id=1, source_target_pairs={{0,1},{1,0},{2,3},{3,2},{4,5},{5,4},{6,7},{7,6},{8,9},{9,8},{10,11... | collective-permute-start | bytes 786440 | tf_op jit(solution)/shard_map/ppermute | solution.py:28
  0.7 1.7 %collective-permute-start.1 = (s32[128]{0:T(128)}, s32[128]{0:T(128)S(1)}, u32[]{:S(2)}, u32[]{:S(2)}) collective-permute-start(s32[128]{0:T(128)} %param.9), channel_id=1, source_target_pairs={{0,1},{1,0},{2,3},{3,2},{4,5},{5,4},{6,7},{7,6},{8,9},{9,8},{10,11... | collective-permute-start | bytes 1544 | tf_op jit(solution)/shard_map/ppermute | solution.py:28
  1.2 6.1 %collective-permute-start.2 = (bf16[128,1024]{1,0:T(8,128)(2,1)}, bf16[128,1024]{1,0:T(8,128)(2,1)S(1)}, u32[]{:S(2)}, u32[]{:S(2)}) collective-permute-start(bf16[128,1024]{1,0:T(8,128)(2,1)} %param.7), channel_id=1, source_target_pairs={{0,1},{1,0},{2,3},{3,2},{4,5},{5,4},{6,7},{7,6},{8,9},{9,8},{10,11... | collective-permute-start | bytes 786440 | tf_op jit(solution)/shard_map/ppermute | solution.py:28
  1.3 1.2 %copy-start.3 = (s32[128]{0:T(128)S(1)}, s32[128]{0:T(128)}, u32[]{:S(2)}) copy-start(s32[128]{0:T(128)} %param.9) | copy-start | bytes 1540
  1.3 5.0 %copy-start = (bf16[128,2048]{1,0:T(8,128)(2,1)S(1)}, bf16[128,2048]{1,0:T(8,128)(2,1)}, u32[]{:S(2)}) copy-start(bf16[128,2048]{1,0:T(8,128)(2,1)} %q) | copy-start | bytes 1572868
  1.3 5.0 %copy-start.1 = (bf16[128,2048]{1,0:T(8,128)(2,1)S(1)}, bf16[128,2048]{1,0:T(8,128)(2,1)}, u32[]{:S(2)}) copy-start(bf16[128,2048]{1,0:T(8,128)(2,1)} %go) | copy-start | bytes 1572868
  2.5 10.6 %collective-permute-start.5 = (bf16[264,512]{1,0:T(8,128)(2,1)S(1)}, bf16[264,512]{1,0:T(8,128)(2,1)S(1)}, u32[]{:S(2)}, u32[]{:S(2)}) collective-permute-start(bf16[264,512]{1,0:T(8,128)(2,1)S(1)} %fusion.1.kc), channel_id=1, source_target_pairs={{0,2},{1,3},{2,4},{3,5},{4,6},{5,7},{6,8},{7,9},{8,10},{9,11},{10,... | collective-permute-start | bytes 811016 | tf_op jit(solution)/shard_map/ppermute | solution.py:34
  5.6 25.3 %collective-permute-start.7 = (bf16[264,512]{1,0:T(8,128)(2,1)S(1)}, bf16[264,512]{1,0:T(8,128)(2,1)S(1)}, u32[]{:S(2)}, u32[]{:S(2)}) collective-permute-start(bf16[264,512]{1,0:T(8,128)(2,1)S(1)} %fusion.1.kc), channel_id=1, source_target_pairs={{4,8},{5,9},{12,16},{13,17},{20,24},{21,25}} | collective-permute-start | bytes 811016 | tf_op jit(solution)/shard_map/ppermute | solution.py:50
  6.3 1.0 %copy-start.2 = (bf16[128,1024]{1,0:T(8,128)(2,1)S(1)}, bf16[128,1024]{1,0:T(8,128)(2,1)}, u32[]{:S(2)}) copy-start(bf16[128,1024]{1,0:T(8,128)(2,1)} %param.7) | copy-start | bytes 786436
  6.4 15.5 %collective-permute-start.4 = (bf16[256,1024]{1,0:T(8,128)(2,1)S(1)}, bf16[256,1024]{1,0:T(8,128)(2,1)S(1)}, u32[]{:S(2)}, u32[]{:S(2)}) collective-permute-start(bf16[256,1024]{1,0:T(8,128)(2,1)S(1)} %pad_maximum_fusion), channel_id=1, source_target_pairs={{0,1},{1,0},{2,3},{3,2},{4,5},{5,4},{6,7},{7,6},{8,9},{9,8},{10,11... | collective-permute-start | bytes 1572872 | tf_op jit(solution)/shard_map/ppermute | solution.py:28
  13.1 17.8 %collective-permute-start.6 = (bf16[264,512]{1,0:T(8,128)(2,1)S(1)}, bf16[264,512]{1,0:T(8,128)(2,1)S(1)}, u32[]{:S(2)}, u32[]{:S(2)}) collective-permute-start(bf16[264,512]{1,0:T(8,128)(2,1)S(1)} %collective-permute-done.5.ka), channel_id=1, source_target_pairs={{0,2},{1,3},{2,4},{3,5},{4,6},{5,7},{8,10},{9,11},{10,12},{11,13},... | collective-permute-start | bytes 811016 | tf_op jit(solution)/shard_map/ppermute | solution.py:45
  14.4 14.1 %collective-permute-start.3 = (bf16[256,512]{1,0:T(8,128)(2,1)S(1)}, bf16[256,512]{1,0:T(8,128)(2,1)S(1)}, u32[]{:S(2)}, u32[]{:S(2)}) collective-permute-start(bf16[256,512]{1,0:T(8,128)(2,1)S(1)} %pad_maximum_fusion.2.vc), channel_id=1, source_target_pairs={{0,2},{1,3},{2,4},{3,5},{4,6},{5,7},{6,8},{7,9},{8,10},{9,11},{10,... | collective-permute-start | bytes 786440 | tf_op jit(solution)/shard_map/ppermute | solution.py:34
  21.2 15.4 %collective-permute-start.9 = (bf16[256,512]{1,0:T(8,128)(2,1)S(1)}, bf16[256,512]{1,0:T(8,128)(2,1)S(1)}, u32[]{:S(2)}, u32[]{:S(2)}) collective-permute-start(bf16[256,512]{1,0:T(8,128)(2,1)S(1)} %pad_maximum_fusion.2.vc), channel_id=1, source_target_pairs={{4,8},{5,9},{12,16},{13,17},{20,24},{21,25}} | collective-permute-start | bytes 786440 | tf_op jit(solution)/shard_map/ppermute | solution.py:50
  28.5 8.9 %collective-permute-start.8 = (bf16[256,512]{1,0:T(8,128)(2,1)S(1)}, bf16[256,512]{1,0:T(8,128)(2,1)S(1)}, u32[]{:S(2)}, u32[]{:S(2)}) collective-permute-start(bf16[256,512]{1,0:T(8,128)(2,1)S(1)} %collective-permute-done.3.va), channel_id=1, source_target_pairs={{0,2},{1,3},{2,4},{3,5},{4,6},{5,7},{8,10},{9,11},{10,12},{11,13},... | collective-permute-start | bytes 786440 | tf_op jit(solution)/shard_map/ppermute | solution.py:45
  32.1 14.3 %collective-permute-start.10 = (bf16[256,512]{1,0:T(8,128)(2,1)S(1)}, bf16[256,512]{1,0:T(8,128)(2,1)S(1)}, u32[]{:S(2)}, u32[]{:S(2)}) collective-permute-start(bf16[256,512]{1,0:T(8,128)(2,1)S(1)} %get-tuple-element.49), channel_id=1, source_target_pairs={{2,0},{3,1},{4,2},{5,3},{6,4},{7,5},{8,6},{9,7},{10,8},{11,9},{12,... | collective-permute-start | bytes 786440 | tf_op jit(solution)/shard_map/ppermute | solution.py:34
  39.0 12.1 %collective-permute-start.12 = (bf16[256,512]{1,0:T(8,128)(2,1)S(1)}, bf16[256,512]{1,0:T(8,128)(2,1)S(1)}, u32[]{:S(2)}, u32[]{:S(2)}) collective-permute-start(bf16[256,512]{1,0:T(8,128)(2,1)S(1)} %get-tuple-element.53), channel_id=1, source_target_pairs={{2,0},{3,1},{4,2},{5,3},{6,4},{7,5},{8,6},{9,7},{10,8},{11,9},{12,... | collective-permute-start | bytes 786440 | tf_op jit(solution)/shard_map/ppermute | solution.py:34
  46.4 11.9 %collective-permute-start.16 = (bf16[256,512]{1,0:T(8,128)(2,1)S(1)}, bf16[256,512]{1,0:T(8,128)(2,1)S(1)}, u32[]{:S(2)}, u32[]{:S(2)}) collective-permute-start(bf16[256,512]{1,0:T(8,128)(2,1)S(1)} %merge.1), channel_id=1, source_target_pairs={{2,0},{3,1},{4,2},{5,3},{6,4},{7,5},{8,6},{9,7},{10,8},{11,9},{12,... | collective-permute-start | bytes 786440 | tf_op jit(solution)/shard_map/ppermute | solution.py:34
  49.7 8.8 %collective-permute-start.11 = (bf16[128,1024]{1,0:T(8,128)(2,1)S(1)}, bf16[128,1024]{1,0:T(8,128)(2,1)S(1)}, u32[]{:S(2)}, u32[]{:S(2)}) collective-permute-start(bf16[128,1024]{1,0:T(8,128)(2,1)S(1)} %get-tuple-element.50), channel_id=1, source_target_pairs={{0,1},{1,0},{2,3},{3,2},{4,5},{5,4},{6,7},{7,6},{8,9},{9,8},{10,11... | collective-permute-start | bytes 786440 | tf_op jit(solution)/shard_map/ppermute | solution.py:28
  49.8 12.1 %collective-permute-start.14 = (f32[128,512]{1,0:T(8,128)S(1)}, f32[128,512]{1,0:T(8,128)S(1)}, u32[]{:S(2)}, u32[]{:S(2)}) collective-permute-start(f32[128,512]{1,0:T(8,128)S(1)} %slice.15), channel_id=1, source_target_pairs={{0,1},{1,0},{2,3},{3,2},{4,5},{5,4},{6,7},{7,6},{8,9},{9,8},{10,11... | collective-permute-start | bytes 786440 | tf_op jit(solution)/shard_map/ppermute | solution.py:28
  51.2 10.8 %collective-permute-start.15 = (bf16[128,512]{1,0:T(8,128)(2,1)S(1)}, bf16[128,512]{1,0:T(8,128)(2,1)S(1)}, u32[]{:S(2)}, u32[]{:S(2)}) collective-permute-start(bf16[128,512]{1,0:T(8,128)(2,1)S(1)} %get-tuple-element.55), channel_id=1, source_target_pairs={{2,1},{3,0},{4,3},{5,2},{6,5},{7,4},{8,7},{9,6},{10,9},{11,8},{12,... | collective-permute-start | bytes 393224 | tf_op jit(solution)/shard_map/ppermute | solution.py:40
  53.1 11.6 %collective-permute-start.13 = (bf16[128,512]{1,0:T(8,128)(2,1)S(1)}, bf16[128,512]{1,0:T(8,128)(2,1)S(1)}, u32[]{:S(2)}, u32[]{:S(2)}) collective-permute-start(bf16[128,512]{1,0:T(8,128)(2,1)S(1)} %get-tuple-element.54), channel_id=1, source_target_pairs={{2,0},{3,1},{4,2},{5,3},{6,4},{7,5},{8,6},{9,7},{10,8},{11,9},{12,... | collective-permute-start | bytes 393224 | tf_op jit(solution)/shard_map/ppermute | solution.py:34
  58.4 1.4 %collective-permute-start.17 = (bf16[128,512]{1,0:T(8,128)(2,1)S(1)}, bf16[128,512]{1,0:T(8,128)(2,1)S(1)}, u32[]{:S(2)}, u32[]{:S(2)}) collective-permute-start(bf16[128,512]{1,0:T(8,128)(2,1)S(1)} %slice.19), channel_id=1, source_target_pairs={{0,1},{1,0},{2,3},{3,2},{4,5},{5,4},{6,7},{7,6},{8,9},{9,8},{10,11... | collective-permute-start | bytes 393224 | tf_op jit(solution)/shard_map/ppermute | solution.py:28
